TPU v7x, 32 devices: a whole 2x2x4 slice. The times are simulated.
32 devices in a mesh: runs: 2 (over y), gx: 16 (over z, x, core).
Axes of the slice: x: 2, y: 2, z: 4, core: 2. Of those that a mesh axis runs over, the one named last changes fastest.
Arguments:
- blocks: float32 [2048, 5, 512], P(('runs', 'gx')), parts along dimension 0, as said below
- owner_list: int32 [2048], P('runs'), parts along dimension 0, may hold values from 0 to 15, as said below
- slot_list: int32 [2048], P('runs'), parts along dimension 0, may hold values from 0 to 63, as said below
Outputs:
- advanced: float32 [5, 256, 32, 128], P(None, ('runs', 'gx')), parts along dimension 1
There are 2 independent parts, one for each index of `runs`. A program takes and returns all parts, laid end to end along the dimension named above; each array names one. Nothing has to cross between parts.
Inputs may be any that keep to these rules, and one draw needn't show every extreme that they name: `owner_list`: entry i names block i's new owner; the 64 blocks listed for one device (entries in aligned groups of 64) go to 8 distinct devices, exactly 8 to each, and every device receives 64 blocks. The pairs (owner_list[i], slot_list[i]) are all distinct. `blocks`: density and pressure are positive in every cell.
All inputs are finite; a program needn't handle non-finite values.
Results may differ from a plain program's by a relative error of at most 0.00002.
Values sent between devices are 32-bit elements; how exact they have to be, the bound alone decides.
No kernel may reach another device: no remote copies, remote signals or barrier semaphores. Data moves between devices by JAX's collectives and lax.ppermute only.
A program may use at most 64 MiB of HBM per device.

v0:
```python
import jax
import jax.numpy as jnp
from jax import lax
from jax.sharding import PartitionSpec as P

BLOCK = 8
BY = 4
BZ = 16


gamma_gas = 1.4
courant = 0.25
smooth_epsilon = 1e-06


def padded_2(shard, sides, width):
    for axis, dim in sides:
        size, length = (lax.axis_size(axis), shard.shape[dim])
        up = [(i, (i + 1) % size) for i in range(size)]
        down = [(j, i) for i, j in up]
        last = lax.slice_in_dim(shard, length - width, length, axis=dim)
        leading = lax.slice_in_dim(shard, 0, width, axis=dim)
        before = lax.ppermute(last, axis, up)
        after = lax.ppermute(leading, axis, down)
        shard = jnp.concatenate([before, shard, after], axis=dim)
    return shard


def primitive(fields):
    density = fields[0]
    velocity = (fields[1] / density, fields[2] / density, fields[3] / density)
    kinetic = 0.5 * (fields[1] * velocity[0] + fields[2] * velocity[1] + fields[3] * velocity[2])
    pressure = (gamma_gas - 1.0) * (fields[4] - kinetic)
    return (density, velocity, pressure)


def wave_speed(fields):
    density, velocity, pressure = primitive(fields)
    sound_speed = jnp.sqrt(gamma_gas * pressure / density)
    fastest = jnp.maximum(
        jnp.maximum(jnp.abs(velocity[0]), jnp.abs(velocity[1])), jnp.abs(velocity[2])
    )
    return fastest + sound_speed


def euler_flux(conserved, direction):
    density, velocity, pressure = primitive(conserved)
    normal_speed = velocity[direction]
    components = [
        conserved[1 + direction],
        conserved[1] * normal_speed,
        conserved[2] * normal_speed,
        conserved[3] * normal_speed,
        (conserved[4] + pressure) * normal_speed,
    ]
    components[1 + direction] = components[1 + direction] + pressure
    return jnp.stack(components, axis=0)


def split_flux(conserved, direction, speed_max):
    flux_total = euler_flux(conserved, direction)
    return (0.5 * (flux_total + speed_max * conserved), 0.5 * (flux_total - speed_max * conserved))


def reconstruct(outer_left, inner_left, centre, inner_right, outer_right):
    smooth_zero = (
        13.0 / 12.0 * (outer_left - 2.0 * inner_left + centre) ** 2
        + 0.25 * (outer_left - 4.0 * inner_left + 3.0 * centre) ** 2
    )
    smooth_one = (
        13.0 / 12.0 * (inner_left - 2.0 * centre + inner_right) ** 2
        + 0.25 * (inner_left - inner_right) ** 2
    )
    smooth_two = (
        13.0 / 12.0 * (centre - 2.0 * inner_right + outer_right) ** 2
        + 0.25 * (3.0 * centre - 4.0 * inner_right + outer_right) ** 2
    )
    guess_zero = (2.0 * outer_left - 7.0 * inner_left + 11.0 * centre) / 6.0
    guess_one = (-inner_left + 5.0 * centre + 2.0 * inner_right) / 6.0
    guess_two = (2.0 * centre + 5.0 * inner_right - outer_right) / 6.0
    weight_zero = 0.1 / (smooth_epsilon + smooth_zero) ** 2
    weight_one = 0.6 / (smooth_epsilon + smooth_one) ** 2
    weight_two = 0.3 / (smooth_epsilon + smooth_two) ** 2
    return (weight_zero * guess_zero + weight_one * guess_one + weight_two * guess_two) / (
        weight_zero + weight_one + weight_two
    )


def rolled_divergence(conserved, direction, speed_max):
    flux_plus, flux_minus = split_flux(conserved, direction, speed_max)
    axis_pos = direction + 1

    def rolled(values, amount):
        return jnp.roll(values, amount, axis=axis_pos)

    face_flux = reconstruct(
        rolled(flux_plus, 3),
        rolled(flux_plus, 2),
        rolled(flux_plus, 1),
        flux_plus,
        rolled(flux_plus, -1),
    ) + reconstruct(
        rolled(flux_minus, -2),
        rolled(flux_minus, -1),
        flux_minus,
        rolled(flux_minus, 1),
        rolled(flux_minus, 2),
    )
    return jnp.roll(face_flux, -1, axis=axis_pos) - face_flux


def window(values, offset, length):
    return values[:, offset : offset + length + 1]


def padded_divergence(padded, speed_max):
    length = padded.shape[1] - 6
    flux_plus, flux_minus = split_flux(padded, 0, speed_max)
    face_flux = reconstruct(
        window(flux_plus, 0, length),
        window(flux_plus, 1, length),
        window(flux_plus, 2, length),
        window(flux_plus, 3, length),
        window(flux_plus, 4, length),
    ) + reconstruct(
        window(flux_minus, 5, length),
        window(flux_minus, 4, length),
        window(flux_minus, 3, length),
        window(flux_minus, 2, length),
        window(flux_minus, 1, length),
    )
    return face_flux[:, 1:] - face_flux[:, :-1]


def tendency(padded, speed_max):
    length = padded.shape[1] - 6
    interior = padded[:, 3 : 3 + length]
    return -(
        padded_divergence(padded, speed_max)
        + rolled_divergence(interior, 1, speed_max)
        + rolled_divergence(interior, 2, speed_max)
    )


def ghost_cells(conserved):
    return padded_2(conserved, (("gx", 1),), 3)


def middle_maximum(conserved):
    return lax.pmax(jnp.max(wave_speed(conserved)), "gx")


def per_device(blocks, owner_list, slot_list):
    dev_count = lax.axis_size("gx")
    own_index = lax.axis_index("gx")
    per_dev = blocks.shape[0]
    capacity = max(2, 2 * per_dev // dev_count)
    owner_grid = owner_list.reshape(dev_count, per_dev)
    same_owner = owner_grid[:, :, None] == owner_grid[:, None, :]
    positions = jnp.arange(per_dev)
    earlier = positions[None, :] < positions[:, None]
    slot_ranks = jnp.sum(same_owner & earlier[None], axis=2).reshape(-1)
    everyone = jnp.arange(owner_list.shape[0], dtype=jnp.int32)
    inverse = jnp.zeros_like(owner_list).at[owner_list * per_dev + slot_list].set(everyone)
    holders = lax.dynamic_slice_in_dim(inverse, own_index * per_dev, per_dev)
    source_dev = holders // per_dev
    source_slot = holders % per_dev
    source_rank = slot_ranks[holders]
    my_owner = lax.dynamic_slice_in_dim(owner_list, own_index * per_dev, per_dev)
    my_rank = lax.dynamic_slice_in_dim(slot_ranks, own_index * per_dev, per_dev)
    send_row = jnp.where(my_owner == own_index, dev_count * capacity, my_owner * capacity + my_rank)
    outgoing = (
        jnp.zeros((dev_count * capacity,) + blocks.shape[1:], blocks.dtype)
        .at[send_row]
        .set(blocks, mode="drop")
    )
    incoming = lax.all_to_all(outgoing, "gx", split_axis=0, concat_axis=0, tiled=True)
    candidates = jnp.concatenate([blocks, incoming], axis=0)
    take_row = jnp.where(
        source_dev == own_index, source_slot, per_dev + source_dev * capacity + source_rank
    )
    arranged = candidates[take_row]
    slab_state = (
        arranged.reshape(BY, BZ, 5, BLOCK, BLOCK, BLOCK)
        .transpose(2, 3, 0, 4, 1, 5)
        .reshape(5, BLOCK, BY * BLOCK, BZ * BLOCK)
    )
    local_speed = jnp.max(wave_speed(slab_state))
    first_max = lax.pmax(local_speed, "gx")
    step_size = courant / first_max
    middle = slab_state + step_size * tendency(ghost_cells(slab_state), first_max)
    second_max = middle_maximum(middle)
    result_state = 0.5 * slab_state + 0.5 * (
        middle + step_size * tendency(ghost_cells(middle), second_max)
    )
    return result_state


def solution(mesh):
    return jax.shard_map(
        per_device,
        mesh=mesh,
        in_specs=(P(("runs", "gx"), None, None), P("runs"), P("runs")),
        out_specs=P(None, ("runs", "gx"), None, None),
        check_vma=False,
    )
```

profile of v0, /device:TPU:0, one launch (start us, length us, event | category | flops | bytes accessed | tf_op | source)
XLA Modules:
  0.0 244.8 jit_solution(12609507487624193129)
XLA Ops:
  3.6 4.3 %scatter_custom_fusion.1 = s32[1024]{0:T(1024)S(1)} fusion(s32[1024]{0:T(1024)S(1)} %compare_select_fusion, s32[1024]{0:T(1024)S(1)} %iota.17, s32[]{:T(128)} %constant.142.clone.1), kind=kCustom, calls=%fused_computation.174 | custom fusion | bytes 4100 | tf_op jit(solution)/shard_map/scatter | solution.py:164
  10.3 8.1 %scatter_fusion = f32[128,5,512]{2,1,0:T(8,128)} fusion(f32[128,5,512]{2,1,0:T(8,128)} %broadcast_in_dim.22, s32[64]{0:T(128)S(1)} %get-tuple-element.100, f32[64,5,512]{2,1,0:T(8,128)S(1)} %copy.24), kind=kCustom, calls=%fused_computation.2 | custom fusion | bytes 1966336 | tf_op jit(solution)/shard_map/scatter | solution.py:175
  18.4 7.4 %all-to-all-start = ((f32[128,5,512]{2,1,0:T(8,128)}), f32[128,5,512]{2,1,0:T(8,128)}, u32[]{:S(2)}, u32[]{:S(2)}) async-start(f32[128,5,512]{2,1,0:T(8,128)} %scatter_fusion), calls=%async_computation | async-start | bytes 4194304 | tf_op jit(solution)/shard_map/all_to_all | solution.py:177
  26.7 40.3 %all-to-all-done = f32[128,5,512]{2,1,0:T(8,128)} async-done(((f32[128,5,512]{2,1,0:T(8,128)}), f32[128,5,512]{2,1,0:T(8,128)}, u32[]{:S(2)}, u32[]{:S(2)}) %all-to-all-start) | async-done | bytes 1310752 | tf_op jit(solution)/shard_map/all_to_all | solution.py:177
  67.0 3.6 %pad_maximum_fusion = f32[192,5,512]{2,1,0:T(8,128)} fusion(f32[128,5,512]{2,1,0:T(8,128)} %all-to-all-done, f32[64,5,512]{2,1,0:T(8,128)S(1)} %copy.24), kind=kLoop, calls=%fused_computation.5 | loop fusion | flops 491520 | bytes 3932160 | tf_op jit(solution)/shard_map/concatenate | solution.py:178
  70.6 2.5 %gather_fusion.1 = f32[64,5,512]{2,1,0:T(8,128)S(1)} fusion(f32[192,5,512]{2,1,0:T(8,128)} %pad_maximum_fusion, s32[1024]{0:T(1024)S(1)} %pad_clamp_fusion), kind=kCustom, calls=%fused_computation.1 | custom fusion | bytes 1310976 | tf_op jit(solution)/shard_map/gather | solution.py:182
  73.6 3.8 %reshape.333 = f32[4,16,5,8,8,8]{1,0,5,4,3,2:T(4,128)} reshape(f32[64,5,512]{0,2,1:T(8,128)S(1)} %copy.25) | data formatting | bytes 1310720 | tf_op jit(solution)/shard_map/reshape | solution.py:184
  77.4 9.4 %copy.33 = f32[4,16,5,8,8,8]{5,1,4,0,3,2:T(8,128)} copy(f32[4,16,5,8,8,8]{1,0,5,4,3,2:T(4,128)} %reshape.333) | data formatting | bytes 1310720 | tf_op jit(solution)/shard_map/transpose | solution.py:185
  86.8 5.6 %copy.35 = f32[4,16,5,8,8,8]{1,5,4,0,3,2:T(8,128)} copy(f32[4,16,5,8,8,8]{1,0,5,4,3,2:T(4,128)} %reshape.333) | data formatting | bytes 1310720 | tf_op jit(solution)/shard_map/reshape | solution.py:184
  92.5 8.0 %reshape.334 = f32[5,8,32,128]{3,2,1,0:T(8,128)S(1)} reshape(f32[5,8,4,8,16,8]{5,4,3,2,1,0:T(8,128)} %bitcast.90) | data formatting | bytes 1310720 | tf_op jit(solution)/shard_map/reshape | solution.py:186
  100.5 6.9 %fusion.45 = (f32[1,8,4,8,16,8]{4,5,3,2,1,0:T(8,128)}, f32[]{:T(128)}, f32[1,8,4,8,16,8]{4,5,3,2,1,0:T(8,128)}, f32[1,8,4,8,16,8]{4,5,3,2,1,0:T(8,128)}, f32[1,8...) fusion(f32[5,8,4,8,16,8]{4,5,3,2,1,0:T(8,128)} %bitcast.91), kind=kLoop, calls=%fused_computation.184 | loop fusion | flops 622591 | bytes 1310724 | tf_op jit(solution)/shard_map/slice | solution.py:31
  113.8 1.9 copy.30
  116.7 1.9 copy.28
  126.0 39.8 %pmax.14 = f32[]{:T(128)} all-reduce(f32[]{:T(128)} %get-tuple-element.17), channel_id=1, replica_groups=mesh['runs'=2,'gx'=16] {'gx'}, use_global_device_ids=true, to_apply=%region_4.5 | all-reduce | flops 1 | bytes 8 | tf_op jit(solution)/shard_map/pmax | solution.py:189
  166.0 4.4 %collective-permute-start.1 = (f32[5,3,32,128]{3,2,1,0:T(8,128)S(1)}, f32[5,3,32,128]{3,2,1,0:T(8,128)S(1)}, u32[]{:S(2)}, u32[]{:S(2)}) collective-permute-start(f32[5,3,32,128]{3,2,1,0:T(8,128)S(1)} %get-tuple-element.96), channel_id=1, source_target_pairs={{1,0},{2,1},{3,2},{4,3},{5,4},{6,5},{7,6},{8,7},{9,8},{10,9},{11,1... | collective-permute-start | bytes 737288 | tf_op jit(solution)/shard_map/ppermute | solution.py:24
  171.8 2.4 %collective-permute-done = f32[5,3,32,128]{3,2,1,0:T(8,128)S(1)} collective-permute-done((f32[5,3,32,128]{3,2,1,0:T(8,128)S(1)}, f32[5,3,32,128]{3,2,1,0:T(8,128)S(1)}, u32[]{:S(2)}, u32[]{:S(2)}) %collective-permute-start) | collective-permute-done | bytes 245792 | tf_op jit(solution)/shard_map/ppermute | solution.py:23
  174.3 2.1 broadcast_multiply_fusion.5
  177.9 4.3 %divide_add_fusion.5 = f32[5,8,32,128]{3,2,1,0:T(8,128)S(1)} fusion(f32[5,8,30,128]{3,2,1,0:T(8,128)S(1)} %get-tuple-element.93, f32[5,8,2,128]{3,2,1,0:T(2,128)S(1)} %get-tuple-element.95, f32[5,8,31,128]{3,2,1,0:T(8,128)S(1)} %get-tuple-element.89, f32[5,8,1,128]{3,2,1,0:T(1,128)S(1)} %get-tuple-element.91, f32[5,8,2,128]{3,2,1,0:T(2,128)S(1)} %get-tuple-element.94, ...), kind=kLoop, calls=%fused_computation.67 | loop fusion | flops 22937600 | bytes 7208964 | tf_op jit(solution)/shard_map/add | solution.py:96
  185.7 4.4 %divide_add_fusion.4 = f32[5,8,32,128]{3,2,1,0:T(8,128)S(1)} fusion(f32[5,8,32,126]{3,2,1,0:T(8,128)S(1)} %get-tuple-element.77, f32[5,8,32,2]{3,2,1,0:T(8,128)S(1)} %get-tuple-element.79, f32[5,8,32,127]{3,2,1,0:T(8,128)S(1)} %get-tuple-element.73, f32[5,8,32,1]{3,2,1,0:T(8,128)S(1)} %get-tuple-element.75, f32[5,8,32,2]{3,2,1,0:T(8,128)S(1)} %get-tuple-element.78, ...), kind=kLoop, calls=%fused_computation.66 | loop fusion | flops 22937600 | bytes 7208964 | tf_op jit(solution)/shard_map/add | solution.py:96
  190.3 3.3 %divide_add_fusion.1 = f32[5,9,32,128]{3,2,1,0:T(8,128)S(1)} fusion(f32[5,14,32,128]{3,2,1,0:T(8,128)S(1)} %get-tuple-element.25, f32[5,14,32,128]{3,2,1,0:T(8,128)S(1)} %get-tuple-element.24), kind=kLoop, calls=%fused_computation.13 | loop fusion | flops 23777280 | bytes 8110080 | tf_op jit(solution)/shard_map/add | solution.py:119
  195.0 30.1 %pmax.15 = f32[]{:T(128)} all-reduce(f32[]{:T(128)} %fusion.39), channel_id=1, replica_groups=mesh['runs'=2,'gx'=16] {'gx'}, use_global_device_ids=true, to_apply=%region_6.7 | all-reduce | flops 1 | bytes 8 | tf_op jit(solution)/shard_map/pmax | solution.py:150
  229.5 4.4 %divide_add_fusion.3 = f32[5,8,32,128]{3,2,1,0:T(8,128)S(1)} fusion(f32[5,8,30,128]{3,2,1,0:T(8,128)S(1)} %get-tuple-element.59, f32[5,8,2,128]{3,2,1,0:T(2,128)S(1)} %get-tuple-element.61, f32[5,8,31,128]{3,2,1,0:T(8,128)S(1)} %get-tuple-element.55, f32[5,8,1,128]{3,2,1,0:T(1,128)S(1)} %get-tuple-element.57, f32[5,8,2,128]{3,2,1,0:T(2,128)S(1)} %get-tuple-element.60, ...), kind=kLoop, calls=%fused_computation.65 | loop fusion | flops 22937600 | bytes 7208964 | tf_op jit(solution)/shard_map/add | solution.py:96
  233.8 4.4 %divide_add_fusion.2 = f32[5,8,32,128]{3,2,1,0:T(8,128)S(1)} fusion(f32[5,8,32,126]{3,2,1,0:T(8,128)S(1)} %get-tuple-element.47, f32[5,8,32,2]{3,2,1,0:T(8,128)S(1)} %get-tuple-element.49, f32[5,8,32,127]{3,2,1,0:T(8,128)S(1)} %get-tuple-element.43, f32[5,8,32,1]{3,2,1,0:T(8,128)S(1)} %get-tuple-element.45, f32[5,8,32,2]{3,2,1,0:T(8,128)S(1)} %get-tuple-element.48, ...), kind=kLoop, calls=%fused_computation.64 | loop fusion | flops 22937600 | bytes 7208964 | tf_op jit(solution)/shard_map/add | solution.py:96
  240.0 3.3 %divide_add_fusion = f32[5,9,32,128]{3,2,1,0:T(8,128)S(1)} fusion(f32[5,14,32,128]{3,2,1,0:T(8,128)S(1)} %get-tuple-element.23, f32[5,14,32,128]{3,2,1,0:T(8,128)S(1)} %get-tuple-element.22), kind=kLoop, calls=%fused_computation.12 | loop fusion | flops 23777280 | bytes 8110080 | tf_op jit(solution)/shard_map/add | solution.py:119
  (106 shorter events, 36.7 us)
Async XLA Ops:
  18.4 48.6 %all-to-all-start = ((f32[128,5,512]{2,1,0:T(8,128)}), f32[128,5,512]{2,1,0:T(8,128)}, u32[]{:S(2)}, u32[]{:S(2)}) async-start(f32[128,5,512]{2,1,0:T(8,128)} %scatter_fusion), calls=%async_computation | async-start | bytes 4194304 | tf_op jit(solution)/shard_map/all_to_all | solution.py:177
  125.4 45.7 %copy-start = (f32[5,8,32,128]{3,2,1,0:T(8,128)S(1)}, f32[5,8,32,128]{3,2,1,0:T(8,128)}, u32[]{:S(2)}) copy-start(f32[5,8,32,128]{3,2,1,0:T(8,128)} %get-tuple-element.82) | copy-start | bytes 1966084
  165.9 8.4 %collective-permute-start = (f32[5,3,32,128]{3,2,1,0:T(8,128)S(1)}, f32[5,3,32,128]{3,2,1,0:T(8,128)S(1)}, u32[]{:S(2)}, u32[]{:S(2)}) collective-permute-start(f32[5,3,32,128]{3,2,1,0:T(8,128)S(1)} %get-tuple-element.97), channel_id=1, source_target_pairs={{0,1},{1,2},{2,3},{3,4},{4,5},{5,6},{6,7},{7,8},{8,9},{9,10},{10,1... | collective-permute-start | bytes 737288 | tf_op jit(solution)/shard_map/ppermute | solution.py:23
  166.0 18.3 %collective-permute-start.1 = (f32[5,3,32,128]{3,2,1,0:T(8,128)S(1)}, f32[5,3,32,128]{3,2,1,0:T(8,128)S(1)}, u32[]{:S(2)}, u32[]{:S(2)}) collective-permute-start(f32[5,3,32,128]{3,2,1,0:T(8,128)S(1)} %get-tuple-element.96), channel_id=1, source_target_pairs={{1,0},{2,1},{3,2},{4,3},{5,4},{6,5},{7,6},{8,7},{9,8},{10,9},{11,1... | collective-permute-start | bytes 737288 | tf_op jit(solution)/shard_map/ppermute | solution.py:24
  176.8 1.1 copy-start.1
  228.9 9.7 %collective-permute-start.3 = (f32[5,3,32,128]{3,2,1,0:T(8,128)S(1)}, f32[5,3,32,128]{3,2,1,0:T(8,128)S(1)}, u32[]{:S(2)}, u32[]{:S(2)}) collective-permute-start(f32[5,3,32,128]{3,2,1,0:T(8,128)S(1)} %get-tuple-element.64), channel_id=1, source_target_pairs={{1,0},{2,1},{3,2},{4,3},{5,4},{6,5},{7,6},{8,7},{9,8},{10,9},{11,1... | collective-permute-start | bytes 737288 | tf_op jit(solution)/shard_map/ppermute | solution.py:24
  229.0 9.7 %collective-permute-start.2 = (f32[5,3,32,128]{3,2,1,0:T(8,128)S(1)}, f32[5,3,32,128]{3,2,1,0:T(8,128)S(1)}, u32[]{:S(2)}, u32[]{:S(2)}) collective-permute-start(f32[5,3,32,128]{3,2,1,0:T(8,128)S(1)} %get-tuple-element.63), channel_id=1, source_target_pairs={{0,1},{1,2},{2,3},{3,4},{4,5},{5,6},{6,7},{7,8},{8,9},{9,10},{10,1... | collective-permute-start | bytes 737288 | tf_op jit(solution)/shard_map/ppermute | solution.py:23
where the time goes:
time: 247 us; the launch traced here: 245 us
  blocking collectives  70 us (28%)
  local copies, waits for them, and re-layouts  69.4 us (28%)
  other arithmetic  49 us (20%)
  waiting for transfers between devices  42.8 us (17%)
  starting transfers between devices  12.5 us (5%)
    all_to_all x1, waiting for transfers between devices, per_device(): lax.all_to_all(outgoing, 'gx', split_axis=0, concat_axis=0, tiled=True)  40.3 us
    pmax x1, blocking collectives, per_device(): first_max = lax.pmax(local_speed, 'gx')  39.8 us
    pmax x1, blocking collectives, middle_maximum(): return lax.pmax(jnp.max(wave_speed(conserved)), 'gx')  30.1 us
    add x4, other arithmetic, rolled_divergence(): reconstruct(rolled(flux_plus, 3), rolled(flux_plus, 2), rolled(flux_plus,...  17.6 us
    transpose x1, local copies, waits for them, and re-layouts, per_device(): slab_state = arranged.reshape(BY, BZ, 5, BLOCK, BLOCK, BLOCK).transpose(2...  9.43 us
    reshape x2, local copies, waits for them, and re-layouts, per_device(): arranged.reshape(BY, BZ, 5, BLOCK, BLOCK, BLOCK).transpose(2, 3, 0, 4, 1, 5)  9.39 us
    scatter x1, local copies, waits for them, and re-layouts, per_device(): outgoing = jnp.zeros((dev_count * capacity,) + blocks.shape[1:], blocks.d...  8.13 us
    reshape x1, local copies, waits for them, and re-layouts, per_device(): slab_state = arranged.reshape(BY, BZ, 5, BLOCK, BLOCK, BLOCK).transpose(2...  8.03 us
  transfers between devices with their start and end apart: 5, of which 2 were waited for; matrix products, arithmetic and copies ran while one was open for 8% of the time, Pallas kernels for 0%

commit v1 on v0

v1 whole, which is shorter than its diff:
```python
import functools
import math

import jax
import jax.numpy as jnp
from jax import lax
from jax.experimental import pallas as pl
from jax.experimental.pallas import tpu as pltpu
from jax.sharding import PartitionSpec as P

BLOCK = 8
BY = 4
BZ = 16
FIELDS = 5
LANES = 128
ROWS = BY * BLOCK
CHUNKS = ((0, 3), (1, 2))

gamma_gas = 1.4
courant = 0.25
smooth_epsilon = 1e-06

VMEM = pl.BlockSpec(memory_space=pltpu.VMEM)
SMEM = pl.BlockSpec(memory_space=pltpu.SMEM)


def params():
    return pltpu.CompilerParams(vmem_limit_bytes=40 * 1024 * 1024)


def cost(flops, size):
    return pl.CostEstimate(flops=flops, bytes_accessed=size, transcendentals=0)


def wave_speed(fields):
    density, mom_x, mom_y, mom_z, energy = fields
    inverse = 1.0 / density
    vel = (mom_x * inverse, mom_y * inverse, mom_z * inverse)
    kinetic = 0.5 * (mom_x * vel[0] + mom_y * vel[1] + mom_z * vel[2])
    pressure = (gamma_gas - 1.0) * (energy - kinetic)
    sound = jnp.sqrt(gamma_gas * pressure * inverse)
    fastest = jnp.maximum(jnp.maximum(jnp.abs(vel[0]), jnp.abs(vel[1])), jnp.abs(vel[2]))
    return fastest + sound


def pack_kernel(dev_count, cap, per_dev, owner_ref, blocks_ref, out_a, out_b, count, best):
    own = lax.axis_index("gx")
    tiles = (2 * FIELDS + 1, 2 * FIELDS)
    outs = (out_a, out_b)

    def clear(dest, carry):
        count[dest] = 0
        return carry

    lax.fori_loop(0, dev_count, clear, 0)

    def place(block, carry):
        dest = owner_ref[own * per_dev + block]
        rank = count[dest]
        count[dest] = rank + 1
        for chunk in range(2):
            base = dest * (tiles[chunk] * cap) + rank
            for half in range(2):
                pair = CHUNKS[chunk][half]
                value = blocks_ref[block, :, pair * LANES : (pair + 1) * LANES]
                outs[chunk][pl.ds(base + half * FIELDS * cap, FIELDS, stride=cap), :] = value
        return carry

    lax.fori_loop(0, per_dev, place, 0, unroll=4)
    best[...] = jnp.zeros_like(best)

    def speeds(dest, carry):
        @pl.when(count[dest] > 0)
        def _():
            for chunk in range(2):
                for half in range(2):
                    base = dest * (tiles[chunk] * cap) + half * FIELDS * cap
                    fields = [
                        outs[chunk][pl.ds(pl.multiple_of(base + f * cap, cap), cap), :]
                        for f in range(FIELDS)
                    ]
                    best[...] = jnp.maximum(best[...], wave_speed(fields))

        return carry

    lax.fori_loop(0, dev_count, speeds, 0)
    top = jnp.full((cap, LANES), jnp.max(best[...]), jnp.float32)

    def publish(dest, carry):
        base = dest * (tiles[0] * cap) + 2 * FIELDS * cap
        out_a[pl.ds(pl.multiple_of(base, cap), cap), :] = top
        return carry

    lax.fori_loop(0, dev_count, publish, 0)


def pack(blocks, owner_list, dev_count, cap):
    per_dev = blocks.shape[0]
    rows_a = dev_count * cap * (2 * FIELDS + 1)
    rows_b = dev_count * cap * 2 * FIELDS
    return pl.pallas_call(
        functools.partial(pack_kernel, dev_count, cap, per_dev),
        out_shape=(
            jax.ShapeDtypeStruct((rows_a, LANES), jnp.float32),
            jax.ShapeDtypeStruct((rows_b, LANES), jnp.float32),
        ),
        in_specs=[SMEM, VMEM],
        out_specs=(VMEM, VMEM),
        scratch_shapes=[
            pltpu.SMEM((dev_count,), jnp.int32),
            pltpu.VMEM((cap, LANES), jnp.float32),
        ],
        compiler_params=params(),
        cost_estimate=cost(10_000_000, 3_000_000),
        name="pack",
    )(owner_list, blocks)


def arrival_rows(owner_list, slot_list, own, per_dev, dev_count, cap):
    owners = owner_list.reshape(dev_count, per_dev)
    slots = slot_list.reshape(dev_count, per_dev)
    mine = owners == own
    spot = jnp.arange(per_dev, dtype=jnp.int32)
    earlier = spot[None, :] < spot[:, None]
    rank = jnp.sum((mine[:, None, :] & earlier[None]).astype(jnp.int32), axis=2)
    row = jnp.arange(dev_count, dtype=jnp.int32)[:, None] * cap + rank
    key = jnp.where(mine, slots, -1)
    hit = key.reshape(1, -1) == spot[:, None]
    return jnp.max(jnp.where(hit, row.reshape(1, -1), 0), axis=1)


def transposed(rows, group):
    rows = list(rows)
    for bit in range(4):
        step = 1 << bit
        low = (group & step) == 0
        for index in range(16):
            if index & step:
                continue
            first, second = rows[index], rows[index | step]
            rows[index] = jnp.where(low, first, pltpu.roll(second, 8 * step, 1))
            rows[index | step] = jnp.where(low, pltpu.roll(first, LANES - 8 * step, 1), second)
    return rows


def unpack_kernel(dev_count, cap, chunk, table, in_ref, *refs):
    tiles = 2 * FIELDS + (1 if chunk == 0 else 0)
    if chunk == 0:
        state, low_halo, high_halo, speed, scratch = refs
    else:
        state, low_halo, high_halo, scratch = refs
    for slot in range(BY * BZ):
        p, q = divmod(slot, BZ)
        where = table[slot]
        base = (where // cap) * (tiles * cap) + where % cap
        for half in range(2):
            value = in_ref[pl.ds(base + half * FIELDS * cap, FIELDS, stride=cap), :]
            scratch[pl.ds(q * 8 + half * 4 + p, FIELDS, stride=BZ * 8), :] = value
    group = lax.broadcasted_iota(jnp.int32, (8, LANES), 1) // 8

    def one_field(f, carry):
        rows = [
            scratch[pl.ds(pl.multiple_of((f * BZ + q) * 8, 8), 8), :] for q in range(BZ)
        ]
        moved = transposed(rows, group)
        for g in range(BZ):
            second, b = divmod(g, BLOCK)
            spot = pl.ds((b % 4) * 8 + b // 4, 4, stride=2)
            for half in range(2):
                value = moved[g][half * 4 : half * 4 + 4]
                plane = 2 * half + second
                state[f, plane, spot, :] = value
                if chunk == 0:
                    if half == 0:
                        low_halo[f, second, spot, :] = value
                    else:
                        high_halo[f, second, spot, :] = value
                else:
                    if plane == 0:
                        low_halo[f, 0, spot, :] = value
                    if plane == 3:
                        high_halo[f, 0, spot, :] = value
        return carry

    lax.fori_loop(0, FIELDS, one_field, 0)
    if chunk == 0:
        best = in_ref[pl.ds(2 * FIELDS * cap, cap), :]
        for source in range(1, dev_count):
            start = source * tiles * cap + 2 * FIELDS * cap
            best = jnp.maximum(best, in_ref[pl.ds(start, cap), :])
        speed[...] = jnp.full((8, LANES), jnp.max(best), jnp.float32)


def unpack(table, arrived, chunk, dev_count, cap):
    planes = 2 if chunk == 0 else 1
    halo = jax.ShapeDtypeStruct((FIELDS, planes, ROWS, LANES), jnp.float32)
    shapes = [jax.ShapeDtypeStruct((FIELDS, 4, ROWS, LANES), jnp.float32), halo, halo]
    if chunk == 0:
        shapes.append(jax.ShapeDtypeStruct((8, LANES), jnp.float32))
    return pl.pallas_call(
        functools.partial(unpack_kernel, dev_count, cap, chunk),
        out_shape=shapes,
        in_specs=[SMEM, VMEM],
        out_specs=[VMEM] * len(shapes),
        scratch_shapes=[pltpu.VMEM((FIELDS * BZ * 8, LANES), jnp.float32)],
        compiler_params=params(),
        cost_estimate=cost(5_000_000, 2_000_000),
        name="unpack",
    )(table, arrived)


def y_up(x):
    return jnp.concatenate([x[8:], pltpu.roll(x[:8], 7, 0)], axis=0)


def y_down(x):
    return jnp.concatenate([pltpu.roll(x[24:], 1, 0), x[:24]], axis=0)


def z_up(x):
    return pltpu.roll(x, LANES - 1, 1)


def z_down(x):
    return pltpu.roll(x, 1, 1)


def inverse(x):
    return 1.0 / x


def smoothness(before, after):
    curve = after - before
    middle = 0.5 * (after + before)
    base = curve * curve * (13.0 / 12.0) + smooth_epsilon
    plus = middle + curve
    minus = middle - curve
    left = inverse(base + plus * plus)
    centre = inverse(base + middle * middle)
    right = inverse(base + minus * minus)
    return curve, left * left, centre * centre, right * right


def upwind_term(left, centre, right, jump_before, jump_after):
    right = 3.0 * right
    top = left * (jump_before + jump_before) + right * jump_after
    return top * inverse(left + 6.0 * centre + right)


def periodic_divergence(half_flux, scaled, up, down):
    plus = half_flux + scaled
    minus = half_flux - scaled

    def side(values):
        after = up(values) - values
        curve, left, centre, right = smoothness(down(after), after)
        jump = up(curve) - curve
        return curve, down(left), centre, up(right), down(jump), jump

    curve, left, centre, right, jump_before, jump_after = side(plus)
    face = 6.0 * (half_flux + up(half_flux)) - curve
    face = face - upwind_term(left, centre, right, jump_before, jump_after)
    curve, left, centre, right, jump_before, jump_after = side(minus)
    face = face + up(upwind_term(right, centre, left, jump_after, jump_before) - curve)
    return face - down(face)


def open_divergence(half_flux, scaled):
    count = len(half_flux)
    plus = [a + b for a, b in zip(half_flux, scaled)]
    minus = [a - b for a, b in zip(half_flux, scaled)]
    faces = [None] * count

    def side(values):
        steps = [values[i + 1] - values[i] for i in range(count - 1)]
        parts = [None] + [smoothness(steps[i - 1], steps[i]) for i in range(1, count - 1)]
        return parts

    parts = side(plus)
    for i in range(2, count - 3):
        jump_before = parts[i][0] - parts[i - 1][0]
        jump_after = parts[i + 1][0] - parts[i][0]
        faces[i] = 6.0 * (half_flux[i] + half_flux[i + 1]) - parts[i][0] - upwind_term(
            parts[i - 1][1], parts[i][2], parts[i + 1][3], jump_before, jump_after
        )
    parts = side(minus)
    for i in range(3, count - 2):
        jump_before = parts[i][0] - parts[i - 1][0]
        jump_after = parts[i + 1][0] - parts[i][0]
        faces[i - 1] = faces[i - 1] + (
            upwind_term(parts[i + 1][3], parts[i][2], parts[i - 1][1], jump_after, jump_before)
            - parts[i][0]
        )
    return [faces[i] - faces[i - 1] for i in range(3, count - 3)]


def half_velocities(fields):
    density, mom_x, mom_y, mom_z, energy = fields
    over = 0.5 / density
    vel = (mom_x * over, mom_y * over, mom_z * over)
    kinetic = mom_x * vel[0] + mom_y * vel[1] + mom_z * vel[2]
    pressure = (gamma_gas - 1.0) * (energy - kinetic)
    return vel, pressure


def half_flux(fields, field, direction, speed, pressure):
    if field == 0:
        return 0.5 * fields[1 + direction]
    if field == 4:
        return (fields[4] + pressure) * speed
    flux = fields[field] * speed
    return flux + 0.5 * pressure if field == 1 + direction else flux


def side_planes(fields, half_speed):
    vel, pressure = half_velocities(fields)
    for field in range(FIELDS):
        scaled = half_speed * fields[field]
        along_z = periodic_divergence(
            half_flux(fields, field, 2, vel[2], pressure), scaled, z_up, z_down
        )
        along_y = periodic_divergence(
            half_flux(fields, field, 1, vel[1], pressure), scaled, y_up, y_down
        )
        yield field, along_y + along_z


def plane_kernel(state, speed, out):
    half_speed = 0.5 * speed[0:1, :]

    def one_plane(plane, carry):
        fields = [state[f, plane] for f in range(FIELDS)]
        for field, total in side_planes(fields, half_speed):
            out[field, plane] = total
        return carry

    lax.fori_loop(0, state.shape[1], one_plane, 0)


def along_planes(state, speed):
    return pl.pallas_call(
        plane_kernel,
        out_shape=jax.ShapeDtypeStruct(state.shape, jnp.float32),
        in_specs=[VMEM, VMEM],
        out_specs=VMEM,
        compiler_params=params(),
        cost_estimate=cost(20_000_000, 1_000_000),
        name="planes",
    )(state, speed)


def across(get, half_speed):
    span = range(-3, BLOCK + 3)
    speeds, pressures = [], []
    for plane in span:
        vel, pressure = half_velocities([get(f, plane) for f in range(FIELDS)])
        speeds.append(vel[0])
        pressures.append(pressure)
    for field in range(FIELDS):
        fluxes, scaled = [], []
        for i, plane in enumerate(span):
            if field == 0:
                flux = 0.5 * get(1, plane)
            elif field == 4:
                flux = (get(4, plane) + pressures[i]) * speeds[i]
            else:
                flux = get(field, plane) * speeds[i]
                if field == 1:
                    flux = flux + 0.5 * pressures[i]
            fluxes.append(flux)
            scaled.append(half_speed * get(field, plane))
        yield field, open_divergence(fluxes, scaled)


def first_kernel(
    state_a, state_b, sides_a, sides_b, below_a, below_b, above_a, above_b, speed,
    middle, low, high, top,
):
    half_speed = 0.5 * speed[0:1, :]
    factor = (courant / 6.0) / speed[0:1, :]
    where = {0: 0, 1: 1, 6: 2, 7: 3}

    def group(j, best):
        rows = pl.ds(pl.multiple_of(j * 8, 8), 8)

        def pick(of_a, of_b, f, plane):
            if plane in where:
                return of_a[f, where[plane], rows, :]
            return of_b[f, plane - 2, rows, :]

        def get(f, plane):
            if plane < 0:
                return below_b[f, 0, rows, :] if plane == -3 else below_a[f, plane + 2, rows, :]
            if plane >= BLOCK:
                return above_b[f, 0, rows, :] if plane == 10 else above_a[f, plane - 8, rows, :]
            return pick(state_a, state_b, f, plane)

        for field, along_x in across(get, half_speed):
            for plane in range(BLOCK):
                total = along_x[plane] + pick(sides_a, sides_b, field, plane)
                value = get(field, plane) - factor * total
                middle[field, plane, rows, :] = value
                if plane < 3:
                    low[field, plane, rows, :] = value
                if plane >= 5:
                    high[field, plane - 5, rows, :] = value
        for plane in range(BLOCK):
            best = jnp.maximum(
                best, wave_speed([middle[f, plane, rows, :] for f in range(FIELDS)])
            )
        return best

    best = lax.fori_loop(0, 4, group, jnp.zeros((8, LANES), jnp.float32))
    top[...] = jnp.full((8, LANES), jnp.max(best), jnp.float32)


def first_stage(*operands):
    whole = jax.ShapeDtypeStruct((FIELDS, BLOCK, ROWS, LANES), jnp.float32)
    halo = jax.ShapeDtypeStruct((FIELDS, 3, ROWS, LANES), jnp.float32)
    return pl.pallas_call(
        first_kernel,
        out_shape=(whole, halo, halo, jax.ShapeDtypeStruct((8, LANES), jnp.float32)),
        in_specs=[VMEM] * len(operands),
        out_specs=(VMEM,) * 4,
        compiler_params=params(),
        cost_estimate=cost(30_000_000, 3_000_000),
        name="first_stage",
    )(*operands)


def second_kernel(
    state_a, state_b, middle, below, above, first_speed, speeds, out, sides
):
    first = first_speed[0:1, :]
    second = speeds[0:1, :]
    half_speed = 0.5 * second
    factor = (courant / 12.0) / first
    where = {0: 0, 1: 1, 6: 2, 7: 3}

    def one_plane(plane, carry):
        fields = [middle[f, plane] for f in range(FIELDS)]
        for field, total in side_planes(fields, half_speed):
            sides[field, plane] = total
        return carry

    lax.fori_loop(0, BLOCK, one_plane, 0)

    def group(j, carry):
        rows = pl.ds(pl.multiple_of(j * 8, 8), 8)
        spread = pl.ds(j, 8, stride=4)

        def get(f, plane):
            if plane < 0:
                return below[f, plane + 3, rows, :]
            if plane >= BLOCK:
                return above[f, plane - BLOCK, rows, :]
            return middle[f, plane, rows, :]

        for field, along_x in across(get, half_speed):
            for plane in range(BLOCK):
                total = along_x[plane] + sides[field, plane, rows, :]
                if plane in where:
                    start = state_a[field, where[plane], rows, :]
                else:
                    start = state_b[field, plane - 2, rows, :]
                value = 0.5 * start + (0.5 * get(field, plane) - factor * total)
                out[field, plane, spread, :] = value
        return carry

    lax.fori_loop(0, 4, group, 0)


def second_stage(*operands):
    whole = (FIELDS, BLOCK, ROWS, LANES)
    return pl.pallas_call(
        second_kernel,
        out_shape=jax.ShapeDtypeStruct(whole, jnp.float32),
        in_specs=[VMEM] * len(operands),
        out_specs=VMEM,
        scratch_shapes=[pltpu.VMEM(whole, jnp.float32)],
        compiler_params=params(),
        cost_estimate=cost(60_000_000, 3_000_000),
        name="second_stage",
    )(*operands)


def everyone_max(value, axis, size):
    reach = 1
    while reach < size:
        copies = [value]
        for times in range(1, 4):
            shift = reach * times
            if shift < size:
                pairs = [(i, (i + shift) % size) for i in range(size)]
                copies.append(lax.ppermute(value, axis, pairs))
        value = functools.reduce(jnp.maximum, copies)
        reach *= 4
    return value


def per_device(blocks, owner_list, slot_list):
    size = lax.axis_size("gx")
    own = lax.axis_index("gx")
    per_dev = blocks.shape[0]
    cap = max(2, 2 * per_dev // size)
    up = [(i, (i + 1) % size) for i in range(size)]
    down = [(j, i) for i, j in up]

    out_a, out_b = pack(blocks, owner_list, size, cap)
    come_a = lax.all_to_all(out_a, "gx", split_axis=0, concat_axis=0, tiled=True)
    come_b = lax.all_to_all(out_b, "gx", split_axis=0, concat_axis=0, tiled=True)
    table = arrival_rows(owner_list, slot_list, own, per_dev, size, cap)
    state_a, low_a, high_a, speed = unpack(table, come_a, 0, size, cap)
    below_a = lax.ppermute(high_a, "gx", up)
    above_a = lax.ppermute(low_a, "gx", down)
    sides_a = along_planes(state_a, speed)
    state_b, low_b, high_b = unpack(table, come_b, 1, size, cap)
    below_b = lax.ppermute(high_b, "gx", up)
    above_b = lax.ppermute(low_b, "gx", down)
    sides_b = along_planes(state_b, speed)
    middle, low, high, top = first_stage(
        state_a, state_b, sides_a, sides_b, below_a, below_b, above_a, above_b, speed
    )
    below = lax.ppermute(high, "gx", up)
    above = lax.ppermute(low, "gx", down)
    second = everyone_max(top, "gx", size)
    return second_stage(state_a, state_b, middle, below, above, speed, second)


def solution(mesh):
    return jax.shard_map(
        per_device,
        mesh=mesh,
        in_specs=(P(("runs", "gx"), None, None), P("runs"), P("runs")),
        out_specs=P(None, ("runs", "gx"), None, None),
        check_vma=False,
    )
```

time: 247 us -> 87.4 us (0.35)
  local copies, waits for them, and re-layouts: 69.4 us -> 2.34 us
  other arithmetic: 49 us -> 0.59 us
  blocking collectives: 70 us -> 26.3 us
  waiting for transfers between devices: 42.8 us -> 13.6 us
  Pallas kernels: 0 us -> 23.5 us
  starting transfers between devices: 12.5 us -> 20.6 us
    pmax x2 -> x0, blocking collectives: 70 us -> none  [the longest x1 39.8 us: per_device(): first_max = lax.pmax(local_speed, 'gx')]
    all_to_all x1, waiting for transfers between devices: 40.3 us -> 8.37 us  [per_device(): lax.all_to_all(out_b, 'gx', split_axis=0, concat_axis=0, tiled=True)]
    all_to_all x0 -> x1, blocking collectives: none -> 26.3 us  [per_device(): lax.all_to_all(out_a, 'gx', split_axis=0, concat_axis=0, tiled=True)]
    add x8 -> x1, other arithmetic: 26.2 us -> 0.07 us  [arrival_rows(): row = jnp.arange(dev_count, dtype=jnp.int32)[:, None] * cap + rank]
    pallas_call x0 -> x7, Pallas kernels: none -> 23.5 us  [the longest x1 8.13 us: second_stage(): pl.pallas_call(second_kernel, out_shape=jax.ShapeDtypeStruct(whole, jnp.f...]
    reshape x4 -> x0, local copies, waits for them, and re-layouts: 17.5 us -> none  [the longest x2 9.39 us: per_device(): arranged.reshape(BY, BZ, 5, BLOCK, BLOCK, BLOCK).transpose(2, 3, 0, 4, 1, 5)]
    slice x46 -> x0, local copies, waits for them, and re-layouts: 16 us -> none  [the longest x4 6.59 us: primitive(): velocity = (fields[1] / density, fields[2] / density, fields[3] / density)]
    scatter x2 -> x0, local copies, waits for them, and re-layouts: 12.4 us -> none  [the longest x1 8.13 us: per_device(): outgoing = jnp.zeros((dev_count * capacity,) + blocks.shape[1:], blocks.d...]
  transfers between devices with their start and end apart: 5 -> 13, of which waited for: 2 -> 6; matrix products, arithmetic and copies ran while one was open for 8% -> 1% of each run, Pallas kernels for 0% -> 12%
where the time goes in v1:
time: 87.4 us; the launch traced here: 87.1 us
  blocking collectives  26.3 us (30%)
  Pallas kernels  23.5 us (27%)
  starting transfers between devices  20.6 us (24%)
  waiting for transfers between devices  13.6 us (16%)
  local copies, waits for them, and re-layouts  2.34 us (3%)
    all_to_all x1, blocking collectives, per_device(): lax.all_to_all(out_a, 'gx', split_axis=0, concat_axis=0, tiled=True)  26.3 us
    all_to_all x1, waiting for transfers between devices, per_device(): lax.all_to_all(out_b, 'gx', split_axis=0, concat_axis=0, tiled=True)  8.37 us
    pallas_call x1, Pallas kernels, second_stage(): pl.pallas_call(second_kernel, out_shape=jax.ShapeDtypeStruct(whole, jnp.f...  8.13 us
    pallas_call x2, Pallas kernels, unpack(): pl.pallas_call(functools.partial(unpack_kernel, dev_count, cap, chunk), o...  5.37 us
    ppermute x6, waiting for transfers between devices, everyone_max(): copies.append(lax.ppermute(value, axis, pairs))  5.17 us
    pallas_call x2, Pallas kernels, along_planes(): pl.pallas_call(plane_kernel, out_shape=jax.ShapeDtypeStruct(state.shape,...  4.99 us
    ppermute x1, starting transfers between devices, per_device(): above_a = lax.ppermute(low_a, 'gx', down)  3.91 us
    all_to_all x1, starting transfers between devices, per_device(): lax.all_to_all(out_b, 'gx', split_axis=0, concat_axis=0, tiled=True)  3.65 us
  transfers between devices with their start and end apart: 13, of which 6 were waited for; matrix products, arithmetic and copies ran while one was open for 1% of the time, Pallas kernels for 12%

profile of v1, /device:TPU:0, one launch (start us, length us, event | category | flops | bytes accessed | tf_op | source)
XLA Modules:
  0.0 87.1 jit_solution(9528865237459747715)
XLA Ops:
  0.0 1.5 %copy.5.blocks_ref = f32[64,5,512]{2,1,0:T(8,128)S(1)} copy(f32[64,5,512]{2,0,1:T(8,128)} %param.3) | data formatting | bytes 1310720 | tf_op args[0]
  1.5 2.5 %pack.1 = (f32[1408,128]{1,0:T(8,128)S(1)}, f32[1280,128]{1,0:T(8,128)}) custom-call(s32[1024]{0:T(1024)S(1)} %copy-done, f32[64,5,512]{2,1,0:T(8,128)S(1)} %copy.5.blocks_ref), custom_call_target="tpu_custom_call" | custom-call | flops 10000000 | bytes 3000000 | tf_op jit(solution)/shard_map/pack/pallas_call | solution.py:101
  4.1 26.3 %all_to_all.22 = f32[16,88,128]{2,1,0:T(8,128)S(1)} all-to-all(f32[16,88,128]{2,1,0:T(8,128)S(1)} %bitcast.6), channel_id=1, replica_groups=mesh['runs'=2,'gx'=16] {'gx'}, dimensions={0} | all-to-all | bytes 1441792 | tf_op jit(solution)/shard_map/all_to_all | solution.py:510
  30.4 3.6 %all-to-all-start.1 = ((f32[16,80,128]{2,1,0:T(8,128)}), f32[16,80,128]{2,1,0:T(8,128)S(1)}, u32[]{:S(2)}, u32[]{:S(2)}) async-start(f32[16,80,128]{2,1,0:T(8,128)} %bitcast.2), calls=%async_computation.1 | async-start | bytes 1310720 | tf_op jit(solution)/shard_map/all_to_all | solution.py:511
  34.0 0.7 copy-done.1
  35.4 2.8 %unpack.2 = (f32[5,4,32,128]{3,2,1,0:T(8,128)S(1)}, f32[5,2,32,128]{3,2,1,0:T(8,128)S(1)}, f32[5,2,32,128]{3,2,1,0:T(8,128)S(1)}, f32[8,128]{1,0:T(8,128)S(1)}) custom-call(s32[64]{0:T(128)S(1)} %select_reduce_fusion.table, f32[1408,128]{1,0:T(8,128)S(1)} %bitcast.4), custom_call_target="tpu_custom_call" | custom-call | flops 5000000 | bytes 2000000 | tf_op jit(solution)/shard_map/unpack/pallas_call | solution.py:200
  38.8 3.9 %collective-permute-start.2 = (f32[5,2,32,128]{3,2,1,0:T(8,128)S(1)}, f32[5,2,32,128]{3,2,1,0:T(8,128)S(1)}, u32[]{:S(2)}, u32[]{:S(2)}) collective-permute-start(f32[5,2,32,128]{3,2,1,0:T(8,128)S(1)} %get-tuple-element.25), channel_id=1, source_target_pairs={{1,0},{2,1},{3,2},{4,3},{5,4},{6,5},{7,6},{8,7},{9,8},{10,9},{11,1... | collective-permute-start | bytes 491528 | tf_op jit(solution)/shard_map/ppermute | solution.py:515
  42.7 8.4 %all-to-all-done.1 = f32[16,80,128]{2,1,0:T(8,128)S(1)} async-done(((f32[16,80,128]{2,1,0:T(8,128)}), f32[16,80,128]{2,1,0:T(8,128)S(1)}, u32[]{:S(2)}, u32[]{:S(2)}) %all-to-all-start.1) | async-done | bytes 655392 | tf_op jit(solution)/shard_map/all_to_all | solution.py:511
  51.1 2.6 %unpack.3 = (f32[5,4,32,128]{3,2,1,0:T(8,128)S(1)}, f32[5,1,32,128]{3,2,1,0:T(8,128)S(1)}, f32[5,1,32,128]{3,2,1,0:T(8,128)S(1)}) custom-call(s32[64]{0:T(128)S(1)} %select_reduce_fusion.table, f32[1280,128]{1,0:T(8,128)S(1)} %bitcast.5), custom_call_target="tpu_custom_call" | custom-call | flops 5000000 | bytes 2000000 | tf_op jit(solution)/shard_map/unpack/pallas_call | solution.py:200
  53.7 1.4 %collective-permute-start.1 = (f32[5,1,32,128]{3,2,1,0:T(8,128)S(1)}, f32[5,1,32,128]{3,2,1,0:T(8,128)S(1)}, u32[]{:S(2)}, u32[]{:S(2)}) collective-permute-start(f32[5,1,32,128]{3,2,1,0:T(8,128)S(1)} %get-tuple-element.24), channel_id=1, source_target_pairs={{0,1},{1,2},{2,3},{3,4},{4,5},{5,6},{6,7},{7,8},{8,9},{9,10},{10,1... | collective-permute-start | bytes 245768 | tf_op jit(solution)/shard_map/ppermute | solution.py:518
  55.1 3.3 %collective-permute-start.3 = (f32[5,1,32,128]{3,2,1,0:T(8,128)S(1)}, f32[5,1,32,128]{3,2,1,0:T(8,128)S(1)}, u32[]{:S(2)}, u32[]{:S(2)}) collective-permute-start(f32[5,1,32,128]{3,2,1,0:T(8,128)S(1)} %get-tuple-element.26), channel_id=1, source_target_pairs={{1,0},{2,1},{3,2},{4,3},{5,4},{6,5},{7,6},{8,7},{9,8},{10,9},{11,1... | collective-permute-start | bytes 245768 | tf_op jit(solution)/shard_map/ppermute | solution.py:519
  58.4 2.5 %planes.2.sides_a = f32[5,4,32,128]{3,2,1,0:T(8,128)S(1)} custom-call(f32[5,4,32,128]{3,2,1,0:T(8,128)S(1)} %get-tuple-element.19.state.state_a, f32[8,128]{1,0:T(8,128)S(1)} %get-tuple-element.22.speed.first_speed), custom_call_target="tpu_custom_call" | custom-call | flops 20000000 | bytes 1000000 | tf_op jit(solution)/shard_map/planes/pallas_call | solution.py:341
  60.9 2.5 %planes.3.sides_b = f32[5,4,32,128]{3,2,1,0:T(8,128)S(1)} custom-call(f32[5,4,32,128]{3,2,1,0:T(8,128)S(1)} %get-tuple-element.21.state.state_b, f32[8,128]{1,0:T(8,128)S(1)} %get-tuple-element.22.speed.first_speed), custom_call_target="tpu_custom_call" | custom-call | flops 20000000 | bytes 1000000 | tf_op jit(solution)/shard_map/planes/pallas_call | solution.py:341
  63.5 2.5 %first_stage.1 = (f32[5,8,32,128]{3,2,1,0:T(8,128)S(1)}, f32[5,3,32,128]{3,2,1,0:T(8,128)S(1)}, f32[5,3,32,128]{3,2,1,0:T(8,128)S(1)}, f32[8,128]{1,0:T(8,128)S(1)}) custom-call(f32[5,4,32,128]{3,2,1,0:T(8,128)S(1)} %get-tuple-element.19.state.state_a, f32[5,4,32,128]{3,2,1,0:T(8,128)S(1)} %get-tuple-element.21.state.state_b, ...), custom_call_target="tpu_custom_call" | custom-call | flops 30000000 | bytes 3000000 | tf_op jit(solution)/shard_map/first_stage/pallas_call | solution.py:420
  66.0 0.9 %collective-permute-start.7 = (f32[8,128]{1,0:T(8,128)S(1)}, f32[8,128]{1,0:T(8,128)S(1)}, u32[]{:S(2)}, u32[]{:S(2)}) collective-permute-start(f32[8,128]{1,0:T(8,128)S(1)} %get-tuple-element.30), channel_id=1, source_target_pairs={{0,2},{1,3},{2,4},{3,5},{4,6},{5,7},{6,8},{7,9},{8,10},{9,11},{10,... | collective-permute-start | bytes 12296 | tf_op jit(solution)/shard_map/ppermute | solution.py:495
  67.3 1.3 %collective-permute-start.4 = (f32[5,3,32,128]{3,2,1,0:T(8,128)S(1)}, f32[5,3,32,128]{3,2,1,0:T(8,128)S(1)}, u32[]{:S(2)}, u32[]{:S(2)}) collective-permute-start(f32[5,3,32,128]{3,2,1,0:T(8,128)S(1)} %get-tuple-element.28), channel_id=1, source_target_pairs={{0,1},{1,2},{2,3},{3,4},{4,5},{5,6},{6,7},{7,8},{8,9},{9,10},{10,1... | collective-permute-start | bytes 737288 | tf_op jit(solution)/shard_map/ppermute | solution.py:524
  68.5 3.2 %collective-permute-start.5 = (f32[5,3,32,128]{3,2,1,0:T(8,128)S(1)}, f32[5,3,32,128]{3,2,1,0:T(8,128)S(1)}, u32[]{:S(2)}, u32[]{:S(2)}) collective-permute-start(f32[5,3,32,128]{3,2,1,0:T(8,128)S(1)} %get-tuple-element.29), channel_id=1, source_target_pairs={{1,0},{2,1},{3,2},{4,3},{5,4},{6,5},{7,6},{8,7},{9,8},{10,9},{11,1... | collective-permute-start | bytes 737288 | tf_op jit(solution)/shard_map/ppermute | solution.py:525
  71.7 0.8 collective-permute-done.7
  72.6 0.9 %collective-permute-start.11 = (f32[8,128]{1,0:T(8,128)S(1)}, f32[8,128]{1,0:T(8,128)S(1)}, u32[]{:S(2)}, u32[]{:S(2)}) collective-permute-start(f32[8,128]{1,0:T(8,128)S(1)} %maximum_maximum_fusion.1), channel_id=1, source_target_pairs={{0,12},{1,13},{2,14},{3,15},{4,0},{5,1},{6,2},{7,3},{8,4},{9,5},{1... | collective-permute-start | bytes 12296 | tf_op jit(solution)/shard_map/ppermute | solution.py:495
  73.5 1.1 %collective-permute-start.9 = (f32[8,128]{1,0:T(8,128)S(1)}, f32[8,128]{1,0:T(8,128)S(1)}, u32[]{:S(2)}, u32[]{:S(2)}) collective-permute-start(f32[8,128]{1,0:T(8,128)S(1)} %maximum_maximum_fusion.1), channel_id=1, source_target_pairs={{0,4},{1,5},{2,6},{3,7},{4,8},{5,9},{6,10},{7,11},{8,12},{9,13},{1... | collective-permute-start | bytes 12296 | tf_op jit(solution)/shard_map/ppermute | solution.py:495
  74.6 1.6 %collective-permute-done.11 = f32[8,128]{1,0:T(8,128)S(1)} collective-permute-done((f32[8,128]{1,0:T(8,128)S(1)}, f32[8,128]{1,0:T(8,128)S(1)}, u32[]{:S(2)}, u32[]{:S(2)}) %collective-permute-start.11) | collective-permute-done | bytes 4128 | tf_op jit(solution)/shard_map/ppermute | solution.py:495
  76.2 1.8 %collective-permute-done.10 = f32[8,128]{1,0:T(8,128)S(1)} collective-permute-done((f32[8,128]{1,0:T(8,128)S(1)}, f32[8,128]{1,0:T(8,128)S(1)}, u32[]{:S(2)}, u32[]{:S(2)}) %collective-permute-start.10) | collective-permute-done | bytes 4128 | tf_op jit(solution)/shard_map/ppermute | solution.py:495
  78.0 0.9 %collective-permute-done.9 = f32[8,128]{1,0:T(8,128)S(1)} collective-permute-done((f32[8,128]{1,0:T(8,128)S(1)}, f32[8,128]{1,0:T(8,128)S(1)}, u32[]{:S(2)}, u32[]{:S(2)}) %collective-permute-start.9) | collective-permute-done | bytes 4128 | tf_op jit(solution)/shard_map/ppermute | solution.py:495
  78.9 8.1 %second_stage.1 = f32[5,8,32,128]{3,2,1,0:T(8,128)} custom-call(f32[5,4,32,128]{3,2,1,0:T(8,128)S(1)} %get-tuple-element.19.state.state_a, f32[5,4,32,128]{3,2,1,0:T(8,128)S(1)} %get-tuple-element.21.state.state_b, f32[5,8,32,128]{3,2,1,0:T(8,128)S(1)} %get-tuple-element.27.middle, f32[5,3,32,128]{3,2,1,0:T(8,128)S(1)} %collective-permute-done.4.below, ...), custom_call_target="tpu_custom_call" | custom-call | flops 60000000 | bytes 3000000 | tf_op jit(solution)/shard_map/second_stage/pallas_call | solution.py:475
  (25 shorter events, 1.9 us)
Async XLA Ops:
  0.0 1.5 %copy-start = (s32[1024]{0:T(1024)S(1)}, s32[1024]{0:T(1024)}, u32[]{:S(2)}) copy-start(s32[1024]{0:T(1024)} %owner_ref.1) | copy-start | bytes 12292
  30.4 20.7 %all-to-all-start.1 = ((f32[16,80,128]{2,1,0:T(8,128)}), f32[16,80,128]{2,1,0:T(8,128)S(1)}, u32[]{:S(2)}, u32[]{:S(2)}) async-start(f32[16,80,128]{2,1,0:T(8,128)} %bitcast.2), calls=%async_computation.1 | async-start | bytes 1310720 | tf_op jit(solution)/shard_map/all_to_all | solution.py:511
  34.0 0.7 copy-start.1
  38.2 25.2 %collective-permute-start = (f32[5,2,32,128]{3,2,1,0:T(8,128)S(1)}, f32[5,2,32,128]{3,2,1,0:T(8,128)S(1)}, u32[]{:S(2)}, u32[]{:S(2)}) collective-permute-start(f32[5,2,32,128]{3,2,1,0:T(8,128)S(1)} %get-tuple-element.23), channel_id=1, source_target_pairs={{0,1},{1,2},{2,3},{3,4},{4,5},{5,6},{6,7},{7,8},{8,9},{9,10},{10,1... | collective-permute-start | bytes 491528 | tf_op jit(solution)/shard_map/ppermute | solution.py:514
  38.8 24.6 %collective-permute-start.2 = (f32[5,2,32,128]{3,2,1,0:T(8,128)S(1)}, f32[5,2,32,128]{3,2,1,0:T(8,128)S(1)}, u32[]{:S(2)}, u32[]{:S(2)}) collective-permute-start(f32[5,2,32,128]{3,2,1,0:T(8,128)S(1)} %get-tuple-element.25), channel_id=1, source_target_pairs={{1,0},{2,1},{3,2},{4,3},{5,4},{6,5},{7,6},{8,7},{9,8},{10,9},{11,1... | collective-permute-start | bytes 491528 | tf_op jit(solution)/shard_map/ppermute | solution.py:515
  53.7 9.7 %collective-permute-start.1 = (f32[5,1,32,128]{3,2,1,0:T(8,128)S(1)}, f32[5,1,32,128]{3,2,1,0:T(8,128)S(1)}, u32[]{:S(2)}, u32[]{:S(2)}) collective-permute-start(f32[5,1,32,128]{3,2,1,0:T(8,128)S(1)} %get-tuple-element.24), channel_id=1, source_target_pairs={{0,1},{1,2},{2,3},{3,4},{4,5},{5,6},{6,7},{7,8},{8,9},{9,10},{10,1... | collective-permute-start | bytes 245768 | tf_op jit(solution)/shard_map/ppermute | solution.py:518
  55.1 8.3 %collective-permute-start.3 = (f32[5,1,32,128]{3,2,1,0:T(8,128)S(1)}, f32[5,1,32,128]{3,2,1,0:T(8,128)S(1)}, u32[]{:S(2)}, u32[]{:S(2)}) collective-permute-start(f32[5,1,32,128]{3,2,1,0:T(8,128)S(1)} %get-tuple-element.26), channel_id=1, source_target_pairs={{1,0},{2,1},{3,2},{4,3},{5,4},{6,5},{7,6},{8,7},{9,8},{10,9},{11,1... | collective-permute-start | bytes 245768 | tf_op jit(solution)/shard_map/ppermute | solution.py:519
  65.9 5.8 %collective-permute-start.8 = (f32[8,128]{1,0:T(8,128)S(1)}, f32[8,128]{1,0:T(8,128)S(1)}, u32[]{:S(2)}, u32[]{:S(2)}) collective-permute-start(f32[8,128]{1,0:T(8,128)S(1)} %get-tuple-element.30), channel_id=1, source_target_pairs={{0,3},{1,4},{2,5},{3,6},{4,7},{5,8},{6,9},{7,10},{8,11},{9,12},{10... | collective-permute-start | bytes 12296 | tf_op jit(solution)/shard_map/ppermute | solution.py:495
  66.0 6.5 %collective-permute-start.7 = (f32[8,128]{1,0:T(8,128)S(1)}, f32[8,128]{1,0:T(8,128)S(1)}, u32[]{:S(2)}, u32[]{:S(2)}) collective-permute-start(f32[8,128]{1,0:T(8,128)S(1)} %get-tuple-element.30), channel_id=1, source_target_pairs={{0,2},{1,3},{2,4},{3,5},{4,6},{5,7},{6,8},{7,9},{8,10},{9,11},{10,... | collective-permute-start | bytes 12296 | tf_op jit(solution)/shard_map/ppermute | solution.py:495
  66.9 5.7 %collective-permute-start.6 = (f32[8,128]{1,0:T(8,128)S(1)}, f32[8,128]{1,0:T(8,128)S(1)}, u32[]{:S(2)}, u32[]{:S(2)}) collective-permute-start(f32[8,128]{1,0:T(8,128)S(1)} %get-tuple-element.30), channel_id=1, source_target_pairs={{0,1},{1,2},{2,3},{3,4},{4,5},{5,6},{6,7},{7,8},{8,9},{9,10},{10,1... | collective-permute-start | bytes 12296 | tf_op jit(solution)/shard_map/ppermute | solution.py:495
  67.3 11.7 %collective-permute-start.4 = (f32[5,3,32,128]{3,2,1,0:T(8,128)S(1)}, f32[5,3,32,128]{3,2,1,0:T(8,128)S(1)}, u32[]{:S(2)}, u32[]{:S(2)}) collective-permute-start(f32[5,3,32,128]{3,2,1,0:T(8,128)S(1)} %get-tuple-element.28), channel_id=1, source_target_pairs={{0,1},{1,2},{2,3},{3,4},{4,5},{5,6},{6,7},{7,8},{8,9},{9,10},{10,1... | collective-permute-start | bytes 737288 | tf_op jit(solution)/shard_map/ppermute | solution.py:524
  68.5 10.4 %collective-permute-start.5 = (f32[5,3,32,128]{3,2,1,0:T(8,128)S(1)}, f32[5,3,32,128]{3,2,1,0:T(8,128)S(1)}, u32[]{:S(2)}, u32[]{:S(2)}) collective-permute-start(f32[5,3,32,128]{3,2,1,0:T(8,128)S(1)} %get-tuple-element.29), channel_id=1, source_target_pairs={{1,0},{2,1},{3,2},{4,3},{5,4},{6,5},{7,6},{8,7},{9,8},{10,9},{11,1... | collective-permute-start | bytes 737288 | tf_op jit(solution)/shard_map/ppermute | solution.py:525
  72.6 3.6 %collective-permute-start.11 = (f32[8,128]{1,0:T(8,128)S(1)}, f32[8,128]{1,0:T(8,128)S(1)}, u32[]{:S(2)}, u32[]{:S(2)}) collective-permute-start(f32[8,128]{1,0:T(8,128)S(1)} %maximum_maximum_fusion.1), channel_id=1, source_target_pairs={{0,12},{1,13},{2,14},{3,15},{4,0},{5,1},{6,2},{7,3},{8,4},{9,5},{1... | collective-permute-start | bytes 12296 | tf_op jit(solution)/shard_map/ppermute | solution.py:495
  73.5 4.5 %collective-permute-start.10 = (f32[8,128]{1,0:T(8,128)S(1)}, f32[8,128]{1,0:T(8,128)S(1)}, u32[]{:S(2)}, u32[]{:S(2)}) collective-permute-start(f32[8,128]{1,0:T(8,128)S(1)} %maximum_maximum_fusion.1), channel_id=1, source_target_pairs={{0,8},{1,9},{2,10},{3,11},{4,12},{5,13},{6,14},{7,15},{8,0},{9,1},... | collective-permute-start | bytes 12296 | tf_op jit(solution)/shard_map/ppermute | solution.py:495
  73.5 5.4 %collective-permute-start.9 = (f32[8,128]{1,0:T(8,128)S(1)}, f32[8,128]{1,0:T(8,128)S(1)}, u32[]{:S(2)}, u32[]{:S(2)}) collective-permute-start(f32[8,128]{1,0:T(8,128)S(1)} %maximum_maximum_fusion.1), channel_id=1, source_target_pairs={{0,4},{1,5},{2,6},{3,7},{4,8},{5,9},{6,10},{7,11},{8,12},{9,13},{1... | collective-permute-start | bytes 12296 | tf_op jit(solution)/shard_map/ppermute | solution.py:495

commit v2 on v1

--- a/solution.py
+++ b/solution.py
@@ -43,90 +43,103 @@
     return fastest + sound
 
 
-def pack_kernel(dev_count, cap, per_dev, owner_ref, blocks_ref, out_a, out_b, count, best):
+def turns(size):
+    half = size // 2
+    order = []
+    for i in range(half - 1, -1, -1):
+        order += [half + i, i]
+    return order
+
+
+def pack_kernel(size, cap, per_dev, owner_ref, blocks_ref, *refs):
+    outs = (refs[:size], refs[size : 2 * size])
+    count, member, best = refs[2 * size :]
     own = lax.axis_index("gx")
-    tiles = (2 * FIELDS + 1, 2 * FIELDS)
-    outs = (out_a, out_b)
 
     def clear(dest, carry):
         count[dest] = 0
         return carry
 
-    lax.fori_loop(0, dev_count, clear, 0)
-
-    def place(block, carry):
+    lax.fori_loop(0, size, clear, 0)
+
+    def note(block, carry):
         dest = owner_ref[own * per_dev + block]
         rank = count[dest]
         count[dest] = rank + 1
-        for chunk in range(2):
-            base = dest * (tiles[chunk] * cap) + rank
-            for half in range(2):
-                pair = CHUNKS[chunk][half]
-                value = blocks_ref[block, :, pair * LANES : (pair + 1) * LANES]
-                outs[chunk][pl.ds(base + half * FIELDS * cap, FIELDS, stride=cap), :] = value
+        member[dest * cap + rank] = block
         return carry
 
-    lax.fori_loop(0, per_dev, place, 0, unroll=4)
+    lax.fori_loop(0, per_dev, note, 0, unroll=8)
     best[...] = jnp.zeros_like(best)
-
-    def speeds(dest, carry):
+    for turn in range(size):
+        dest = own ^ turn
+
         @pl.when(count[dest] > 0)
         def _():
+            for rank in range(cap):
+                block = member[dest * cap + rank]
+                for chunk in range(2):
+                    for half in range(2):
+                        pair = CHUNKS[chunk][half]
+                        spot = pl.ds(half * FIELDS * cap + rank, FIELDS, stride=cap)
+                        outs[chunk][turn][spot, :] = blocks_ref[
+                            block, :, pair * LANES : (pair + 1) * LANES
+                        ]
             for chunk in range(2):
                 for half in range(2):
-                    base = dest * (tiles[chunk] * cap) + half * FIELDS * cap
+                    first = half * FIELDS * cap
                     fields = [
-                        outs[chunk][pl.ds(pl.multiple_of(base + f * cap, cap), cap), :]
+                        outs[chunk][turn][first + f * cap : first + (f + 1) * cap, :]
                         for f in range(FIELDS)
                     ]
                     best[...] = jnp.maximum(best[...], wave_speed(fields))
 
-        return carry
-
-    lax.fori_loop(0, dev_count, speeds, 0)
     top = jnp.full((cap, LANES), jnp.max(best[...]), jnp.float32)
-
-    def publish(dest, carry):
-        base = dest * (tiles[0] * cap) + 2 * FIELDS * cap
-        out_a[pl.ds(pl.multiple_of(base, cap), cap), :] = top
-        return carry
-
-    lax.fori_loop(0, dev_count, publish, 0)
-
-
-def pack(blocks, owner_list, dev_count, cap):
+    for turn in range(size):
+        outs[0][turn][2 * FIELDS * cap :, :] = top
+
+
+def pack(blocks, owner_list, size, cap):
     per_dev = blocks.shape[0]
-    rows_a = dev_count * cap * (2 * FIELDS + 1)
-    rows_b = dev_count * cap * 2 * FIELDS
-    return pl.pallas_call(
-        functools.partial(pack_kernel, dev_count, cap, per_dev),
-        out_shape=(
-            jax.ShapeDtypeStruct((rows_a, LANES), jnp.float32),
-            jax.ShapeDtypeStruct((rows_b, LANES), jnp.float32),
-        ),
+    shape_a = jax.ShapeDtypeStruct((cap * (2 * FIELDS + 1), LANES), jnp.float32)
+    shape_b = jax.ShapeDtypeStruct((cap * 2 * FIELDS, LANES), jnp.float32)
+    out = pl.pallas_call(
+        functools.partial(pack_kernel, size, cap, per_dev),
+        out_shape=[shape_a] * size + [shape_b] * size,
         in_specs=[SMEM, VMEM],
-        out_specs=(VMEM, VMEM),
+        out_specs=[VMEM] * (2 * size),
         scratch_shapes=[
-            pltpu.SMEM((dev_count,), jnp.int32),
+            pltpu.SMEM((size,), jnp.int32),
+            pltpu.SMEM((size * cap,), jnp.int32),
             pltpu.VMEM((cap, LANES), jnp.float32),
         ],
         compiler_params=params(),
         cost_estimate=cost(10_000_000, 3_000_000),
         name="pack",
     )(owner_list, blocks)
-
-
-def arrival_rows(owner_list, slot_list, own, per_dev, dev_count, cap):
-    owners = owner_list.reshape(dev_count, per_dev)
-    slots = slot_list.reshape(dev_count, per_dev)
+    return out[:size], out[size:]
+
+
+def exchanged(parts, axis, size):
+    come = list(parts)
+    for turn in turns(size):
+        if turn:
+            pairs = [(i, i ^ turn) for i in range(size)]
+            come[turn] = lax.ppermute(parts[turn], axis, pairs)
+    return come
+
+
+def arrivals(owner_list, slot_list, own, per_dev, size, cap):
+    owners = owner_list.reshape(size, per_dev)
+    slots = slot_list.reshape(size, per_dev)
     mine = owners == own
     spot = jnp.arange(per_dev, dtype=jnp.int32)
     earlier = spot[None, :] < spot[:, None]
     rank = jnp.sum((mine[:, None, :] & earlier[None]).astype(jnp.int32), axis=2)
-    row = jnp.arange(dev_count, dtype=jnp.int32)[:, None] * cap + rank
-    key = jnp.where(mine, slots, -1)
-    hit = key.reshape(1, -1) == spot[:, None]
-    return jnp.max(jnp.where(hit, row.reshape(1, -1), 0), axis=1)
+    row = (slots % BZ) * 8 + slots // BZ
+    order = jnp.arange(cap, dtype=jnp.int32)
+    hit = mine[:, None, :] & (rank[:, None, :] == order[None, :, None])
+    return jnp.max(jnp.where(hit, row[:, None, :], -1), axis=2).reshape(-1)
 
 
 def transposed(rows, group):
@@ -143,19 +156,24 @@
     return rows
 
 
-def unpack_kernel(dev_count, cap, chunk, table, in_ref, *refs):
-    tiles = 2 * FIELDS + (1 if chunk == 0 else 0)
+def unpack_kernel(size, cap, chunk, table, *refs):
+    come, refs = refs[:size], refs[size:]
     if chunk == 0:
         state, low_halo, high_halo, speed, scratch = refs
     else:
         state, low_halo, high_halo, scratch = refs
-    for slot in range(BY * BZ):
-        p, q = divmod(slot, BZ)
-        where = table[slot]
-        base = (where // cap) * (tiles * cap) + where % cap
-        for half in range(2):
-            value = in_ref[pl.ds(base + half * FIELDS * cap, FIELDS, stride=cap), :]
-            scratch[pl.ds(q * 8 + half * 4 + p, FIELDS, stride=BZ * 8), :] = value
+    own = lax.axis_index("gx")
+    for turn in range(size):
+        source = own ^ turn
+
+        @pl.when(table[source * cap] >= 0)
+        def _():
+            for rank in range(cap):
+                row = table[source * cap + rank]
+                for half in range(2):
+                    value = come[turn][pl.ds(half * FIELDS * cap + rank, FIELDS, stride=cap), :]
+                    scratch[pl.ds(row + half * 4, FIELDS, stride=BZ * 8), :] = value
+
     group = lax.broadcasted_iota(jnp.int32, (8, LANES), 1) // 8
 
     def one_field(f, carry):
@@ -184,29 +202,28 @@
 
     lax.fori_loop(0, FIELDS, one_field, 0)
     if chunk == 0:
-        best = in_ref[pl.ds(2 * FIELDS * cap, cap), :]
-        for source in range(1, dev_count):
-            start = source * tiles * cap + 2 * FIELDS * cap
-            best = jnp.maximum(best, in_ref[pl.ds(start, cap), :])
+        best = come[0][2 * FIELDS * cap :, :]
+        for other in come[1:]:
+            best = jnp.maximum(best, other[2 * FIELDS * cap :, :])
         speed[...] = jnp.full((8, LANES), jnp.max(best), jnp.float32)
 
 
-def unpack(table, arrived, chunk, dev_count, cap):
+def unpack(table, come, chunk, size, cap):
     planes = 2 if chunk == 0 else 1
     halo = jax.ShapeDtypeStruct((FIELDS, planes, ROWS, LANES), jnp.float32)
     shapes = [jax.ShapeDtypeStruct((FIELDS, 4, ROWS, LANES), jnp.float32), halo, halo]
     if chunk == 0:
         shapes.append(jax.ShapeDtypeStruct((8, LANES), jnp.float32))
     return pl.pallas_call(
-        functools.partial(unpack_kernel, dev_count, cap, chunk),
+        functools.partial(unpack_kernel, size, cap, chunk),
         out_shape=shapes,
-        in_specs=[SMEM, VMEM],
+        in_specs=[SMEM] + [VMEM] * size,
         out_specs=[VMEM] * len(shapes),
         scratch_shapes=[pltpu.VMEM((FIELDS * BZ * 8, LANES), jnp.float32)],
         compiler_params=params(),
         cost_estimate=cost(5_000_000, 2_000_000),
         name="unpack",
-    )(table, arrived)
+    )(table, *come)
 
 
 def y_up(x):
@@ -489,9 +506,9 @@
     while reach < size:
         copies = [value]
         for times in range(1, 4):
-            shift = reach * times
-            if shift < size:
-                pairs = [(i, (i + shift) % size) for i in range(size)]
+            turn = reach * times
+            if turn < size:
+                pairs = [(i, i ^ turn) for i in range(size)]
                 copies.append(lax.ppermute(value, axis, pairs))
         value = functools.reduce(jnp.maximum, copies)
         reach *= 4
@@ -506,10 +523,10 @@
     up = [(i, (i + 1) % size) for i in range(size)]
     down = [(j, i) for i, j in up]
 
-    out_a, out_b = pack(blocks, owner_list, size, cap)
-    come_a = lax.all_to_all(out_a, "gx", split_axis=0, concat_axis=0, tiled=True)
-    come_b = lax.all_to_all(out_b, "gx", split_axis=0, concat_axis=0, tiled=True)
-    table = arrival_rows(owner_list, slot_list, own, per_dev, size, cap)
+    parts_a, parts_b = pack(blocks, owner_list, size, cap)
+    come_a = exchanged(parts_a, "gx", size)
+    come_b = exchanged(parts_b, "gx", size)
+    table = arrivals(owner_list, slot_list, own, per_dev, size, cap)
     state_a, low_a, high_a, speed = unpack(table, come_a, 0, size, cap)
     below_a = lax.ppermute(high_a, "gx", up)
     above_a = lax.ppermute(low_a, "gx", down)

time: 87.4 us -> 92.7 us (1.061)
  starting transfers between devices: 20.6 us -> 61.8 us
  blocking collectives: 26.3 us -> 0 us
  waiting for transfers between devices: 13.6 us -> 5.67 us
  Pallas kernels: 23.5 us -> 22.4 us
    ppermute x0 -> x30, starting transfers between devices: none -> 42 us  [exchanged(): come[turn] = lax.ppermute(parts[turn], axis, pairs)]
    all_to_all x1 -> x0, blocking collectives: 26.3 us -> none  [per_device(): lax.all_to_all(out_a, 'gx', split_axis=0, concat_axis=0, tiled=True)]
    all_to_all x1 -> x0, waiting for transfers between devices: 8.37 us -> none  [per_device(): lax.all_to_all(out_b, 'gx', split_axis=0, concat_axis=0, tiled=True)]
    ppermute x0 -> x30, waiting for transfers between devices: none -> 4.06 us  [exchanged(): come[turn] = lax.ppermute(parts[turn], axis, pairs)]
    all_to_all x1 -> x0, starting transfers between devices: 3.65 us -> none  [per_device(): lax.all_to_all(out_b, 'gx', split_axis=0, concat_axis=0, tiled=True)]
    ppermute x6, waiting for transfers between devices: 5.17 us -> 1.59 us  [everyone_max(): copies.append(lax.ppermute(value, axis, pairs))]
    ppermute x6, starting transfers between devices: 3.36 us -> 6.36 us  [everyone_max(): copies.append(lax.ppermute(value, axis, pairs))]
    ppermute x1, starting transfers between devices: 1.27 us -> 0.01 us  [per_device(): below = lax.ppermute(high, 'gx', up)]
  transfers between devices with their start and end apart: 13 -> 42, of which waited for: 6 -> 6; matrix products, arithmetic and copies ran while one was open for 1% -> 1% of each run, Pallas kernels for 12% -> 11%
where the time goes in v2:
time: 92.7 us; the launch traced here: 92.6 us
  starting transfers between devices  61.8 us (67%)
  Pallas kernels  22.4 us (24%)
  waiting for transfers between devices  5.67 us (6%)
  local copies, waits for them, and re-layouts  1.75 us (2%)
    ppermute x30, starting transfers between devices, exchanged(): come[turn] = lax.ppermute(parts[turn], axis, pairs)  42 us
    pallas_call x1, Pallas kernels, second_stage(): pl.pallas_call(second_kernel, out_shape=jax.ShapeDtypeStruct(whole, jnp.f...  8.13 us
    ppermute x6, starting transfers between devices, everyone_max(): copies.append(lax.ppermute(value, axis, pairs))  6.36 us
    pallas_call x2, Pallas kernels, unpack(): pl.pallas_call(functools.partial(unpack_kernel, size, cap, chunk), out_sh...  5.04 us
    pallas_call x2, Pallas kernels, along_planes(): pl.pallas_call(plane_kernel, out_shape=jax.ShapeDtypeStruct(state.shape,...  4.99 us
    ppermute x1, starting transfers between devices, per_device(): above = lax.ppermute(low, 'gx', down)  4.44 us
    ppermute x1, starting transfers between devices, per_device(): above_a = lax.ppermute(low_a, 'gx', down)  4.27 us
    ppermute x30, waiting for transfers between devices, exchanged(): come[turn] = lax.ppermute(parts[turn], axis, pairs)  4.06 us
  transfers between devices with their start and end apart: 42, of which 6 were waited for; matrix products, arithmetic and copies ran while one was open for 1% of the time, Pallas kernels for 11%

profile of v2, /device:TPU:0, one launch (start us, length us, event | category | flops | bytes accessed | tf_op | source)
XLA Modules:
  0.0 92.6 jit_solution(9386976443096241616)
XLA Ops:
  1.5 1.8 %pack.1 = (f32[88,128]{1,0:T(8,128)S(1)}, f32[88,128]{1,0:T(8,128)S(1)}, f32[88,128]{1,0:T(8,128)S(1)}, f32[88,128]{1,0:T(8,128)S(1)}, f32[88,128]{1,0:T(8,128)S...) custom-call(s32[1024]{0:T(1024)S(1)} %copy-done, ...), custom_call_target="tpu_custom_call" | custom-call | flops 10000000 | bytes 3000000 | tf_op jit(solution)/shard_map/pack/pallas_call | solution.py:106
  3.8 2.6 %collective-permute-start.16 = (f32[80,128]{1,0:T(8,128)S(1)}, f32[80,128]{1,0:T(8,128)S(1)}, u32[]{:S(2)}, u32[]{:S(2)}) collective-permute-start(f32[80,128]{1,0:T(8,128)S(1)} %get-tuple-element.67), channel_id=1, source_target_pairs={{0,2},{1,3},{2,0},{3,1},{4,6},{5,7},{6,4},{7,5},{8,10},{9,11},{10,... | collective-permute-start | bytes 122888 | tf_op jit(solution)/shard_map/ppermute | solution.py:128
  6.5 1.8 %collective-permute-start.18 = (f32[80,128]{1,0:T(8,128)S(1)}, f32[80,128]{1,0:T(8,128)S(1)}, u32[]{:S(2)}, u32[]{:S(2)}) collective-permute-start(f32[80,128]{1,0:T(8,128)S(1)} %get-tuple-element.69), channel_id=1, source_target_pairs={{0,4},{1,5},{2,6},{3,7},{4,0},{5,1},{6,2},{7,3},{8,12},{9,13},{10,... | collective-permute-start | bytes 122888 | tf_op jit(solution)/shard_map/ppermute | solution.py:128
  8.4 2.6 %collective-permute-start.20 = (f32[80,128]{1,0:T(8,128)S(1)}, f32[80,128]{1,0:T(8,128)S(1)}, u32[]{:S(2)}, u32[]{:S(2)}) collective-permute-start(f32[80,128]{1,0:T(8,128)S(1)} %get-tuple-element.71), channel_id=1, source_target_pairs={{0,6},{1,7},{2,4},{3,5},{4,2},{5,3},{6,0},{7,1},{8,14},{9,15},{10,... | collective-permute-start | bytes 122888 | tf_op jit(solution)/shard_map/ppermute | solution.py:128
  15.7 2.0 %collective-permute-start.5 = (f32[88,128]{1,0:T(8,128)S(1)}, f32[88,128]{1,0:T(8,128)S(1)}, u32[]{:S(2)}, u32[]{:S(2)}) collective-permute-start(f32[88,128]{1,0:T(8,128)S(1)} %get-tuple-element.54), channel_id=1, source_target_pairs={{0,6},{1,7},{2,4},{3,5},{4,2},{5,3},{6,0},{7,1},{8,14},{9,15},{10,... | collective-permute-start | bytes 135176 | tf_op jit(solution)/shard_map/ppermute | solution.py:128
  18.4 2.6 %collective-permute-start.7 = (f32[88,128]{1,0:T(8,128)S(1)}, f32[88,128]{1,0:T(8,128)S(1)}, u32[]{:S(2)}, u32[]{:S(2)}) collective-permute-start(f32[88,128]{1,0:T(8,128)S(1)} %get-tuple-element.56), channel_id=1, source_target_pairs={{0,8},{1,9},{2,10},{3,11},{4,12},{5,13},{6,14},{7,15},{8,0},{9,1},... | collective-permute-start | bytes 135176 | tf_op jit(solution)/shard_map/ppermute | solution.py:128
  21.1 3.2 %collective-permute-start.9 = (f32[88,128]{1,0:T(8,128)S(1)}, f32[88,128]{1,0:T(8,128)S(1)}, u32[]{:S(2)}, u32[]{:S(2)}) collective-permute-start(f32[88,128]{1,0:T(8,128)S(1)} %get-tuple-element.58), channel_id=1, source_target_pairs={{0,10},{1,11},{2,8},{3,9},{4,14},{5,15},{6,12},{7,13},{8,2},{9,3},... | collective-permute-start | bytes 135176 | tf_op jit(solution)/shard_map/ppermute | solution.py:128
  24.7 3.6 %collective-permute-start.11 = (f32[88,128]{1,0:T(8,128)S(1)}, f32[88,128]{1,0:T(8,128)S(1)}, u32[]{:S(2)}, u32[]{:S(2)}) collective-permute-start(f32[88,128]{1,0:T(8,128)S(1)} %get-tuple-element.60), channel_id=1, source_target_pairs={{0,12},{1,13},{2,14},{3,15},{4,8},{5,9},{6,10},{7,11},{8,4},{9,5},... | collective-permute-start | bytes 135176 | tf_op jit(solution)/shard_map/ppermute | solution.py:128
  28.4 3.8 %collective-permute-start.13 = (f32[88,128]{1,0:T(8,128)S(1)}, f32[88,128]{1,0:T(8,128)S(1)}, u32[]{:S(2)}, u32[]{:S(2)}) collective-permute-start(f32[88,128]{1,0:T(8,128)S(1)} %get-tuple-element.62), channel_id=1, source_target_pairs={{0,14},{1,15},{2,12},{3,13},{4,10},{5,11},{6,8},{7,9},{8,6},{9,7},... | collective-permute-start | bytes 135176 | tf_op jit(solution)/shard_map/ppermute | solution.py:128
  33.5 2.7 %collective-permute-start.23 = (f32[80,128]{1,0:T(8,128)S(1)}, f32[80,128]{1,0:T(8,128)S(1)}, u32[]{:S(2)}, u32[]{:S(2)}) collective-permute-start(f32[80,128]{1,0:T(8,128)S(1)} %get-tuple-element.74), channel_id=1, source_target_pairs={{0,9},{1,8},{2,11},{3,10},{4,13},{5,12},{6,15},{7,14},{8,1},{9,0},... | collective-permute-start | bytes 122888 | tf_op jit(solution)/shard_map/ppermute | solution.py:128
  37.3 3.5 %collective-permute-start.25 = (f32[80,128]{1,0:T(8,128)S(1)}, f32[80,128]{1,0:T(8,128)S(1)}, u32[]{:S(2)}, u32[]{:S(2)}) collective-permute-start(f32[80,128]{1,0:T(8,128)S(1)} %get-tuple-element.76), channel_id=1, source_target_pairs={{0,11},{1,10},{2,9},{3,8},{4,15},{5,14},{6,13},{7,12},{8,3},{9,2},... | collective-permute-start | bytes 122888 | tf_op jit(solution)/shard_map/ppermute | solution.py:128
  40.8 2.2 %collective-permute-start.26 = (f32[80,128]{1,0:T(8,128)S(1)}, f32[80,128]{1,0:T(8,128)S(1)}, u32[]{:S(2)}, u32[]{:S(2)}) collective-permute-start(f32[80,128]{1,0:T(8,128)S(1)} %get-tuple-element.77), channel_id=1, source_target_pairs={{0,12},{1,13},{2,14},{3,15},{4,8},{5,9},{6,10},{7,11},{8,4},{9,5},... | collective-permute-start | bytes 122888 | tf_op jit(solution)/shard_map/ppermute | solution.py:128
  43.4 2.6 %unpack.2 = (f32[5,4,32,128]{3,2,1,0:T(8,128)S(1)}, f32[5,2,32,128]{3,2,1,0:T(8,128)S(1)}, f32[5,2,32,128]{3,2,1,0:T(8,128)S(1)}, f32[8,128]{1,0:T(8,128)S(1)}) custom-call(s32[128]{0:T(128)S(1)} %reshape.78.table, f32[88,128]{1,0:T(8,128)S(1)} %get-tuple-element.48.refs_0_, f32[88,128]{1,0:T(8,128)S(1)} %collective-permute-done.refs_1_, ...), custom_call_target="tpu_custom_call" | custom-call | flops 5000000 | bytes 2000000 | tf_op jit(solution)/shard_map/unpack/pallas_call | solution.py:217
  46.2 4.3 %collective-permute-start.32 = (f32[5,2,32,128]{3,2,1,0:T(8,128)S(1)}, f32[5,2,32,128]{3,2,1,0:T(8,128)S(1)}, u32[]{:S(2)}, u32[]{:S(2)}) collective-permute-start(f32[5,2,32,128]{3,2,1,0:T(8,128)S(1)} %get-tuple-element.85), channel_id=1, source_target_pairs={{1,0},{2,1},{3,2},{4,3},{5,4},{6,5},{7,6},{8,7},{9,8},{10,9},{11,1... | collective-permute-start | bytes 491528 | tf_op jit(solution)/shard_map/ppermute | solution.py:532
  51.0 3.6 %collective-permute-start.29 = (f32[80,128]{1,0:T(8,128)S(1)}, f32[80,128]{1,0:T(8,128)S(1)}, u32[]{:S(2)}, u32[]{:S(2)}) collective-permute-start(f32[80,128]{1,0:T(8,128)S(1)} %get-tuple-element.80), channel_id=1, source_target_pairs={{0,15},{1,14},{2,13},{3,12},{4,11},{5,10},{6,9},{7,8},{8,7},{9,6},... | collective-permute-start | bytes 122888 | tf_op jit(solution)/shard_map/ppermute | solution.py:128
  55.7 1.8 %collective-permute-done.28.refs_14_ = f32[80,128]{1,0:T(8,128)S(1)} collective-permute-done((f32[80,128]{1,0:T(8,128)S(1)}, f32[80,128]{1,0:T(8,128)S(1)}, u32[]{:S(2)}, u32[]{:S(2)}) %collective-permute-start.28) | collective-permute-done | bytes 40992 | tf_op jit(solution)/shard_map/ppermute | solution.py:128
  57.5 2.4 %unpack.3 = (f32[5,4,32,128]{3,2,1,0:T(8,128)S(1)}, f32[5,1,32,128]{3,2,1,0:T(8,128)S(1)}, f32[5,1,32,128]{3,2,1,0:T(8,128)S(1)}) custom-call(s32[128]{0:T(128)S(1)} %reshape.78.table, f32[80,128]{1,0:T(8,128)S(1)} %get-tuple-element.65.refs_0_, f32[80,128]{1,0:T(8,128)S(1)} %collective-permute-done.15.refs_1_, ...), custom_call_target="tpu_custom_call" | custom-call | flops 5000000 | bytes 2000000 | tf_op jit(solution)/shard_map/unpack/pallas_call | solution.py:217
  60.6 3.8 %collective-permute-start.33 = (f32[5,1,32,128]{3,2,1,0:T(8,128)S(1)}, f32[5,1,32,128]{3,2,1,0:T(8,128)S(1)}, u32[]{:S(2)}, u32[]{:S(2)}) collective-permute-start(f32[5,1,32,128]{3,2,1,0:T(8,128)S(1)} %get-tuple-element.86), channel_id=1, source_target_pairs={{1,0},{2,1},{3,2},{4,3},{5,4},{6,5},{7,6},{8,7},{9,8},{10,9},{11,1... | collective-permute-start | bytes 245768 | tf_op jit(solution)/shard_map/ppermute | solution.py:536
  64.5 2.5 %planes.2.sides_a = f32[5,4,32,128]{3,2,1,0:T(8,128)S(1)} custom-call(f32[5,4,32,128]{3,2,1,0:T(8,128)S(1)} %get-tuple-element.64.state.state_a, f32[8,128]{1,0:T(8,128)S(1)} %get-tuple-element.82.speed.first_speed), custom_call_target="tpu_custom_call" | custom-call | flops 20000000 | bytes 1000000 | tf_op jit(solution)/shard_map/planes/pallas_call | solution.py:358
  67.0 2.5 %planes.3.sides_b = f32[5,4,32,128]{3,2,1,0:T(8,128)S(1)} custom-call(f32[5,4,32,128]{3,2,1,0:T(8,128)S(1)} %get-tuple-element.81.state.state_b, f32[8,128]{1,0:T(8,128)S(1)} %get-tuple-element.82.speed.first_speed), custom_call_target="tpu_custom_call" | custom-call | flops 20000000 | bytes 1000000 | tf_op jit(solution)/shard_map/planes/pallas_call | solution.py:358
  69.5 2.5 %first_stage.1 = (f32[5,8,32,128]{3,2,1,0:T(8,128)S(1)}, f32[5,3,32,128]{3,2,1,0:T(8,128)S(1)}, f32[5,3,32,128]{3,2,1,0:T(8,128)S(1)}, f32[8,128]{1,0:T(8,128)S(1)}) custom-call(f32[5,4,32,128]{3,2,1,0:T(8,128)S(1)} %get-tuple-element.64.state.state_a, f32[5,4,32,128]{3,2,1,0:T(8,128)S(1)} %get-tuple-element.81.state.state_b, ...), custom_call_target="tpu_custom_call" | custom-call | flops 30000000 | bytes 3000000 | tf_op jit(solution)/shard_map/first_stage/pallas_call | solution.py:437
  73.9 4.4 %collective-permute-start.35 = (f32[5,3,32,128]{3,2,1,0:T(8,128)S(1)}, f32[5,3,32,128]{3,2,1,0:T(8,128)S(1)}, u32[]{:S(2)}, u32[]{:S(2)}) collective-permute-start(f32[5,3,32,128]{3,2,1,0:T(8,128)S(1)} %get-tuple-element.89), channel_id=1, source_target_pairs={{1,0},{2,1},{3,2},{4,3},{5,4},{6,5},{7,6},{8,7},{9,8},{10,9},{11,1... | collective-permute-start | bytes 737288 | tf_op jit(solution)/shard_map/ppermute | solution.py:542
  79.0 3.8 %collective-permute-start.39 = (f32[8,128]{1,0:T(8,128)S(1)}, f32[8,128]{1,0:T(8,128)S(1)}, u32[]{:S(2)}, u32[]{:S(2)}) collective-permute-start(f32[8,128]{1,0:T(8,128)S(1)} %maximum_maximum_fusion.1), channel_id=1, source_target_pairs={{0,4},{1,5},{2,6},{3,7},{4,0},{5,1},{6,2},{7,3},{8,12},{9,13},{10,... | collective-permute-start | bytes 12296 | tf_op jit(solution)/shard_map/ppermute | solution.py:512
  84.5 8.1 %second_stage.1 = f32[5,8,32,128]{3,2,1,0:T(8,128)} custom-call(f32[5,4,32,128]{3,2,1,0:T(8,128)S(1)} %get-tuple-element.64.state.state_a, f32[5,4,32,128]{3,2,1,0:T(8,128)S(1)} %get-tuple-element.81.state.state_b, f32[5,8,32,128]{3,2,1,0:T(8,128)S(1)} %get-tuple-element.87.middle, f32[5,3,32,128]{3,2,1,0:T(8,128)S(1)} %collective-permute-done.34.below, ...), custom_call_target="tpu_custom_call" | custom-call | flops 60000000 | bytes 3000000 | tf_op jit(solution)/shard_map/second_stage/pallas_call | solution.py:492
  (82 shorter events, 17.6 us)
Async XLA Ops:
  3.8 7.2 %collective-permute-start.16 = (f32[80,128]{1,0:T(8,128)S(1)}, f32[80,128]{1,0:T(8,128)S(1)}, u32[]{:S(2)}, u32[]{:S(2)}) collective-permute-start(f32[80,128]{1,0:T(8,128)S(1)} %get-tuple-element.67), channel_id=1, source_target_pairs={{0,2},{1,3},{2,0},{3,1},{4,6},{5,7},{6,4},{7,5},{8,10},{9,11},{10,... | collective-permute-start | bytes 122888 | tf_op jit(solution)/shard_map/ppermute | solution.py:128
  14.0 7.1 %collective-permute-start.3 = (f32[88,128]{1,0:T(8,128)S(1)}, f32[88,128]{1,0:T(8,128)S(1)}, u32[]{:S(2)}, u32[]{:S(2)}) collective-permute-start(f32[88,128]{1,0:T(8,128)S(1)} %get-tuple-element.52), channel_id=1, source_target_pairs={{0,4},{1,5},{2,6},{3,7},{4,0},{5,1},{6,2},{7,3},{8,12},{9,13},{10,... | collective-permute-start | bytes 135176 | tf_op jit(solution)/shard_map/ppermute | solution.py:128
  15.7 8.7 %collective-permute-start.5 = (f32[88,128]{1,0:T(8,128)S(1)}, f32[88,128]{1,0:T(8,128)S(1)}, u32[]{:S(2)}, u32[]{:S(2)}) collective-permute-start(f32[88,128]{1,0:T(8,128)S(1)} %get-tuple-element.54), channel_id=1, source_target_pairs={{0,6},{1,7},{2,4},{3,5},{4,2},{5,3},{6,0},{7,1},{8,14},{9,15},{10,... | collective-permute-start | bytes 135176 | tf_op jit(solution)/shard_map/ppermute | solution.py:128
  17.7 7.0 %collective-permute-start.6 = (f32[88,128]{1,0:T(8,128)S(1)}, f32[88,128]{1,0:T(8,128)S(1)}, u32[]{:S(2)}, u32[]{:S(2)}) collective-permute-start(f32[88,128]{1,0:T(8,128)S(1)} %get-tuple-element.55), channel_id=1, source_target_pairs={{0,7},{1,6},{2,5},{3,4},{4,3},{5,2},{6,1},{7,0},{8,15},{9,14},{10,... | collective-permute-start | bytes 135176 | tf_op jit(solution)/shard_map/ppermute | solution.py:128
  18.4 9.9 %collective-permute-start.7 = (f32[88,128]{1,0:T(8,128)S(1)}, f32[88,128]{1,0:T(8,128)S(1)}, u32[]{:S(2)}, u32[]{:S(2)}) collective-permute-start(f32[88,128]{1,0:T(8,128)S(1)} %get-tuple-element.56), channel_id=1, source_target_pairs={{0,8},{1,9},{2,10},{3,11},{4,12},{5,13},{6,14},{7,15},{8,0},{9,1},... | collective-permute-start | bytes 135176 | tf_op jit(solution)/shard_map/ppermute | solution.py:128
  21.0 7.4 %collective-permute-start.8 = (f32[88,128]{1,0:T(8,128)S(1)}, f32[88,128]{1,0:T(8,128)S(1)}, u32[]{:S(2)}, u32[]{:S(2)}) collective-permute-start(f32[88,128]{1,0:T(8,128)S(1)} %get-tuple-element.57), channel_id=1, source_target_pairs={{0,9},{1,8},{2,11},{3,10},{4,13},{5,12},{6,15},{7,14},{8,1},{9,0},... | collective-permute-start | bytes 135176 | tf_op jit(solution)/shard_map/ppermute | solution.py:128
  21.1 11.2 %collective-permute-start.9 = (f32[88,128]{1,0:T(8,128)S(1)}, f32[88,128]{1,0:T(8,128)S(1)}, u32[]{:S(2)}, u32[]{:S(2)}) collective-permute-start(f32[88,128]{1,0:T(8,128)S(1)} %get-tuple-element.58), channel_id=1, source_target_pairs={{0,10},{1,11},{2,8},{3,9},{4,14},{5,15},{6,12},{7,13},{8,2},{9,3},... | collective-permute-start | bytes 135176 | tf_op jit(solution)/shard_map/ppermute | solution.py:128
  24.4 9.1 %collective-permute-start.10 = (f32[88,128]{1,0:T(8,128)S(1)}, f32[88,128]{1,0:T(8,128)S(1)}, u32[]{:S(2)}, u32[]{:S(2)}) collective-permute-start(f32[88,128]{1,0:T(8,128)S(1)} %get-tuple-element.59), channel_id=1, source_target_pairs={{0,11},{1,10},{2,9},{3,8},{4,15},{5,14},{6,13},{7,12},{8,3},{9,2},... | collective-permute-start | bytes 135176 | tf_op jit(solution)/shard_map/ppermute | solution.py:128
  24.7 8.8 %collective-permute-start.11 = (f32[88,128]{1,0:T(8,128)S(1)}, f32[88,128]{1,0:T(8,128)S(1)}, u32[]{:S(2)}, u32[]{:S(2)}) collective-permute-start(f32[88,128]{1,0:T(8,128)S(1)} %get-tuple-element.60), channel_id=1, source_target_pairs={{0,12},{1,13},{2,14},{3,15},{4,8},{5,9},{6,10},{7,11},{8,4},{9,5},... | collective-permute-start | bytes 135176 | tf_op jit(solution)/shard_map/ppermute | solution.py:128
  28.3 8.0 %collective-permute-start.12 = (f32[88,128]{1,0:T(8,128)S(1)}, f32[88,128]{1,0:T(8,128)S(1)}, u32[]{:S(2)}, u32[]{:S(2)}) collective-permute-start(f32[88,128]{1,0:T(8,128)S(1)} %get-tuple-element.61), channel_id=1, source_target_pairs={{0,13},{1,12},{2,15},{3,14},{4,9},{5,8},{6,11},{7,10},{8,5},{9,4},... | collective-permute-start | bytes 135176 | tf_op jit(solution)/shard_map/ppermute | solution.py:128
  28.4 8.9 %collective-permute-start.13 = (f32[88,128]{1,0:T(8,128)S(1)}, f32[88,128]{1,0:T(8,128)S(1)}, u32[]{:S(2)}, u32[]{:S(2)}) collective-permute-start(f32[88,128]{1,0:T(8,128)S(1)} %get-tuple-element.62), channel_id=1, source_target_pairs={{0,14},{1,15},{2,12},{3,13},{4,10},{5,11},{6,8},{7,9},{8,6},{9,7},... | collective-permute-start | bytes 135176 | tf_op jit(solution)/shard_map/ppermute | solution.py:128
  32.2 8.6 %collective-permute-start.14 = (f32[88,128]{1,0:T(8,128)S(1)}, f32[88,128]{1,0:T(8,128)S(1)}, u32[]{:S(2)}, u32[]{:S(2)}) collective-permute-start(f32[88,128]{1,0:T(8,128)S(1)} %get-tuple-element.63), channel_id=1, source_target_pairs={{0,15},{1,14},{2,13},{3,12},{4,11},{5,10},{6,9},{7,8},{8,7},{9,6},... | collective-permute-start | bytes 135176 | tf_op jit(solution)/shard_map/ppermute | solution.py:128
  33.4 12.5 %collective-permute-start.22 = (f32[80,128]{1,0:T(8,128)S(1)}, f32[80,128]{1,0:T(8,128)S(1)}, u32[]{:S(2)}, u32[]{:S(2)}) collective-permute-start(f32[80,128]{1,0:T(8,128)S(1)} %get-tuple-element.73), channel_id=1, source_target_pairs={{0,8},{1,9},{2,10},{3,11},{4,12},{5,13},{6,14},{7,15},{8,0},{9,1},... | collective-permute-start | bytes 122888 | tf_op jit(solution)/shard_map/ppermute | solution.py:128
  33.5 12.7 %collective-permute-start.23 = (f32[80,128]{1,0:T(8,128)S(1)}, f32[80,128]{1,0:T(8,128)S(1)}, u32[]{:S(2)}, u32[]{:S(2)}) collective-permute-start(f32[80,128]{1,0:T(8,128)S(1)} %get-tuple-element.74), channel_id=1, source_target_pairs={{0,9},{1,8},{2,11},{3,10},{4,13},{5,12},{6,15},{7,14},{8,1},{9,0},... | collective-permute-start | bytes 122888 | tf_op jit(solution)/shard_map/ppermute | solution.py:128
  36.3 14.2 %collective-permute-start.24 = (f32[80,128]{1,0:T(8,128)S(1)}, f32[80,128]{1,0:T(8,128)S(1)}, u32[]{:S(2)}, u32[]{:S(2)}) collective-permute-start(f32[80,128]{1,0:T(8,128)S(1)} %get-tuple-element.75), channel_id=1, source_target_pairs={{0,10},{1,11},{2,8},{3,9},{4,14},{5,15},{6,12},{7,13},{8,2},{9,3},... | collective-permute-start | bytes 122888 | tf_op jit(solution)/shard_map/ppermute | solution.py:128
  37.3 13.2 %collective-permute-start.25 = (f32[80,128]{1,0:T(8,128)S(1)}, f32[80,128]{1,0:T(8,128)S(1)}, u32[]{:S(2)}, u32[]{:S(2)}) collective-permute-start(f32[80,128]{1,0:T(8,128)S(1)} %get-tuple-element.76), channel_id=1, source_target_pairs={{0,11},{1,10},{2,9},{3,8},{4,15},{5,14},{6,13},{7,12},{8,3},{9,2},... | collective-permute-start | bytes 122888 | tf_op jit(solution)/shard_map/ppermute | solution.py:128
  40.8 10.2 %collective-permute-start.26 = (f32[80,128]{1,0:T(8,128)S(1)}, f32[80,128]{1,0:T(8,128)S(1)}, u32[]{:S(2)}, u32[]{:S(2)}) collective-permute-start(f32[80,128]{1,0:T(8,128)S(1)} %get-tuple-element.77), channel_id=1, source_target_pairs={{0,12},{1,13},{2,14},{3,15},{4,8},{5,9},{6,10},{7,11},{8,4},{9,5},... | collective-permute-start | bytes 122888 | tf_op jit(solution)/shard_map/ppermute | solution.py:128
  46.0 23.5 %collective-permute-start.30 = (f32[5,2,32,128]{3,2,1,0:T(8,128)S(1)}, f32[5,2,32,128]{3,2,1,0:T(8,128)S(1)}, u32[]{:S(2)}, u32[]{:S(2)}) collective-permute-start(f32[5,2,32,128]{3,2,1,0:T(8,128)S(1)} %get-tuple-element.83), channel_id=1, source_target_pairs={{0,1},{1,2},{2,3},{3,4},{4,5},{5,6},{6,7},{7,8},{8,9},{9,10},{10,1... | collective-permute-start | bytes 491528 | tf_op jit(solution)/shard_map/ppermute | solution.py:531
  46.2 23.3 %collective-permute-start.32 = (f32[5,2,32,128]{3,2,1,0:T(8,128)S(1)}, f32[5,2,32,128]{3,2,1,0:T(8,128)S(1)}, u32[]{:S(2)}, u32[]{:S(2)}) collective-permute-start(f32[5,2,32,128]{3,2,1,0:T(8,128)S(1)} %get-tuple-element.85), channel_id=1, source_target_pairs={{1,0},{2,1},{3,2},{4,3},{5,4},{6,5},{7,6},{8,7},{9,8},{10,9},{11,1... | collective-permute-start | bytes 491528 | tf_op jit(solution)/shard_map/ppermute | solution.py:532
  50.5 7.0 %collective-permute-start.28 = (f32[80,128]{1,0:T(8,128)S(1)}, f32[80,128]{1,0:T(8,128)S(1)}, u32[]{:S(2)}, u32[]{:S(2)}) collective-permute-start(f32[80,128]{1,0:T(8,128)S(1)} %get-tuple-element.79), channel_id=1, source_target_pairs={{0,14},{1,15},{2,12},{3,13},{4,10},{5,11},{6,8},{7,9},{8,6},{9,7},... | collective-permute-start | bytes 122888 | tf_op jit(solution)/shard_map/ppermute | solution.py:128
  60.0 9.5 %collective-permute-start.31 = (f32[5,1,32,128]{3,2,1,0:T(8,128)S(1)}, f32[5,1,32,128]{3,2,1,0:T(8,128)S(1)}, u32[]{:S(2)}, u32[]{:S(2)}) collective-permute-start(f32[5,1,32,128]{3,2,1,0:T(8,128)S(1)} %get-tuple-element.84), channel_id=1, source_target_pairs={{0,1},{1,2},{2,3},{3,4},{4,5},{5,6},{6,7},{7,8},{8,9},{9,10},{10,1... | collective-permute-start | bytes 245768 | tf_op jit(solution)/shard_map/ppermute | solution.py:535
  60.6 8.9 %collective-permute-start.33 = (f32[5,1,32,128]{3,2,1,0:T(8,128)S(1)}, f32[5,1,32,128]{3,2,1,0:T(8,128)S(1)}, u32[]{:S(2)}, u32[]{:S(2)}) collective-permute-start(f32[5,1,32,128]{3,2,1,0:T(8,128)S(1)} %get-tuple-element.86), channel_id=1, source_target_pairs={{1,0},{2,1},{3,2},{4,3},{5,4},{6,5},{7,6},{8,7},{9,8},{10,9},{11,1... | collective-permute-start | bytes 245768 | tf_op jit(solution)/shard_map/ppermute | solution.py:536
  73.9 10.5 %collective-permute-start.34 = (f32[5,3,32,128]{3,2,1,0:T(8,128)S(1)}, f32[5,3,32,128]{3,2,1,0:T(8,128)S(1)}, u32[]{:S(2)}, u32[]{:S(2)}) collective-permute-start(f32[5,3,32,128]{3,2,1,0:T(8,128)S(1)} %get-tuple-element.88), channel_id=1, source_target_pairs={{0,1},{1,2},{2,3},{3,4},{4,5},{5,6},{6,7},{7,8},{8,9},{9,10},{10,1... | collective-permute-start | bytes 737288 | tf_op jit(solution)/shard_map/ppermute | solution.py:541
  73.9 10.5 %collective-permute-start.35 = (f32[5,3,32,128]{3,2,1,0:T(8,128)S(1)}, f32[5,3,32,128]{3,2,1,0:T(8,128)S(1)}, u32[]{:S(2)}, u32[]{:S(2)}) collective-permute-start(f32[5,3,32,128]{3,2,1,0:T(8,128)S(1)} %get-tuple-element.89), channel_id=1, source_target_pairs={{1,0},{2,1},{3,2},{4,3},{5,4},{6,5},{7,6},{8,7},{9,8},{10,9},{11,1... | collective-permute-start | bytes 737288 | tf_op jit(solution)/shard_map/ppermute | solution.py:542
  (20 other events, 104.8 us)

commit v3 on v1

--- a/solution.py
+++ b/solution.py
@@ -1,5 +1,4 @@
 import functools
-import math
 
 import jax
 import jax.numpy as jnp
@@ -14,7 +13,8 @@
 FIELDS = 5
 LANES = 128
 ROWS = BY * BLOCK
-CHUNKS = ((0, 3), (1, 2))
+PAIRS = BLOCK // 2
+TILES = PAIRS * FIELDS
 
 gamma_gas = 1.4
 courant = 0.25
@@ -43,93 +43,84 @@
     return fastest + sound
 
 
-def pack_kernel(dev_count, cap, per_dev, owner_ref, blocks_ref, out_a, out_b, count, best):
+def tiled_rows(blocks):
+    count = blocks.shape[0] // 8
+    groups = blocks.reshape(count, 8, FIELDS, PAIRS, LANES).transpose(2, 0, 3, 1, 4)
+    return groups.reshape(FIELDS * count * PAIRS * 8, LANES)
+
+
+def pack_kernel(size, cap, per_dev, owner_ref, rows_ref, out, count):
     own = lax.axis_index("gx")
-    tiles = (2 * FIELDS + 1, 2 * FIELDS)
-    outs = (out_a, out_b)
 
     def clear(dest, carry):
         count[dest] = 0
         return carry
 
-    lax.fori_loop(0, dev_count, clear, 0)
-
-    def place(block, carry):
-        dest = owner_ref[own * per_dev + block]
-        rank = count[dest]
-        count[dest] = rank + 1
-        for chunk in range(2):
-            base = dest * (tiles[chunk] * cap) + rank
-            for half in range(2):
-                pair = CHUNKS[chunk][half]
-                value = blocks_ref[block, :, pair * LANES : (pair + 1) * LANES]
-                outs[chunk][pl.ds(base + half * FIELDS * cap, FIELDS, stride=cap), :] = value
+    lax.fori_loop(0, size, clear, 0)
+
+    def place(group, carry):
+        for member in range(8):
+            dest = owner_ref[own * per_dev + group * 8 + member]
+            rank = count[dest]
+            count[dest] = rank + 1
+            to = dest * (TILES * cap) + rank
+            for pair in range(PAIRS):
+                source = pl.ds((group * PAIRS + pair) * 8 + member, FIELDS, stride=per_dev * PAIRS)
+                target = pl.ds(to + pair * (FIELDS * cap), FIELDS, stride=cap)
+                out[target, :] = rows_ref[source, :]
         return carry
 
-    lax.fori_loop(0, per_dev, place, 0, unroll=4)
-    best[...] = jnp.zeros_like(best)
-
-    def speeds(dest, carry):
-        @pl.when(count[dest] > 0)
-        def _():
-            for chunk in range(2):
-                for half in range(2):
-                    base = dest * (tiles[chunk] * cap) + half * FIELDS * cap
-                    fields = [
-                        outs[chunk][pl.ds(pl.multiple_of(base + f * cap, cap), cap), :]
-                        for f in range(FIELDS)
-                    ]
-                    best[...] = jnp.maximum(best[...], wave_speed(fields))
-
-        return carry
-
-    lax.fori_loop(0, dev_count, speeds, 0)
-    top = jnp.full((cap, LANES), jnp.max(best[...]), jnp.float32)
-
-    def publish(dest, carry):
-        base = dest * (tiles[0] * cap) + 2 * FIELDS * cap
-        out_a[pl.ds(pl.multiple_of(base, cap), cap), :] = top
-        return carry
-
-    lax.fori_loop(0, dev_count, publish, 0)
-
-
-def pack(blocks, owner_list, dev_count, cap):
-    per_dev = blocks.shape[0]
-    rows_a = dev_count * cap * (2 * FIELDS + 1)
-    rows_b = dev_count * cap * 2 * FIELDS
+    lax.fori_loop(0, per_dev // 8, place, 0, unroll=2)
+
+
+def pack(rows, owner_list, size, cap, per_dev):
     return pl.pallas_call(
-        functools.partial(pack_kernel, dev_count, cap, per_dev),
-        out_shape=(
-            jax.ShapeDtypeStruct((rows_a, LANES), jnp.float32),
-            jax.ShapeDtypeStruct((rows_b, LANES), jnp.float32),
-        ),
+        functools.partial(pack_kernel, size, cap, per_dev),
+        out_shape=jax.ShapeDtypeStruct((size * TILES * cap, LANES), jnp.float32),
         in_specs=[SMEM, VMEM],
-        out_specs=(VMEM, VMEM),
-        scratch_shapes=[
-            pltpu.SMEM((dev_count,), jnp.int32),
-            pltpu.VMEM((cap, LANES), jnp.float32),
-        ],
+        out_specs=VMEM,
+        scratch_shapes=[pltpu.SMEM((size,), jnp.int32)],
         compiler_params=params(),
-        cost_estimate=cost(10_000_000, 3_000_000),
+        cost_estimate=cost(1_000_000, 3_000_000),
         name="pack",
-    )(owner_list, blocks)
-
-
-def arrival_rows(owner_list, slot_list, own, per_dev, dev_count, cap):
-    owners = owner_list.reshape(dev_count, per_dev)
-    slots = slot_list.reshape(dev_count, per_dev)
+    )(owner_list, rows)
+
+
+def fastest_kernel(rows_ref, out):
+    best = jnp.zeros((8, LANES), jnp.float32)
+    step = rows_ref.shape[0] // FIELDS
+    for first in range(0, step, 8):
+        fields = [rows_ref[f * step + first : f * step + first + 8, :] for f in range(FIELDS)]
+        best = jnp.maximum(best, wave_speed(fields))
+    out[...] = jnp.full((8, LANES), jnp.max(best), jnp.float32)
+
+
+def fastest(rows):
+    return pl.pallas_call(
+        fastest_kernel,
+        out_shape=jax.ShapeDtypeStruct((8, LANES), jnp.float32),
+        in_specs=[VMEM],
+        out_specs=VMEM,
+        compiler_params=params(),
+        cost_estimate=cost(2_000_000, 700_000),
+        name="fastest",
+    )(rows)
+
+
+def arrival_spots(owner_list, slot_list, own, per_dev, size, cap):
+    owners = owner_list.reshape(size, per_dev)
+    slots = slot_list.reshape(size, per_dev)
     mine = owners == own
     spot = jnp.arange(per_dev, dtype=jnp.int32)
     earlier = spot[None, :] < spot[:, None]
     rank = jnp.sum((mine[:, None, :] & earlier[None]).astype(jnp.int32), axis=2)
-    row = jnp.arange(dev_count, dtype=jnp.int32)[:, None] * cap + rank
+    row = jnp.arange(size, dtype=jnp.int32)[:, None] * cap + rank
     key = jnp.where(mine, slots, -1)
     hit = key.reshape(1, -1) == spot[:, None]
     return jnp.max(jnp.where(hit, row.reshape(1, -1), 0), axis=1)
 
 
-def transposed(rows, group):
+def exchanged_bits(rows, group):
     rows = list(rows)
     for bit in range(4):
         step = 1 << bit
@@ -143,70 +134,56 @@
     return rows
 
 
-def unpack_kernel(dev_count, cap, chunk, table, in_ref, *refs):
-    tiles = 2 * FIELDS + (1 if chunk == 0 else 0)
-    if chunk == 0:
-        state, low_halo, high_halo, speed, scratch = refs
-    else:
-        state, low_halo, high_halo, scratch = refs
+def unpack_kernel(cap, table, come, state, low_halo, high_halo, scratch):
     for slot in range(BY * BZ):
         p, q = divmod(slot, BZ)
         where = table[slot]
-        base = (where // cap) * (tiles * cap) + where % cap
-        for half in range(2):
-            value = in_ref[pl.ds(base + half * FIELDS * cap, FIELDS, stride=cap), :]
-            scratch[pl.ds(q * 8 + half * 4 + p, FIELDS, stride=BZ * 8), :] = value
-    group = lax.broadcasted_iota(jnp.int32, (8, LANES), 1) // 8
-
-    def one_field(f, carry):
-        rows = [
-            scratch[pl.ds(pl.multiple_of((f * BZ + q) * 8, 8), 8), :] for q in range(BZ)
-        ]
-        moved = transposed(rows, group)
-        for g in range(BZ):
-            second, b = divmod(g, BLOCK)
-            spot = pl.ds((b % 4) * 8 + b // 4, 4, stride=2)
-            for half in range(2):
-                value = moved[g][half * 4 : half * 4 + 4]
-                plane = 2 * half + second
-                state[f, plane, spot, :] = value
-                if chunk == 0:
-                    if half == 0:
-                        low_halo[f, second, spot, :] = value
-                    else:
-                        high_halo[f, second, spot, :] = value
-                else:
-                    if plane == 0:
-                        low_halo[f, 0, spot, :] = value
-                    if plane == 3:
-                        high_halo[f, 0, spot, :] = value
-        return carry
-
-    lax.fori_loop(0, FIELDS, one_field, 0)
-    if chunk == 0:
-        best = in_ref[pl.ds(2 * FIELDS * cap, cap), :]
-        for source in range(1, dev_count):
-            start = source * tiles * cap + 2 * FIELDS * cap
-            best = jnp.maximum(best, in_ref[pl.ds(start, cap), :])
-        speed[...] = jnp.full((8, LANES), jnp.max(best), jnp.float32)
-
-
-def unpack(table, arrived, chunk, dev_count, cap):
-    planes = 2 if chunk == 0 else 1
-    halo = jax.ShapeDtypeStruct((FIELDS, planes, ROWS, LANES), jnp.float32)
-    shapes = [jax.ShapeDtypeStruct((FIELDS, 4, ROWS, LANES), jnp.float32), halo, halo]
-    if chunk == 0:
-        shapes.append(jax.ShapeDtypeStruct((8, LANES), jnp.float32))
+        source = lax.div(where, cap)
+        rank = lax.rem(where, cap)
+        for pair in range(PAIRS):
+            couple, h = divmod(pair, 2)
+            base = source * (TILES * cap) + rank + pair * (FIELDS * cap)
+            value = come[pl.ds(base, FIELDS, stride=cap), :]
+            row = (couple * BZ + q) * 8 + 2 * p + h
+            scratch[pl.ds(row, FIELDS, stride=PAIRS // 2 * BZ * 8), :] = value
+    group = lax.broadcasted_iota(jnp.int32, (8, LANES), 1) // BLOCK
+    even = lax.broadcasted_iota(jnp.int32, (8, LANES), 0) % 2 == 0
+
+    for f in range(FIELDS):
+        for couple in range(PAIRS // 2):
+            first = (f * (PAIRS // 2) + couple) * BZ * 8
+            rows = [scratch[first + q * 8 : first + q * 8 + 8, :] for q in range(BZ)]
+            moved = exchanged_bits(rows, group)
+            for second in range(2):
+                for j in range(4):
+                    lower = moved[second * BLOCK + j]
+                    upper = moved[second * BLOCK + j + 4]
+                    planes = (
+                        jnp.where(even, lower, pltpu.roll(upper, 1, 0)),
+                        jnp.where(even, pltpu.roll(lower, 7, 0), upper),
+                    )
+                    rows = slice(j * 8, j * 8 + 8)
+                    for h in range(2):
+                        plane = 4 * couple + 2 * h + second
+                        state[f, plane, rows, :] = planes[h]
+                        if plane < 3:
+                            low_halo[f, plane, rows, :] = planes[h]
+                        if plane >= 5:
+                            high_halo[f, plane - 5, rows, :] = planes[h]
+
+
+def unpack(table, come, cap):
+    halo = jax.ShapeDtypeStruct((FIELDS, 3, ROWS, LANES), jnp.float32)
     return pl.pallas_call(
-        functools.partial(unpack_kernel, dev_count, cap, chunk),
-        out_shape=shapes,
+        functools.partial(unpack_kernel, cap),
+        out_shape=(jax.ShapeDtypeStruct((FIELDS, BLOCK, ROWS, LANES), jnp.float32), halo, halo),
         in_specs=[SMEM, VMEM],
-        out_specs=[VMEM] * len(shapes),
-        scratch_shapes=[pltpu.VMEM((FIELDS * BZ * 8, LANES), jnp.float32)],
+        out_specs=(VMEM,) * 3,
+        scratch_shapes=[pltpu.VMEM((FIELDS * (PAIRS // 2) * BZ * 8, LANES), jnp.float32)],
         compiler_params=params(),
         cost_estimate=cost(5_000_000, 2_000_000),
         name="unpack",
-    )(table, arrived)
+    )(table, come)
 
 
 def y_up(x):
@@ -372,32 +349,23 @@
         yield field, open_divergence(fluxes, scaled)
 
 
-def first_kernel(
-    state_a, state_b, sides_a, sides_b, below_a, below_b, above_a, above_b, speed,
-    middle, low, high, top,
-):
+def first_kernel(state, sides, below, above, speed, middle, low, high, top):
     half_speed = 0.5 * speed[0:1, :]
     factor = (courant / 6.0) / speed[0:1, :]
-    where = {0: 0, 1: 1, 6: 2, 7: 3}
 
     def group(j, best):
         rows = pl.ds(pl.multiple_of(j * 8, 8), 8)
 
-        def pick(of_a, of_b, f, plane):
-            if plane in where:
-                return of_a[f, where[plane], rows, :]
-            return of_b[f, plane - 2, rows, :]
-
         def get(f, plane):
             if plane < 0:
-                return below_b[f, 0, rows, :] if plane == -3 else below_a[f, plane + 2, rows, :]
+                return below[f, plane + 3, rows, :]
             if plane >= BLOCK:
-                return above_b[f, 0, rows, :] if plane == 10 else above_a[f, plane - 8, rows, :]
-            return pick(state_a, state_b, f, plane)
+                return above[f, plane - BLOCK, rows, :]
+            return state[f, plane, rows, :]
 
         for field, along_x in across(get, half_speed):
             for plane in range(BLOCK):
-                total = along_x[plane] + pick(sides_a, sides_b, field, plane)
+                total = along_x[plane] + sides[field, plane, rows, :]
                 value = get(field, plane) - factor * total
                 middle[field, plane, rows, :] = value
                 if plane < 3:
@@ -411,15 +379,18 @@
         return best
 
     best = lax.fori_loop(0, 4, group, jnp.zeros((8, LANES), jnp.float32))
-    top[...] = jnp.full((8, LANES), jnp.max(best), jnp.float32)
-
-
-def first_stage(*operands):
+    size = top.shape[0] // 8
+    most = jnp.full((8, LANES), jnp.max(best), jnp.float32)
+    for dest in range(size):
+        top[dest * 8 : dest * 8 + 8, :] = most
+
+
+def first_stage(size, *operands):
     whole = jax.ShapeDtypeStruct((FIELDS, BLOCK, ROWS, LANES), jnp.float32)
     halo = jax.ShapeDtypeStruct((FIELDS, 3, ROWS, LANES), jnp.float32)
     return pl.pallas_call(
         first_kernel,
-        out_shape=(whole, halo, halo, jax.ShapeDtypeStruct((8, LANES), jnp.float32)),
+        out_shape=(whole, halo, halo, jax.ShapeDtypeStruct((size * 8, LANES), jnp.float32)),
         in_specs=[VMEM] * len(operands),
         out_specs=(VMEM,) * 4,
         compiler_params=params(),
@@ -428,14 +399,11 @@
     )(*operands)
 
 
-def second_kernel(
-    state_a, state_b, middle, below, above, first_speed, speeds, out, sides
-):
+def second_kernel(start, middle, below, above, first_speed, speeds, out, sides):
     first = first_speed[0:1, :]
-    second = speeds[0:1, :]
+    second = jnp.full((1, LANES), jnp.max(speeds[...]), jnp.float32)
     half_speed = 0.5 * second
     factor = (courant / 12.0) / first
-    where = {0: 0, 1: 1, 6: 2, 7: 3}
 
     def one_plane(plane, carry):
         fields = [middle[f, plane] for f in range(FIELDS)]
@@ -459,11 +427,9 @@
         for field, along_x in across(get, half_speed):
             for plane in range(BLOCK):
                 total = along_x[plane] + sides[field, plane, rows, :]
-                if plane in where:
-                    start = state_a[field, where[plane], rows, :]
-                else:
-                    start = state_b[field, plane - 2, rows, :]
-                value = 0.5 * start + (0.5 * get(field, plane) - factor * total)
+                value = 0.5 * start[field, plane, rows, :] + (
+                    0.5 * get(field, plane) - factor * total
+                )
                 out[field, plane, spread, :] = value
         return carry
 
@@ -489,9 +455,9 @@
     while reach < size:
         copies = [value]
         for times in range(1, 4):
-            shift = reach * times
-            if shift < size:
-                pairs = [(i, (i + shift) % size) for i in range(size)]
+            turn = reach * times
+            if turn < size:
+                pairs = [(i, i ^ turn) for i in range(size)]
                 copies.append(lax.ppermute(value, axis, pairs))
         value = functools.reduce(jnp.maximum, copies)
         reach *= 4
@@ -506,25 +472,23 @@
     up = [(i, (i + 1) % size) for i in range(size)]
     down = [(j, i) for i, j in up]
 
-    out_a, out_b = pack(blocks, owner_list, size, cap)
-    come_a = lax.all_to_all(out_a, "gx", split_axis=0, concat_axis=0, tiled=True)
-    come_b = lax.all_to_all(out_b, "gx", split_axis=0, concat_axis=0, tiled=True)
-    table = arrival_rows(owner_list, slot_list, own, per_dev, size, cap)
-    state_a, low_a, high_a, speed = unpack(table, come_a, 0, size, cap)
-    below_a = lax.ppermute(high_a, "gx", up)
-    above_a = lax.ppermute(low_a, "gx", down)
-    sides_a = along_planes(state_a, speed)
-    state_b, low_b, high_b = unpack(table, come_b, 1, size, cap)
-    below_b = lax.ppermute(high_b, "gx", up)
-    above_b = lax.ppermute(low_b, "gx", down)
-    sides_b = along_planes(state_b, speed)
-    middle, low, high, top = first_stage(
-        state_a, state_b, sides_a, sides_b, below_a, below_b, above_a, above_b, speed
+    rows = tiled_rows(blocks)
+    parts = pack(rows, owner_list, size, cap, per_dev)
+    parts, rows, owner_list, slot_list = lax.optimization_barrier(
+        (parts, rows, owner_list, slot_list)
     )
+    come = lax.all_to_all(parts, "gx", split_axis=0, concat_axis=0, tiled=True)
+    table = arrival_spots(owner_list, slot_list, own, per_dev, size, cap)
+    speed = everyone_max(fastest(rows), "gx", size)
+    state, low, high = unpack(table, come, cap)
     below = lax.ppermute(high, "gx", up)
     above = lax.ppermute(low, "gx", down)
-    second = everyone_max(top, "gx", size)
-    return second_stage(state_a, state_b, middle, below, above, speed, second)
+    sides = along_planes(state, speed)
+    middle, low, high, top = first_stage(size, state, sides, below, above, speed)
+    speeds = lax.all_to_all(top, "gx", split_axis=0, concat_axis=0, tiled=True)
+    below = lax.ppermute(high, "gx", up)
+    above = lax.ppermute(low, "gx", down)
+    return second_stage(state, middle, below, above, speed, speeds)
 
 
 def solution(mesh):

time: 87.4 us -> 85.1 us (0.974)
  blocking collectives: 26.3 us -> 9.47 us
  waiting for transfers between devices: 13.6 us -> 26.4 us
  starting transfers between devices: 20.6 us -> 25.2 us
  Pallas kernels: 23.5 us -> 21.1 us
    all_to_all x1, blocking collectives: 26.3 us -> 9.47 us  [per_device(): speeds = lax.all_to_all(top, 'gx', split_axis=0, concat_axis=0, tiled=True)]
    all_to_all x1, waiting for transfers between devices: 8.37 us -> 24.3 us  [per_device(): come = lax.all_to_all(parts, 'gx', split_axis=0, concat_axis=0, tiled=True)]
    ppermute x4 -> x0, starting transfers between devices: 9.2 us -> none  [the longest x1 3.91 us: per_device(): above_a = lax.ppermute(low_a, 'gx', down)]
    ppermute x1 -> x2, starting transfers between devices: 3.18 us -> 10.3 us  [per_device(): above = lax.ppermute(low, 'gx', down)]
    all_to_all x1, starting transfers between devices: 3.65 us -> 7.49 us  [per_device(): come = lax.all_to_all(parts, 'gx', split_axis=0, concat_axis=0, tiled=True)]
    ppermute x6, starting transfers between devices: 3.36 us -> 6.58 us  [everyone_max(): copies.append(lax.ppermute(value, axis, pairs))]
    ppermute x6, waiting for transfers between devices: 5.17 us -> 2.13 us  [everyone_max(): copies.append(lax.ppermute(value, axis, pairs))]
    pallas_call x3, Pallas kernels: 7.92 us -> 5.34 us  [the longest x1 2.79 us: unpack(): pl.pallas_call(functools.partial(unpack_kernel, cap), out_shape=(jax.Shap...]
  transfers between devices with their start and end apart: 13 -> 11, of which waited for: 6 -> 3; matrix products, arithmetic and copies ran while one was open for 1% -> 1% of each run, Pallas kernels for 12% -> 9%
where the time goes in v3:
time: 85.1 us; the launch traced here: 84.8 us
  waiting for transfers between devices  26.4 us (31%)
  starting transfers between devices  25.2 us (30%)
  Pallas kernels  21.1 us (25%)
  blocking collectives  9.47 us (11%)
  local copies, waits for them, and re-layouts  1.94 us (2%)
    all_to_all x1, waiting for transfers between devices, per_device(): come = lax.all_to_all(parts, 'gx', split_axis=0, concat_axis=0, tiled=True)  24.3 us
    ppermute x2, starting transfers between devices, per_device(): above = lax.ppermute(low, 'gx', down)  10.3 us
    all_to_all x1, blocking collectives, per_device(): speeds = lax.all_to_all(top, 'gx', split_axis=0, concat_axis=0, tiled=True)  9.47 us
    pallas_call x1, Pallas kernels, second_stage(): pl.pallas_call(second_kernel, out_shape=jax.ShapeDtypeStruct(whole, jnp.f...  8.25 us
    all_to_all x1, starting transfers between devices, per_device(): come = lax.all_to_all(parts, 'gx', split_axis=0, concat_axis=0, tiled=True)  7.49 us
    ppermute x6, starting transfers between devices, everyone_max(): copies.append(lax.ppermute(value, axis, pairs))  6.58 us
    pallas_call x1, Pallas kernels, along_planes(): pl.pallas_call(plane_kernel, out_shape=jax.ShapeDtypeStruct(state.shape,...  4.99 us
    pallas_call x1, Pallas kernels, unpack(): pl.pallas_call(functools.partial(unpack_kernel, cap), out_shape=(jax.Shap...  2.79 us
  transfers between devices with their start and end apart: 11, of which 3 were waited for; matrix products, arithmetic and copies ran while one was open for 1% of the time, Pallas kernels for 9%

profile of v3, /device:TPU:0, one launch (start us, length us, event | category | flops | bytes accessed | tf_op | source)
XLA Modules:
  0.0 84.8 jit_solution(11094716321319972095)
XLA Ops:
  0.0 1.1 %copy-done = f32[64,5,512]{2,0,1:T(8,128)S(1)} copy-done((f32[64,5,512]{2,0,1:T(8,128)S(1)}, f32[64,5,512]{2,0,1:T(8,128)}, u32[]{:S(2)}) %copy-start) | copy-done | bytes 655384
  1.1 0.7 copy-done.2
  1.8 2.3 %pack.1 = f32[2560,128]{1,0:T(8,128)} custom-call(s32[1024]{0:T(1024)S(1)} %copy-done.2, f32[1280,128]{1,0:T(8,128)S(1)} %bitcast.10), custom_call_target="tpu_custom_call" | custom-call | flops 1000000 | bytes 3000000 | tf_op jit(solution)/shard_map/pack/pallas_call | solution.py:77
  4.1 7.5 %all-to-all-start = ((f32[16,160,128]{2,1,0:T(8,128)}), f32[16,160,128]{2,1,0:T(8,128)S(1)}, u32[]{:S(2)}, u32[]{:S(2)}) async-start(f32[16,160,128]{2,1,0:T(8,128)} %bitcast.3), calls=%async_computation | async-start | bytes 2621440 | tf_op jit(solution)/shard_map/all_to_all | solution.py:480
  11.6 0.2 fastest.1
  11.9 1.7 %collective-permute-start.2 = (f32[8,128]{1,0:T(8,128)S(1)}, f32[8,128]{1,0:T(8,128)S(1)}, u32[]{:S(2)}, u32[]{:S(2)}) collective-permute-start(f32[8,128]{1,0:T(8,128)S(1)} %fastest.1), channel_id=1, source_target_pairs={{0,3},{1,2},{2,1},{3,0},{4,7},{5,6},{6,5},{7,4},{8,11},{9,10},{10,... | collective-permute-start | bytes 12296 | tf_op jit(solution)/shard_map/ppermute | solution.py:461
  13.6 0.4 collective-permute-start.1
  14.0 0.1 eq.33
  14.1 0.3 convert_reduce_fusion
  14.6 0.1 select_reduce_fusion.table
  14.7 24.3 %all-to-all-done = f32[16,160,128]{2,1,0:T(8,128)S(1)} async-done(((f32[16,160,128]{2,1,0:T(8,128)}), f32[16,160,128]{2,1,0:T(8,128)S(1)}, u32[]{:S(2)}, u32[]{:S(2)}) %all-to-all-start) | async-done | bytes 1310752 | tf_op jit(solution)/shard_map/all_to_all | solution.py:480
  39.0 2.8 %unpack.1 = (f32[5,8,32,128]{3,2,1,0:T(8,128)S(1)}, f32[5,3,32,128]{3,2,1,0:T(8,128)S(1)}, f32[5,3,32,128]{3,2,1,0:T(8,128)S(1)}) custom-call(s32[64]{0:T(128)S(1)} %select_reduce_fusion.table, f32[2560,128]{1,0:T(8,128)S(1)} %bitcast.9), custom_call_target="tpu_custom_call" | custom-call | flops 5000000 | bytes 2000000 | tf_op jit(solution)/shard_map/unpack/pallas_call | solution.py:177
  41.8 0.8 collective-permute-start.6
  42.6 5.8 %collective-permute-start.7 = (f32[5,3,32,128]{3,2,1,0:T(8,128)S(1)}, f32[5,3,32,128]{3,2,1,0:T(8,128)S(1)}, u32[]{:S(2)}, u32[]{:S(2)}) collective-permute-start(f32[5,3,32,128]{3,2,1,0:T(8,128)S(1)} %get-tuple-element.22), channel_id=1, source_target_pairs={{1,0},{2,1},{3,2},{4,3},{5,4},{6,5},{7,6},{8,7},{9,8},{10,9},{11,1... | collective-permute-start | bytes 737288 | tf_op jit(solution)/shard_map/ppermute | solution.py:485
  48.5 0.1 collective-permute-start.5
  48.6 2.3 %collective-permute-start.4 = (f32[8,128]{1,0:T(8,128)S(1)}, f32[8,128]{1,0:T(8,128)S(1)}, u32[]{:S(2)}, u32[]{:S(2)}) collective-permute-start(f32[8,128]{1,0:T(8,128)S(1)} %maximum_maximum_fusion.1), channel_id=1, source_target_pairs={{0,8},{1,9},{2,10},{3,11},{4,12},{5,13},{6,14},{7,15},{8,0},{9,1},... | collective-permute-start | bytes 12296 | tf_op jit(solution)/shard_map/ppermute | solution.py:461
  50.9 2.1 %collective-permute-start.3 = (f32[8,128]{1,0:T(8,128)S(1)}, f32[8,128]{1,0:T(8,128)S(1)}, u32[]{:S(2)}, u32[]{:S(2)}) collective-permute-start(f32[8,128]{1,0:T(8,128)S(1)} %maximum_maximum_fusion.1), channel_id=1, source_target_pairs={{0,4},{1,5},{2,6},{3,7},{4,0},{5,1},{6,2},{7,3},{8,12},{9,13},{10,... | collective-permute-start | bytes 12296 | tf_op jit(solution)/shard_map/ppermute | solution.py:461
  52.9 1.1 %collective-permute-done.5 = f32[8,128]{1,0:T(8,128)S(1)} collective-permute-done((f32[8,128]{1,0:T(8,128)S(1)}, f32[8,128]{1,0:T(8,128)S(1)}, u32[]{:S(2)}, u32[]{:S(2)}) %collective-permute-start.5) | collective-permute-done | bytes 4128 | tf_op jit(solution)/shard_map/ppermute | solution.py:461
  54.0 1.0 %collective-permute-done.4 = f32[8,128]{1,0:T(8,128)S(1)} collective-permute-done((f32[8,128]{1,0:T(8,128)S(1)}, f32[8,128]{1,0:T(8,128)S(1)}, u32[]{:S(2)}, u32[]{:S(2)}) %collective-permute-start.4) | collective-permute-done | bytes 4128 | tf_op jit(solution)/shard_map/ppermute | solution.py:461
  55.1 5.0 %planes.1.sides = f32[5,8,32,128]{3,2,1,0:T(8,128)S(1)} custom-call(f32[5,8,32,128]{3,2,1,0:T(8,128)S(1)} %get-tuple-element.19.state.start, f32[8,128]{1,0:T(8,128)S(1)} %maximum_maximum_fusion.speed.first_speed), custom_call_target="tpu_custom_call" | custom-call | flops 20000000 | bytes 1000000 | tf_op jit(solution)/shard_map/planes/pallas_call | solution.py:318
  60.1 2.5 %first_stage.1 = (f32[5,8,32,128]{3,2,1,0:T(8,128)S(1)}, f32[5,3,32,128]{3,2,1,0:T(8,128)S(1)}, f32[5,3,32,128]{3,2,1,0:T(8,128)S(1)}, f32[128,128]{1,0:T(8,128)S(1)}) custom-call(f32[5,8,32,128]{3,2,1,0:T(8,128)S(1)} %get-tuple-element.19.state.start, f32[5,8,32,128]{3,2,1,0:T(8,128)S(1)} %planes.1.sides, ...), custom_call_target="tpu_custom_call" | custom-call | flops 30000000 | bytes 3000000 | tf_op jit(solution)/shard_map/first_stage/pallas_call | solution.py:391
  62.6 4.4 %collective-permute-start.9 = (f32[5,3,32,128]{3,2,1,0:T(8,128)S(1)}, f32[5,3,32,128]{3,2,1,0:T(8,128)S(1)}, u32[]{:S(2)}, u32[]{:S(2)}) collective-permute-start(f32[5,3,32,128]{3,2,1,0:T(8,128)S(1)} %get-tuple-element.25), channel_id=1, source_target_pairs={{1,0},{2,1},{3,2},{4,3},{5,4},{6,5},{7,6},{8,7},{9,8},{10,9},{11,1... | collective-permute-start | bytes 737288 | tf_op jit(solution)/shard_map/ppermute | solution.py:490
  67.1 9.5 %all_to_all.22 = f32[16,8,128]{2,1,0:T(8,128)S(1)} all-to-all(f32[16,8,128]{2,1,0:T(8,128)S(1)} %bitcast.13), channel_id=1, replica_groups=mesh['runs'=2,'gx'=16] {'gx'}, dimensions={0} | all-to-all | bytes 131072 | tf_op jit(solution)/shard_map/all_to_all | solution.py:488
  76.5 8.2 %second_stage.1 = f32[5,8,32,128]{3,2,1,0:T(8,128)} custom-call(f32[5,8,32,128]{3,2,1,0:T(8,128)S(1)} %get-tuple-element.19.state.start, f32[5,8,32,128]{3,2,1,0:T(8,128)S(1)} %get-tuple-element.23.middle, f32[5,3,32,128]{3,2,1,0:T(8,128)S(1)} %collective-permute-done.8.below, f32[5,3,32,128]{3,2,1,0:T(8,128)S(1)} %collective-permute-done.9.above, ...), custom_call_target="tpu_custom_call" | custom-call | flops 60000000 | bytes 3000000 | tf_op jit(solution)/shard_map/second_stage/pallas_call | solution.py:441
  (25 shorter events, 0.3 us)
Async XLA Ops:
  0.0 1.1 %copy-start = (f32[64,5,512]{2,0,1:T(8,128)S(1)}, f32[64,5,512]{2,0,1:T(8,128)}, u32[]{:S(2)}) copy-start(f32[64,5,512]{2,0,1:T(8,128)} %param.3) | copy-start | bytes 1966084
  1.1 0.7 copy-start.2
  4.1 7.5 %copy-start.1 = (f32[64,5,512]{2,0,1:T(8,128)S(1)}, f32[64,5,512]{2,0,1:T(8,128)}, u32[]{:S(2)}) copy-start(f32[64,5,512]{2,0,1:T(8,128)} %param.3) | copy-start | bytes 1966084
  4.1 9.9 %copy-start.3 = (s32[1024]{0:T(1024)S(1)}, s32[1024]{0:T(1024)}, u32[]{:S(2)}) copy-start(s32[1024]{0:T(1024)} %owner_ref.1) | copy-start | bytes 12292
  4.1 9.9 %copy-start.4 = (s32[1024]{0:T(1024)S(1)}, s32[1024]{0:T(1024)}, u32[]{:S(2)}) copy-start(s32[1024]{0:T(1024)} %param.5) | copy-start | bytes 12292
  4.1 34.9 %all-to-all-start = ((f32[16,160,128]{2,1,0:T(8,128)}), f32[16,160,128]{2,1,0:T(8,128)S(1)}, u32[]{:S(2)}, u32[]{:S(2)}) async-start(f32[16,160,128]{2,1,0:T(8,128)} %bitcast.3), calls=%async_computation | async-start | bytes 2621440 | tf_op jit(solution)/shard_map/all_to_all | solution.py:480
  11.9 36.6 %collective-permute-start.2 = (f32[8,128]{1,0:T(8,128)S(1)}, f32[8,128]{1,0:T(8,128)S(1)}, u32[]{:S(2)}, u32[]{:S(2)}) collective-permute-start(f32[8,128]{1,0:T(8,128)S(1)} %fastest.1), channel_id=1, source_target_pairs={{0,3},{1,2},{2,1},{3,0},{4,7},{5,6},{6,5},{7,4},{8,11},{9,10},{10,... | collective-permute-start | bytes 12296 | tf_op jit(solution)/shard_map/ppermute | solution.py:461
  13.6 34.9 %collective-permute-start.1 = (f32[8,128]{1,0:T(8,128)S(1)}, f32[8,128]{1,0:T(8,128)S(1)}, u32[]{:S(2)}, u32[]{:S(2)}) collective-permute-start(f32[8,128]{1,0:T(8,128)S(1)} %fastest.1), channel_id=1, source_target_pairs={{0,2},{1,3},{2,0},{3,1},{4,6},{5,7},{6,4},{7,5},{8,10},{9,11},{10,... | collective-permute-start | bytes 12296 | tf_op jit(solution)/shard_map/ppermute | solution.py:461
  14.0 34.5 %collective-permute-start = (f32[8,128]{1,0:T(8,128)S(1)}, f32[8,128]{1,0:T(8,128)S(1)}, u32[]{:S(2)}, u32[]{:S(2)}) collective-permute-start(f32[8,128]{1,0:T(8,128)S(1)} %fastest.1), channel_id=1, source_target_pairs={{0,1},{1,0},{2,3},{3,2},{4,5},{5,4},{6,7},{7,6},{8,9},{9,8},{10,11... | collective-permute-start | bytes 12296 | tf_op jit(solution)/shard_map/ppermute | solution.py:461
  41.8 18.3 %collective-permute-start.6 = (f32[5,3,32,128]{3,2,1,0:T(8,128)S(1)}, f32[5,3,32,128]{3,2,1,0:T(8,128)S(1)}, u32[]{:S(2)}, u32[]{:S(2)}) collective-permute-start(f32[5,3,32,128]{3,2,1,0:T(8,128)S(1)} %get-tuple-element.21), channel_id=1, source_target_pairs={{0,1},{1,2},{2,3},{3,4},{4,5},{5,6},{6,7},{7,8},{8,9},{9,10},{10,1... | collective-permute-start | bytes 737288 | tf_op jit(solution)/shard_map/ppermute | solution.py:484
  42.6 17.5 %collective-permute-start.7 = (f32[5,3,32,128]{3,2,1,0:T(8,128)S(1)}, f32[5,3,32,128]{3,2,1,0:T(8,128)S(1)}, u32[]{:S(2)}, u32[]{:S(2)}) collective-permute-start(f32[5,3,32,128]{3,2,1,0:T(8,128)S(1)} %get-tuple-element.22), channel_id=1, source_target_pairs={{1,0},{2,1},{3,2},{4,3},{5,4},{6,5},{7,6},{8,7},{9,8},{10,9},{11,1... | collective-permute-start | bytes 737288 | tf_op jit(solution)/shard_map/ppermute | solution.py:485
  48.5 5.6 %collective-permute-start.5 = (f32[8,128]{1,0:T(8,128)S(1)}, f32[8,128]{1,0:T(8,128)S(1)}, u32[]{:S(2)}, u32[]{:S(2)}) collective-permute-start(f32[8,128]{1,0:T(8,128)S(1)} %maximum_maximum_fusion.1), channel_id=1, source_target_pairs={{0,12},{1,13},{2,14},{3,15},{4,8},{5,9},{6,10},{7,11},{8,4},{9,5},... | collective-permute-start | bytes 12296 | tf_op jit(solution)/shard_map/ppermute | solution.py:461
  48.6 6.5 %collective-permute-start.4 = (f32[8,128]{1,0:T(8,128)S(1)}, f32[8,128]{1,0:T(8,128)S(1)}, u32[]{:S(2)}, u32[]{:S(2)}) collective-permute-start(f32[8,128]{1,0:T(8,128)S(1)} %maximum_maximum_fusion.1), channel_id=1, source_target_pairs={{0,8},{1,9},{2,10},{3,11},{4,12},{5,13},{6,14},{7,15},{8,0},{9,1},... | collective-permute-start | bytes 12296 | tf_op jit(solution)/shard_map/ppermute | solution.py:461
  50.9 4.2 %collective-permute-start.3 = (f32[8,128]{1,0:T(8,128)S(1)}, f32[8,128]{1,0:T(8,128)S(1)}, u32[]{:S(2)}, u32[]{:S(2)}) collective-permute-start(f32[8,128]{1,0:T(8,128)S(1)} %maximum_maximum_fusion.1), channel_id=1, source_target_pairs={{0,4},{1,5},{2,6},{3,7},{4,0},{5,1},{6,2},{7,3},{8,12},{9,13},{10,... | collective-permute-start | bytes 12296 | tf_op jit(solution)/shard_map/ppermute | solution.py:461
  62.6 14.0 %collective-permute-start.8 = (f32[5,3,32,128]{3,2,1,0:T(8,128)S(1)}, f32[5,3,32,128]{3,2,1,0:T(8,128)S(1)}, u32[]{:S(2)}, u32[]{:S(2)}) collective-permute-start(f32[5,3,32,128]{3,2,1,0:T(8,128)S(1)} %get-tuple-element.24), channel_id=1, source_target_pairs={{0,1},{1,2},{2,3},{3,4},{4,5},{5,6},{6,7},{7,8},{8,9},{9,10},{10,1... | collective-permute-start | bytes 737288 | tf_op jit(solution)/shard_map/ppermute | solution.py:489
  62.6 13.9 %collective-permute-start.9 = (f32[5,3,32,128]{3,2,1,0:T(8,128)S(1)}, f32[5,3,32,128]{3,2,1,0:T(8,128)S(1)}, u32[]{:S(2)}, u32[]{:S(2)}) collective-permute-start(f32[5,3,32,128]{3,2,1,0:T(8,128)S(1)} %get-tuple-element.25), channel_id=1, source_target_pairs={{1,0},{2,1},{3,2},{4,3},{5,4},{6,5},{7,6},{8,7},{9,8},{10,9},{11,1... | collective-permute-start | bytes 737288 | tf_op jit(solution)/shard_map/ppermute | solution.py:490

commit v4 on v3

--- a/solution.py
+++ b/solution.py
@@ -45,53 +45,60 @@
 
 def tiled_rows(blocks):
     count = blocks.shape[0] // 8
-    groups = blocks.reshape(count, 8, FIELDS, PAIRS, LANES).transpose(2, 0, 3, 1, 4)
-    return groups.reshape(FIELDS * count * PAIRS * 8, LANES)
-
-
-def pack_kernel(size, cap, per_dev, owner_ref, rows_ref, out, count):
+    return blocks.reshape(count, 8, FIELDS, PAIRS, LANES).transpose(2, 0, 3, 1, 4)
+
+
+def pack_kernel(size, per_dev, owner_hbm, rows_hbm, out, owner, count, sems):
     own = lax.axis_index("gx")
+    fetch = pltpu.make_async_copy(owner_hbm, owner, sems.at[0])
+    fetch.start()
 
     def clear(dest, carry):
         count[dest] = 0
         return carry
 
     lax.fori_loop(0, size, clear, 0)
-
-    def place(group, carry):
-        for member in range(8):
-            dest = owner_ref[own * per_dev + group * 8 + member]
-            rank = count[dest]
-            count[dest] = rank + 1
-            to = dest * (TILES * cap) + rank
-            for pair in range(PAIRS):
-                source = pl.ds((group * PAIRS + pair) * 8 + member, FIELDS, stride=per_dev * PAIRS)
-                target = pl.ds(to + pair * (FIELDS * cap), FIELDS, stride=cap)
-                out[target, :] = rows_ref[source, :]
+    fetch.wait()
+
+    def place(block, carry):
+        dest = owner[own * per_dev + block]
+        rank = count[dest]
+        count[dest] = rank + 1
+        pltpu.make_async_copy(
+            rows_hbm.at[:, lax.div(block, 8), :, lax.rem(block, 8)],
+            out.at[dest, :, :, rank],
+            sems.at[1],
+        ).start()
         return carry
 
-    lax.fori_loop(0, per_dev // 8, place, 0, unroll=2)
+    lax.fori_loop(0, per_dev, place, 0, unroll=8)
+    half = out.at[pl.ds(0, size // 2)]
+    pltpu.make_async_copy(half, half, sems.at[1]).wait()
 
 
 def pack(rows, owner_list, size, cap, per_dev):
     return pl.pallas_call(
-        functools.partial(pack_kernel, size, cap, per_dev),
-        out_shape=jax.ShapeDtypeStruct((size * TILES * cap, LANES), jnp.float32),
-        in_specs=[SMEM, VMEM],
+        functools.partial(pack_kernel, size, per_dev),
+        out_shape=jax.ShapeDtypeStruct((size, FIELDS, PAIRS, cap, 1, LANES), jnp.float32),
+        in_specs=[pl.BlockSpec(memory_space=pltpu.HBM)] * 2,
         out_specs=VMEM,
-        scratch_shapes=[pltpu.SMEM((size,), jnp.int32)],
+        scratch_shapes=[
+            pltpu.SMEM(owner_list.shape, jnp.int32),
+            pltpu.SMEM((size,), jnp.int32),
+            pltpu.SemaphoreType.DMA((2,)),
+        ],
         compiler_params=params(),
         cost_estimate=cost(1_000_000, 3_000_000),
         name="pack",
-    )(owner_list, rows)
+    )(owner_list, rows[:, :, :, :, None, :])
 
 
 def fastest_kernel(rows_ref, out):
     best = jnp.zeros((8, LANES), jnp.float32)
-    step = rows_ref.shape[0] // FIELDS
-    for first in range(0, step, 8):
-        fields = [rows_ref[f * step + first : f * step + first + 8, :] for f in range(FIELDS)]
-        best = jnp.maximum(best, wave_speed(fields))
+    for group in range(rows_ref.shape[1]):
+        for pair in range(PAIRS):
+            fields = [rows_ref[f, group, pair] for f in range(FIELDS)]
+            best = jnp.maximum(best, wave_speed(fields))
     out[...] = jnp.full((8, LANES), jnp.max(best), jnp.float32)
 
 
@@ -142,8 +149,8 @@
         rank = lax.rem(where, cap)
         for pair in range(PAIRS):
             couple, h = divmod(pair, 2)
-            base = source * (TILES * cap) + rank + pair * (FIELDS * cap)
-            value = come[pl.ds(base, FIELDS, stride=cap), :]
+            base = source * (TILES * cap) + rank + pair * cap
+            value = come[pl.ds(base, FIELDS, stride=PAIRS * cap), :]
             row = (couple * BZ + q) * 8 + 2 * p + h
             scratch[pl.ds(row, FIELDS, stride=PAIRS // 2 * BZ * 8), :] = value
     group = lax.broadcasted_iota(jnp.int32, (8, LANES), 1) // BLOCK
@@ -379,18 +386,15 @@
         return best
 
     best = lax.fori_loop(0, 4, group, jnp.zeros((8, LANES), jnp.float32))
-    size = top.shape[0] // 8
-    most = jnp.full((8, LANES), jnp.max(best), jnp.float32)
-    for dest in range(size):
-        top[dest * 8 : dest * 8 + 8, :] = most
-
-
-def first_stage(size, *operands):
+    top[...] = jnp.full((8, LANES), jnp.max(best), jnp.float32)
+
+
+def first_stage(*operands):
     whole = jax.ShapeDtypeStruct((FIELDS, BLOCK, ROWS, LANES), jnp.float32)
     halo = jax.ShapeDtypeStruct((FIELDS, 3, ROWS, LANES), jnp.float32)
     return pl.pallas_call(
         first_kernel,
-        out_shape=(whole, halo, halo, jax.ShapeDtypeStruct((size * 8, LANES), jnp.float32)),
+        out_shape=(whole, halo, halo, jax.ShapeDtypeStruct((8, LANES), jnp.float32)),
         in_specs=[VMEM] * len(operands),
         out_specs=(VMEM,) * 4,
         compiler_params=params(),
@@ -399,19 +403,9 @@
     )(*operands)
 
 
-def second_kernel(start, middle, below, above, first_speed, speeds, out, sides):
-    first = first_speed[0:1, :]
-    second = jnp.full((1, LANES), jnp.max(speeds[...]), jnp.float32)
-    half_speed = 0.5 * second
-    factor = (courant / 12.0) / first
-
-    def one_plane(plane, carry):
-        fields = [middle[f, plane] for f in range(FIELDS)]
-        for field, total in side_planes(fields, half_speed):
-            sides[field, plane] = total
-        return carry
-
-    lax.fori_loop(0, BLOCK, one_plane, 0)
+def second_kernel(start, middle, sides, below, above, first_speed, speed, out):
+    half_speed = 0.5 * speed[0:1, :]
+    factor = (courant / 12.0) / first_speed[0:1, :]
 
     def group(j, carry):
         rows = pl.ds(pl.multiple_of(j * 8, 8), 8)
@@ -437,15 +431,13 @@
 
 
 def second_stage(*operands):
-    whole = (FIELDS, BLOCK, ROWS, LANES)
     return pl.pallas_call(
         second_kernel,
-        out_shape=jax.ShapeDtypeStruct(whole, jnp.float32),
+        out_shape=jax.ShapeDtypeStruct((FIELDS, BLOCK, ROWS, LANES), jnp.float32),
         in_specs=[VMEM] * len(operands),
         out_specs=VMEM,
-        scratch_shapes=[pltpu.VMEM(whole, jnp.float32)],
-        compiler_params=params(),
-        cost_estimate=cost(60_000_000, 3_000_000),
+        compiler_params=params(),
+        cost_estimate=cost(30_000_000, 3_000_000),
         name="second_stage",
     )(*operands)
 
@@ -477,18 +469,22 @@
     parts, rows, owner_list, slot_list = lax.optimization_barrier(
         (parts, rows, owner_list, slot_list)
     )
+    parts = parts.reshape(size * TILES * cap, LANES)
     come = lax.all_to_all(parts, "gx", split_axis=0, concat_axis=0, tiled=True)
     table = arrival_spots(owner_list, slot_list, own, per_dev, size, cap)
-    speed = everyone_max(fastest(rows), "gx", size)
+    speed = jnp.max(lax.all_gather(fastest(rows), "gx"), axis=0)
+    come, table, speed = lax.optimization_barrier((come, table, speed))
     state, low, high = unpack(table, come, cap)
     below = lax.ppermute(high, "gx", up)
     above = lax.ppermute(low, "gx", down)
     sides = along_planes(state, speed)
-    middle, low, high, top = first_stage(size, state, sides, below, above, speed)
-    speeds = lax.all_to_all(top, "gx", split_axis=0, concat_axis=0, tiled=True)
+    middle, low, high, top = first_stage(state, sides, below, above, speed)
+    second = everyone_max(top, "gx", size)
+    low, high, second = lax.optimization_barrier((low, high, second))
     below = lax.ppermute(high, "gx", up)
     above = lax.ppermute(low, "gx", down)
-    return second_stage(state, middle, below, above, speed, speeds)
+    sides = along_planes(middle, second)
+    return second_stage(state, middle, sides, below, above, speed, second)
 
 
 def solution(mesh):

time: 85.1 us -> 91.7 us (1.078)
  blocking collectives: 9.47 us -> 37.1 us
  waiting for transfers between devices: 26.4 us -> 5.55 us
    all_gather x0 -> x1, blocking collectives: none -> 37.1 us  [per_device(): speed = jnp.max(lax.all_gather(fastest(rows), 'gx'), axis=0)]
    all_to_all x1, waiting for transfers between devices: 24.3 us -> 0.01 us  [per_device(): come = lax.all_to_all(parts, 'gx', split_axis=0, concat_axis=0, tiled=True)]
    all_to_all x1 -> x0, blocking collectives: 9.47 us -> none  [per_device(): speeds = lax.all_to_all(top, 'gx', split_axis=0, concat_axis=0, tiled=True)]
    pallas_call x1 -> x2, Pallas kernels: 4.99 us -> 9.98 us  [along_planes(): pl.pallas_call(plane_kernel, out_shape=jax.ShapeDtypeStruct(state.shape,...]
    pallas_call x2, Pallas kernels: 10.6 us -> 5.78 us  [the longest x1 3.16 us: second_stage(): pl.pallas_call(second_kernel, out_shape=jax.ShapeDtypeStruct((FIELDS, BLO...]
    ppermute x6, waiting for transfers between devices: 2.13 us -> 5.54 us  [everyone_max(): copies.append(lax.ppermute(value, axis, pairs))]
  transfers between devices with their start and end apart: 11 -> 11, of which waited for: 3 -> 4; matrix products, arithmetic and copies ran while one was open for 1% -> 1% of each run, Pallas kernels for 9% -> 11%
where the time goes in v4:
time: 91.7 us; the launch traced here: 91.2 us
  blocking collectives  37.1 us (40%)
  starting transfers between devices  24.3 us (26%)
  Pallas kernels  21.5 us (23%)
  waiting for transfers between devices  5.55 us (6%)
  local copies, waits for them, and re-layouts  1.94 us (2%)
    all_gather x1, blocking collectives, per_device(): speed = jnp.max(lax.all_gather(fastest(rows), 'gx'), axis=0)  37.1 us
    pallas_call x2, Pallas kernels, along_planes(): pl.pallas_call(plane_kernel, out_shape=jax.ShapeDtypeStruct(state.shape,...  9.98 us
    ppermute x2, starting transfers between devices, per_device(): above = lax.ppermute(low, 'gx', down)  9.8 us
    all_to_all x1, starting transfers between devices, per_device(): come = lax.all_to_all(parts, 'gx', split_axis=0, concat_axis=0, tiled=True)  7.5 us
    ppermute x6, starting transfers between devices, everyone_max(): copies.append(lax.ppermute(value, axis, pairs))  6.59 us
    ppermute x6, waiting for transfers between devices, everyone_max(): copies.append(lax.ppermute(value, axis, pairs))  5.54 us
    pallas_call x1, Pallas kernels, second_stage(): pl.pallas_call(second_kernel, out_shape=jax.ShapeDtypeStruct((FIELDS, BLO...  3.16 us
    pallas_call x1, Pallas kernels, unpack(): pl.pallas_call(functools.partial(unpack_kernel, cap), out_shape=(jax.Shap...  3.06 us
  transfers between devices with their start and end apart: 11, of which 4 were waited for; matrix products, arithmetic and copies ran while one was open for 1% of the time, Pallas kernels for 11%

profile of v4, /device:TPU:0, one launch (start us, length us, event | category | flops | bytes accessed | tf_op | source)
XLA Modules:
  0.0 91.2 jit_solution(8951748439394129846)
XLA Ops:
  0.0 1.1 %copy-done = f32[64,5,512]{2,0,1:T(8,128)S(1)} copy-done((f32[64,5,512]{2,0,1:T(8,128)S(1)}, f32[64,5,512]{2,0,1:T(8,128)}, u32[]{:S(2)}) %copy-start) | copy-done | bytes 655384
  1.1 0.7 copy-done.2
  1.8 2.6 %pack.1 = f32[16,5,4,8,1,128]{5,4,3,2,1,0:T(1,128)} custom-call(s32[1024]{0:T(1024)S(1)} %copy-done.2, f32[5,8,4,8,1,128]{5,4,3,2,1,0:T(1,128)S(1)} %bitcast.12), custom_call_target="tpu_custom_call" | custom-call | flops 1000000 | bytes 3000000 | tf_op jit(solution)/shard_map/pack/pallas_call | solution.py:80
  4.4 7.5 %all-to-all-start = ((f32[16,160,128]{2,1,0:T(8,128)}), f32[16,160,128]{2,1,0:T(8,128)S(1)}, u32[]{:S(2)}, u32[]{:S(2)}) async-start(f32[16,160,128]{2,1,0:T(8,128)} %bitcast.4), calls=%async_computation | async-start | bytes 2621440 | tf_op jit(solution)/shard_map/all_to_all | solution.py:473
  12.1 0.3 convert_reduce_fusion
  12.6 0.2 fastest.1
  12.8 37.1 %all-gather = f32[128,128]{1,0:T(8,128)S(1)} all-gather(f32[8,128]{1,0:T(8,128)S(1)} %fastest.1), channel_id=2, replica_groups=mesh['runs'=2,'gx'=16] {'gx'}, dimensions={0}, use_global_device_ids=true | all-gather | bytes 69632 | tf_op jit(solution)/shard_map/all_gather | solution.py:475
  50.1 3.1 %unpack.1 = (f32[5,8,32,128]{3,2,1,0:T(8,128)S(1)}, f32[5,3,32,128]{3,2,1,0:T(8,128)S(1)}, f32[5,3,32,128]{3,2,1,0:T(8,128)S(1)}) custom-call(s32[64]{0:T(128)S(1)} %select_reduce_fusion.table, f32[2560,128]{1,0:T(8,128)S(1)} %bitcast.11), custom_call_target="tpu_custom_call" | custom-call | flops 5000000 | bytes 2000000 | tf_op jit(solution)/shard_map/unpack/pallas_call | solution.py:184
  53.2 0.4 collective-permute-start
  53.6 5.4 %collective-permute-start.1 = (f32[5,3,32,128]{3,2,1,0:T(8,128)S(1)}, f32[5,3,32,128]{3,2,1,0:T(8,128)S(1)}, u32[]{:S(2)}, u32[]{:S(2)}) collective-permute-start(f32[5,3,32,128]{3,2,1,0:T(8,128)S(1)} %get-tuple-element.31), channel_id=1, source_target_pairs={{1,0},{2,1},{3,2},{4,3},{5,4},{6,5},{7,6},{8,7},{9,8},{10,9},{11,1... | collective-permute-start | bytes 737288 | tf_op jit(solution)/shard_map/ppermute | solution.py:479
  58.9 5.0 %planes.2.sides = f32[5,8,32,128]{3,2,1,0:T(8,128)S(1)} custom-call(f32[5,8,32,128]{3,2,1,0:T(8,128)S(1)} %get-tuple-element.28.state.start, f32[8,128]{1,0:T(8,128)S(1)} %bitcast_reduce_fusion.speed.first_speed), custom_call_target="tpu_custom_call" | custom-call | flops 20000000 | bytes 1000000 | tf_op jit(solution)/shard_map/planes/pallas_call | solution.py:325
  63.9 2.5 %first_stage.1 = (f32[5,8,32,128]{3,2,1,0:T(8,128)S(1)}, f32[5,3,32,128]{3,2,1,0:T(8,128)S(1)}, f32[5,3,32,128]{3,2,1,0:T(8,128)S(1)}, f32[8,128]{1,0:T(8,128)S(1)}) custom-call(f32[5,8,32,128]{3,2,1,0:T(8,128)S(1)} %get-tuple-element.28.state.start, f32[5,8,32,128]{3,2,1,0:T(8,128)S(1)} %planes.2.sides, f32[5,3,32,128]{3,2,1,0:T(8,128)S(1)} %collective-permute-done.below, ...), custom_call_target="tpu_custom_call" | custom-call | flops 30000000 | bytes 3000000 | tf_op jit(solution)/shard_map/first_stage/pallas_call | solution.py:395
  66.4 1.9 %collective-permute-start.4 = (f32[8,128]{1,0:T(8,128)S(1)}, f32[8,128]{1,0:T(8,128)S(1)}, u32[]{:S(2)}, u32[]{:S(2)}) collective-permute-start(f32[8,128]{1,0:T(8,128)S(1)} %get-tuple-element.35), channel_id=1, source_target_pairs={{0,3},{1,2},{2,1},{3,0},{4,7},{5,6},{6,5},{7,4},{8,11},{9,10},{10,... | collective-permute-start | bytes 12296 | tf_op jit(solution)/shard_map/ppermute | solution.py:453
  68.3 0.3 collective-permute-start.3
  68.6 1.1 %collective-permute-done.4 = f32[8,128]{1,0:T(8,128)S(1)} collective-permute-done((f32[8,128]{1,0:T(8,128)S(1)}, f32[8,128]{1,0:T(8,128)S(1)}, u32[]{:S(2)}, u32[]{:S(2)}) %collective-permute-start.4) | collective-permute-done | bytes 4128 | tf_op jit(solution)/shard_map/ppermute | solution.py:453
  69.6 2.3 %collective-permute-done.3 = f32[8,128]{1,0:T(8,128)S(1)} collective-permute-done((f32[8,128]{1,0:T(8,128)S(1)}, f32[8,128]{1,0:T(8,128)S(1)}, u32[]{:S(2)}, u32[]{:S(2)}) %collective-permute-start.3) | collective-permute-done | bytes 4128 | tf_op jit(solution)/shard_map/ppermute | solution.py:453
  71.9 2.1 %collective-permute-start.7 = (f32[8,128]{1,0:T(8,128)S(1)}, f32[8,128]{1,0:T(8,128)S(1)}, u32[]{:S(2)}, u32[]{:S(2)}) collective-permute-start(f32[8,128]{1,0:T(8,128)S(1)} %maximum_maximum_fusion.1), channel_id=1, source_target_pairs={{0,12},{1,13},{2,14},{3,15},{4,8},{5,9},{6,10},{7,11},{8,4},{9,5},... | collective-permute-start | bytes 12296 | tf_op jit(solution)/shard_map/ppermute | solution.py:453
  74.0 0.9 collective-permute-start.6
  74.9 1.5 %collective-permute-start.5 = (f32[8,128]{1,0:T(8,128)S(1)}, f32[8,128]{1,0:T(8,128)S(1)}, u32[]{:S(2)}, u32[]{:S(2)}) collective-permute-start(f32[8,128]{1,0:T(8,128)S(1)} %maximum_maximum_fusion.1), channel_id=1, source_target_pairs={{0,4},{1,5},{2,6},{3,7},{4,0},{5,1},{6,2},{7,3},{8,12},{9,13},{10,... | collective-permute-start | bytes 12296 | tf_op jit(solution)/shard_map/ppermute | solution.py:453
  76.4 1.0 %collective-permute-done.7 = f32[8,128]{1,0:T(8,128)S(1)} collective-permute-done((f32[8,128]{1,0:T(8,128)S(1)}, f32[8,128]{1,0:T(8,128)S(1)}, u32[]{:S(2)}, u32[]{:S(2)}) %collective-permute-start.7) | collective-permute-done | bytes 4128 | tf_op jit(solution)/shard_map/ppermute | solution.py:453
  77.4 1.2 %collective-permute-done.6 = f32[8,128]{1,0:T(8,128)S(1)} collective-permute-done((f32[8,128]{1,0:T(8,128)S(1)}, f32[8,128]{1,0:T(8,128)S(1)}, u32[]{:S(2)}, u32[]{:S(2)}) %collective-permute-start.6) | collective-permute-done | bytes 4128 | tf_op jit(solution)/shard_map/ppermute | solution.py:453
  78.6 4.4 %collective-permute-start.9 = (f32[5,3,32,128]{3,2,1,0:T(8,128)S(1)}, f32[5,3,32,128]{3,2,1,0:T(8,128)S(1)}, u32[]{:S(2)}, u32[]{:S(2)}) collective-permute-start(f32[5,3,32,128]{3,2,1,0:T(8,128)S(1)} %get-tuple-element.38), channel_id=1, source_target_pairs={{1,0},{2,1},{3,2},{4,3},{5,4},{6,5},{7,6},{8,7},{9,8},{10,9},{11,1... | collective-permute-start | bytes 737288 | tf_op jit(solution)/shard_map/ppermute | solution.py:485
  83.1 5.0 %planes.3.sides = f32[5,8,32,128]{3,2,1,0:T(8,128)S(1)} custom-call(f32[5,8,32,128]{3,2,1,0:T(8,128)S(1)} %get-tuple-element.32.state.middle, f32[8,128]{1,0:T(8,128)S(1)} %maximum_maximum_fusion.speed), custom_call_target="tpu_custom_call" | custom-call | flops 20000000 | bytes 1000000 | tf_op jit(solution)/shard_map/planes/pallas_call | solution.py:325
  88.1 3.2 %second_stage.1 = f32[5,8,32,128]{3,2,1,0:T(8,128)} custom-call(f32[5,8,32,128]{3,2,1,0:T(8,128)S(1)} %get-tuple-element.28.state.start, f32[5,8,32,128]{3,2,1,0:T(8,128)S(1)} %get-tuple-element.32.state.middle, f32[5,8,32,128]{3,2,1,0:T(8,128)S(1)} %planes.3.sides, f32[5,3,32,128]{3,2,1,0:T(8,128)S(1)} %collective-permute-done.8.below, ...), custom_call_target="tpu_custom_call" | custom-call | flops 30000000 | bytes 3000000 | tf_op jit(solution)/shard_map/second_stage/pallas_call | solution.py:434
  (27 shorter events, 0.5 us)
Async XLA Ops:
  0.0 1.1 %copy-start = (f32[64,5,512]{2,0,1:T(8,128)S(1)}, f32[64,5,512]{2,0,1:T(8,128)}, u32[]{:S(2)}) copy-start(f32[64,5,512]{2,0,1:T(8,128)} %param.3) | copy-start | bytes 1966084
  1.1 0.7 copy-start.2
  4.4 7.6 %copy-start.3 = (s32[1024]{0:T(1024)S(1)}, s32[1024]{0:T(1024)}, u32[]{:S(2)}) copy-start(s32[1024]{0:T(1024)} %owner_hbm.1) | copy-start | bytes 12292
  4.4 7.5 %copy-start.4 = (s32[1024]{0:T(1024)S(1)}, s32[1024]{0:T(1024)}, u32[]{:S(2)}) copy-start(s32[1024]{0:T(1024)} %param.5) | copy-start | bytes 12292
  4.4 8.2 %copy-start.1 = (f32[64,5,512]{2,0,1:T(8,128)S(1)}, f32[64,5,512]{2,0,1:T(8,128)}, u32[]{:S(2)}) copy-start(f32[64,5,512]{2,0,1:T(8,128)} %param.3) | copy-start | bytes 1966084
  4.4 45.6 %all-to-all-start = ((f32[16,160,128]{2,1,0:T(8,128)}), f32[16,160,128]{2,1,0:T(8,128)S(1)}, u32[]{:S(2)}, u32[]{:S(2)}) async-start(f32[16,160,128]{2,1,0:T(8,128)} %bitcast.4), calls=%async_computation | async-start | bytes 2621440 | tf_op jit(solution)/shard_map/all_to_all | solution.py:473
  53.2 10.8 %collective-permute-start = (f32[5,3,32,128]{3,2,1,0:T(8,128)S(1)}, f32[5,3,32,128]{3,2,1,0:T(8,128)S(1)}, u32[]{:S(2)}, u32[]{:S(2)}) collective-permute-start(f32[5,3,32,128]{3,2,1,0:T(8,128)S(1)} %get-tuple-element.30), channel_id=1, source_target_pairs={{0,1},{1,2},{2,3},{3,4},{4,5},{5,6},{6,7},{7,8},{8,9},{9,10},{10,1... | collective-permute-start | bytes 737288 | tf_op jit(solution)/shard_map/ppermute | solution.py:478
  53.6 10.4 %collective-permute-start.1 = (f32[5,3,32,128]{3,2,1,0:T(8,128)S(1)}, f32[5,3,32,128]{3,2,1,0:T(8,128)S(1)}, u32[]{:S(2)}, u32[]{:S(2)}) collective-permute-start(f32[5,3,32,128]{3,2,1,0:T(8,128)S(1)} %get-tuple-element.31), channel_id=1, source_target_pairs={{1,0},{2,1},{3,2},{4,3},{5,4},{6,5},{7,6},{8,7},{9,8},{10,9},{11,1... | collective-permute-start | bytes 737288 | tf_op jit(solution)/shard_map/ppermute | solution.py:479
  66.4 3.2 %collective-permute-start.4 = (f32[8,128]{1,0:T(8,128)S(1)}, f32[8,128]{1,0:T(8,128)S(1)}, u32[]{:S(2)}, u32[]{:S(2)}) collective-permute-start(f32[8,128]{1,0:T(8,128)S(1)} %get-tuple-element.35), channel_id=1, source_target_pairs={{0,3},{1,2},{2,1},{3,0},{4,7},{5,6},{6,5},{7,4},{8,11},{9,10},{10,... | collective-permute-start | bytes 12296 | tf_op jit(solution)/shard_map/ppermute | solution.py:453
  68.3 3.6 %collective-permute-start.3 = (f32[8,128]{1,0:T(8,128)S(1)}, f32[8,128]{1,0:T(8,128)S(1)}, u32[]{:S(2)}, u32[]{:S(2)}) collective-permute-start(f32[8,128]{1,0:T(8,128)S(1)} %get-tuple-element.35), channel_id=1, source_target_pairs={{0,2},{1,3},{2,0},{3,1},{4,6},{5,7},{6,4},{7,5},{8,10},{9,11},{10,... | collective-permute-start | bytes 12296 | tf_op jit(solution)/shard_map/ppermute | solution.py:453
  68.6 3.4 %collective-permute-start.2 = (f32[8,128]{1,0:T(8,128)S(1)}, f32[8,128]{1,0:T(8,128)S(1)}, u32[]{:S(2)}, u32[]{:S(2)}) collective-permute-start(f32[8,128]{1,0:T(8,128)S(1)} %get-tuple-element.35), channel_id=1, source_target_pairs={{0,1},{1,0},{2,3},{3,2},{4,5},{5,4},{6,7},{7,6},{8,9},{9,8},{10,11... | collective-permute-start | bytes 12296 | tf_op jit(solution)/shard_map/ppermute | solution.py:453
  71.9 5.5 %collective-permute-start.7 = (f32[8,128]{1,0:T(8,128)S(1)}, f32[8,128]{1,0:T(8,128)S(1)}, u32[]{:S(2)}, u32[]{:S(2)}) collective-permute-start(f32[8,128]{1,0:T(8,128)S(1)} %maximum_maximum_fusion.1), channel_id=1, source_target_pairs={{0,12},{1,13},{2,14},{3,15},{4,8},{5,9},{6,10},{7,11},{8,4},{9,5},... | collective-permute-start | bytes 12296 | tf_op jit(solution)/shard_map/ppermute | solution.py:453
  74.0 4.5 %collective-permute-start.6 = (f32[8,128]{1,0:T(8,128)S(1)}, f32[8,128]{1,0:T(8,128)S(1)}, u32[]{:S(2)}, u32[]{:S(2)}) collective-permute-start(f32[8,128]{1,0:T(8,128)S(1)} %maximum_maximum_fusion.1), channel_id=1, source_target_pairs={{0,8},{1,9},{2,10},{3,11},{4,12},{5,13},{6,14},{7,15},{8,0},{9,1},... | collective-permute-start | bytes 12296 | tf_op jit(solution)/shard_map/ppermute | solution.py:453
  74.9 3.7 %collective-permute-start.5 = (f32[8,128]{1,0:T(8,128)S(1)}, f32[8,128]{1,0:T(8,128)S(1)}, u32[]{:S(2)}, u32[]{:S(2)}) collective-permute-start(f32[8,128]{1,0:T(8,128)S(1)} %maximum_maximum_fusion.1), channel_id=1, source_target_pairs={{0,4},{1,5},{2,6},{3,7},{4,0},{5,1},{6,2},{7,3},{8,12},{9,13},{10,... | collective-permute-start | bytes 12296 | tf_op jit(solution)/shard_map/ppermute | solution.py:453
  78.6 9.5 %collective-permute-start.8 = (f32[5,3,32,128]{3,2,1,0:T(8,128)S(1)}, f32[5,3,32,128]{3,2,1,0:T(8,128)S(1)}, u32[]{:S(2)}, u32[]{:S(2)}) collective-permute-start(f32[5,3,32,128]{3,2,1,0:T(8,128)S(1)} %get-tuple-element.37), channel_id=1, source_target_pairs={{0,1},{1,2},{2,3},{3,4},{4,5},{5,6},{6,7},{7,8},{8,9},{9,10},{10,1... | collective-permute-start | bytes 737288 | tf_op jit(solution)/shard_map/ppermute | solution.py:484
  78.6 9.4 %collective-permute-start.9 = (f32[5,3,32,128]{3,2,1,0:T(8,128)S(1)}, f32[5,3,32,128]{3,2,1,0:T(8,128)S(1)}, u32[]{:S(2)}, u32[]{:S(2)}) collective-permute-start(f32[5,3,32,128]{3,2,1,0:T(8,128)S(1)} %get-tuple-element.38), channel_id=1, source_target_pairs={{1,0},{2,1},{3,2},{4,3},{5,4},{6,5},{7,6},{8,7},{9,8},{10,9},{11,1... | collective-permute-start | bytes 737288 | tf_op jit(solution)/shard_map/ppermute | solution.py:485

commit v5 on v4

--- a/solution.py
+++ b/solution.py
@@ -24,8 +24,8 @@
 SMEM = pl.BlockSpec(memory_space=pltpu.SMEM)
 
 
-def params():
-    return pltpu.CompilerParams(vmem_limit_bytes=40 * 1024 * 1024)
+def params(mebibytes=40):
+    return pltpu.CompilerParams(vmem_limit_bytes=mebibytes * 1024 * 1024)
 
 
 def cost(flops, size):
@@ -81,13 +81,13 @@
         functools.partial(pack_kernel, size, per_dev),
         out_shape=jax.ShapeDtypeStruct((size, FIELDS, PAIRS, cap, 1, LANES), jnp.float32),
         in_specs=[pl.BlockSpec(memory_space=pltpu.HBM)] * 2,
-        out_specs=VMEM,
+        out_specs=pl.BlockSpec(memory_space=pltpu.HBM),
         scratch_shapes=[
             pltpu.SMEM(owner_list.shape, jnp.int32),
             pltpu.SMEM((size,), jnp.int32),
             pltpu.SemaphoreType.DMA((2,)),
         ],
-        compiler_params=params(),
+        compiler_params=params(62),
         cost_estimate=cost(1_000_000, 3_000_000),
         name="pack",
     )(owner_list, rows[:, :, :, :, None, :])
@@ -456,6 +456,24 @@
     return value
 
 
+def swapped_max(value, axis, size):
+    reach = 1
+    while reach < size:
+        width = min(4, size // reach)
+        groups = [
+            [first + reach * times for times in range(width)]
+            for first in range(size)
+            if first // reach % width == 0
+        ]
+        copies = jnp.broadcast_to(value[None], (width,) + value.shape)
+        copies = lax.all_to_all(
+            copies, axis, split_axis=0, concat_axis=0, tiled=True, axis_index_groups=groups
+        )
+        value = jnp.max(copies, axis=0)
+        reach *= width
+    return value
+
+
 def per_device(blocks, owner_list, slot_list):
     size = lax.axis_size("gx")
     own = lax.axis_index("gx")
@@ -472,15 +490,14 @@
     parts = parts.reshape(size * TILES * cap, LANES)
     come = lax.all_to_all(parts, "gx", split_axis=0, concat_axis=0, tiled=True)
     table = arrival_spots(owner_list, slot_list, own, per_dev, size, cap)
-    speed = jnp.max(lax.all_gather(fastest(rows), "gx"), axis=0)
+    speed = everyone_max(fastest(rows), "gx", size)
     come, table, speed = lax.optimization_barrier((come, table, speed))
     state, low, high = unpack(table, come, cap)
     below = lax.ppermute(high, "gx", up)
     above = lax.ppermute(low, "gx", down)
     sides = along_planes(state, speed)
     middle, low, high, top = first_stage(state, sides, below, above, speed)
-    second = everyone_max(top, "gx", size)
-    low, high, second = lax.optimization_barrier((low, high, second))
+    second = swapped_max(top, "gx", size)
     below = lax.ppermute(high, "gx", up)
     above = lax.ppermute(low, "gx", down)
     sides = along_planes(middle, second)

time: 91.7 us -> 104 us (1.13)
  blocking collectives: 37.1 us -> 14.1 us
  Pallas kernels: 21.5 us -> 40.6 us
  waiting for transfers between devices: 5.55 us -> 24.2 us
  local copies, waits for them, and re-layouts: 1.94 us -> 0.18 us
    all_gather x1 -> x0, blocking collectives: 37.1 us -> none  [per_device(): speed = jnp.max(lax.all_gather(fastest(rows), 'gx'), axis=0)]
    pallas_call x1, Pallas kernels: 2.62 us -> 21.7 us  [pack(): pl.pallas_call(functools.partial(pack_kernel, size, per_dev), out_shape=j...]
    ppermute x6, waiting for transfers between devices: 5.54 us -> 24.2 us  [everyone_max(): copies.append(lax.ppermute(value, axis, pairs))]
    all_to_all x0 -> x2, blocking collectives: none -> 14.1 us  [swapped_max(): lax.all_to_all(copies, axis, split_axis=0, concat_axis=0, tiled=True, axi...]
    unnamed x10 -> x6, local copies, waits for them, and re-layouts: 1.79 us -> 0.02 us
    ppermute x2, starting transfers between devices: 9.8 us -> 8.45 us  [per_device(): above = lax.ppermute(low, 'gx', down)]
  transfers between devices with their start and end apart: 11 -> 11, of which waited for: 4 -> 4; matrix products, arithmetic and copies ran while one was open for 1% -> 1% of each run, Pallas kernels for 11% -> 10%
where the time goes in v5:
time: 104 us
  Pallas kernels  40.6 us (39%)
  waiting for transfers between devices  24.2 us (23%)
  starting transfers between devices  23.8 us (23%)
  blocking collectives  14.1 us (14%)
    ppermute x6, waiting for transfers between devices, everyone_max(): copies.append(lax.ppermute(value, axis, pairs))  24.2 us
    pallas_call x1, Pallas kernels, pack(): pl.pallas_call(functools.partial(pack_kernel, size, per_dev), out_shape=j...  21.7 us
    all_to_all x2, blocking collectives, swapped_max(): lax.all_to_all(copies, axis, split_axis=0, concat_axis=0, tiled=True, axi...  14.1 us
    pallas_call x2, Pallas kernels, along_planes(): pl.pallas_call(plane_kernel, out_shape=jax.ShapeDtypeStruct(state.shape,...  9.98 us
    ppermute x2, starting transfers between devices, per_device(): above = lax.ppermute(low, 'gx', down)  8.45 us
    all_to_all x1, starting transfers between devices, per_device(): come = lax.all_to_all(parts, 'gx', split_axis=0, concat_axis=0, tiled=True)  7.5 us
    ppermute x6, starting transfers between devices, everyone_max(): copies.append(lax.ppermute(value, axis, pairs))  7.31 us
    pallas_call x1, Pallas kernels, second_stage(): pl.pallas_call(second_kernel, out_shape=jax.ShapeDtypeStruct((FIELDS, BLO...  3.16 us
  transfers between devices with their start and end apart: 11, of which 4 were waited for; matrix products, arithmetic and copies ran while one was open for 1% of the time, Pallas kernels for 10%

profile of v5, /device:TPU:0, one launch (start us, length us, event | category | flops | bytes accessed | tf_op | source)
XLA Modules:
  0.0 103.7 jit_solution(5559415900674078059)
XLA Ops:
  0.0 21.7 %pack.1 = f32[16,5,4,8,1,128]{5,4,3,2,1,0:T(1,128)} custom-call(s32[1024]{0:T(1024)} %owner_hbm.1, f32[5,8,4,8,1,128]{5,4,3,2,1,0:T(1,128)} %bitcast.10), custom_call_target="tpu_custom_call" | custom-call | flops 1000000 | bytes 3000000 | tf_op jit(solution)/shard_map/pack/pallas_call | solution.py:80
  21.8 7.5 %all-to-all-start = ((f32[16,160,128]{2,1,0:T(8,128)}), f32[16,160,128]{2,1,0:T(8,128)S(1)}, u32[]{:S(2)}, u32[]{:S(2)}) async-start(f32[16,160,128]{2,1,0:T(8,128)} %bitcast.12), calls=%async_computation | async-start | bytes 2621440 | tf_op jit(solution)/shard_map/all_to_all | solution.py:491
  29.3 0.2 fastest.1
  29.5 1.7 %collective-permute-start.2 = (f32[8,128]{1,0:T(8,128)S(1)}, f32[8,128]{1,0:T(8,128)S(1)}, u32[]{:S(2)}, u32[]{:S(2)}) collective-permute-start(f32[8,128]{1,0:T(8,128)S(1)} %fastest.1), channel_id=1, source_target_pairs={{0,3},{1,2},{2,1},{3,0},{4,7},{5,6},{6,5},{7,4},{8,11},{9,10},{10,... | collective-permute-start | bytes 12296 | tf_op jit(solution)/shard_map/ppermute | solution.py:453
  31.3 0.4 collective-permute-start.1
  31.7 0.1 eq.33
  31.8 0.3 convert_reduce_fusion
  32.3 5.9 %collective-permute-done.2 = f32[8,128]{1,0:T(8,128)S(1)} collective-permute-done((f32[8,128]{1,0:T(8,128)S(1)}, f32[8,128]{1,0:T(8,128)S(1)}, u32[]{:S(2)}, u32[]{:S(2)}) %collective-permute-start.2) | collective-permute-done | bytes 4128 | tf_op jit(solution)/shard_map/ppermute | solution.py:453
  38.2 0.6 collective-permute-done.1
  38.9 4.5 %collective-permute-start.5 = (f32[8,128]{1,0:T(8,128)S(1)}, f32[8,128]{1,0:T(8,128)S(1)}, u32[]{:S(2)}, u32[]{:S(2)}) collective-permute-start(f32[8,128]{1,0:T(8,128)S(1)} %maximum_maximum_fusion.1), channel_id=1, source_target_pairs={{0,12},{1,13},{2,14},{3,15},{4,8},{5,9},{6,10},{7,11},{8,4},{9,5},... | collective-permute-start | bytes 12296 | tf_op jit(solution)/shard_map/ppermute | solution.py:453
  43.4 0.6 collective-permute-start.3
  44.0 0.1 select_reduce_fusion.table
  44.2 11.5 %collective-permute-done.5 = f32[8,128]{1,0:T(8,128)S(1)} collective-permute-done((f32[8,128]{1,0:T(8,128)S(1)}, f32[8,128]{1,0:T(8,128)S(1)}, u32[]{:S(2)}, u32[]{:S(2)}) %collective-permute-start.5) | collective-permute-done | bytes 4128 | tf_op jit(solution)/shard_map/ppermute | solution.py:453
  55.7 6.1 %collective-permute-done.4 = f32[8,128]{1,0:T(8,128)S(1)} collective-permute-done((f32[8,128]{1,0:T(8,128)S(1)}, f32[8,128]{1,0:T(8,128)S(1)}, u32[]{:S(2)}, u32[]{:S(2)}) %collective-permute-start.4) | collective-permute-done | bytes 4128 | tf_op jit(solution)/shard_map/ppermute | solution.py:453
  61.9 3.1 %unpack.1 = (f32[5,8,32,128]{3,2,1,0:T(8,128)S(1)}, f32[5,3,32,128]{3,2,1,0:T(8,128)S(1)}, f32[5,3,32,128]{3,2,1,0:T(8,128)S(1)}) custom-call(s32[64]{0:T(128)S(1)} %select_reduce_fusion.table, f32[2560,128]{1,0:T(8,128)S(1)} %bitcast.9), custom_call_target="tpu_custom_call" | custom-call | flops 5000000 | bytes 2000000 | tf_op jit(solution)/shard_map/unpack/pallas_call | solution.py:184
  65.0 4.4 %collective-permute-start.7 = (f32[5,3,32,128]{3,2,1,0:T(8,128)S(1)}, f32[5,3,32,128]{3,2,1,0:T(8,128)S(1)}, u32[]{:S(2)}, u32[]{:S(2)}) collective-permute-start(f32[5,3,32,128]{3,2,1,0:T(8,128)S(1)} %get-tuple-element.28), channel_id=1, source_target_pairs={{1,0},{2,1},{3,2},{4,3},{5,4},{6,5},{7,6},{8,7},{9,8},{10,9},{11,1... | collective-permute-start | bytes 737288 | tf_op jit(solution)/shard_map/ppermute | solution.py:497
  69.4 5.0 %planes.2.sides = f32[5,8,32,128]{3,2,1,0:T(8,128)S(1)} custom-call(f32[5,8,32,128]{3,2,1,0:T(8,128)S(1)} %get-tuple-element.25.state.start, f32[8,128]{1,0:T(8,128)S(1)} %maximum_maximum_fusion.speed.first_speed), custom_call_target="tpu_custom_call" | custom-call | flops 20000000 | bytes 1000000 | tf_op jit(solution)/shard_map/planes/pallas_call | solution.py:325
  74.4 2.5 %first_stage.1 = (f32[5,8,32,128]{3,2,1,0:T(8,128)S(1)}, f32[5,3,32,128]{3,2,1,0:T(8,128)S(1)}, f32[5,3,32,128]{3,2,1,0:T(8,128)S(1)}, f32[8,128]{1,0:T(8,128)S(1)}) custom-call(f32[5,8,32,128]{3,2,1,0:T(8,128)S(1)} %get-tuple-element.25.state.start, f32[5,8,32,128]{3,2,1,0:T(8,128)S(1)} %planes.2.sides, f32[5,3,32,128]{3,2,1,0:T(8,128)S(1)} %collective-permute-done.6.below, ...), custom_call_target="tpu_custom_call" | custom-call | flops 30000000 | bytes 3000000 | tf_op jit(solution)/shard_map/first_stage/pallas_call | solution.py:395
  76.9 0.5 collective-permute-start.8
  77.4 4.0 %collective-permute-start.9 = (f32[5,3,32,128]{3,2,1,0:T(8,128)S(1)}, f32[5,3,32,128]{3,2,1,0:T(8,128)S(1)}, u32[]{:S(2)}, u32[]{:S(2)}) collective-permute-start(f32[5,3,32,128]{3,2,1,0:T(8,128)S(1)} %get-tuple-element.32), channel_id=1, source_target_pairs={{1,0},{2,1},{3,2},{4,3},{5,4},{6,5},{7,6},{8,7},{9,8},{10,9},{11,1... | collective-permute-start | bytes 737288 | tf_op jit(solution)/shard_map/ppermute | solution.py:502
  81.4 6.2 %all_to_all.22 = f32[4,8,128]{2,1,0:T(8,128)S(1)} all-to-all(f32[4,8,128]{2,1,0:T(8,128)S(1)} %broadcast_in_dim.41), channel_id=1, replica_groups={{0,1,2,3},{4,5,6,7},{8,9,10,11},{12,13,14,15},{16,17,18,19},{20,21,22,2..., dimensions={0} | all-to-all | bytes 32768 | tf_op jit(solution)/shard_map/all_to_all | solution.py:469
  87.6 8.0 %all_to_all.23 = f32[4,8,128]{2,1,0:T(8,128)S(1)} all-to-all(f32[4,8,128]{2,1,0:T(8,128)S(1)} %broadcast_in_dim.42), channel_id=1, replica_groups={{0,4,8,12},{1,5,9,13},{2,6,10,14},{3,7,11,15},{16,20,24,28},{17,21,25,2..., dimensions={0} | all-to-all | bytes 32768 | tf_op jit(solution)/shard_map/all_to_all | solution.py:469
  95.6 5.0 %planes.3.sides = f32[5,8,32,128]{3,2,1,0:T(8,128)S(1)} custom-call(f32[5,8,32,128]{3,2,1,0:T(8,128)S(1)} %get-tuple-element.29.state.middle, f32[8,128]{1,0:T(8,128)S(1)} %reduce_max.29.speed), custom_call_target="tpu_custom_call" | custom-call | flops 20000000 | bytes 1000000 | tf_op jit(solution)/shard_map/planes/pallas_call | solution.py:325
  100.6 3.2 %second_stage.1 = f32[5,8,32,128]{3,2,1,0:T(8,128)} custom-call(f32[5,8,32,128]{3,2,1,0:T(8,128)S(1)} %get-tuple-element.25.state.start, f32[5,8,32,128]{3,2,1,0:T(8,128)S(1)} %get-tuple-element.29.state.middle, f32[5,8,32,128]{3,2,1,0:T(8,128)S(1)} %planes.3.sides, f32[5,3,32,128]{3,2,1,0:T(8,128)S(1)} %collective-permute-done.8.below, ...), custom_call_target="tpu_custom_call" | custom-call | flops 30000000 | bytes 3000000 | tf_op jit(solution)/shard_map/second_stage/pallas_call | solution.py:434
  (27 shorter events, 0.3 us)
Async XLA Ops:
  21.7 7.5 %copy-start = (f32[64,5,512]{2,0,1:T(8,128)S(1)}, f32[64,5,512]{2,0,1:T(8,128)}, u32[]{:S(2)}) copy-start(f32[64,5,512]{2,0,1:T(8,128)} %param.3) | copy-start | bytes 1966084
  21.7 9.9 %copy-start.1 = (s32[1024]{0:T(1024)S(1)}, s32[1024]{0:T(1024)}, u32[]{:S(2)}) copy-start(s32[1024]{0:T(1024)} %owner_hbm.1) | copy-start | bytes 12292
  21.8 9.9 %copy-start.2 = (s32[1024]{0:T(1024)S(1)}, s32[1024]{0:T(1024)}, u32[]{:S(2)}) copy-start(s32[1024]{0:T(1024)} %param.5) | copy-start | bytes 12292
  21.8 40.1 %all-to-all-start = ((f32[16,160,128]{2,1,0:T(8,128)}), f32[16,160,128]{2,1,0:T(8,128)S(1)}, u32[]{:S(2)}, u32[]{:S(2)}) async-start(f32[16,160,128]{2,1,0:T(8,128)} %bitcast.12), calls=%async_computation | async-start | bytes 2621440 | tf_op jit(solution)/shard_map/all_to_all | solution.py:491
  29.5 8.7 %collective-permute-start.2 = (f32[8,128]{1,0:T(8,128)S(1)}, f32[8,128]{1,0:T(8,128)S(1)}, u32[]{:S(2)}, u32[]{:S(2)}) collective-permute-start(f32[8,128]{1,0:T(8,128)S(1)} %fastest.1), channel_id=1, source_target_pairs={{0,3},{1,2},{2,1},{3,0},{4,7},{5,6},{6,5},{7,4},{8,11},{9,10},{10,... | collective-permute-start | bytes 12296 | tf_op jit(solution)/shard_map/ppermute | solution.py:453
  31.3 7.6 %collective-permute-start.1 = (f32[8,128]{1,0:T(8,128)S(1)}, f32[8,128]{1,0:T(8,128)S(1)}, u32[]{:S(2)}, u32[]{:S(2)}) collective-permute-start(f32[8,128]{1,0:T(8,128)S(1)} %fastest.1), channel_id=1, source_target_pairs={{0,2},{1,3},{2,0},{3,1},{4,6},{5,7},{6,4},{7,5},{8,10},{9,11},{10,... | collective-permute-start | bytes 12296 | tf_op jit(solution)/shard_map/ppermute | solution.py:453
  31.7 7.2 %collective-permute-start = (f32[8,128]{1,0:T(8,128)S(1)}, f32[8,128]{1,0:T(8,128)S(1)}, u32[]{:S(2)}, u32[]{:S(2)}) collective-permute-start(f32[8,128]{1,0:T(8,128)S(1)} %fastest.1), channel_id=1, source_target_pairs={{0,1},{1,0},{2,3},{3,2},{4,5},{5,4},{6,7},{7,6},{8,9},{9,8},{10,11... | collective-permute-start | bytes 12296 | tf_op jit(solution)/shard_map/ppermute | solution.py:453
  38.9 16.8 %collective-permute-start.5 = (f32[8,128]{1,0:T(8,128)S(1)}, f32[8,128]{1,0:T(8,128)S(1)}, u32[]{:S(2)}, u32[]{:S(2)}) collective-permute-start(f32[8,128]{1,0:T(8,128)S(1)} %maximum_maximum_fusion.1), channel_id=1, source_target_pairs={{0,12},{1,13},{2,14},{3,15},{4,8},{5,9},{6,10},{7,11},{8,4},{9,5},... | collective-permute-start | bytes 12296 | tf_op jit(solution)/shard_map/ppermute | solution.py:453
  43.4 18.4 %collective-permute-start.4 = (f32[8,128]{1,0:T(8,128)S(1)}, f32[8,128]{1,0:T(8,128)S(1)}, u32[]{:S(2)}, u32[]{:S(2)}) collective-permute-start(f32[8,128]{1,0:T(8,128)S(1)} %maximum_maximum_fusion.1), channel_id=1, source_target_pairs={{0,8},{1,9},{2,10},{3,11},{4,12},{5,13},{6,14},{7,15},{8,0},{9,1},... | collective-permute-start | bytes 12296 | tf_op jit(solution)/shard_map/ppermute | solution.py:453
  43.4 18.4 %collective-permute-start.3 = (f32[8,128]{1,0:T(8,128)S(1)}, f32[8,128]{1,0:T(8,128)S(1)}, u32[]{:S(2)}, u32[]{:S(2)}) collective-permute-start(f32[8,128]{1,0:T(8,128)S(1)} %maximum_maximum_fusion.1), channel_id=1, source_target_pairs={{0,4},{1,5},{2,6},{3,7},{4,0},{5,1},{6,2},{7,3},{8,12},{9,13},{10,... | collective-permute-start | bytes 12296 | tf_op jit(solution)/shard_map/ppermute | solution.py:453
  64.9 9.5 %collective-permute-start.6 = (f32[5,3,32,128]{3,2,1,0:T(8,128)S(1)}, f32[5,3,32,128]{3,2,1,0:T(8,128)S(1)}, u32[]{:S(2)}, u32[]{:S(2)}) collective-permute-start(f32[5,3,32,128]{3,2,1,0:T(8,128)S(1)} %get-tuple-element.27), channel_id=1, source_target_pairs={{0,1},{1,2},{2,3},{3,4},{4,5},{5,6},{6,7},{7,8},{8,9},{9,10},{10,1... | collective-permute-start | bytes 737288 | tf_op jit(solution)/shard_map/ppermute | solution.py:496
  65.0 9.4 %collective-permute-start.7 = (f32[5,3,32,128]{3,2,1,0:T(8,128)S(1)}, f32[5,3,32,128]{3,2,1,0:T(8,128)S(1)}, u32[]{:S(2)}, u32[]{:S(2)}) collective-permute-start(f32[5,3,32,128]{3,2,1,0:T(8,128)S(1)} %get-tuple-element.28), channel_id=1, source_target_pairs={{1,0},{2,1},{3,2},{4,3},{5,4},{6,5},{7,6},{8,7},{9,8},{10,9},{11,1... | collective-permute-start | bytes 737288 | tf_op jit(solution)/shard_map/ppermute | solution.py:497
  76.9 23.7 %collective-permute-start.8 = (f32[5,3,32,128]{3,2,1,0:T(8,128)S(1)}, f32[5,3,32,128]{3,2,1,0:T(8,128)S(1)}, u32[]{:S(2)}, u32[]{:S(2)}) collective-permute-start(f32[5,3,32,128]{3,2,1,0:T(8,128)S(1)} %get-tuple-element.31), channel_id=1, source_target_pairs={{0,1},{1,2},{2,3},{3,4},{4,5},{5,6},{6,7},{7,8},{8,9},{9,10},{10,1... | collective-permute-start | bytes 737288 | tf_op jit(solution)/shard_map/ppermute | solution.py:501
  77.4 23.2 %collective-permute-start.9 = (f32[5,3,32,128]{3,2,1,0:T(8,128)S(1)}, f32[5,3,32,128]{3,2,1,0:T(8,128)S(1)}, u32[]{:S(2)}, u32[]{:S(2)}) collective-permute-start(f32[5,3,32,128]{3,2,1,0:T(8,128)S(1)} %get-tuple-element.32), channel_id=1, source_target_pairs={{1,0},{2,1},{3,2},{4,3},{5,4},{6,5},{7,6},{8,7},{9,8},{10,9},{11,1... | collective-permute-start | bytes 737288 | tf_op jit(solution)/shard_map/ppermute | solution.py:502

commit v6 on v4

--- a/solution.py
+++ b/solution.py
@@ -24,8 +24,8 @@
 SMEM = pl.BlockSpec(memory_space=pltpu.SMEM)
 
 
-def params():
-    return pltpu.CompilerParams(vmem_limit_bytes=40 * 1024 * 1024)
+def params(mebibytes=40):
+    return pltpu.CompilerParams(vmem_limit_bytes=mebibytes * 1024 * 1024)
 
 
 def cost(flops, size):
@@ -45,60 +45,83 @@
 
 def tiled_rows(blocks):
     count = blocks.shape[0] // 8
-    return blocks.reshape(count, 8, FIELDS, PAIRS, LANES).transpose(2, 0, 3, 1, 4)
-
-
-def pack_kernel(size, per_dev, owner_hbm, rows_hbm, out, owner, count, sems):
+    groups = blocks.reshape(count, 8, FIELDS, PAIRS, LANES).transpose(2, 0, 3, 1, 4)
+    return groups.reshape(FIELDS * count * PAIRS * 8, LANES)
+
+
+def pack_kernel(
+    size, cap, per_dev, owner_hbm, rows_hbm, out_hbm, owner, rows, out, count, member, sems
+):
     own = lax.axis_index("gx")
-    fetch = pltpu.make_async_copy(owner_hbm, owner, sems.at[0])
-    fetch.start()
+    fetch_owner = pltpu.make_async_copy(owner_hbm, owner, sems.at[0])
+    fetch_rows = pltpu.make_async_copy(rows_hbm, rows, sems.at[1])
+    fetch_owner.start()
+    fetch_rows.start()
 
     def clear(dest, carry):
         count[dest] = 0
         return carry
 
-    lax.fori_loop(0, size, clear, 0)
-    fetch.wait()
-
-    def place(block, carry):
+    lax.fori_loop(0, size, clear, 0, unroll=8)
+    fetch_owner.wait()
+
+    def note(block, carry):
         dest = owner[own * per_dev + block]
         rank = count[dest]
         count[dest] = rank + 1
-        pltpu.make_async_copy(
-            rows_hbm.at[:, lax.div(block, 8), :, lax.rem(block, 8)],
-            out.at[dest, :, :, rank],
-            sems.at[1],
-        ).start()
+        member[dest * cap + rank] = lax.div(block, 8) * (PAIRS * 8) + lax.rem(block, 8)
         return carry
 
-    lax.fori_loop(0, per_dev, place, 0, unroll=8)
-    half = out.at[pl.ds(0, size // 2)]
-    pltpu.make_async_copy(half, half, sems.at[1]).wait()
+    lax.fori_loop(0, per_dev, note, 0, unroll=8)
+    fetch_rows.wait()
+    tiles = TILES * cap
+
+    def message(dest, carry):
+        @pl.when(count[dest] > 0)
+        def _():
+            for rank in range(cap):
+                first = member[dest * cap + rank]
+                for pair in range(PAIRS):
+                    source = pl.ds(first + pair * 8, FIELDS, stride=per_dev * PAIRS)
+                    to = dest * tiles + pair * (FIELDS * cap) + rank
+                    out[pl.ds(to, FIELDS, stride=cap), :] = rows[source, :]
+            part = pl.ds(pl.multiple_of(dest * tiles, tiles), tiles)
+            pltpu.make_async_copy(out.at[part], out_hbm.at[part], sems.at[2]).start()
+
+        return carry
+
+    lax.fori_loop(0, size, message, 0)
+    half = out.at[pl.ds(0, per_dev * TILES)]
+    pltpu.make_async_copy(half, half, sems.at[2]).wait()
 
 
 def pack(rows, owner_list, size, cap, per_dev):
+    send = (size * TILES * cap, LANES)
     return pl.pallas_call(
-        functools.partial(pack_kernel, size, per_dev),
-        out_shape=jax.ShapeDtypeStruct((size, FIELDS, PAIRS, cap, 1, LANES), jnp.float32),
+        functools.partial(pack_kernel, size, cap, per_dev),
+        out_shape=jax.ShapeDtypeStruct(send, jnp.float32),
         in_specs=[pl.BlockSpec(memory_space=pltpu.HBM)] * 2,
-        out_specs=VMEM,
+        out_specs=pl.BlockSpec(memory_space=pltpu.HBM),
         scratch_shapes=[
             pltpu.SMEM(owner_list.shape, jnp.int32),
+            pltpu.VMEM(rows.shape, jnp.float32),
+            pltpu.VMEM(send, jnp.float32),
             pltpu.SMEM((size,), jnp.int32),
-            pltpu.SemaphoreType.DMA((2,)),
+            pltpu.SMEM((size * cap,), jnp.int32),
+            pltpu.SemaphoreType.DMA((3,)),
         ],
-        compiler_params=params(),
+        compiler_params=params(62),
         cost_estimate=cost(1_000_000, 3_000_000),
         name="pack",
-    )(owner_list, rows[:, :, :, :, None, :])
+    )(owner_list, rows)
 
 
 def fastest_kernel(rows_ref, out):
     best = jnp.zeros((8, LANES), jnp.float32)
-    for group in range(rows_ref.shape[1]):
-        for pair in range(PAIRS):
-            fields = [rows_ref[f, group, pair] for f in range(FIELDS)]
-            best = jnp.maximum(best, wave_speed(fields))
+    step = rows_ref.shape[0] // FIELDS
+    for first in range(0, step, 8):
+        fields = [rows_ref[f * step + first : f * step + first + 8, :] for f in range(FIELDS)]
+        best = jnp.maximum(best, wave_speed(fields))
     out[...] = jnp.full((8, LANES), jnp.max(best), jnp.float32)
 
 
@@ -149,8 +172,8 @@
         rank = lax.rem(where, cap)
         for pair in range(PAIRS):
             couple, h = divmod(pair, 2)
-            base = source * (TILES * cap) + rank + pair * cap
-            value = come[pl.ds(base, FIELDS, stride=PAIRS * cap), :]
+            base = source * (TILES * cap) + rank + pair * (FIELDS * cap)
+            value = come[pl.ds(base, FIELDS, stride=cap), :]
             row = (couple * BZ + q) * 8 + 2 * p + h
             scratch[pl.ds(row, FIELDS, stride=PAIRS // 2 * BZ * 8), :] = value
     group = lax.broadcasted_iota(jnp.int32, (8, LANES), 1) // BLOCK
@@ -469,10 +492,9 @@
     parts, rows, owner_list, slot_list = lax.optimization_barrier(
         (parts, rows, owner_list, slot_list)
     )
-    parts = parts.reshape(size * TILES * cap, LANES)
     come = lax.all_to_all(parts, "gx", split_axis=0, concat_axis=0, tiled=True)
     table = arrival_spots(owner_list, slot_list, own, per_dev, size, cap)
-    speed = jnp.max(lax.all_gather(fastest(rows), "gx"), axis=0)
+    speed = everyone_max(fastest(rows), "gx", size)
     come, table, speed = lax.optimization_barrier((come, table, speed))
     state, low, high = unpack(table, come, cap)
     below = lax.ppermute(high, "gx", up)
@@ -480,7 +502,6 @@
     sides = along_planes(state, speed)
     middle, low, high, top = first_stage(state, sides, below, above, speed)
     second = everyone_max(top, "gx", size)
-    low, high, second = lax.optimization_barrier((low, high, second))
     below = lax.ppermute(high, "gx", up)
     above = lax.ppermute(low, "gx", down)
     sides = along_planes(middle, second)

time: 91.7 us -> 78.4 us (0.85)
  blocking collectives: 37.1 us -> 0 us
  waiting for transfers between devices: 5.55 us -> 25.8 us
  starting transfers between devices: 24.3 us -> 30.3 us
  local copies, waits for them, and re-layouts: 1.94 us -> 0.17 us
    all_gather x1 -> x0, blocking collectives: 37.1 us -> none  [per_device(): speed = jnp.max(lax.all_gather(fastest(rows), 'gx'), axis=0)]
    ppermute x6 -> x12, waiting for transfers between devices: 5.54 us -> 25.8 us  [everyone_max(): copies.append(lax.ppermute(value, axis, pairs))]
    ppermute x6 -> x12, starting transfers between devices: 6.59 us -> 13.9 us  [everyone_max(): copies.append(lax.ppermute(value, axis, pairs))]
    unnamed x10 -> x6, local copies, waits for them, and re-layouts: 1.79 us -> 0.02 us
    ppermute x2, starting transfers between devices: 9.8 us -> 8.36 us  [per_device(): above = lax.ppermute(low, 'gx', down)]
  transfers between devices with their start and end apart: 11 -> 17, of which waited for: 4 -> 7; matrix products, arithmetic and copies ran while one was open for 1% -> 1% of each run, Pallas kernels for 11% -> 13%
where the time goes in v6:
time: 78.4 us; the launch traced here: 78.2 us
  starting transfers between devices  30.3 us (39%)
  waiting for transfers between devices  25.8 us (33%)
  Pallas kernels  21.1 us (27%)
    ppermute x12, waiting for transfers between devices, everyone_max(): copies.append(lax.ppermute(value, axis, pairs))  25.8 us
    ppermute x12, starting transfers between devices, everyone_max(): copies.append(lax.ppermute(value, axis, pairs))  13.9 us
    pallas_call x2, Pallas kernels, along_planes(): pl.pallas_call(plane_kernel, out_shape=jax.ShapeDtypeStruct(state.shape,...  9.98 us
    ppermute x2, starting transfers between devices, per_device(): above = lax.ppermute(low, 'gx', down)  8.36 us
    all_to_all x1, starting transfers between devices, per_device(): come = lax.all_to_all(parts, 'gx', split_axis=0, concat_axis=0, tiled=True)  7.49 us
    pallas_call x1, Pallas kernels, second_stage(): pl.pallas_call(second_kernel, out_shape=jax.ShapeDtypeStruct((FIELDS, BLO...  3.16 us
    pallas_call x1, Pallas kernels, unpack(): pl.pallas_call(functools.partial(unpack_kernel, cap), out_shape=(jax.Shap...  2.79 us
    pallas_call x1, Pallas kernels, pack(): pl.pallas_call(functools.partial(pack_kernel, size, cap, per_dev), out_sh...  2.47 us
  transfers between devices with their start and end apart: 17, of which 7 were waited for; matrix products, arithmetic and copies ran while one was open for 1% of the time, Pallas kernels for 13%

profile of v6, /device:TPU:0, one launch (start us, length us, event | category | flops | bytes accessed | tf_op | source)
XLA Modules:
  0.0 78.2 jit_solution(17494626603270633000)
XLA Ops:
  0.0 2.5 %pack.1 = f32[2560,128]{1,0:T(8,128)} custom-call(s32[1024]{0:T(1024)} %owner_hbm.1, f32[1280,128]{1,0:T(8,128)} %bitcast.8), custom_call_target="tpu_custom_call" | custom-call | flops 1000000 | bytes 3000000 | tf_op jit(solution)/shard_map/pack/pallas_call | solution.py:100
  2.5 7.5 %all-to-all-start = ((f32[16,160,128]{2,1,0:T(8,128)}), f32[16,160,128]{2,1,0:T(8,128)S(1)}, u32[]{:S(2)}, u32[]{:S(2)}) async-start(f32[16,160,128]{2,1,0:T(8,128)} %bitcast.10), calls=%async_computation | async-start | bytes 2621440 | tf_op jit(solution)/shard_map/all_to_all | solution.py:495
  10.3 1.7 %collective-permute-start.2 = (f32[8,128]{1,0:T(8,128)S(1)}, f32[8,128]{1,0:T(8,128)S(1)}, u32[]{:S(2)}, u32[]{:S(2)}) collective-permute-start(f32[8,128]{1,0:T(8,128)S(1)} %fastest.1), channel_id=1, source_target_pairs={{0,3},{1,2},{2,1},{3,0},{4,7},{5,6},{6,5},{7,4},{8,11},{9,10},{10,... | collective-permute-start | bytes 12296 | tf_op jit(solution)/shard_map/ppermute | solution.py:476
  12.0 0.4 collective-permute-start.1
  12.5 0.3 convert_reduce_fusion
  13.0 5.9 %collective-permute-done.2 = f32[8,128]{1,0:T(8,128)S(1)} collective-permute-done((f32[8,128]{1,0:T(8,128)S(1)}, f32[8,128]{1,0:T(8,128)S(1)}, u32[]{:S(2)}, u32[]{:S(2)}) %collective-permute-start.2) | collective-permute-done | bytes 4128 | tf_op jit(solution)/shard_map/ppermute | solution.py:476
  19.0 0.6 collective-permute-done.1
  19.6 4.5 %collective-permute-start.5 = (f32[8,128]{1,0:T(8,128)S(1)}, f32[8,128]{1,0:T(8,128)S(1)}, u32[]{:S(2)}, u32[]{:S(2)}) collective-permute-start(f32[8,128]{1,0:T(8,128)S(1)} %maximum_maximum_fusion.3), channel_id=1, source_target_pairs={{0,12},{1,13},{2,14},{3,15},{4,8},{5,9},{6,10},{7,11},{8,4},{9,5},... | collective-permute-start | bytes 12296 | tf_op jit(solution)/shard_map/ppermute | solution.py:476
  24.1 0.6 collective-permute-start.3
  24.9 11.5 %collective-permute-done.5 = f32[8,128]{1,0:T(8,128)S(1)} collective-permute-done((f32[8,128]{1,0:T(8,128)S(1)}, f32[8,128]{1,0:T(8,128)S(1)}, u32[]{:S(2)}, u32[]{:S(2)}) %collective-permute-start.5) | collective-permute-done | bytes 4128 | tf_op jit(solution)/shard_map/ppermute | solution.py:476
  36.4 6.1 %collective-permute-done.4 = f32[8,128]{1,0:T(8,128)S(1)} collective-permute-done((f32[8,128]{1,0:T(8,128)S(1)}, f32[8,128]{1,0:T(8,128)S(1)}, u32[]{:S(2)}, u32[]{:S(2)}) %collective-permute-start.4) | collective-permute-done | bytes 4128 | tf_op jit(solution)/shard_map/ppermute | solution.py:476
  42.6 2.8 %unpack.1 = (f32[5,8,32,128]{3,2,1,0:T(8,128)S(1)}, f32[5,3,32,128]{3,2,1,0:T(8,128)S(1)}, f32[5,3,32,128]{3,2,1,0:T(8,128)S(1)}) custom-call(s32[64]{0:T(128)S(1)} %select_reduce_fusion.table, f32[2560,128]{1,0:T(8,128)S(1)} %bitcast.7), custom_call_target="tpu_custom_call" | custom-call | flops 5000000 | bytes 2000000 | tf_op jit(solution)/shard_map/unpack/pallas_call | solution.py:207
  45.5 4.4 %collective-permute-start.7 = (f32[5,3,32,128]{3,2,1,0:T(8,128)S(1)}, f32[5,3,32,128]{3,2,1,0:T(8,128)S(1)}, u32[]{:S(2)}, u32[]{:S(2)}) collective-permute-start(f32[5,3,32,128]{3,2,1,0:T(8,128)S(1)} %get-tuple-element.28), channel_id=1, source_target_pairs={{1,0},{2,1},{3,2},{4,3},{5,4},{6,5},{7,6},{8,7},{9,8},{10,9},{11,1... | collective-permute-start | bytes 737288 | tf_op jit(solution)/shard_map/ppermute | solution.py:501
  49.9 5.0 %planes.2.sides = f32[5,8,32,128]{3,2,1,0:T(8,128)S(1)} custom-call(f32[5,8,32,128]{3,2,1,0:T(8,128)S(1)} %get-tuple-element.25.state.start, f32[8,128]{1,0:T(8,128)S(1)} %maximum_maximum_fusion.2.speed.first_speed), custom_call_target="tpu_custom_call" | custom-call | flops 20000000 | bytes 1000000 | tf_op jit(solution)/shard_map/planes/pallas_call | solution.py:348
  54.9 2.5 %first_stage.1 = (f32[5,8,32,128]{3,2,1,0:T(8,128)S(1)}, f32[5,3,32,128]{3,2,1,0:T(8,128)S(1)}, f32[5,3,32,128]{3,2,1,0:T(8,128)S(1)}, f32[8,128]{1,0:T(8,128)S(1)}) custom-call(f32[5,8,32,128]{3,2,1,0:T(8,128)S(1)} %get-tuple-element.25.state.start, f32[5,8,32,128]{3,2,1,0:T(8,128)S(1)} %planes.2.sides, f32[5,3,32,128]{3,2,1,0:T(8,128)S(1)} %collective-permute-done.6.below, ...), custom_call_target="tpu_custom_call" | custom-call | flops 30000000 | bytes 3000000 | tf_op jit(solution)/shard_map/first_stage/pallas_call | solution.py:418
  57.5 2.1 %collective-permute-start.9 = (f32[8,128]{1,0:T(8,128)S(1)}, f32[8,128]{1,0:T(8,128)S(1)}, u32[]{:S(2)}, u32[]{:S(2)}) collective-permute-start(f32[8,128]{1,0:T(8,128)S(1)} %get-tuple-element.30), channel_id=1, source_target_pairs={{0,2},{1,3},{2,0},{3,1},{4,6},{5,7},{6,4},{7,5},{8,10},{9,11},{10,... | collective-permute-start | bytes 12296 | tf_op jit(solution)/shard_map/ppermute | solution.py:476
  59.5 0.5 collective-permute-start.14
  60.0 3.9 %collective-permute-start.15 = (f32[5,3,32,128]{3,2,1,0:T(8,128)S(1)}, f32[5,3,32,128]{3,2,1,0:T(8,128)S(1)}, u32[]{:S(2)}, u32[]{:S(2)}) collective-permute-start(f32[5,3,32,128]{3,2,1,0:T(8,128)S(1)} %get-tuple-element.32), channel_id=1, source_target_pairs={{1,0},{2,1},{3,2},{4,3},{5,4},{6,5},{7,6},{8,7},{9,8},{10,9},{11,1... | collective-permute-start | bytes 737288 | tf_op jit(solution)/shard_map/ppermute | solution.py:506
  64.0 1.0 %collective-permute-start.13 = (f32[8,128]{1,0:T(8,128)S(1)}, f32[8,128]{1,0:T(8,128)S(1)}, u32[]{:S(2)}, u32[]{:S(2)}) collective-permute-start(f32[8,128]{1,0:T(8,128)S(1)} %maximum_maximum_fusion.1), channel_id=1, source_target_pairs={{0,12},{1,13},{2,14},{3,15},{4,8},{5,9},{6,10},{7,11},{8,4},{9,5},... | collective-permute-start | bytes 12296 | tf_op jit(solution)/shard_map/ppermute | solution.py:476
  65.0 3.4 %collective-permute-start.11 = (f32[8,128]{1,0:T(8,128)S(1)}, f32[8,128]{1,0:T(8,128)S(1)}, u32[]{:S(2)}, u32[]{:S(2)}) collective-permute-start(f32[8,128]{1,0:T(8,128)S(1)} %maximum_maximum_fusion.1), channel_id=1, source_target_pairs={{0,4},{1,5},{2,6},{3,7},{4,0},{5,1},{6,2},{7,3},{8,12},{9,13},{10,... | collective-permute-start | bytes 12296 | tf_op jit(solution)/shard_map/ppermute | solution.py:476
  68.4 1.0 %collective-permute-done.13 = f32[8,128]{1,0:T(8,128)S(1)} collective-permute-done((f32[8,128]{1,0:T(8,128)S(1)}, f32[8,128]{1,0:T(8,128)S(1)}, u32[]{:S(2)}, u32[]{:S(2)}) %collective-permute-start.13) | collective-permute-done | bytes 4128 | tf_op jit(solution)/shard_map/ppermute | solution.py:476
  69.5 0.5 collective-permute-done.11
  70.0 5.0 %planes.3.sides = f32[5,8,32,128]{3,2,1,0:T(8,128)S(1)} custom-call(f32[5,8,32,128]{3,2,1,0:T(8,128)S(1)} %get-tuple-element.29.state.middle, f32[8,128]{1,0:T(8,128)S(1)} %maximum_maximum_fusion.speed), custom_call_target="tpu_custom_call" | custom-call | flops 20000000 | bytes 1000000 | tf_op jit(solution)/shard_map/planes/pallas_call | solution.py:348
  75.1 3.2 %second_stage.1 = f32[5,8,32,128]{3,2,1,0:T(8,128)} custom-call(f32[5,8,32,128]{3,2,1,0:T(8,128)S(1)} %get-tuple-element.25.state.start, f32[5,8,32,128]{3,2,1,0:T(8,128)S(1)} %get-tuple-element.29.state.middle, f32[5,8,32,128]{3,2,1,0:T(8,128)S(1)} %planes.3.sides, f32[5,3,32,128]{3,2,1,0:T(8,128)S(1)} %collective-permute-done.14.below, ...), custom_call_target="tpu_custom_call" | custom-call | flops 30000000 | bytes 3000000 | tf_op jit(solution)/shard_map/second_stage/pallas_call | solution.py:457
  (35 shorter events, 0.9 us)
Async XLA Ops:
  2.5 7.5 %copy-start = (f32[64,5,512]{2,0,1:T(8,128)S(1)}, f32[64,5,512]{2,0,1:T(8,128)}, u32[]{:S(2)}) copy-start(f32[64,5,512]{2,0,1:T(8,128)} %param.3) | copy-start | bytes 1966084
  2.5 9.9 %copy-start.1 = (s32[1024]{0:T(1024)S(1)}, s32[1024]{0:T(1024)}, u32[]{:S(2)}) copy-start(s32[1024]{0:T(1024)} %owner_hbm.1) | copy-start | bytes 12292
  2.5 9.9 %copy-start.2 = (s32[1024]{0:T(1024)S(1)}, s32[1024]{0:T(1024)}, u32[]{:S(2)}) copy-start(s32[1024]{0:T(1024)} %param.5) | copy-start | bytes 12292
  2.5 40.1 %all-to-all-start = ((f32[16,160,128]{2,1,0:T(8,128)}), f32[16,160,128]{2,1,0:T(8,128)S(1)}, u32[]{:S(2)}, u32[]{:S(2)}) async-start(f32[16,160,128]{2,1,0:T(8,128)} %bitcast.10), calls=%async_computation | async-start | bytes 2621440 | tf_op jit(solution)/shard_map/all_to_all | solution.py:495
  10.3 8.7 %collective-permute-start.2 = (f32[8,128]{1,0:T(8,128)S(1)}, f32[8,128]{1,0:T(8,128)S(1)}, u32[]{:S(2)}, u32[]{:S(2)}) collective-permute-start(f32[8,128]{1,0:T(8,128)S(1)} %fastest.1), channel_id=1, source_target_pairs={{0,3},{1,2},{2,1},{3,0},{4,7},{5,6},{6,5},{7,4},{8,11},{9,10},{10,... | collective-permute-start | bytes 12296 | tf_op jit(solution)/shard_map/ppermute | solution.py:476
  12.0 7.6 %collective-permute-start.1 = (f32[8,128]{1,0:T(8,128)S(1)}, f32[8,128]{1,0:T(8,128)S(1)}, u32[]{:S(2)}, u32[]{:S(2)}) collective-permute-start(f32[8,128]{1,0:T(8,128)S(1)} %fastest.1), channel_id=1, source_target_pairs={{0,2},{1,3},{2,0},{3,1},{4,6},{5,7},{6,4},{7,5},{8,10},{9,11},{10,... | collective-permute-start | bytes 12296 | tf_op jit(solution)/shard_map/ppermute | solution.py:476
  12.4 7.2 %collective-permute-start = (f32[8,128]{1,0:T(8,128)S(1)}, f32[8,128]{1,0:T(8,128)S(1)}, u32[]{:S(2)}, u32[]{:S(2)}) collective-permute-start(f32[8,128]{1,0:T(8,128)S(1)} %fastest.1), channel_id=1, source_target_pairs={{0,1},{1,0},{2,3},{3,2},{4,5},{5,4},{6,7},{7,6},{8,9},{9,8},{10,11... | collective-permute-start | bytes 12296 | tf_op jit(solution)/shard_map/ppermute | solution.py:476
  19.6 16.8 %collective-permute-start.5 = (f32[8,128]{1,0:T(8,128)S(1)}, f32[8,128]{1,0:T(8,128)S(1)}, u32[]{:S(2)}, u32[]{:S(2)}) collective-permute-start(f32[8,128]{1,0:T(8,128)S(1)} %maximum_maximum_fusion.3), channel_id=1, source_target_pairs={{0,12},{1,13},{2,14},{3,15},{4,8},{5,9},{6,10},{7,11},{8,4},{9,5},... | collective-permute-start | bytes 12296 | tf_op jit(solution)/shard_map/ppermute | solution.py:476
  24.1 18.4 %collective-permute-start.4 = (f32[8,128]{1,0:T(8,128)S(1)}, f32[8,128]{1,0:T(8,128)S(1)}, u32[]{:S(2)}, u32[]{:S(2)}) collective-permute-start(f32[8,128]{1,0:T(8,128)S(1)} %maximum_maximum_fusion.3), channel_id=1, source_target_pairs={{0,8},{1,9},{2,10},{3,11},{4,12},{5,13},{6,14},{7,15},{8,0},{9,1},... | collective-permute-start | bytes 12296 | tf_op jit(solution)/shard_map/ppermute | solution.py:476
  24.1 18.4 %collective-permute-start.3 = (f32[8,128]{1,0:T(8,128)S(1)}, f32[8,128]{1,0:T(8,128)S(1)}, u32[]{:S(2)}, u32[]{:S(2)}) collective-permute-start(f32[8,128]{1,0:T(8,128)S(1)} %maximum_maximum_fusion.3), channel_id=1, source_target_pairs={{0,4},{1,5},{2,6},{3,7},{4,0},{5,1},{6,2},{7,3},{8,12},{9,13},{10,... | collective-permute-start | bytes 12296 | tf_op jit(solution)/shard_map/ppermute | solution.py:476
  45.4 9.5 %collective-permute-start.6 = (f32[5,3,32,128]{3,2,1,0:T(8,128)S(1)}, f32[5,3,32,128]{3,2,1,0:T(8,128)S(1)}, u32[]{:S(2)}, u32[]{:S(2)}) collective-permute-start(f32[5,3,32,128]{3,2,1,0:T(8,128)S(1)} %get-tuple-element.27), channel_id=1, source_target_pairs={{0,1},{1,2},{2,3},{3,4},{4,5},{5,6},{6,7},{7,8},{8,9},{9,10},{10,1... | collective-permute-start | bytes 737288 | tf_op jit(solution)/shard_map/ppermute | solution.py:500
  45.5 9.4 %collective-permute-start.7 = (f32[5,3,32,128]{3,2,1,0:T(8,128)S(1)}, f32[5,3,32,128]{3,2,1,0:T(8,128)S(1)}, u32[]{:S(2)}, u32[]{:S(2)}) collective-permute-start(f32[5,3,32,128]{3,2,1,0:T(8,128)S(1)} %get-tuple-element.28), channel_id=1, source_target_pairs={{1,0},{2,1},{3,2},{4,3},{5,4},{6,5},{7,6},{8,7},{9,8},{10,9},{11,1... | collective-permute-start | bytes 737288 | tf_op jit(solution)/shard_map/ppermute | solution.py:501
  57.4 6.6 %collective-permute-start.10 = (f32[8,128]{1,0:T(8,128)S(1)}, f32[8,128]{1,0:T(8,128)S(1)}, u32[]{:S(2)}, u32[]{:S(2)}) collective-permute-start(f32[8,128]{1,0:T(8,128)S(1)} %get-tuple-element.30), channel_id=1, source_target_pairs={{0,3},{1,2},{2,1},{3,0},{4,7},{5,6},{6,5},{7,4},{8,11},{9,10},{10,... | collective-permute-start | bytes 12296 | tf_op jit(solution)/shard_map/ppermute | solution.py:476
  57.5 6.5 %collective-permute-start.9 = (f32[8,128]{1,0:T(8,128)S(1)}, f32[8,128]{1,0:T(8,128)S(1)}, u32[]{:S(2)}, u32[]{:S(2)}) collective-permute-start(f32[8,128]{1,0:T(8,128)S(1)} %get-tuple-element.30), channel_id=1, source_target_pairs={{0,2},{1,3},{2,0},{3,1},{4,6},{5,7},{6,4},{7,5},{8,10},{9,11},{10,... | collective-permute-start | bytes 12296 | tf_op jit(solution)/shard_map/ppermute | solution.py:476
  59.5 4.5 %collective-permute-start.8 = (f32[8,128]{1,0:T(8,128)S(1)}, f32[8,128]{1,0:T(8,128)S(1)}, u32[]{:S(2)}, u32[]{:S(2)}) collective-permute-start(f32[8,128]{1,0:T(8,128)S(1)} %get-tuple-element.30), channel_id=1, source_target_pairs={{0,1},{1,0},{2,3},{3,2},{4,5},{5,4},{6,7},{7,6},{8,9},{9,8},{10,11... | collective-permute-start | bytes 12296 | tf_op jit(solution)/shard_map/ppermute | solution.py:476
  59.5 15.5 %collective-permute-start.14 = (f32[5,3,32,128]{3,2,1,0:T(8,128)S(1)}, f32[5,3,32,128]{3,2,1,0:T(8,128)S(1)}, u32[]{:S(2)}, u32[]{:S(2)}) collective-permute-start(f32[5,3,32,128]{3,2,1,0:T(8,128)S(1)} %get-tuple-element.31), channel_id=1, source_target_pairs={{0,1},{1,2},{2,3},{3,4},{4,5},{5,6},{6,7},{7,8},{8,9},{9,10},{10,1... | collective-permute-start | bytes 737288 | tf_op jit(solution)/shard_map/ppermute | solution.py:505
  60.0 15.0 %collective-permute-start.15 = (f32[5,3,32,128]{3,2,1,0:T(8,128)S(1)}, f32[5,3,32,128]{3,2,1,0:T(8,128)S(1)}, u32[]{:S(2)}, u32[]{:S(2)}) collective-permute-start(f32[5,3,32,128]{3,2,1,0:T(8,128)S(1)} %get-tuple-element.32), channel_id=1, source_target_pairs={{1,0},{2,1},{3,2},{4,3},{5,4},{6,5},{7,6},{8,7},{9,8},{10,9},{11,1... | collective-permute-start | bytes 737288 | tf_op jit(solution)/shard_map/ppermute | solution.py:506
  64.0 5.5 %collective-permute-start.13 = (f32[8,128]{1,0:T(8,128)S(1)}, f32[8,128]{1,0:T(8,128)S(1)}, u32[]{:S(2)}, u32[]{:S(2)}) collective-permute-start(f32[8,128]{1,0:T(8,128)S(1)} %maximum_maximum_fusion.1), channel_id=1, source_target_pairs={{0,12},{1,13},{2,14},{3,15},{4,8},{5,9},{6,10},{7,11},{8,4},{9,5},... | collective-permute-start | bytes 12296 | tf_op jit(solution)/shard_map/ppermute | solution.py:476
  65.0 4.5 %collective-permute-start.12 = (f32[8,128]{1,0:T(8,128)S(1)}, f32[8,128]{1,0:T(8,128)S(1)}, u32[]{:S(2)}, u32[]{:S(2)}) collective-permute-start(f32[8,128]{1,0:T(8,128)S(1)} %maximum_maximum_fusion.1), channel_id=1, source_target_pairs={{0,8},{1,9},{2,10},{3,11},{4,12},{5,13},{6,14},{7,15},{8,0},{9,1},... | collective-permute-start | bytes 12296 | tf_op jit(solution)/shard_map/ppermute | solution.py:476
  65.0 5.0 %collective-permute-start.11 = (f32[8,128]{1,0:T(8,128)S(1)}, f32[8,128]{1,0:T(8,128)S(1)}, u32[]{:S(2)}, u32[]{:S(2)}) collective-permute-start(f32[8,128]{1,0:T(8,128)S(1)} %maximum_maximum_fusion.1), channel_id=1, source_target_pairs={{0,4},{1,5},{2,6},{3,7},{4,0},{5,1},{6,2},{7,3},{8,12},{9,13},{10,... | collective-permute-start | bytes 12296 | tf_op jit(solution)/shard_map/ppermute | solution.py:476

commit v7 on v6

--- a/solution.py
+++ b/solution.py
@@ -50,7 +50,7 @@
 
 
 def pack_kernel(
-    size, cap, per_dev, owner_hbm, rows_hbm, out_hbm, owner, rows, out, count, member, sems
+    size, cap, per_dev, owner_hbm, rows_hbm, out_hbm, owner, rows, out, top, count, member, sems
 ):
     own = lax.axis_index("gx")
     fetch_owner = pltpu.make_async_copy(owner_hbm, owner, sems.at[0])
@@ -85,56 +85,46 @@
                     source = pl.ds(first + pair * 8, FIELDS, stride=per_dev * PAIRS)
                     to = dest * tiles + pair * (FIELDS * cap) + rank
                     out[pl.ds(to, FIELDS, stride=cap), :] = rows[source, :]
-            part = pl.ds(pl.multiple_of(dest * tiles, tiles), tiles)
-            pltpu.make_async_copy(out.at[part], out_hbm.at[part], sems.at[2]).start()
+            part = out.at[pl.ds(pl.multiple_of(dest * tiles, tiles), tiles)]
+            pltpu.make_async_copy(part, out_hbm.at[dest, pl.ds(0, tiles), 0], sems.at[2]).start()
 
         return carry
 
     lax.fori_loop(0, size, message, 0)
+    best = jnp.zeros((8, LANES), jnp.float32)
+    step = per_dev * PAIRS
+    for first in range(0, step, 8):
+        fields = [rows[f * step + first : f * step + first + 8, :] for f in range(FIELDS)]
+        best = jnp.maximum(best, wave_speed(fields))
+    top[...] = jnp.full(top.shape, jnp.max(best), jnp.float32)
+    for dest in range(size):
+        pltpu.make_async_copy(
+            top.at[pl.ds(dest, 1)], out_hbm.at[dest, tiles], sems.at[3]
+        ).start()
     half = out.at[pl.ds(0, per_dev * TILES)]
     pltpu.make_async_copy(half, half, sems.at[2]).wait()
+    pltpu.make_async_copy(top, top, sems.at[3]).wait()
 
 
 def pack(rows, owner_list, size, cap, per_dev):
-    send = (size * TILES * cap, LANES)
     return pl.pallas_call(
         functools.partial(pack_kernel, size, cap, per_dev),
-        out_shape=jax.ShapeDtypeStruct(send, jnp.float32),
+        out_shape=jax.ShapeDtypeStruct((size, TILES * cap + 1, 1, LANES), jnp.float32),
         in_specs=[pl.BlockSpec(memory_space=pltpu.HBM)] * 2,
         out_specs=pl.BlockSpec(memory_space=pltpu.HBM),
         scratch_shapes=[
             pltpu.SMEM(owner_list.shape, jnp.int32),
             pltpu.VMEM(rows.shape, jnp.float32),
-            pltpu.VMEM(send, jnp.float32),
+            pltpu.VMEM((size * TILES * cap, LANES), jnp.float32),
+            pltpu.VMEM((size, LANES), jnp.float32),
             pltpu.SMEM((size,), jnp.int32),
             pltpu.SMEM((size * cap,), jnp.int32),
-            pltpu.SemaphoreType.DMA((3,)),
+            pltpu.SemaphoreType.DMA((4,)),
         ],
         compiler_params=params(62),
         cost_estimate=cost(1_000_000, 3_000_000),
         name="pack",
     )(owner_list, rows)
-
-
-def fastest_kernel(rows_ref, out):
-    best = jnp.zeros((8, LANES), jnp.float32)
-    step = rows_ref.shape[0] // FIELDS
-    for first in range(0, step, 8):
-        fields = [rows_ref[f * step + first : f * step + first + 8, :] for f in range(FIELDS)]
-        best = jnp.maximum(best, wave_speed(fields))
-    out[...] = jnp.full((8, LANES), jnp.max(best), jnp.float32)
-
-
-def fastest(rows):
-    return pl.pallas_call(
-        fastest_kernel,
-        out_shape=jax.ShapeDtypeStruct((8, LANES), jnp.float32),
-        in_specs=[VMEM],
-        out_specs=VMEM,
-        compiler_params=params(),
-        cost_estimate=cost(2_000_000, 700_000),
-        name="fastest",
-    )(rows)
 
 
 def arrival_spots(owner_list, slot_list, own, per_dev, size, cap):
@@ -164,7 +154,12 @@
     return rows
 
 
-def unpack_kernel(cap, table, come, state, low_halo, high_halo, scratch):
+def unpack_kernel(size, cap, table, come, state, low_halo, high_halo, speed, scratch):
+    message = TILES * cap + 1
+    best = come[message - 1 : message, :]
+    for source in range(1, size):
+        best = jnp.maximum(best, come[(source + 1) * message - 1 : (source + 1) * message, :])
+    speed[...] = jnp.broadcast_to(best, speed.shape)
     for slot in range(BY * BZ):
         p, q = divmod(slot, BZ)
         where = table[slot]
@@ -172,7 +167,7 @@
         rank = lax.rem(where, cap)
         for pair in range(PAIRS):
             couple, h = divmod(pair, 2)
-            base = source * (TILES * cap) + rank + pair * (FIELDS * cap)
+            base = source * message + rank + pair * (FIELDS * cap)
             value = come[pl.ds(base, FIELDS, stride=cap), :]
             row = (couple * BZ + q) * 8 + 2 * p + h
             scratch[pl.ds(row, FIELDS, stride=PAIRS // 2 * BZ * 8), :] = value
@@ -202,13 +197,18 @@
                             high_halo[f, plane - 5, rows, :] = planes[h]
 
 
-def unpack(table, come, cap):
+def unpack(table, come, size, cap):
     halo = jax.ShapeDtypeStruct((FIELDS, 3, ROWS, LANES), jnp.float32)
     return pl.pallas_call(
-        functools.partial(unpack_kernel, cap),
-        out_shape=(jax.ShapeDtypeStruct((FIELDS, BLOCK, ROWS, LANES), jnp.float32), halo, halo),
+        functools.partial(unpack_kernel, size, cap),
+        out_shape=(
+            jax.ShapeDtypeStruct((FIELDS, BLOCK, ROWS, LANES), jnp.float32),
+            halo,
+            halo,
+            jax.ShapeDtypeStruct((8, LANES), jnp.float32),
+        ),
         in_specs=[SMEM, VMEM],
-        out_specs=(VMEM,) * 3,
+        out_specs=(VMEM,) * 4,
         scratch_shapes=[pltpu.VMEM((FIELDS * (PAIRS // 2) * BZ * 8, LANES), jnp.float32)],
         compiler_params=params(),
         cost_estimate=cost(5_000_000, 2_000_000),
@@ -224,8 +224,16 @@
     return jnp.concatenate([pltpu.roll(x[24:], 1, 0), x[:24]], axis=0)
 
 
+def y_up_two(x):
+    return jnp.concatenate([x[16:], pltpu.roll(x[:8], 7, 0), pltpu.roll(x[8:16], 7, 0)], axis=0)
+
+
 def z_up(x):
     return pltpu.roll(x, LANES - 1, 1)
+
+
+def z_up_two(x):
+    return pltpu.roll(x, LANES - 2, 1)
 
 
 def z_down(x):
@@ -254,21 +262,21 @@
     return top * inverse(left + 6.0 * centre + right)
 
 
-def periodic_divergence(half_flux, scaled, up, down):
+def periodic_divergence(half_flux, scaled, up, up_two, down):
     plus = half_flux + scaled
     minus = half_flux - scaled
 
     def side(values):
         after = up(values) - values
         curve, left, centre, right = smoothness(down(after), after)
-        jump = up(curve) - curve
-        return curve, down(left), centre, up(right), down(jump), jump
-
-    curve, left, centre, right, jump_before, jump_after = side(plus)
+        above = up(curve)
+        return curve, above, left, centre, right, above - curve
+
+    curve, _, left, centre, right, jump = side(plus)
     face = 6.0 * (half_flux + up(half_flux)) - curve
-    face = face - upwind_term(left, centre, right, jump_before, jump_after)
-    curve, left, centre, right, jump_before, jump_after = side(minus)
-    face = face + up(upwind_term(right, centre, left, jump_after, jump_before) - curve)
+    face = face - upwind_term(down(left), centre, up(right), down(jump), jump)
+    _, curve, left, centre, right, jump = side(minus)
+    face = face + (upwind_term(up_two(right), up(centre), left, up(jump), jump) - curve)
     return face - down(face)
 
 
@@ -323,13 +331,14 @@
     vel, pressure = half_velocities(fields)
     for field in range(FIELDS):
         scaled = half_speed * fields[field]
-        along_z = periodic_divergence(
-            half_flux(fields, field, 2, vel[2], pressure), scaled, z_up, z_down
+        along_y = periodic_divergence(
+            half_flux(fields, field, 1, vel[1], pressure), scaled, y_up, y_up_two, y_down
         )
-        along_y = periodic_divergence(
-            half_flux(fields, field, 1, vel[1], pressure), scaled, y_up, y_down
-        )
-        yield field, along_y + along_z
+        flux = half_flux(fields, field, 2, vel[2], pressure)
+        for first in range(0, ROWS, 8):
+            rows = slice(first, first + 8)
+            along_z = periodic_divergence(flux[rows], scaled[rows], z_up, z_up_two, z_down)
+            yield field, rows, along_y[rows] + along_z
 
 
 def plane_kernel(state, speed, out):
@@ -337,8 +346,8 @@
 
     def one_plane(plane, carry):
         fields = [state[f, plane] for f in range(FIELDS)]
-        for field, total in side_planes(fields, half_speed):
-            out[field, plane] = total
+        for field, rows, total in side_planes(fields, half_speed):
+            out[field, plane, rows, :] = total
         return carry
 
     lax.fori_loop(0, state.shape[1], one_plane, 0)
@@ -487,16 +496,11 @@
     up = [(i, (i + 1) % size) for i in range(size)]
     down = [(j, i) for i, j in up]
 
-    rows = tiled_rows(blocks)
-    parts = pack(rows, owner_list, size, cap, per_dev)
-    parts, rows, owner_list, slot_list = lax.optimization_barrier(
-        (parts, rows, owner_list, slot_list)
-    )
+    parts = pack(tiled_rows(blocks), owner_list, size, cap, per_dev)
+    parts, owner_list, slot_list = lax.optimization_barrier((parts, owner_list, slot_list))
     come = lax.all_to_all(parts, "gx", split_axis=0, concat_axis=0, tiled=True)
     table = arrival_spots(owner_list, slot_list, own, per_dev, size, cap)
-    speed = everyone_max(fastest(rows), "gx", size)
-    come, table, speed = lax.optimization_barrier((come, table, speed))
-    state, low, high = unpack(table, come, cap)
+    state, low, high, speed = unpack(table, come.reshape(-1, LANES), size, cap)
     below = lax.ppermute(high, "gx", up)
     above = lax.ppermute(low, "gx", down)
     sides = along_planes(state, speed)

time: 78.4 us -> 75.3 us (0.960)
  starting transfers between devices: 30.3 us -> 24.9 us
  waiting for transfers between devices: 25.8 us -> 28.4 us
    all_to_all x1, waiting for transfers between devices: 0.01 us -> 26.8 us  [per_device(): come = lax.all_to_all(parts, 'gx', split_axis=0, concat_axis=0, tiled=True)]
    ppermute x12 -> x6, waiting for transfers between devices: 25.8 us -> 1.59 us  [everyone_max(): copies.append(lax.ppermute(value, axis, pairs))]
    ppermute x12 -> x6, starting transfers between devices: 13.9 us -> 6.38 us  [everyone_max(): copies.append(lax.ppermute(value, axis, pairs))]
    ppermute x2, starting transfers between devices: 8.36 us -> 10.3 us  [per_device(): above = lax.ppermute(low, 'gx', down)]
    pallas_call x2 -> x1, Pallas kernels: 3.03 us -> 2.79 us  [unpack(): pl.pallas_call(functools.partial(unpack_kernel, size, cap), out_shape=(ja...]
  transfers between devices with their start and end apart: 17 -> 11, of which waited for: 7 -> 4; matrix products, arithmetic and copies ran while one was open for 1% -> 1% of each run, Pallas kernels for 13% -> 13%
where the time goes in v7:
time: 75.3 us; the launch traced here: 75.1 us
  waiting for transfers between devices  28.4 us (38%)
  starting transfers between devices  24.9 us (33%)
  Pallas kernels  20.9 us (28%)
    all_to_all x1, waiting for transfers between devices, per_device(): come = lax.all_to_all(parts, 'gx', split_axis=0, concat_axis=0, tiled=True)  26.8 us
    ppermute x2, starting transfers between devices, per_device(): above = lax.ppermute(low, 'gx', down)  10.3 us
    pallas_call x2, Pallas kernels, along_planes(): pl.pallas_call(plane_kernel, out_shape=jax.ShapeDtypeStruct(state.shape,...  9.77 us
    all_to_all x1, starting transfers between devices, per_device(): come = lax.all_to_all(parts, 'gx', split_axis=0, concat_axis=0, tiled=True)  7.37 us
    ppermute x6, starting transfers between devices, everyone_max(): copies.append(lax.ppermute(value, axis, pairs))  6.38 us
    pallas_call x1, Pallas kernels, second_stage(): pl.pallas_call(second_kernel, out_shape=jax.ShapeDtypeStruct((FIELDS, BLO...  3.16 us
    pallas_call x1, Pallas kernels, unpack(): pl.pallas_call(functools.partial(unpack_kernel, size, cap), out_shape=(ja...  2.79 us
    pallas_call x1, Pallas kernels, pack(): pl.pallas_call(functools.partial(pack_kernel, size, cap, per_dev), out_sh...  2.74 us
  transfers between devices with their start and end apart: 11, of which 4 were waited for; matrix products, arithmetic and copies ran while one was open for 1% of the time, Pallas kernels for 13%

profile of v7, /device:TPU:0, one launch (start us, length us, event | category | flops | bytes accessed | tf_op | source)
XLA Modules:
  0.0 75.1 jit_solution(743726350303524961)
XLA Ops:
  0.0 2.7 %pack.1 = f32[16,161,1,128]{3,2,1,0:T(1,128)} custom-call(s32[1024]{0:T(1024)} %owner_hbm.1, f32[1280,128]{1,0:T(8,128)} %bitcast.7), custom_call_target="tpu_custom_call" | custom-call | flops 1000000 | bytes 3000000 | tf_op jit(solution)/shard_map/pack/pallas_call | solution.py:110
  2.8 7.4 %all-to-all-start = ((f32[16,161,1,128]{3,2,1,0:T(1,128)}), f32[16,161,1,128]{3,2,1,0:T(1,128)S(1)}, u32[]{:S(2)}, u32[]{:S(2)}) async-start(f32[16,161,1,128]{3,2,1,0:T(1,128)} %pack.1), calls=%async_computation | async-start | bytes 2637824 | tf_op jit(solution)/shard_map/all_to_all | solution.py:501
  10.2 0.1 eq.33
  10.3 0.3 convert_reduce_fusion
  10.7 0.1 add.17
  10.8 0.1 select_reduce_fusion.table
  10.9 26.8 %all-to-all-done = f32[16,161,1,128]{3,2,1,0:T(1,128)S(1)} async-done(((f32[16,161,1,128]{3,2,1,0:T(1,128)}), f32[16,161,1,128]{3,2,1,0:T(1,128)S(1)}, u32[]{:S(2)}, u32[]{:S(2)}) %all-to-all-start) | async-done | bytes 1318944 | tf_op jit(solution)/shard_map/all_to_all | solution.py:501
  37.7 2.8 %unpack.1 = (f32[5,8,32,128]{3,2,1,0:T(8,128)S(1)}, f32[5,3,32,128]{3,2,1,0:T(8,128)S(1)}, f32[5,3,32,128]{3,2,1,0:T(8,128)S(1)}, f32[8,128]{1,0:T(8,128)S(1)}) custom-call(s32[64]{0:T(128)S(1)} %select_reduce_fusion.table, f32[2576,128]{1,0:T(8,128)S(1)} %bitcast.6), custom_call_target="tpu_custom_call" | custom-call | flops 5000000 | bytes 2000000 | tf_op jit(solution)/shard_map/unpack/pallas_call | solution.py:202
  40.5 0.8 %collective-permute-start = (f32[5,3,32,128]{3,2,1,0:T(8,128)S(1)}, f32[5,3,32,128]{3,2,1,0:T(8,128)S(1)}, u32[]{:S(2)}, u32[]{:S(2)}) collective-permute-start(f32[5,3,32,128]{3,2,1,0:T(8,128)S(1)} %get-tuple-element.21), channel_id=1, source_target_pairs={{0,1},{1,2},{2,3},{3,4},{4,5},{5,6},{6,7},{7,8},{8,9},{9,10},{10,1... | collective-permute-start | bytes 737288 | tf_op jit(solution)/shard_map/ppermute | solution.py:504
  41.3 5.9 %collective-permute-start.1 = (f32[5,3,32,128]{3,2,1,0:T(8,128)S(1)}, f32[5,3,32,128]{3,2,1,0:T(8,128)S(1)}, u32[]{:S(2)}, u32[]{:S(2)}) collective-permute-start(f32[5,3,32,128]{3,2,1,0:T(8,128)S(1)} %get-tuple-element.22), channel_id=1, source_target_pairs={{1,0},{2,1},{3,2},{4,3},{5,4},{6,5},{7,6},{8,7},{9,8},{10,9},{11,1... | collective-permute-start | bytes 737288 | tf_op jit(solution)/shard_map/ppermute | solution.py:505
  47.2 4.9 %planes.2.sides = f32[5,8,32,128]{3,2,1,0:T(8,128)S(1)} custom-call(f32[5,8,32,128]{3,2,1,0:T(8,128)S(1)} %get-tuple-element.19.state.start, f32[8,128]{1,0:T(8,128)S(1)} %get-tuple-element.20.speed.first_speed), custom_call_target="tpu_custom_call" | custom-call | flops 20000000 | bytes 1000000 | tf_op jit(solution)/shard_map/planes/pallas_call | solution.py:357
  52.1 2.5 %first_stage.1 = (f32[5,8,32,128]{3,2,1,0:T(8,128)S(1)}, f32[5,3,32,128]{3,2,1,0:T(8,128)S(1)}, f32[5,3,32,128]{3,2,1,0:T(8,128)S(1)}, f32[8,128]{1,0:T(8,128)S(1)}) custom-call(f32[5,8,32,128]{3,2,1,0:T(8,128)S(1)} %get-tuple-element.19.state.start, f32[5,8,32,128]{3,2,1,0:T(8,128)S(1)} %planes.2.sides, f32[5,3,32,128]{3,2,1,0:T(8,128)S(1)} %collective-permute-done.below, ...), custom_call_target="tpu_custom_call" | custom-call | flops 30000000 | bytes 3000000 | tf_op jit(solution)/shard_map/first_stage/pallas_call | solution.py:427
  54.6 0.3 collective-permute-start.4
  54.9 0.5 collective-permute-start.3
  55.4 1.1 %collective-permute-start.2 = (f32[8,128]{1,0:T(8,128)S(1)}, f32[8,128]{1,0:T(8,128)S(1)}, u32[]{:S(2)}, u32[]{:S(2)}) collective-permute-start(f32[8,128]{1,0:T(8,128)S(1)} %get-tuple-element.24), channel_id=1, source_target_pairs={{0,1},{1,0},{2,3},{3,2},{4,5},{5,4},{6,7},{7,6},{8,9},{9,8},{10,11... | collective-permute-start | bytes 12296 | tf_op jit(solution)/shard_map/ppermute | solution.py:485
  56.5 4.4 %collective-permute-start.9 = (f32[5,3,32,128]{3,2,1,0:T(8,128)S(1)}, f32[5,3,32,128]{3,2,1,0:T(8,128)S(1)}, u32[]{:S(2)}, u32[]{:S(2)}) collective-permute-start(f32[5,3,32,128]{3,2,1,0:T(8,128)S(1)} %get-tuple-element.26), channel_id=1, source_target_pairs={{1,0},{2,1},{3,2},{4,3},{5,4},{6,5},{7,6},{8,7},{9,8},{10,9},{11,1... | collective-permute-start | bytes 737288 | tf_op jit(solution)/shard_map/ppermute | solution.py:510
  61.0 1.3 %collective-permute-start.7 = (f32[8,128]{1,0:T(8,128)S(1)}, f32[8,128]{1,0:T(8,128)S(1)}, u32[]{:S(2)}, u32[]{:S(2)}) collective-permute-start(f32[8,128]{1,0:T(8,128)S(1)} %maximum_maximum_fusion.1), channel_id=1, source_target_pairs={{0,12},{1,13},{2,14},{3,15},{4,8},{5,9},{6,10},{7,11},{8,4},{9,5},... | collective-permute-start | bytes 12296 | tf_op jit(solution)/shard_map/ppermute | solution.py:485
  62.3 0.5 collective-permute-start.6
  62.7 2.7 %collective-permute-start.5 = (f32[8,128]{1,0:T(8,128)S(1)}, f32[8,128]{1,0:T(8,128)S(1)}, u32[]{:S(2)}, u32[]{:S(2)}) collective-permute-start(f32[8,128]{1,0:T(8,128)S(1)} %maximum_maximum_fusion.1), channel_id=1, source_target_pairs={{0,4},{1,5},{2,6},{3,7},{4,0},{5,1},{6,2},{7,3},{8,12},{9,13},{10,... | collective-permute-start | bytes 12296 | tf_op jit(solution)/shard_map/ppermute | solution.py:485
  65.4 1.0 %collective-permute-done.7 = f32[8,128]{1,0:T(8,128)S(1)} collective-permute-done((f32[8,128]{1,0:T(8,128)S(1)}, f32[8,128]{1,0:T(8,128)S(1)}, u32[]{:S(2)}, u32[]{:S(2)}) %collective-permute-start.7) | collective-permute-done | bytes 4128 | tf_op jit(solution)/shard_map/ppermute | solution.py:485
  66.4 0.4 collective-permute-done.6
  66.8 0.2 collective-permute-done.5
  67.0 4.9 %planes.3.sides = f32[5,8,32,128]{3,2,1,0:T(8,128)S(1)} custom-call(f32[5,8,32,128]{3,2,1,0:T(8,128)S(1)} %get-tuple-element.23.state.middle, f32[8,128]{1,0:T(8,128)S(1)} %maximum_maximum_fusion.speed), custom_call_target="tpu_custom_call" | custom-call | flops 20000000 | bytes 1000000 | tf_op jit(solution)/shard_map/planes/pallas_call | solution.py:357
  71.9 3.2 %second_stage.1 = f32[5,8,32,128]{3,2,1,0:T(8,128)} custom-call(f32[5,8,32,128]{3,2,1,0:T(8,128)S(1)} %get-tuple-element.19.state.start, f32[5,8,32,128]{3,2,1,0:T(8,128)S(1)} %get-tuple-element.23.state.middle, f32[5,8,32,128]{3,2,1,0:T(8,128)S(1)} %planes.3.sides, f32[5,3,32,128]{3,2,1,0:T(8,128)S(1)} %collective-permute-done.8.below, ...), custom_call_target="tpu_custom_call" | custom-call | flops 30000000 | bytes 3000000 | tf_op jit(solution)/shard_map/second_stage/pallas_call | solution.py:466
  (18 shorter events, 0.1 us)
Async XLA Ops:
  2.7 7.4 %copy-start = (s32[1024]{0:T(1024)S(1)}, s32[1024]{0:T(1024)}, u32[]{:S(2)}) copy-start(s32[1024]{0:T(1024)} %owner_hbm.1) | copy-start | bytes 12292
  2.8 7.4 %copy-start.1 = (s32[1024]{0:T(1024)S(1)}, s32[1024]{0:T(1024)}, u32[]{:S(2)}) copy-start(s32[1024]{0:T(1024)} %param.5) | copy-start | bytes 12292
  2.8 34.9 %all-to-all-start = ((f32[16,161,1,128]{3,2,1,0:T(1,128)}), f32[16,161,1,128]{3,2,1,0:T(1,128)S(1)}, u32[]{:S(2)}, u32[]{:S(2)}) async-start(f32[16,161,1,128]{3,2,1,0:T(1,128)} %pack.1), calls=%async_computation | async-start | bytes 2637824 | tf_op jit(solution)/shard_map/all_to_all | solution.py:501
  40.5 11.6 %collective-permute-start = (f32[5,3,32,128]{3,2,1,0:T(8,128)S(1)}, f32[5,3,32,128]{3,2,1,0:T(8,128)S(1)}, u32[]{:S(2)}, u32[]{:S(2)}) collective-permute-start(f32[5,3,32,128]{3,2,1,0:T(8,128)S(1)} %get-tuple-element.21), channel_id=1, source_target_pairs={{0,1},{1,2},{2,3},{3,4},{4,5},{5,6},{6,7},{7,8},{8,9},{9,10},{10,1... | collective-permute-start | bytes 737288 | tf_op jit(solution)/shard_map/ppermute | solution.py:504
  41.3 10.8 %collective-permute-start.1 = (f32[5,3,32,128]{3,2,1,0:T(8,128)S(1)}, f32[5,3,32,128]{3,2,1,0:T(8,128)S(1)}, u32[]{:S(2)}, u32[]{:S(2)}) collective-permute-start(f32[5,3,32,128]{3,2,1,0:T(8,128)S(1)} %get-tuple-element.22), channel_id=1, source_target_pairs={{1,0},{2,1},{3,2},{4,3},{5,4},{6,5},{7,6},{8,7},{9,8},{10,9},{11,1... | collective-permute-start | bytes 737288 | tf_op jit(solution)/shard_map/ppermute | solution.py:505
  54.6 6.4 %collective-permute-start.4 = (f32[8,128]{1,0:T(8,128)S(1)}, f32[8,128]{1,0:T(8,128)S(1)}, u32[]{:S(2)}, u32[]{:S(2)}) collective-permute-start(f32[8,128]{1,0:T(8,128)S(1)} %get-tuple-element.24), channel_id=1, source_target_pairs={{0,3},{1,2},{2,1},{3,0},{4,7},{5,6},{6,5},{7,4},{8,11},{9,10},{10,... | collective-permute-start | bytes 12296 | tf_op jit(solution)/shard_map/ppermute | solution.py:485
  54.9 6.1 %collective-permute-start.3 = (f32[8,128]{1,0:T(8,128)S(1)}, f32[8,128]{1,0:T(8,128)S(1)}, u32[]{:S(2)}, u32[]{:S(2)}) collective-permute-start(f32[8,128]{1,0:T(8,128)S(1)} %get-tuple-element.24), channel_id=1, source_target_pairs={{0,2},{1,3},{2,0},{3,1},{4,6},{5,7},{6,4},{7,5},{8,10},{9,11},{10,... | collective-permute-start | bytes 12296 | tf_op jit(solution)/shard_map/ppermute | solution.py:485
  55.4 5.5 %collective-permute-start.2 = (f32[8,128]{1,0:T(8,128)S(1)}, f32[8,128]{1,0:T(8,128)S(1)}, u32[]{:S(2)}, u32[]{:S(2)}) collective-permute-start(f32[8,128]{1,0:T(8,128)S(1)} %get-tuple-element.24), channel_id=1, source_target_pairs={{0,1},{1,0},{2,3},{3,2},{4,5},{5,4},{6,7},{7,6},{8,9},{9,8},{10,11... | collective-permute-start | bytes 12296 | tf_op jit(solution)/shard_map/ppermute | solution.py:485
  56.5 15.4 %collective-permute-start.8 = (f32[5,3,32,128]{3,2,1,0:T(8,128)S(1)}, f32[5,3,32,128]{3,2,1,0:T(8,128)S(1)}, u32[]{:S(2)}, u32[]{:S(2)}) collective-permute-start(f32[5,3,32,128]{3,2,1,0:T(8,128)S(1)} %get-tuple-element.25), channel_id=1, source_target_pairs={{0,1},{1,2},{2,3},{3,4},{4,5},{5,6},{6,7},{7,8},{8,9},{9,10},{10,1... | collective-permute-start | bytes 737288 | tf_op jit(solution)/shard_map/ppermute | solution.py:509
  56.5 15.4 %collective-permute-start.9 = (f32[5,3,32,128]{3,2,1,0:T(8,128)S(1)}, f32[5,3,32,128]{3,2,1,0:T(8,128)S(1)}, u32[]{:S(2)}, u32[]{:S(2)}) collective-permute-start(f32[5,3,32,128]{3,2,1,0:T(8,128)S(1)} %get-tuple-element.26), channel_id=1, source_target_pairs={{1,0},{2,1},{3,2},{4,3},{5,4},{6,5},{7,6},{8,7},{9,8},{10,9},{11,1... | collective-permute-start | bytes 737288 | tf_op jit(solution)/shard_map/ppermute | solution.py:510
  61.0 5.5 %collective-permute-start.7 = (f32[8,128]{1,0:T(8,128)S(1)}, f32[8,128]{1,0:T(8,128)S(1)}, u32[]{:S(2)}, u32[]{:S(2)}) collective-permute-start(f32[8,128]{1,0:T(8,128)S(1)} %maximum_maximum_fusion.1), channel_id=1, source_target_pairs={{0,12},{1,13},{2,14},{3,15},{4,8},{5,9},{6,10},{7,11},{8,4},{9,5},... | collective-permute-start | bytes 12296 | tf_op jit(solution)/shard_map/ppermute | solution.py:485
  62.3 4.5 %collective-permute-start.6 = (f32[8,128]{1,0:T(8,128)S(1)}, f32[8,128]{1,0:T(8,128)S(1)}, u32[]{:S(2)}, u32[]{:S(2)}) collective-permute-start(f32[8,128]{1,0:T(8,128)S(1)} %maximum_maximum_fusion.1), channel_id=1, source_target_pairs={{0,8},{1,9},{2,10},{3,11},{4,12},{5,13},{6,14},{7,15},{8,0},{9,1},... | collective-permute-start | bytes 12296 | tf_op jit(solution)/shard_map/ppermute | solution.py:485
  62.7 4.3 %collective-permute-start.5 = (f32[8,128]{1,0:T(8,128)S(1)}, f32[8,128]{1,0:T(8,128)S(1)}, u32[]{:S(2)}, u32[]{:S(2)}) collective-permute-start(f32[8,128]{1,0:T(8,128)S(1)} %maximum_maximum_fusion.1), channel_id=1, source_target_pairs={{0,4},{1,5},{2,6},{3,7},{4,0},{5,1},{6,2},{7,3},{8,12},{9,13},{10,... | collective-permute-start | bytes 12296 | tf_op jit(solution)/shard_map/ppermute | solution.py:485

commit v8 on v7

--- a/solution.py
+++ b/solution.py
@@ -474,18 +474,9 @@
     )(*operands)
 
 
-def everyone_max(value, axis, size):
-    reach = 1
-    while reach < size:
-        copies = [value]
-        for times in range(1, 4):
-            turn = reach * times
-            if turn < size:
-                pairs = [(i, i ^ turn) for i in range(size)]
-                copies.append(lax.ppermute(value, axis, pairs))
-        value = functools.reduce(jnp.maximum, copies)
-        reach *= 4
-    return value
+def partners_values(value, axis, size, reach):
+    turns = [reach * times for times in range(1, 4) if reach * times < size]
+    return [lax.ppermute(value, axis, [(i, i ^ turn) for i in range(size)]) for turn in turns]
 
 
 def per_device(blocks, owner_list, slot_list):
@@ -505,7 +496,13 @@
     above = lax.ppermute(low, "gx", down)
     sides = along_planes(state, speed)
     middle, low, high, top = first_stage(state, sides, below, above, speed)
-    second = everyone_max(top, "gx", size)
+    second, reach = top, 1
+    while reach < size:
+        come = partners_values(second, "gx", size, reach)
+        if reach * 4 >= size:
+            low, high, come[0] = lax.optimization_barrier((low, high, come[0]))
+        second = functools.reduce(jnp.maximum, come, second)
+        reach *= 4
     below = lax.ppermute(high, "gx", up)
     above = lax.ppermute(low, "gx", down)
     sides = along_planes(middle, second)

time: 75.3 us -> 81.3 us (1.080)
  waiting for transfers between devices: 28.4 us -> 34.4 us
    ppermute x6, waiting for transfers between devices: 1.59 us -> 7.64 us  [partners_values(): lax.ppermute(value, axis, [(i, i ^ turn) for i in range(size)])]
  transfers between devices with their start and end apart: 11 -> 11, of which waited for: 4 -> 6; matrix products, arithmetic and copies ran while one was open for 1% -> 1% of each run, Pallas kernels for 13% -> 12%
where the time goes in v8:
time: 81.3 us; the launch traced here: 81.1 us
  waiting for transfers between devices  34.4 us (42%)
  starting transfers between devices  24.9 us (31%)
  Pallas kernels  20.9 us (26%)
    all_to_all x1, waiting for transfers between devices, per_device(): come = lax.all_to_all(parts, 'gx', split_axis=0, concat_axis=0, tiled=True)  26.8 us
    ppermute x2, starting transfers between devices, per_device(): above = lax.ppermute(low, 'gx', down)  10.3 us
    pallas_call x2, Pallas kernels, along_planes(): pl.pallas_call(plane_kernel, out_shape=jax.ShapeDtypeStruct(state.shape,...  9.77 us
    ppermute x6, waiting for transfers between devices, partners_values(): lax.ppermute(value, axis, [(i, i ^ turn) for i in range(size)])  7.64 us
    all_to_all x1, starting transfers between devices, per_device(): come = lax.all_to_all(parts, 'gx', split_axis=0, concat_axis=0, tiled=True)  7.37 us
    ppermute x6, starting transfers between devices, partners_values(): lax.ppermute(value, axis, [(i, i ^ turn) for i in range(size)])  6.39 us
    pallas_call x1, Pallas kernels, second_stage(): pl.pallas_call(second_kernel, out_shape=jax.ShapeDtypeStruct((FIELDS, BLO...  3.16 us
    pallas_call x1, Pallas kernels, unpack(): pl.pallas_call(functools.partial(unpack_kernel, size, cap), out_shape=(ja...  2.79 us
  transfers between devices with their start and end apart: 11, of which 6 were waited for; matrix products, arithmetic and copies ran while one was open for 1% of the time, Pallas kernels for 12%

profile of v8, /device:TPU:0, one launch (start us, length us, event | category | flops | bytes accessed | tf_op | source)
XLA Modules:
  0.0 81.1 jit_solution(13253453218559234751)
XLA Ops:
  0.0 2.7 %pack.1 = f32[16,161,1,128]{3,2,1,0:T(1,128)} custom-call(s32[1024]{0:T(1024)} %owner_hbm.1, f32[1280,128]{1,0:T(8,128)} %bitcast.7), custom_call_target="tpu_custom_call" | custom-call | flops 1000000 | bytes 3000000 | tf_op jit(solution)/shard_map/pack/pallas_call | solution.py:110
  2.8 7.4 %all-to-all-start = ((f32[16,161,1,128]{3,2,1,0:T(1,128)}), f32[16,161,1,128]{3,2,1,0:T(1,128)S(1)}, u32[]{:S(2)}, u32[]{:S(2)}) async-start(f32[16,161,1,128]{3,2,1,0:T(1,128)} %pack.1), calls=%async_computation | async-start | bytes 2637824 | tf_op jit(solution)/shard_map/all_to_all | solution.py:492
  10.3 0.3 convert_reduce_fusion
  10.8 0.1 select_reduce_fusion.table
  10.9 26.8 %all-to-all-done = f32[16,161,1,128]{3,2,1,0:T(1,128)S(1)} async-done(((f32[16,161,1,128]{3,2,1,0:T(1,128)}), f32[16,161,1,128]{3,2,1,0:T(1,128)S(1)}, u32[]{:S(2)}, u32[]{:S(2)}) %all-to-all-start) | async-done | bytes 1318944 | tf_op jit(solution)/shard_map/all_to_all | solution.py:492
  37.7 2.8 %unpack.1 = (f32[5,8,32,128]{3,2,1,0:T(8,128)S(1)}, f32[5,3,32,128]{3,2,1,0:T(8,128)S(1)}, f32[5,3,32,128]{3,2,1,0:T(8,128)S(1)}, f32[8,128]{1,0:T(8,128)S(1)}) custom-call(s32[64]{0:T(128)S(1)} %select_reduce_fusion.table, f32[2576,128]{1,0:T(8,128)S(1)} %bitcast.6), custom_call_target="tpu_custom_call" | custom-call | flops 5000000 | bytes 2000000 | tf_op jit(solution)/shard_map/unpack/pallas_call | solution.py:202
  40.5 0.8 %collective-permute-start = (f32[5,3,32,128]{3,2,1,0:T(8,128)S(1)}, f32[5,3,32,128]{3,2,1,0:T(8,128)S(1)}, u32[]{:S(2)}, u32[]{:S(2)}) collective-permute-start(f32[5,3,32,128]{3,2,1,0:T(8,128)S(1)} %get-tuple-element.24), channel_id=1, source_target_pairs={{0,1},{1,2},{2,3},{3,4},{4,5},{5,6},{6,7},{7,8},{8,9},{9,10},{10,1... | collective-permute-start | bytes 737288 | tf_op jit(solution)/shard_map/ppermute | solution.py:495
  41.3 5.9 %collective-permute-start.1 = (f32[5,3,32,128]{3,2,1,0:T(8,128)S(1)}, f32[5,3,32,128]{3,2,1,0:T(8,128)S(1)}, u32[]{:S(2)}, u32[]{:S(2)}) collective-permute-start(f32[5,3,32,128]{3,2,1,0:T(8,128)S(1)} %get-tuple-element.25), channel_id=1, source_target_pairs={{1,0},{2,1},{3,2},{4,3},{5,4},{6,5},{7,6},{8,7},{9,8},{10,9},{11,1... | collective-permute-start | bytes 737288 | tf_op jit(solution)/shard_map/ppermute | solution.py:496
  47.2 4.9 %planes.2.sides = f32[5,8,32,128]{3,2,1,0:T(8,128)S(1)} custom-call(f32[5,8,32,128]{3,2,1,0:T(8,128)S(1)} %get-tuple-element.22.state.start, f32[8,128]{1,0:T(8,128)S(1)} %get-tuple-element.23.speed.first_speed), custom_call_target="tpu_custom_call" | custom-call | flops 20000000 | bytes 1000000 | tf_op jit(solution)/shard_map/planes/pallas_call | solution.py:357
  52.1 2.5 %first_stage.1 = (f32[5,8,32,128]{3,2,1,0:T(8,128)S(1)}, f32[5,3,32,128]{3,2,1,0:T(8,128)S(1)}, f32[5,3,32,128]{3,2,1,0:T(8,128)S(1)}, f32[8,128]{1,0:T(8,128)S(1)}) custom-call(f32[5,8,32,128]{3,2,1,0:T(8,128)S(1)} %get-tuple-element.22.state.start, f32[5,8,32,128]{3,2,1,0:T(8,128)S(1)} %planes.2.sides, f32[5,3,32,128]{3,2,1,0:T(8,128)S(1)} %collective-permute-done.below, ...), custom_call_target="tpu_custom_call" | custom-call | flops 30000000 | bytes 3000000 | tf_op jit(solution)/shard_map/first_stage/pallas_call | solution.py:427
  54.6 0.3 collective-permute-start.4
  54.9 0.5 collective-permute-start.3
  55.4 1.1 %collective-permute-start.2 = (f32[8,128]{1,0:T(8,128)S(1)}, f32[8,128]{1,0:T(8,128)S(1)}, u32[]{:S(2)}, u32[]{:S(2)}) collective-permute-start(f32[8,128]{1,0:T(8,128)S(1)} %get-tuple-element.27), channel_id=1, source_target_pairs={{0,1},{1,0},{2,3},{3,2},{4,5},{5,4},{6,7},{7,6},{8,9},{9,8},{10,11... | collective-permute-start | bytes 12296 | tf_op jit(solution)/shard_map/ppermute | solution.py:479
  56.5 1.2 %collective-permute-done.4 = f32[8,128]{1,0:T(8,128)S(1)} collective-permute-done((f32[8,128]{1,0:T(8,128)S(1)}, f32[8,128]{1,0:T(8,128)S(1)}, u32[]{:S(2)}, u32[]{:S(2)}) %collective-permute-start.4) | collective-permute-done | bytes 4128 | tf_op jit(solution)/shard_map/ppermute | solution.py:479
  57.7 0.8 %collective-permute-done.3 = f32[8,128]{1,0:T(8,128)S(1)} collective-permute-done((f32[8,128]{1,0:T(8,128)S(1)}, f32[8,128]{1,0:T(8,128)S(1)}, u32[]{:S(2)}, u32[]{:S(2)}) %collective-permute-start.3) | collective-permute-done | bytes 4128 | tf_op jit(solution)/shard_map/ppermute | solution.py:479
  58.5 2.8 %collective-permute-start.5 = (f32[8,128]{1,0:T(8,128)S(1)}, f32[8,128]{1,0:T(8,128)S(1)}, u32[]{:S(2)}, u32[]{:S(2)}) collective-permute-start(f32[8,128]{1,0:T(8,128)S(1)} %maximum_maximum_fusion.1), channel_id=1, source_target_pairs={{0,4},{1,5},{2,6},{3,7},{4,0},{5,1},{6,2},{7,3},{8,12},{9,13},{10,... | collective-permute-start | bytes 12296 | tf_op jit(solution)/shard_map/ppermute | solution.py:479
  61.3 1.6 %collective-permute-done.5 = f32[8,128]{1,0:T(8,128)S(1)} collective-permute-done((f32[8,128]{1,0:T(8,128)S(1)}, f32[8,128]{1,0:T(8,128)S(1)}, u32[]{:S(2)}, u32[]{:S(2)}) %collective-permute-start.5) | collective-permute-done | bytes 4128 | tf_op jit(solution)/shard_map/ppermute | solution.py:479
  62.9 4.4 %collective-permute-start.9 = (f32[5,3,32,128]{3,2,1,0:T(8,128)S(1)}, f32[5,3,32,128]{3,2,1,0:T(8,128)S(1)}, u32[]{:S(2)}, u32[]{:S(2)}) collective-permute-start(f32[5,3,32,128]{3,2,1,0:T(8,128)S(1)} %get-tuple-element.32), channel_id=1, source_target_pairs={{1,0},{2,1},{3,2},{4,3},{5,4},{6,5},{7,6},{8,7},{9,8},{10,9},{11,1... | collective-permute-start | bytes 737288 | tf_op jit(solution)/shard_map/ppermute | solution.py:507
  67.3 1.2 %collective-permute-start.7 = (f32[8,128]{1,0:T(8,128)S(1)}, f32[8,128]{1,0:T(8,128)S(1)}, u32[]{:S(2)}, u32[]{:S(2)}) collective-permute-start(f32[8,128]{1,0:T(8,128)S(1)} %maximum_maximum_fusion.1), channel_id=1, source_target_pairs={{0,12},{1,13},{2,14},{3,15},{4,8},{5,9},{6,10},{7,11},{8,4},{9,5},... | collective-permute-start | bytes 12296 | tf_op jit(solution)/shard_map/ppermute | solution.py:479
  68.5 0.5 collective-permute-start.6
  69.0 3.8 %collective-permute-done.7 = f32[8,128]{1,0:T(8,128)S(1)} collective-permute-done((f32[8,128]{1,0:T(8,128)S(1)}, f32[8,128]{1,0:T(8,128)S(1)}, u32[]{:S(2)}, u32[]{:S(2)}) %collective-permute-start.7) | collective-permute-done | bytes 4128 | tf_op jit(solution)/shard_map/ppermute | solution.py:479
  72.8 0.3 collective-permute-done.6
  73.1 4.9 %planes.3.sides = f32[5,8,32,128]{3,2,1,0:T(8,128)S(1)} custom-call(f32[5,8,32,128]{3,2,1,0:T(8,128)S(1)} %get-tuple-element.26.state.middle, f32[8,128]{1,0:T(8,128)S(1)} %maximum_maximum_fusion.speed), custom_call_target="tpu_custom_call" | custom-call | flops 20000000 | bytes 1000000 | tf_op jit(solution)/shard_map/planes/pallas_call | solution.py:357
  78.0 3.2 %second_stage.1 = f32[5,8,32,128]{3,2,1,0:T(8,128)} custom-call(f32[5,8,32,128]{3,2,1,0:T(8,128)S(1)} %get-tuple-element.22.state.start, f32[5,8,32,128]{3,2,1,0:T(8,128)S(1)} %get-tuple-element.26.state.middle, f32[5,8,32,128]{3,2,1,0:T(8,128)S(1)} %planes.3.sides, f32[5,3,32,128]{3,2,1,0:T(8,128)S(1)} %collective-permute-done.8.below, ...), custom_call_target="tpu_custom_call" | custom-call | flops 30000000 | bytes 3000000 | tf_op jit(solution)/shard_map/second_stage/pallas_call | solution.py:466
  (18 shorter events, 0.3 us)
Async XLA Ops:
  2.7 7.4 %copy-start = (s32[1024]{0:T(1024)S(1)}, s32[1024]{0:T(1024)}, u32[]{:S(2)}) copy-start(s32[1024]{0:T(1024)} %owner_hbm.1) | copy-start | bytes 12292
  2.8 7.4 %copy-start.1 = (s32[1024]{0:T(1024)S(1)}, s32[1024]{0:T(1024)}, u32[]{:S(2)}) copy-start(s32[1024]{0:T(1024)} %param.5) | copy-start | bytes 12292
  2.8 34.9 %all-to-all-start = ((f32[16,161,1,128]{3,2,1,0:T(1,128)}), f32[16,161,1,128]{3,2,1,0:T(1,128)S(1)}, u32[]{:S(2)}, u32[]{:S(2)}) async-start(f32[16,161,1,128]{3,2,1,0:T(1,128)} %pack.1), calls=%async_computation | async-start | bytes 2637824 | tf_op jit(solution)/shard_map/all_to_all | solution.py:492
  40.5 11.6 %collective-permute-start = (f32[5,3,32,128]{3,2,1,0:T(8,128)S(1)}, f32[5,3,32,128]{3,2,1,0:T(8,128)S(1)}, u32[]{:S(2)}, u32[]{:S(2)}) collective-permute-start(f32[5,3,32,128]{3,2,1,0:T(8,128)S(1)} %get-tuple-element.24), channel_id=1, source_target_pairs={{0,1},{1,2},{2,3},{3,4},{4,5},{5,6},{6,7},{7,8},{8,9},{9,10},{10,1... | collective-permute-start | bytes 737288 | tf_op jit(solution)/shard_map/ppermute | solution.py:495
  41.3 10.8 %collective-permute-start.1 = (f32[5,3,32,128]{3,2,1,0:T(8,128)S(1)}, f32[5,3,32,128]{3,2,1,0:T(8,128)S(1)}, u32[]{:S(2)}, u32[]{:S(2)}) collective-permute-start(f32[5,3,32,128]{3,2,1,0:T(8,128)S(1)} %get-tuple-element.25), channel_id=1, source_target_pairs={{1,0},{2,1},{3,2},{4,3},{5,4},{6,5},{7,6},{8,7},{9,8},{10,9},{11,1... | collective-permute-start | bytes 737288 | tf_op jit(solution)/shard_map/ppermute | solution.py:496
  54.6 3.1 %collective-permute-start.4 = (f32[8,128]{1,0:T(8,128)S(1)}, f32[8,128]{1,0:T(8,128)S(1)}, u32[]{:S(2)}, u32[]{:S(2)}) collective-permute-start(f32[8,128]{1,0:T(8,128)S(1)} %get-tuple-element.27), channel_id=1, source_target_pairs={{0,3},{1,2},{2,1},{3,0},{4,7},{5,6},{6,5},{7,4},{8,11},{9,10},{10,... | collective-permute-start | bytes 12296 | tf_op jit(solution)/shard_map/ppermute | solution.py:479
  54.9 3.6 %collective-permute-start.3 = (f32[8,128]{1,0:T(8,128)S(1)}, f32[8,128]{1,0:T(8,128)S(1)}, u32[]{:S(2)}, u32[]{:S(2)}) collective-permute-start(f32[8,128]{1,0:T(8,128)S(1)} %get-tuple-element.27), channel_id=1, source_target_pairs={{0,2},{1,3},{2,0},{3,1},{4,6},{5,7},{6,4},{7,5},{8,10},{9,11},{10,... | collective-permute-start | bytes 12296 | tf_op jit(solution)/shard_map/ppermute | solution.py:479
  55.4 3.1 %collective-permute-start.2 = (f32[8,128]{1,0:T(8,128)S(1)}, f32[8,128]{1,0:T(8,128)S(1)}, u32[]{:S(2)}, u32[]{:S(2)}) collective-permute-start(f32[8,128]{1,0:T(8,128)S(1)} %get-tuple-element.27), channel_id=1, source_target_pairs={{0,1},{1,0},{2,3},{3,2},{4,5},{5,4},{6,7},{7,6},{8,9},{9,8},{10,11... | collective-permute-start | bytes 12296 | tf_op jit(solution)/shard_map/ppermute | solution.py:479
  58.5 4.4 %collective-permute-start.5 = (f32[8,128]{1,0:T(8,128)S(1)}, f32[8,128]{1,0:T(8,128)S(1)}, u32[]{:S(2)}, u32[]{:S(2)}) collective-permute-start(f32[8,128]{1,0:T(8,128)S(1)} %maximum_maximum_fusion.1), channel_id=1, source_target_pairs={{0,4},{1,5},{2,6},{3,7},{4,0},{5,1},{6,2},{7,3},{8,12},{9,13},{10,... | collective-permute-start | bytes 12296 | tf_op jit(solution)/shard_map/ppermute | solution.py:479
  62.9 15.1 %collective-permute-start.8 = (f32[5,3,32,128]{3,2,1,0:T(8,128)S(1)}, f32[5,3,32,128]{3,2,1,0:T(8,128)S(1)}, u32[]{:S(2)}, u32[]{:S(2)}) collective-permute-start(f32[5,3,32,128]{3,2,1,0:T(8,128)S(1)} %get-tuple-element.31), channel_id=1, source_target_pairs={{0,1},{1,2},{2,3},{3,4},{4,5},{5,6},{6,7},{7,8},{8,9},{9,10},{10,1... | collective-permute-start | bytes 737288 | tf_op jit(solution)/shard_map/ppermute | solution.py:506
  62.9 15.1 %collective-permute-start.9 = (f32[5,3,32,128]{3,2,1,0:T(8,128)S(1)}, f32[5,3,32,128]{3,2,1,0:T(8,128)S(1)}, u32[]{:S(2)}, u32[]{:S(2)}) collective-permute-start(f32[5,3,32,128]{3,2,1,0:T(8,128)S(1)} %get-tuple-element.32), channel_id=1, source_target_pairs={{1,0},{2,1},{3,2},{4,3},{5,4},{6,5},{7,6},{8,7},{9,8},{10,9},{11,1... | collective-permute-start | bytes 737288 | tf_op jit(solution)/shard_map/ppermute | solution.py:507
  67.3 5.4 %collective-permute-start.7 = (f32[8,128]{1,0:T(8,128)S(1)}, f32[8,128]{1,0:T(8,128)S(1)}, u32[]{:S(2)}, u32[]{:S(2)}) collective-permute-start(f32[8,128]{1,0:T(8,128)S(1)} %maximum_maximum_fusion.1), channel_id=1, source_target_pairs={{0,12},{1,13},{2,14},{3,15},{4,8},{5,9},{6,10},{7,11},{8,4},{9,5},... | collective-permute-start | bytes 12296 | tf_op jit(solution)/shard_map/ppermute | solution.py:479
  68.5 4.5 %collective-permute-start.6 = (f32[8,128]{1,0:T(8,128)S(1)}, f32[8,128]{1,0:T(8,128)S(1)}, u32[]{:S(2)}, u32[]{:S(2)}) collective-permute-start(f32[8,128]{1,0:T(8,128)S(1)} %maximum_maximum_fusion.1), channel_id=1, source_target_pairs={{0,8},{1,9},{2,10},{3,11},{4,12},{5,13},{6,14},{7,15},{8,0},{9,1},... | collective-permute-start | bytes 12296 | tf_op jit(solution)/shard_map/ppermute | solution.py:479

commit v9 on v8

--- a/solution.py
+++ b/solution.py
@@ -159,7 +159,7 @@
     best = come[message - 1 : message, :]
     for source in range(1, size):
         best = jnp.maximum(best, come[(source + 1) * message - 1 : (source + 1) * message, :])
-    speed[...] = jnp.broadcast_to(best, speed.shape)
+    speed[0] = best
     for slot in range(BY * BZ):
         p, q = divmod(slot, BZ)
         where = table[slot]
@@ -205,7 +205,7 @@
             jax.ShapeDtypeStruct((FIELDS, BLOCK, ROWS, LANES), jnp.float32),
             halo,
             halo,
-            jax.ShapeDtypeStruct((8, LANES), jnp.float32),
+            jax.ShapeDtypeStruct((1, 1, LANES), jnp.float32),
         ),
         in_specs=[SMEM, VMEM],
         out_specs=(VMEM,) * 4,
@@ -341,8 +341,15 @@
             yield field, rows, along_y[rows] + along_z
 
 
-def plane_kernel(state, speed, out):
-    half_speed = 0.5 * speed[0:1, :]
+def fastest_of(speeds):
+    best = speeds[0]
+    for source in range(1, speeds.shape[0]):
+        best = jnp.maximum(best, speeds[source])
+    return best
+
+
+def plane_kernel(state, speeds, out):
+    half_speed = 0.5 * fastest_of(speeds)
 
     def one_plane(plane, carry):
         fields = [state[f, plane] for f in range(FIELDS)]
@@ -389,8 +396,8 @@
 
 
 def first_kernel(state, sides, below, above, speed, middle, low, high, top):
-    half_speed = 0.5 * speed[0:1, :]
-    factor = (courant / 6.0) / speed[0:1, :]
+    half_speed = 0.5 * speed[0]
+    factor = (courant / 6.0) / speed[0]
 
     def group(j, best):
         rows = pl.ds(pl.multiple_of(j * 8, 8), 8)
@@ -418,15 +425,17 @@
         return best
 
     best = lax.fori_loop(0, 4, group, jnp.zeros((8, LANES), jnp.float32))
-    top[...] = jnp.full((8, LANES), jnp.max(best), jnp.float32)
-
-
-def first_stage(*operands):
+    most = jnp.full((1, LANES), jnp.max(best), jnp.float32)
+    for dest in range(top.shape[0]):
+        top[dest] = most
+
+
+def first_stage(size, *operands):
     whole = jax.ShapeDtypeStruct((FIELDS, BLOCK, ROWS, LANES), jnp.float32)
     halo = jax.ShapeDtypeStruct((FIELDS, 3, ROWS, LANES), jnp.float32)
     return pl.pallas_call(
         first_kernel,
-        out_shape=(whole, halo, halo, jax.ShapeDtypeStruct((8, LANES), jnp.float32)),
+        out_shape=(whole, halo, halo, jax.ShapeDtypeStruct((size, 1, LANES), jnp.float32)),
         in_specs=[VMEM] * len(operands),
         out_specs=(VMEM,) * 4,
         compiler_params=params(),
@@ -435,9 +444,9 @@
     )(*operands)
 
 
-def second_kernel(start, middle, sides, below, above, first_speed, speed, out):
-    half_speed = 0.5 * speed[0:1, :]
-    factor = (courant / 12.0) / first_speed[0:1, :]
+def second_kernel(start, middle, sides, below, above, first_speed, speeds, out):
+    half_speed = 0.5 * fastest_of(speeds)
+    factor = (courant / 12.0) / first_speed[0]
 
     def group(j, carry):
         rows = pl.ds(pl.multiple_of(j * 8, 8), 8)
@@ -474,11 +483,6 @@
     )(*operands)
 
 
-def partners_values(value, axis, size, reach):
-    turns = [reach * times for times in range(1, 4) if reach * times < size]
-    return [lax.ppermute(value, axis, [(i, i ^ turn) for i in range(size)]) for turn in turns]
-
-
 def per_device(blocks, owner_list, slot_list):
     size = lax.axis_size("gx")
     own = lax.axis_index("gx")
@@ -495,14 +499,9 @@
     below = lax.ppermute(high, "gx", up)
     above = lax.ppermute(low, "gx", down)
     sides = along_planes(state, speed)
-    middle, low, high, top = first_stage(state, sides, below, above, speed)
-    second, reach = top, 1
-    while reach < size:
-        come = partners_values(second, "gx", size, reach)
-        if reach * 4 >= size:
-            low, high, come[0] = lax.optimization_barrier((low, high, come[0]))
-        second = functools.reduce(jnp.maximum, come, second)
-        reach *= 4
+    middle, low, high, top = first_stage(size, state, sides, below, above, speed)
+    second = lax.all_to_all(top, "gx", split_axis=0, concat_axis=0, tiled=True)
+    low, high, second = lax.optimization_barrier((low, high, second))
     below = lax.ppermute(high, "gx", up)
     above = lax.ppermute(low, "gx", down)
     sides = along_planes(middle, second)

time: 81.3 us -> 78.4 us (0.964)
  blocking collectives: 0 us -> 11 us
  waiting for transfers between devices: 34.4 us -> 26.8 us
  starting transfers between devices: 24.9 us -> 18.5 us
    all_to_all x0 -> x1, blocking collectives: none -> 11 us  [per_device(): second = lax.all_to_all(top, 'gx', split_axis=0, concat_axis=0, tiled=True)]
    ppermute x6 -> x0, waiting for transfers between devices: 7.64 us -> none  [partners_values(): lax.ppermute(value, axis, [(i, i ^ turn) for i in range(size)])]
    ppermute x6 -> x0, starting transfers between devices: 6.39 us -> none  [partners_values(): lax.ppermute(value, axis, [(i, i ^ turn) for i in range(size)])]
  transfers between devices with their start and end apart: 11 -> 5, of which waited for: 6 -> 1; matrix products, arithmetic and copies ran while one was open for 1% -> 1% of each run, Pallas kernels for 12% -> 13%
where the time goes in v9:
time: 78.4 us; the launch traced here: 78.1 us
  waiting for transfers between devices  26.8 us (34%)
  Pallas kernels  20.9 us (27%)
  starting transfers between devices  18.5 us (24%)
  blocking collectives  11 us (14%)
    all_to_all x1, waiting for transfers between devices, per_device(): come = lax.all_to_all(parts, 'gx', split_axis=0, concat_axis=0, tiled=True)  26.8 us
    all_to_all x1, blocking collectives, per_device(): second = lax.all_to_all(top, 'gx', split_axis=0, concat_axis=0, tiled=True)  11 us
    ppermute x2, starting transfers between devices, per_device(): above = lax.ppermute(low, 'gx', down)  10.3 us
    pallas_call x2, Pallas kernels, along_planes(): pl.pallas_call(plane_kernel, out_shape=jax.ShapeDtypeStruct(state.shape,...  9.77 us
    all_to_all x1, starting transfers between devices, per_device(): come = lax.all_to_all(parts, 'gx', split_axis=0, concat_axis=0, tiled=True)  7.37 us
    pallas_call x1, Pallas kernels, second_stage(): pl.pallas_call(second_kernel, out_shape=jax.ShapeDtypeStruct((FIELDS, BLO...  3.17 us
    pallas_call x1, Pallas kernels, unpack(): pl.pallas_call(functools.partial(unpack_kernel, size, cap), out_shape=(ja...  2.79 us
    pallas_call x1, Pallas kernels, pack(): pl.pallas_call(functools.partial(pack_kernel, size, cap, per_dev), out_sh...  2.74 us
  transfers between devices with their start and end apart: 5, of which 1 were waited for; matrix products, arithmetic and copies ran while one was open for 1% of the time, Pallas kernels for 13%

profile of v9, /device:TPU:0, one launch (start us, length us, event | category | flops | bytes accessed | tf_op | source)
XLA Modules:
  0.0 78.1 jit_solution(10364286552700626511)
XLA Ops:
  0.0 2.7 %pack.1 = f32[16,161,1,128]{3,2,1,0:T(1,128)} custom-call(s32[1024]{0:T(1024)} %owner_hbm.1, f32[1280,128]{1,0:T(8,128)} %bitcast.7), custom_call_target="tpu_custom_call" | custom-call | flops 1000000 | bytes 3000000 | tf_op jit(solution)/shard_map/pack/pallas_call | solution.py:110
  2.8 0.0 copy-start
  2.8 0.0 copy-start.1
  2.8 7.4 %all-to-all-start = ((f32[16,161,1,128]{3,2,1,0:T(1,128)}), f32[16,161,1,128]{3,2,1,0:T(1,128)S(1)}, u32[]{:S(2)}, u32[]{:S(2)}) async-start(f32[16,161,1,128]{3,2,1,0:T(1,128)} %pack.1), calls=%async_computation | async-start | bytes 2637824 | tf_op jit(solution)/shard_map/all_to_all | solution.py:496
  10.2 0.1 eq.33
  10.3 0.3 convert_reduce_fusion
  10.6 0.1 broadcast_add_fusion
  10.7 0.1 add.17
  10.8 0.1 select_reduce_fusion.table
  10.9 26.8 %all-to-all-done = f32[16,161,1,128]{3,2,1,0:T(1,128)S(1)} async-done(((f32[16,161,1,128]{3,2,1,0:T(1,128)}), f32[16,161,1,128]{3,2,1,0:T(1,128)S(1)}, u32[]{:S(2)}, u32[]{:S(2)}) %all-to-all-start) | async-done | bytes 1318944 | tf_op jit(solution)/shard_map/all_to_all | solution.py:496
  37.7 2.8 %unpack.1 = (f32[5,8,32,128]{3,2,1,0:T(8,128)S(1)}, f32[5,3,32,128]{3,2,1,0:T(8,128)S(1)}, f32[5,3,32,128]{3,2,1,0:T(8,128)S(1)}, f32[1,1,128]{2,1,0:T(1,128)S(1)}) custom-call(s32[64]{0:T(128)S(1)} %select_reduce_fusion.table, f32[2576,128]{1,0:T(8,128)S(1)} %bitcast.6), custom_call_target="tpu_custom_call" | custom-call | flops 5000000 | bytes 2000000 | tf_op jit(solution)/shard_map/unpack/pallas_call | solution.py:202
  40.5 0.8 %collective-permute-start = (f32[5,3,32,128]{3,2,1,0:T(8,128)S(1)}, f32[5,3,32,128]{3,2,1,0:T(8,128)S(1)}, u32[]{:S(2)}, u32[]{:S(2)}) collective-permute-start(f32[5,3,32,128]{3,2,1,0:T(8,128)S(1)} %get-tuple-element.24), channel_id=1, source_target_pairs={{0,1},{1,2},{2,3},{3,4},{4,5},{5,6},{6,7},{7,8},{8,9},{9,10},{10,1... | collective-permute-start | bytes 737288 | tf_op jit(solution)/shard_map/ppermute | solution.py:499
  41.3 5.9 %collective-permute-start.1 = (f32[5,3,32,128]{3,2,1,0:T(8,128)S(1)}, f32[5,3,32,128]{3,2,1,0:T(8,128)S(1)}, u32[]{:S(2)}, u32[]{:S(2)}) collective-permute-start(f32[5,3,32,128]{3,2,1,0:T(8,128)S(1)} %get-tuple-element.25), channel_id=1, source_target_pairs={{1,0},{2,1},{3,2},{4,3},{5,4},{6,5},{7,6},{8,7},{9,8},{10,9},{11,1... | collective-permute-start | bytes 737288 | tf_op jit(solution)/shard_map/ppermute | solution.py:500
  47.2 4.9 %planes.2.sides = f32[5,8,32,128]{3,2,1,0:T(8,128)S(1)} custom-call(f32[5,8,32,128]{3,2,1,0:T(8,128)S(1)} %get-tuple-element.22.state.start, f32[1,1,128]{2,1,0:T(1,128)S(1)} %get-tuple-element.23.speeds.speed.first_speed), custom_call_target="tpu_custom_call" | custom-call | flops 20000000 | bytes 1000000 | tf_op jit(solution)/shard_map/planes/pallas_call | solution.py:364
  52.1 0.0 collective-permute-done.below
  52.1 0.0 collective-permute-done.1.above
  52.1 2.5 %first_stage.1 = (f32[5,8,32,128]{3,2,1,0:T(8,128)S(1)}, f32[5,3,32,128]{3,2,1,0:T(8,128)S(1)}, f32[5,3,32,128]{3,2,1,0:T(8,128)S(1)}, f32[16,1,128]{2,1,0:T(1,128)S(1)}) custom-call(f32[5,8,32,128]{3,2,1,0:T(8,128)S(1)} %get-tuple-element.22.state.start, f32[5,8,32,128]{3,2,1,0:T(8,128)S(1)} %planes.2.sides, ...), custom_call_target="tpu_custom_call" | custom-call | flops 30000000 | bytes 3000000 | tf_op jit(solution)/shard_map/first_stage/pallas_call | solution.py:436
  54.6 11.0 %all_to_all.10.speeds = f32[16,1,128]{2,1,0:T(1,128)S(1)} all-to-all(f32[16,1,128]{2,1,0:T(1,128)S(1)} %get-tuple-element.29), channel_id=1, replica_groups=mesh['runs'=2,'gx'=16] {'gx'}, dimensions={0} | all-to-all | bytes 16384 | tf_op jit(solution)/shard_map/all_to_all | solution.py:503
  65.6 0.0 collective-permute-start.2
  65.6 4.4 %collective-permute-start.3 = (f32[5,3,32,128]{3,2,1,0:T(8,128)S(1)}, f32[5,3,32,128]{3,2,1,0:T(8,128)S(1)}, u32[]{:S(2)}, u32[]{:S(2)}) collective-permute-start(f32[5,3,32,128]{3,2,1,0:T(8,128)S(1)} %get-tuple-element.32), channel_id=1, source_target_pairs={{1,0},{2,1},{3,2},{4,3},{5,4},{6,5},{7,6},{8,7},{9,8},{10,9},{11,1... | collective-permute-start | bytes 737288 | tf_op jit(solution)/shard_map/ppermute | solution.py:506
  70.0 4.9 %planes.3.sides = f32[5,8,32,128]{3,2,1,0:T(8,128)S(1)} custom-call(f32[5,8,32,128]{3,2,1,0:T(8,128)S(1)} %get-tuple-element.26.state.middle, f32[16,1,128]{2,1,0:T(1,128)S(1)} %all_to_all.10.speeds), custom_call_target="tpu_custom_call" | custom-call | flops 20000000 | bytes 1000000 | tf_op jit(solution)/shard_map/planes/pallas_call | solution.py:364
  74.9 0.0 collective-permute-done.2.below
  74.9 0.0 collective-permute-done.3.above
  74.9 3.2 %second_stage.1 = f32[5,8,32,128]{3,2,1,0:T(8,128)} custom-call(f32[5,8,32,128]{3,2,1,0:T(8,128)S(1)} %get-tuple-element.22.state.start, f32[5,8,32,128]{3,2,1,0:T(8,128)S(1)} %get-tuple-element.26.state.middle, f32[5,8,32,128]{3,2,1,0:T(8,128)S(1)} %planes.3.sides, f32[5,3,32,128]{3,2,1,0:T(8,128)S(1)} %collective-permute-done.2.below, ...), custom_call_target="tpu_custom_call" | custom-call | flops 30000000 | bytes 3000000 | tf_op jit(solution)/shard_map/second_stage/pallas_call | solution.py:475
  (5 shorter events, 0.0 us)
Async XLA Ops:
  2.8 7.4 %copy-start = (s32[1024]{0:T(1024)S(1)}, s32[1024]{0:T(1024)}, u32[]{:S(2)}) copy-start(s32[1024]{0:T(1024)} %owner_hbm.1) | copy-start | bytes 12292
  2.8 7.4 %copy-start.1 = (s32[1024]{0:T(1024)S(1)}, s32[1024]{0:T(1024)}, u32[]{:S(2)}) copy-start(s32[1024]{0:T(1024)} %param.5) | copy-start | bytes 12292
  2.8 34.9 %all-to-all-start = ((f32[16,161,1,128]{3,2,1,0:T(1,128)}), f32[16,161,1,128]{3,2,1,0:T(1,128)S(1)}, u32[]{:S(2)}, u32[]{:S(2)}) async-start(f32[16,161,1,128]{3,2,1,0:T(1,128)} %pack.1), calls=%async_computation | async-start | bytes 2637824 | tf_op jit(solution)/shard_map/all_to_all | solution.py:496
  40.5 11.6 %collective-permute-start = (f32[5,3,32,128]{3,2,1,0:T(8,128)S(1)}, f32[5,3,32,128]{3,2,1,0:T(8,128)S(1)}, u32[]{:S(2)}, u32[]{:S(2)}) collective-permute-start(f32[5,3,32,128]{3,2,1,0:T(8,128)S(1)} %get-tuple-element.24), channel_id=1, source_target_pairs={{0,1},{1,2},{2,3},{3,4},{4,5},{5,6},{6,7},{7,8},{8,9},{9,10},{10,1... | collective-permute-start | bytes 737288 | tf_op jit(solution)/shard_map/ppermute | solution.py:499
  41.3 10.8 %collective-permute-start.1 = (f32[5,3,32,128]{3,2,1,0:T(8,128)S(1)}, f32[5,3,32,128]{3,2,1,0:T(8,128)S(1)}, u32[]{:S(2)}, u32[]{:S(2)}) collective-permute-start(f32[5,3,32,128]{3,2,1,0:T(8,128)S(1)} %get-tuple-element.25), channel_id=1, source_target_pairs={{1,0},{2,1},{3,2},{4,3},{5,4},{6,5},{7,6},{8,7},{9,8},{10,9},{11,1... | collective-permute-start | bytes 737288 | tf_op jit(solution)/shard_map/ppermute | solution.py:500
  65.6 9.3 %collective-permute-start.2 = (f32[5,3,32,128]{3,2,1,0:T(8,128)S(1)}, f32[5,3,32,128]{3,2,1,0:T(8,128)S(1)}, u32[]{:S(2)}, u32[]{:S(2)}) collective-permute-start(f32[5,3,32,128]{3,2,1,0:T(8,128)S(1)} %get-tuple-element.31), channel_id=1, source_target_pairs={{0,1},{1,2},{2,3},{3,4},{4,5},{5,6},{6,7},{7,8},{8,9},{9,10},{10,1... | collective-permute-start | bytes 737288 | tf_op jit(solution)/shard_map/ppermute | solution.py:505
  65.6 9.4 %collective-permute-start.3 = (f32[5,3,32,128]{3,2,1,0:T(8,128)S(1)}, f32[5,3,32,128]{3,2,1,0:T(8,128)S(1)}, u32[]{:S(2)}, u32[]{:S(2)}) collective-permute-start(f32[5,3,32,128]{3,2,1,0:T(8,128)S(1)} %get-tuple-element.32), channel_id=1, source_target_pairs={{1,0},{2,1},{3,2},{4,3},{5,4},{6,5},{7,6},{8,7},{9,8},{10,9},{11,1... | collective-permute-start | bytes 737288 | tf_op jit(solution)/shard_map/ppermute | solution.py:506

commit v10 on v7

--- a/solution.py
+++ b/solution.py
@@ -476,7 +476,9 @@
 
 def everyone_max(value, axis, size):
     reach = 1
-    while reach < size:
+    while reach * 4 < size:
+        reach *= 4
+    while reach:
         copies = [value]
         for times in range(1, 4):
             turn = reach * times
@@ -484,7 +486,7 @@
                 pairs = [(i, i ^ turn) for i in range(size)]
                 copies.append(lax.ppermute(value, axis, pairs))
         value = functools.reduce(jnp.maximum, copies)
-        reach *= 4
+        reach //= 4
     return value
 
 

time: 75.3 us -> 75.8 us (level)
  transfers between devices with their start and end apart: 11 -> 11, of which waited for: 4 -> 3; matrix products, arithmetic and copies ran while one was open for 1% -> 1% of each run, Pallas kernels for 13% -> 13%
where the time goes in v10:
time: 75.8 us; the launch traced here: 75.6 us
  waiting for transfers between devices  28.9 us (38%)
  starting transfers between devices  24.9 us (33%)
  Pallas kernels  20.9 us (28%)
    all_to_all x1, waiting for transfers between devices, per_device(): come = lax.all_to_all(parts, 'gx', split_axis=0, concat_axis=0, tiled=True)  26.8 us
    ppermute x2, starting transfers between devices, per_device(): above = lax.ppermute(low, 'gx', down)  10.3 us
    pallas_call x2, Pallas kernels, along_planes(): pl.pallas_call(plane_kernel, out_shape=jax.ShapeDtypeStruct(state.shape,...  9.77 us
    all_to_all x1, starting transfers between devices, per_device(): come = lax.all_to_all(parts, 'gx', split_axis=0, concat_axis=0, tiled=True)  7.37 us
    ppermute x6, starting transfers between devices, everyone_max(): copies.append(lax.ppermute(value, axis, pairs))  6.36 us
    pallas_call x1, Pallas kernels, second_stage(): pl.pallas_call(second_kernel, out_shape=jax.ShapeDtypeStruct((FIELDS, BLO...  3.16 us
    pallas_call x1, Pallas kernels, unpack(): pl.pallas_call(functools.partial(unpack_kernel, size, cap), out_shape=(ja...  2.79 us
    pallas_call x1, Pallas kernels, pack(): pl.pallas_call(functools.partial(pack_kernel, size, cap, per_dev), out_sh...  2.74 us
  transfers between devices with their start and end apart: 11, of which 3 were waited for; matrix products, arithmetic and copies ran while one was open for 1% of the time, Pallas kernels for 13%

profile of v10, /device:TPU:0, one launch (start us, length us, event | category | flops | bytes accessed | tf_op | source)
XLA Modules:
  0.0 75.6 jit_solution(4913593127094164692)
XLA Ops:
  0.0 2.7 %pack.1 = f32[16,161,1,128]{3,2,1,0:T(1,128)} custom-call(s32[1024]{0:T(1024)} %owner_hbm.1, f32[1280,128]{1,0:T(8,128)} %bitcast.7), custom_call_target="tpu_custom_call" | custom-call | flops 1000000 | bytes 3000000 | tf_op jit(solution)/shard_map/pack/pallas_call | solution.py:110
  2.8 7.4 %all-to-all-start = ((f32[16,161,1,128]{3,2,1,0:T(1,128)}), f32[16,161,1,128]{3,2,1,0:T(1,128)S(1)}, u32[]{:S(2)}, u32[]{:S(2)}) async-start(f32[16,161,1,128]{3,2,1,0:T(1,128)} %pack.1), calls=%async_computation | async-start | bytes 2637824 | tf_op jit(solution)/shard_map/all_to_all | solution.py:503
  10.2 0.1 eq.33
  10.3 0.3 convert_reduce_fusion
  10.6 0.1 broadcast_add_fusion
  10.7 0.1 add.17
  10.8 0.1 select_reduce_fusion.table
  10.9 26.8 %all-to-all-done = f32[16,161,1,128]{3,2,1,0:T(1,128)S(1)} async-done(((f32[16,161,1,128]{3,2,1,0:T(1,128)}), f32[16,161,1,128]{3,2,1,0:T(1,128)S(1)}, u32[]{:S(2)}, u32[]{:S(2)}) %all-to-all-start) | async-done | bytes 1318944 | tf_op jit(solution)/shard_map/all_to_all | solution.py:503
  37.7 2.8 %unpack.1 = (f32[5,8,32,128]{3,2,1,0:T(8,128)S(1)}, f32[5,3,32,128]{3,2,1,0:T(8,128)S(1)}, f32[5,3,32,128]{3,2,1,0:T(8,128)S(1)}, f32[8,128]{1,0:T(8,128)S(1)}) custom-call(s32[64]{0:T(128)S(1)} %select_reduce_fusion.table, f32[2576,128]{1,0:T(8,128)S(1)} %bitcast.6), custom_call_target="tpu_custom_call" | custom-call | flops 5000000 | bytes 2000000 | tf_op jit(solution)/shard_map/unpack/pallas_call | solution.py:202
  40.5 0.8 %collective-permute-start = (f32[5,3,32,128]{3,2,1,0:T(8,128)S(1)}, f32[5,3,32,128]{3,2,1,0:T(8,128)S(1)}, u32[]{:S(2)}, u32[]{:S(2)}) collective-permute-start(f32[5,3,32,128]{3,2,1,0:T(8,128)S(1)} %get-tuple-element.21), channel_id=1, source_target_pairs={{0,1},{1,2},{2,3},{3,4},{4,5},{5,6},{6,7},{7,8},{8,9},{9,10},{10,1... | collective-permute-start | bytes 737288 | tf_op jit(solution)/shard_map/ppermute | solution.py:506
  41.3 5.9 %collective-permute-start.1 = (f32[5,3,32,128]{3,2,1,0:T(8,128)S(1)}, f32[5,3,32,128]{3,2,1,0:T(8,128)S(1)}, u32[]{:S(2)}, u32[]{:S(2)}) collective-permute-start(f32[5,3,32,128]{3,2,1,0:T(8,128)S(1)} %get-tuple-element.22), channel_id=1, source_target_pairs={{1,0},{2,1},{3,2},{4,3},{5,4},{6,5},{7,6},{8,7},{9,8},{10,9},{11,1... | collective-permute-start | bytes 737288 | tf_op jit(solution)/shard_map/ppermute | solution.py:507
  47.2 4.9 %planes.2.sides = f32[5,8,32,128]{3,2,1,0:T(8,128)S(1)} custom-call(f32[5,8,32,128]{3,2,1,0:T(8,128)S(1)} %get-tuple-element.19.state.start, f32[8,128]{1,0:T(8,128)S(1)} %get-tuple-element.20.speed.first_speed), custom_call_target="tpu_custom_call" | custom-call | flops 20000000 | bytes 1000000 | tf_op jit(solution)/shard_map/planes/pallas_call | solution.py:357
  52.1 2.5 %first_stage.1 = (f32[5,8,32,128]{3,2,1,0:T(8,128)S(1)}, f32[5,3,32,128]{3,2,1,0:T(8,128)S(1)}, f32[5,3,32,128]{3,2,1,0:T(8,128)S(1)}, f32[8,128]{1,0:T(8,128)S(1)}) custom-call(f32[5,8,32,128]{3,2,1,0:T(8,128)S(1)} %get-tuple-element.19.state.start, f32[5,8,32,128]{3,2,1,0:T(8,128)S(1)} %planes.2.sides, f32[5,3,32,128]{3,2,1,0:T(8,128)S(1)} %collective-permute-done.below, ...), custom_call_target="tpu_custom_call" | custom-call | flops 30000000 | bytes 3000000 | tf_op jit(solution)/shard_map/first_stage/pallas_call | solution.py:427
  54.6 0.1 collective-permute-start.4
  54.6 2.3 %collective-permute-start.3 = (f32[8,128]{1,0:T(8,128)S(1)}, f32[8,128]{1,0:T(8,128)S(1)}, u32[]{:S(2)}, u32[]{:S(2)}) collective-permute-start(f32[8,128]{1,0:T(8,128)S(1)} %get-tuple-element.24), channel_id=1, source_target_pairs={{0,8},{1,9},{2,10},{3,11},{4,12},{5,13},{6,14},{7,15},{8,0},{9,1},... | collective-permute-start | bytes 12296 | tf_op jit(solution)/shard_map/ppermute | solution.py:487
  57.0 2.1 %collective-permute-start.2 = (f32[8,128]{1,0:T(8,128)S(1)}, f32[8,128]{1,0:T(8,128)S(1)}, u32[]{:S(2)}, u32[]{:S(2)}) collective-permute-start(f32[8,128]{1,0:T(8,128)S(1)} %get-tuple-element.24), channel_id=1, source_target_pairs={{0,4},{1,5},{2,6},{3,7},{4,0},{5,1},{6,2},{7,3},{8,12},{9,13},{10,... | collective-permute-start | bytes 12296 | tf_op jit(solution)/shard_map/ppermute | solution.py:487
  59.0 4.4 %collective-permute-start.9 = (f32[5,3,32,128]{3,2,1,0:T(8,128)S(1)}, f32[5,3,32,128]{3,2,1,0:T(8,128)S(1)}, u32[]{:S(2)}, u32[]{:S(2)}) collective-permute-start(f32[5,3,32,128]{3,2,1,0:T(8,128)S(1)} %get-tuple-element.26), channel_id=1, source_target_pairs={{1,0},{2,1},{3,2},{4,3},{5,4},{6,5},{7,6},{8,7},{9,8},{10,9},{11,1... | collective-permute-start | bytes 737288 | tf_op jit(solution)/shard_map/ppermute | solution.py:512
  63.5 0.1 collective-permute-start.7
  63.6 0.1 collective-permute-start.6
  63.6 1.8 %collective-permute-start.5 = (f32[8,128]{1,0:T(8,128)S(1)}, f32[8,128]{1,0:T(8,128)S(1)}, u32[]{:S(2)}, u32[]{:S(2)}) collective-permute-start(f32[8,128]{1,0:T(8,128)S(1)} %maximum_maximum_fusion.1), channel_id=1, source_target_pairs={{0,1},{1,0},{2,3},{3,2},{4,5},{5,4},{6,7},{7,6},{8,9},{9,8},{10,11... | collective-permute-start | bytes 12296 | tf_op jit(solution)/shard_map/ppermute | solution.py:487
  65.4 1.6 %collective-permute-done.7 = f32[8,128]{1,0:T(8,128)S(1)} collective-permute-done((f32[8,128]{1,0:T(8,128)S(1)}, f32[8,128]{1,0:T(8,128)S(1)}, u32[]{:S(2)}, u32[]{:S(2)}) %collective-permute-start.7) | collective-permute-done | bytes 4128 | tf_op jit(solution)/shard_map/ppermute | solution.py:487
  67.0 0.5 collective-permute-done.6
  67.5 4.9 %planes.3.sides = f32[5,8,32,128]{3,2,1,0:T(8,128)S(1)} custom-call(f32[5,8,32,128]{3,2,1,0:T(8,128)S(1)} %get-tuple-element.23.state.middle, f32[8,128]{1,0:T(8,128)S(1)} %maximum_maximum_fusion.speed), custom_call_target="tpu_custom_call" | custom-call | flops 20000000 | bytes 1000000 | tf_op jit(solution)/shard_map/planes/pallas_call | solution.py:357
  72.4 3.2 %second_stage.1 = f32[5,8,32,128]{3,2,1,0:T(8,128)} custom-call(f32[5,8,32,128]{3,2,1,0:T(8,128)S(1)} %get-tuple-element.19.state.start, f32[5,8,32,128]{3,2,1,0:T(8,128)S(1)} %get-tuple-element.23.state.middle, f32[5,8,32,128]{3,2,1,0:T(8,128)S(1)} %planes.3.sides, f32[5,3,32,128]{3,2,1,0:T(8,128)S(1)} %collective-permute-done.8.below, ...), custom_call_target="tpu_custom_call" | custom-call | flops 30000000 | bytes 3000000 | tf_op jit(solution)/shard_map/second_stage/pallas_call | solution.py:466
  (18 shorter events, 0.1 us)
Async XLA Ops:
  2.7 7.4 %copy-start = (s32[1024]{0:T(1024)S(1)}, s32[1024]{0:T(1024)}, u32[]{:S(2)}) copy-start(s32[1024]{0:T(1024)} %owner_hbm.1) | copy-start | bytes 12292
  2.8 7.4 %copy-start.1 = (s32[1024]{0:T(1024)S(1)}, s32[1024]{0:T(1024)}, u32[]{:S(2)}) copy-start(s32[1024]{0:T(1024)} %param.5) | copy-start | bytes 12292
  2.8 34.9 %all-to-all-start = ((f32[16,161,1,128]{3,2,1,0:T(1,128)}), f32[16,161,1,128]{3,2,1,0:T(1,128)S(1)}, u32[]{:S(2)}, u32[]{:S(2)}) async-start(f32[16,161,1,128]{3,2,1,0:T(1,128)} %pack.1), calls=%async_computation | async-start | bytes 2637824 | tf_op jit(solution)/shard_map/all_to_all | solution.py:503
  40.5 11.6 %collective-permute-start = (f32[5,3,32,128]{3,2,1,0:T(8,128)S(1)}, f32[5,3,32,128]{3,2,1,0:T(8,128)S(1)}, u32[]{:S(2)}, u32[]{:S(2)}) collective-permute-start(f32[5,3,32,128]{3,2,1,0:T(8,128)S(1)} %get-tuple-element.21), channel_id=1, source_target_pairs={{0,1},{1,2},{2,3},{3,4},{4,5},{5,6},{6,7},{7,8},{8,9},{9,10},{10,1... | collective-permute-start | bytes 737288 | tf_op jit(solution)/shard_map/ppermute | solution.py:506
  41.3 10.8 %collective-permute-start.1 = (f32[5,3,32,128]{3,2,1,0:T(8,128)S(1)}, f32[5,3,32,128]{3,2,1,0:T(8,128)S(1)}, u32[]{:S(2)}, u32[]{:S(2)}) collective-permute-start(f32[5,3,32,128]{3,2,1,0:T(8,128)S(1)} %get-tuple-element.22), channel_id=1, source_target_pairs={{1,0},{2,1},{3,2},{4,3},{5,4},{6,5},{7,6},{8,7},{9,8},{10,9},{11,1... | collective-permute-start | bytes 737288 | tf_op jit(solution)/shard_map/ppermute | solution.py:507
  54.6 8.9 %collective-permute-start.4 = (f32[8,128]{1,0:T(8,128)S(1)}, f32[8,128]{1,0:T(8,128)S(1)}, u32[]{:S(2)}, u32[]{:S(2)}) collective-permute-start(f32[8,128]{1,0:T(8,128)S(1)} %get-tuple-element.24), channel_id=1, source_target_pairs={{0,12},{1,13},{2,14},{3,15},{4,8},{5,9},{6,10},{7,11},{8,4},{9,5},... | collective-permute-start | bytes 12296 | tf_op jit(solution)/shard_map/ppermute | solution.py:487
  54.6 8.8 %collective-permute-start.3 = (f32[8,128]{1,0:T(8,128)S(1)}, f32[8,128]{1,0:T(8,128)S(1)}, u32[]{:S(2)}, u32[]{:S(2)}) collective-permute-start(f32[8,128]{1,0:T(8,128)S(1)} %get-tuple-element.24), channel_id=1, source_target_pairs={{0,8},{1,9},{2,10},{3,11},{4,12},{5,13},{6,14},{7,15},{8,0},{9,1},... | collective-permute-start | bytes 12296 | tf_op jit(solution)/shard_map/ppermute | solution.py:487
  57.0 6.5 %collective-permute-start.2 = (f32[8,128]{1,0:T(8,128)S(1)}, f32[8,128]{1,0:T(8,128)S(1)}, u32[]{:S(2)}, u32[]{:S(2)}) collective-permute-start(f32[8,128]{1,0:T(8,128)S(1)} %get-tuple-element.24), channel_id=1, source_target_pairs={{0,4},{1,5},{2,6},{3,7},{4,0},{5,1},{6,2},{7,3},{8,12},{9,13},{10,... | collective-permute-start | bytes 12296 | tf_op jit(solution)/shard_map/ppermute | solution.py:487
  59.0 13.4 %collective-permute-start.8 = (f32[5,3,32,128]{3,2,1,0:T(8,128)S(1)}, f32[5,3,32,128]{3,2,1,0:T(8,128)S(1)}, u32[]{:S(2)}, u32[]{:S(2)}) collective-permute-start(f32[5,3,32,128]{3,2,1,0:T(8,128)S(1)} %get-tuple-element.25), channel_id=1, source_target_pairs={{0,1},{1,2},{2,3},{3,4},{4,5},{5,6},{6,7},{7,8},{8,9},{9,10},{10,1... | collective-permute-start | bytes 737288 | tf_op jit(solution)/shard_map/ppermute | solution.py:511
  59.0 13.4 %collective-permute-start.9 = (f32[5,3,32,128]{3,2,1,0:T(8,128)S(1)}, f32[5,3,32,128]{3,2,1,0:T(8,128)S(1)}, u32[]{:S(2)}, u32[]{:S(2)}) collective-permute-start(f32[5,3,32,128]{3,2,1,0:T(8,128)S(1)} %get-tuple-element.26), channel_id=1, source_target_pairs={{1,0},{2,1},{3,2},{4,3},{5,4},{6,5},{7,6},{8,7},{9,8},{10,9},{11,1... | collective-permute-start | bytes 737288 | tf_op jit(solution)/shard_map/ppermute | solution.py:512
  63.5 3.5 %collective-permute-start.7 = (f32[8,128]{1,0:T(8,128)S(1)}, f32[8,128]{1,0:T(8,128)S(1)}, u32[]{:S(2)}, u32[]{:S(2)}) collective-permute-start(f32[8,128]{1,0:T(8,128)S(1)} %maximum_maximum_fusion.1), channel_id=1, source_target_pairs={{0,3},{1,2},{2,1},{3,0},{4,7},{5,6},{6,5},{7,4},{8,11},{9,10},{10,... | collective-permute-start | bytes 12296 | tf_op jit(solution)/shard_map/ppermute | solution.py:487
  63.6 3.9 %collective-permute-start.6 = (f32[8,128]{1,0:T(8,128)S(1)}, f32[8,128]{1,0:T(8,128)S(1)}, u32[]{:S(2)}, u32[]{:S(2)}) collective-permute-start(f32[8,128]{1,0:T(8,128)S(1)} %maximum_maximum_fusion.1), channel_id=1, source_target_pairs={{0,2},{1,3},{2,0},{3,1},{4,6},{5,7},{6,4},{7,5},{8,10},{9,11},{10,... | collective-permute-start | bytes 12296 | tf_op jit(solution)/shard_map/ppermute | solution.py:487
  63.6 3.8 %collective-permute-start.5 = (f32[8,128]{1,0:T(8,128)S(1)}, f32[8,128]{1,0:T(8,128)S(1)}, u32[]{:S(2)}, u32[]{:S(2)}) collective-permute-start(f32[8,128]{1,0:T(8,128)S(1)} %maximum_maximum_fusion.1), channel_id=1, source_target_pairs={{0,1},{1,0},{2,3},{3,2},{4,5},{5,4},{6,7},{7,6},{8,9},{9,8},{10,11... | collective-permute-start | bytes 12296 | tf_op jit(solution)/shard_map/ppermute | solution.py:487

commit v11 on v10

--- a/solution.py
+++ b/solution.py
@@ -228,18 +228,6 @@
     return jnp.concatenate([x[16:], pltpu.roll(x[:8], 7, 0), pltpu.roll(x[8:16], 7, 0)], axis=0)
 
 
-def z_up(x):
-    return pltpu.roll(x, LANES - 1, 1)
-
-
-def z_up_two(x):
-    return pltpu.roll(x, LANES - 2, 1)
-
-
-def z_down(x):
-    return pltpu.roll(x, 1, 1)
-
-
 def inverse(x):
     return 1.0 / x
 
@@ -278,6 +266,35 @@
     _, curve, left, centre, right, jump = side(minus)
     face = face + (upwind_term(up_two(right), up(centre), left, up(jump), jump) - curve)
     return face - down(face)
+
+
+def ring_divergence(half_flux, scaled):
+    count = len(half_flux)
+
+    def up(values):
+        return values[1:] + [pltpu.roll(values[0], 7, 0)]
+
+    def down(values):
+        return [pltpu.roll(values[-1], 1, 0)] + values[:-1]
+
+    def side(values):
+        after = [above - value for above, value in zip(up(values), values)]
+        parts = [smoothness(before, step) for before, step in zip(down(after), after)]
+        curve, left, centre, right = (list(part) for part in zip(*parts))
+        jump = [above - value for above, value in zip(up(curve), curve)]
+        return curve, left, centre, right, jump
+
+    curve, left, centre, right, jump = side([a + b for a, b in zip(half_flux, scaled)])
+    terms = zip(down(left), centre, up(right), down(jump), jump)
+    face = [
+        6.0 * (here + above) - bend - upwind_term(*term)
+        for here, above, bend, term in zip(half_flux, up(half_flux), curve, terms)
+    ]
+    curve, left, centre, right, jump = side([a - b for a, b in zip(half_flux, scaled)])
+    terms = zip(up(right), centre, down(left), jump, down(jump))
+    other = [upwind_term(*term) - bend for bend, term in zip(curve, terms)]
+    face = [one + two for one, two in zip(face, up(other))]
+    return [here - below for here, below in zip(face, down(face))]
 
 
 def open_divergence(half_flux, scaled):
@@ -327,30 +344,44 @@
     return flux + 0.5 * pressure if field == 1 + direction else flux
 
 
-def side_planes(fields, half_speed):
-    vel, pressure = half_velocities(fields)
-    for field in range(FIELDS):
-        scaled = half_speed * fields[field]
-        along_y = periodic_divergence(
-            half_flux(fields, field, 1, vel[1], pressure), scaled, y_up, y_up_two, y_down
-        )
-        flux = half_flux(fields, field, 2, vel[2], pressure)
-        for first in range(0, ROWS, 8):
-            rows = slice(first, first + 8)
-            along_z = periodic_divergence(flux[rows], scaled[rows], z_up, z_up_two, z_down)
-            yield field, rows, along_y[rows] + along_z
-
-
-def plane_kernel(state, speed, out):
+def plane_kernel(state, speed, out, turned):
     half_speed = 0.5 * speed[0:1, :]
-
-    def one_plane(plane, carry):
-        fields = [state[f, plane] for f in range(FIELDS)]
-        for field, rows, total in side_planes(fields, half_speed):
-            out[field, plane, rows, :] = total
+    lane = lax.broadcasted_iota(jnp.int32, (LANES, LANES), 1)
+    to_turned = (lane % 8) * 16 + lane // 8
+    to_plain = (lane % 16) * 8 + lane // 16
+
+    def four_planes(part, carry):
+        planes = pl.ds(part * 4, 4)
+        for f in range(FIELDS):
+            plain = state[f, planes].reshape(LANES, LANES)
+            turned[f] = jnp.take_along_axis(plain, to_turned, axis=1).T
+        for place in range(4):
+            fields = [state[f, part * 4 + place] for f in range(FIELDS)]
+            vel, pressure = half_velocities(fields)
+            for field in range(FIELDS):
+                out[field, part * 4 + place] = periodic_divergence(
+                    half_flux(fields, field, 1, vel[1], pressure),
+                    half_speed * fields[field],
+                    y_up,
+                    y_up_two,
+                    y_down,
+                )
+        columns = [
+            [turned[f, row : row + 8] for row in range(0, LANES, 8)] for f in range(FIELDS)
+        ]
+        along = [half_velocities(fields) for fields in zip(*columns)]
+        for field in range(FIELDS):
+            fluxes = [
+                half_flux(fields, field, 2, vel[2], pressure)
+                for fields, (vel, pressure) in zip(zip(*columns), along)
+            ]
+            scaled = [half_speed * value for value in columns[field]]
+            total = jnp.concatenate(ring_divergence(fluxes, scaled), axis=0)
+            plain = jnp.take_along_axis(total.T, to_plain, axis=1)
+            out[field, planes] += plain.reshape(4, ROWS, LANES)
         return carry
 
-    lax.fori_loop(0, state.shape[1], one_plane, 0)
+    lax.fori_loop(0, state.shape[1] // 4, four_planes, 0)
 
 
 def along_planes(state, speed):
@@ -359,6 +390,7 @@
         out_shape=jax.ShapeDtypeStruct(state.shape, jnp.float32),
         in_specs=[VMEM, VMEM],
         out_specs=VMEM,
+        scratch_shapes=[pltpu.VMEM((FIELDS, LANES, LANES), jnp.float32)],
         compiler_params=params(),
         cost_estimate=cost(20_000_000, 1_000_000),
         name="planes",

time: 75.8 us -> 74.1 us (0.978)
  Pallas kernels: 20.9 us -> 19.3 us
    pallas_call x2, Pallas kernels: 9.77 us -> 8.11 us  [along_planes(): pl.pallas_call(plane_kernel, out_shape=jax.ShapeDtypeStruct(state.shape,...]
  transfers between devices with their start and end apart: 11 -> 11, of which waited for: 3 -> 3; matrix products, arithmetic and copies ran while one was open for 1% -> 1% of each run, Pallas kernels for 13% -> 11%
where the time goes in v11:
time: 74.1 us; the launch traced here: 73.9 us
  waiting for transfers between devices  28.9 us (39%)
  starting transfers between devices  24.9 us (34%)
  Pallas kernels  19.3 us (26%)
    all_to_all x1, waiting for transfers between devices, per_device(): come = lax.all_to_all(parts, 'gx', split_axis=0, concat_axis=0, tiled=True)  26.8 us
    ppermute x2, starting transfers between devices, per_device(): above = lax.ppermute(low, 'gx', down)  10.3 us
    pallas_call x2, Pallas kernels, along_planes(): pl.pallas_call(plane_kernel, out_shape=jax.ShapeDtypeStruct(state.shape,...  8.11 us
    all_to_all x1, starting transfers between devices, per_device(): come = lax.all_to_all(parts, 'gx', split_axis=0, concat_axis=0, tiled=True)  7.37 us
    ppermute x6, starting transfers between devices, everyone_max(): copies.append(lax.ppermute(value, axis, pairs))  6.36 us
    pallas_call x1, Pallas kernels, second_stage(): pl.pallas_call(second_kernel, out_shape=jax.ShapeDtypeStruct((FIELDS, BLO...  3.16 us
    pallas_call x1, Pallas kernels, unpack(): pl.pallas_call(functools.partial(unpack_kernel, size, cap), out_shape=(ja...  2.79 us
    pallas_call x1, Pallas kernels, pack(): pl.pallas_call(functools.partial(pack_kernel, size, cap, per_dev), out_sh...  2.74 us
  transfers between devices with their start and end apart: 11, of which 3 were waited for; matrix products, arithmetic and copies ran while one was open for 1% of the time, Pallas kernels for 11%

profile of v11, /device:TPU:0, one launch (start us, length us, event | category | flops | bytes accessed | tf_op | source)
XLA Modules:
  0.0 73.9 jit_solution(12792910831553841298)
XLA Ops:
  0.0 2.7 %pack.1 = f32[16,161,1,128]{3,2,1,0:T(1,128)} custom-call(s32[1024]{0:T(1024)} %owner_hbm.1, f32[1280,128]{1,0:T(8,128)} %bitcast.7), custom_call_target="tpu_custom_call" | custom-call | flops 1000000 | bytes 3000000 | tf_op jit(solution)/shard_map/pack/pallas_call | solution.py:110
  2.8 7.4 %all-to-all-start = ((f32[16,161,1,128]{3,2,1,0:T(1,128)}), f32[16,161,1,128]{3,2,1,0:T(1,128)S(1)}, u32[]{:S(2)}, u32[]{:S(2)}) async-start(f32[16,161,1,128]{3,2,1,0:T(1,128)} %pack.1), calls=%async_computation | async-start | bytes 2637824 | tf_op jit(solution)/shard_map/all_to_all | solution.py:535
  10.2 0.1 eq.33
  10.3 0.3 convert_reduce_fusion
  10.6 0.1 broadcast_add_fusion
  10.7 0.1 add.17
  10.8 0.1 select_reduce_fusion.table
  10.9 26.8 %all-to-all-done = f32[16,161,1,128]{3,2,1,0:T(1,128)S(1)} async-done(((f32[16,161,1,128]{3,2,1,0:T(1,128)}), f32[16,161,1,128]{3,2,1,0:T(1,128)S(1)}, u32[]{:S(2)}, u32[]{:S(2)}) %all-to-all-start) | async-done | bytes 1318944 | tf_op jit(solution)/shard_map/all_to_all | solution.py:535
  37.7 2.8 %unpack.1 = (f32[5,8,32,128]{3,2,1,0:T(8,128)S(1)}, f32[5,3,32,128]{3,2,1,0:T(8,128)S(1)}, f32[5,3,32,128]{3,2,1,0:T(8,128)S(1)}, f32[8,128]{1,0:T(8,128)S(1)}) custom-call(s32[64]{0:T(128)S(1)} %select_reduce_fusion.table, f32[2576,128]{1,0:T(8,128)S(1)} %bitcast.6), custom_call_target="tpu_custom_call" | custom-call | flops 5000000 | bytes 2000000 | tf_op jit(solution)/shard_map/unpack/pallas_call | solution.py:202
  40.5 0.8 %collective-permute-start = (f32[5,3,32,128]{3,2,1,0:T(8,128)S(1)}, f32[5,3,32,128]{3,2,1,0:T(8,128)S(1)}, u32[]{:S(2)}, u32[]{:S(2)}) collective-permute-start(f32[5,3,32,128]{3,2,1,0:T(8,128)S(1)} %get-tuple-element.21), channel_id=1, source_target_pairs={{0,1},{1,2},{2,3},{3,4},{4,5},{5,6},{6,7},{7,8},{8,9},{9,10},{10,1... | collective-permute-start | bytes 737288 | tf_op jit(solution)/shard_map/ppermute | solution.py:538
  41.3 5.9 %collective-permute-start.1 = (f32[5,3,32,128]{3,2,1,0:T(8,128)S(1)}, f32[5,3,32,128]{3,2,1,0:T(8,128)S(1)}, u32[]{:S(2)}, u32[]{:S(2)}) collective-permute-start(f32[5,3,32,128]{3,2,1,0:T(8,128)S(1)} %get-tuple-element.22), channel_id=1, source_target_pairs={{1,0},{2,1},{3,2},{4,3},{5,4},{6,5},{7,6},{8,7},{9,8},{10,9},{11,1... | collective-permute-start | bytes 737288 | tf_op jit(solution)/shard_map/ppermute | solution.py:539
  47.2 4.0 %planes.2.sides = f32[5,8,32,128]{3,2,1,0:T(8,128)S(1)} custom-call(f32[5,8,32,128]{3,2,1,0:T(8,128)S(1)} %get-tuple-element.19.state.start, f32[8,128]{1,0:T(8,128)S(1)} %get-tuple-element.20.speed.first_speed), custom_call_target="tpu_custom_call" | custom-call | flops 20000000 | bytes 1000000 | tf_op jit(solution)/shard_map/planes/pallas_call | solution.py:388
  51.3 2.5 %first_stage.1 = (f32[5,8,32,128]{3,2,1,0:T(8,128)S(1)}, f32[5,3,32,128]{3,2,1,0:T(8,128)S(1)}, f32[5,3,32,128]{3,2,1,0:T(8,128)S(1)}, f32[8,128]{1,0:T(8,128)S(1)}) custom-call(f32[5,8,32,128]{3,2,1,0:T(8,128)S(1)} %get-tuple-element.19.state.start, f32[5,8,32,128]{3,2,1,0:T(8,128)S(1)} %planes.2.sides, f32[5,3,32,128]{3,2,1,0:T(8,128)S(1)} %collective-permute-done.below, ...), custom_call_target="tpu_custom_call" | custom-call | flops 30000000 | bytes 3000000 | tf_op jit(solution)/shard_map/first_stage/pallas_call | solution.py:459
  53.7 0.1 collective-permute-start.4
  53.8 2.3 %collective-permute-start.3 = (f32[8,128]{1,0:T(8,128)S(1)}, f32[8,128]{1,0:T(8,128)S(1)}, u32[]{:S(2)}, u32[]{:S(2)}) collective-permute-start(f32[8,128]{1,0:T(8,128)S(1)} %get-tuple-element.24), channel_id=1, source_target_pairs={{0,8},{1,9},{2,10},{3,11},{4,12},{5,13},{6,14},{7,15},{8,0},{9,1},... | collective-permute-start | bytes 12296 | tf_op jit(solution)/shard_map/ppermute | solution.py:519
  56.1 2.1 %collective-permute-start.2 = (f32[8,128]{1,0:T(8,128)S(1)}, f32[8,128]{1,0:T(8,128)S(1)}, u32[]{:S(2)}, u32[]{:S(2)}) collective-permute-start(f32[8,128]{1,0:T(8,128)S(1)} %get-tuple-element.24), channel_id=1, source_target_pairs={{0,4},{1,5},{2,6},{3,7},{4,0},{5,1},{6,2},{7,3},{8,12},{9,13},{10,... | collective-permute-start | bytes 12296 | tf_op jit(solution)/shard_map/ppermute | solution.py:519
  58.2 4.4 %collective-permute-start.9 = (f32[5,3,32,128]{3,2,1,0:T(8,128)S(1)}, f32[5,3,32,128]{3,2,1,0:T(8,128)S(1)}, u32[]{:S(2)}, u32[]{:S(2)}) collective-permute-start(f32[5,3,32,128]{3,2,1,0:T(8,128)S(1)} %get-tuple-element.26), channel_id=1, source_target_pairs={{1,0},{2,1},{3,2},{4,3},{5,4},{6,5},{7,6},{8,7},{9,8},{10,9},{11,1... | collective-permute-start | bytes 737288 | tf_op jit(solution)/shard_map/ppermute | solution.py:544
  62.7 0.1 collective-permute-start.7
  62.7 0.1 collective-permute-start.6
  62.8 1.8 %collective-permute-start.5 = (f32[8,128]{1,0:T(8,128)S(1)}, f32[8,128]{1,0:T(8,128)S(1)}, u32[]{:S(2)}, u32[]{:S(2)}) collective-permute-start(f32[8,128]{1,0:T(8,128)S(1)} %maximum_maximum_fusion.1), channel_id=1, source_target_pairs={{0,1},{1,0},{2,3},{3,2},{4,5},{5,4},{6,7},{7,6},{8,9},{9,8},{10,11... | collective-permute-start | bytes 12296 | tf_op jit(solution)/shard_map/ppermute | solution.py:519
  64.6 1.6 %collective-permute-done.7 = f32[8,128]{1,0:T(8,128)S(1)} collective-permute-done((f32[8,128]{1,0:T(8,128)S(1)}, f32[8,128]{1,0:T(8,128)S(1)}, u32[]{:S(2)}, u32[]{:S(2)}) %collective-permute-start.7) | collective-permute-done | bytes 4128 | tf_op jit(solution)/shard_map/ppermute | solution.py:519
  66.1 0.5 collective-permute-done.6
  66.7 4.1 %planes.3.sides = f32[5,8,32,128]{3,2,1,0:T(8,128)S(1)} custom-call(f32[5,8,32,128]{3,2,1,0:T(8,128)S(1)} %get-tuple-element.23.state.middle, f32[8,128]{1,0:T(8,128)S(1)} %maximum_maximum_fusion.speed), custom_call_target="tpu_custom_call" | custom-call | flops 20000000 | bytes 1000000 | tf_op jit(solution)/shard_map/planes/pallas_call | solution.py:388
  70.8 3.2 %second_stage.1 = f32[5,8,32,128]{3,2,1,0:T(8,128)} custom-call(f32[5,8,32,128]{3,2,1,0:T(8,128)S(1)} %get-tuple-element.19.state.start, f32[5,8,32,128]{3,2,1,0:T(8,128)S(1)} %get-tuple-element.23.state.middle, f32[5,8,32,128]{3,2,1,0:T(8,128)S(1)} %planes.3.sides, f32[5,3,32,128]{3,2,1,0:T(8,128)S(1)} %collective-permute-done.8.below, ...), custom_call_target="tpu_custom_call" | custom-call | flops 30000000 | bytes 3000000 | tf_op jit(solution)/shard_map/second_stage/pallas_call | solution.py:498
  (18 shorter events, 0.1 us)
Async XLA Ops:
  2.7 7.4 %copy-start = (s32[1024]{0:T(1024)S(1)}, s32[1024]{0:T(1024)}, u32[]{:S(2)}) copy-start(s32[1024]{0:T(1024)} %owner_hbm.1) | copy-start | bytes 12292
  2.8 7.4 %copy-start.1 = (s32[1024]{0:T(1024)S(1)}, s32[1024]{0:T(1024)}, u32[]{:S(2)}) copy-start(s32[1024]{0:T(1024)} %param.5) | copy-start | bytes 12292
  2.8 34.9 %all-to-all-start = ((f32[16,161,1,128]{3,2,1,0:T(1,128)}), f32[16,161,1,128]{3,2,1,0:T(1,128)S(1)}, u32[]{:S(2)}, u32[]{:S(2)}) async-start(f32[16,161,1,128]{3,2,1,0:T(1,128)} %pack.1), calls=%async_computation | async-start | bytes 2637824 | tf_op jit(solution)/shard_map/all_to_all | solution.py:535
  40.5 10.7 %collective-permute-start = (f32[5,3,32,128]{3,2,1,0:T(8,128)S(1)}, f32[5,3,32,128]{3,2,1,0:T(8,128)S(1)}, u32[]{:S(2)}, u32[]{:S(2)}) collective-permute-start(f32[5,3,32,128]{3,2,1,0:T(8,128)S(1)} %get-tuple-element.21), channel_id=1, source_target_pairs={{0,1},{1,2},{2,3},{3,4},{4,5},{5,6},{6,7},{7,8},{8,9},{9,10},{10,1... | collective-permute-start | bytes 737288 | tf_op jit(solution)/shard_map/ppermute | solution.py:538
  41.3 9.9 %collective-permute-start.1 = (f32[5,3,32,128]{3,2,1,0:T(8,128)S(1)}, f32[5,3,32,128]{3,2,1,0:T(8,128)S(1)}, u32[]{:S(2)}, u32[]{:S(2)}) collective-permute-start(f32[5,3,32,128]{3,2,1,0:T(8,128)S(1)} %get-tuple-element.22), channel_id=1, source_target_pairs={{1,0},{2,1},{3,2},{4,3},{5,4},{6,5},{7,6},{8,7},{9,8},{10,9},{11,1... | collective-permute-start | bytes 737288 | tf_op jit(solution)/shard_map/ppermute | solution.py:539
  53.7 8.9 %collective-permute-start.4 = (f32[8,128]{1,0:T(8,128)S(1)}, f32[8,128]{1,0:T(8,128)S(1)}, u32[]{:S(2)}, u32[]{:S(2)}) collective-permute-start(f32[8,128]{1,0:T(8,128)S(1)} %get-tuple-element.24), channel_id=1, source_target_pairs={{0,12},{1,13},{2,14},{3,15},{4,8},{5,9},{6,10},{7,11},{8,4},{9,5},... | collective-permute-start | bytes 12296 | tf_op jit(solution)/shard_map/ppermute | solution.py:519
  53.8 8.8 %collective-permute-start.3 = (f32[8,128]{1,0:T(8,128)S(1)}, f32[8,128]{1,0:T(8,128)S(1)}, u32[]{:S(2)}, u32[]{:S(2)}) collective-permute-start(f32[8,128]{1,0:T(8,128)S(1)} %get-tuple-element.24), channel_id=1, source_target_pairs={{0,8},{1,9},{2,10},{3,11},{4,12},{5,13},{6,14},{7,15},{8,0},{9,1},... | collective-permute-start | bytes 12296 | tf_op jit(solution)/shard_map/ppermute | solution.py:519
  56.1 6.5 %collective-permute-start.2 = (f32[8,128]{1,0:T(8,128)S(1)}, f32[8,128]{1,0:T(8,128)S(1)}, u32[]{:S(2)}, u32[]{:S(2)}) collective-permute-start(f32[8,128]{1,0:T(8,128)S(1)} %get-tuple-element.24), channel_id=1, source_target_pairs={{0,4},{1,5},{2,6},{3,7},{4,0},{5,1},{6,2},{7,3},{8,12},{9,13},{10,... | collective-permute-start | bytes 12296 | tf_op jit(solution)/shard_map/ppermute | solution.py:519
  58.2 12.6 %collective-permute-start.8 = (f32[5,3,32,128]{3,2,1,0:T(8,128)S(1)}, f32[5,3,32,128]{3,2,1,0:T(8,128)S(1)}, u32[]{:S(2)}, u32[]{:S(2)}) collective-permute-start(f32[5,3,32,128]{3,2,1,0:T(8,128)S(1)} %get-tuple-element.25), channel_id=1, source_target_pairs={{0,1},{1,2},{2,3},{3,4},{4,5},{5,6},{6,7},{7,8},{8,9},{9,10},{10,1... | collective-permute-start | bytes 737288 | tf_op jit(solution)/shard_map/ppermute | solution.py:543
  58.2 12.6 %collective-permute-start.9 = (f32[5,3,32,128]{3,2,1,0:T(8,128)S(1)}, f32[5,3,32,128]{3,2,1,0:T(8,128)S(1)}, u32[]{:S(2)}, u32[]{:S(2)}) collective-permute-start(f32[5,3,32,128]{3,2,1,0:T(8,128)S(1)} %get-tuple-element.26), channel_id=1, source_target_pairs={{1,0},{2,1},{3,2},{4,3},{5,4},{6,5},{7,6},{8,7},{9,8},{10,9},{11,1... | collective-permute-start | bytes 737288 | tf_op jit(solution)/shard_map/ppermute | solution.py:544
  62.7 3.5 %collective-permute-start.7 = (f32[8,128]{1,0:T(8,128)S(1)}, f32[8,128]{1,0:T(8,128)S(1)}, u32[]{:S(2)}, u32[]{:S(2)}) collective-permute-start(f32[8,128]{1,0:T(8,128)S(1)} %maximum_maximum_fusion.1), channel_id=1, source_target_pairs={{0,3},{1,2},{2,1},{3,0},{4,7},{5,6},{6,5},{7,4},{8,11},{9,10},{10,... | collective-permute-start | bytes 12296 | tf_op jit(solution)/shard_map/ppermute | solution.py:519
  62.7 3.9 %collective-permute-start.6 = (f32[8,128]{1,0:T(8,128)S(1)}, f32[8,128]{1,0:T(8,128)S(1)}, u32[]{:S(2)}, u32[]{:S(2)}) collective-permute-start(f32[8,128]{1,0:T(8,128)S(1)} %maximum_maximum_fusion.1), channel_id=1, source_target_pairs={{0,2},{1,3},{2,0},{3,1},{4,6},{5,7},{6,4},{7,5},{8,10},{9,11},{10,... | collective-permute-start | bytes 12296 | tf_op jit(solution)/shard_map/ppermute | solution.py:519
  62.8 3.9 %collective-permute-start.5 = (f32[8,128]{1,0:T(8,128)S(1)}, f32[8,128]{1,0:T(8,128)S(1)}, u32[]{:S(2)}, u32[]{:S(2)}) collective-permute-start(f32[8,128]{1,0:T(8,128)S(1)} %maximum_maximum_fusion.1), channel_id=1, source_target_pairs={{0,1},{1,0},{2,3},{3,2},{4,5},{5,4},{6,7},{7,6},{8,9},{9,8},{10,11... | collective-permute-start | bytes 12296 | tf_op jit(solution)/shard_map/ppermute | solution.py:519

commit v12 on v11

--- a/solution.py
+++ b/solution.py
@@ -43,6 +43,16 @@
     return fastest + sound
 
 
+def device_at(place, size):
+    if size < 4 or size & (size - 1):
+        return place
+    return (place % 2) * (size // 2) + (place // 2 % 2) * (size // 4) + place // 4
+
+
+def exchange_order(size):
+    return [device_at(place, size) for place in range(size)]
+
+
 def tiled_rows(blocks):
     count = blocks.shape[0] // 8
     groups = blocks.reshape(count, 8, FIELDS, PAIRS, LANES).transpose(2, 0, 3, 1, 4)
@@ -76,17 +86,19 @@
     fetch_rows.wait()
     tiles = TILES * cap
 
-    def message(dest, carry):
+    def message(place, carry):
+        dest = device_at(place, size)
+
         @pl.when(count[dest] > 0)
         def _():
             for rank in range(cap):
                 first = member[dest * cap + rank]
                 for pair in range(PAIRS):
                     source = pl.ds(first + pair * 8, FIELDS, stride=per_dev * PAIRS)
-                    to = dest * tiles + pair * (FIELDS * cap) + rank
+                    to = place * tiles + pair * (FIELDS * cap) + rank
                     out[pl.ds(to, FIELDS, stride=cap), :] = rows[source, :]
-            part = out.at[pl.ds(pl.multiple_of(dest * tiles, tiles), tiles)]
-            pltpu.make_async_copy(part, out_hbm.at[dest, pl.ds(0, tiles), 0], sems.at[2]).start()
+            part = out.at[pl.ds(pl.multiple_of(place * tiles, tiles), tiles)]
+            pltpu.make_async_copy(part, out_hbm.at[place, pl.ds(0, tiles), 0], sems.at[2]).start()
 
         return carry
 
@@ -134,7 +146,9 @@
     spot = jnp.arange(per_dev, dtype=jnp.int32)
     earlier = spot[None, :] < spot[:, None]
     rank = jnp.sum((mine[:, None, :] & earlier[None]).astype(jnp.int32), axis=2)
-    row = jnp.arange(size, dtype=jnp.int32)[:, None] * cap + rank
+    order = exchange_order(size)
+    places = jnp.array([order.index(source) for source in range(size)], jnp.int32)
+    row = places[:, None] * cap + rank
     key = jnp.where(mine, slots, -1)
     hit = key.reshape(1, -1) == spot[:, None]
     return jnp.max(jnp.where(hit, row.reshape(1, -1), 0), axis=1)
@@ -532,7 +546,14 @@
 
     parts = pack(tiled_rows(blocks), owner_list, size, cap, per_dev)
     parts, owner_list, slot_list = lax.optimization_barrier((parts, owner_list, slot_list))
-    come = lax.all_to_all(parts, "gx", split_axis=0, concat_axis=0, tiled=True)
+    come = lax.all_to_all(
+        parts,
+        "gx",
+        split_axis=0,
+        concat_axis=0,
+        tiled=True,
+        axis_index_groups=[exchange_order(size)],
+    )
     table = arrival_spots(owner_list, slot_list, own, per_dev, size, cap)
     state, low, high, speed = unpack(table, come.reshape(-1, LANES), size, cap)
     below = lax.ppermute(high, "gx", up)

time: 74.1 us -> 78.5 us (1.059)
  waiting for transfers between devices: 28.9 us -> 35.1 us
  starting transfers between devices: 24.9 us -> 22.8 us
    all_to_all x1, waiting for transfers between devices: 26.8 us -> 31.5 us  [per_device(): lax.all_to_all(parts, 'gx', split_axis=0, concat_axis=0, tiled=True, axis...]
    ppermute x2, starting transfers between devices: 10.3 us -> 8.41 us  [per_device(): above = lax.ppermute(low, 'gx', down)]
    ppermute x6, waiting for transfers between devices: 2.09 us -> 3.53 us  [everyone_max(): copies.append(lax.ppermute(value, axis, pairs))]
  transfers between devices with their start and end apart: 11 -> 11, of which waited for: 3 -> 3; matrix products, arithmetic and copies ran while one was open for 1% -> 1% of each run, Pallas kernels for 11% -> 10%
where the time goes in v12:
time: 78.5 us; the launch traced here: 78.3 us
  waiting for transfers between devices  35.1 us (45%)
  starting transfers between devices  22.8 us (29%)
  Pallas kernels  19.5 us (25%)
    all_to_all x1, waiting for transfers between devices, per_device(): lax.all_to_all(parts, 'gx', split_axis=0, concat_axis=0, tiled=True, axis...  31.5 us
    ppermute x2, starting transfers between devices, per_device(): above = lax.ppermute(low, 'gx', down)  8.41 us
    pallas_call x2, Pallas kernels, along_planes(): pl.pallas_call(plane_kernel, out_shape=jax.ShapeDtypeStruct(state.shape,...  8.14 us
    all_to_all x1, starting transfers between devices, per_device(): lax.all_to_all(parts, 'gx', split_axis=0, concat_axis=0, tiled=True, axis...  7.5 us
    ppermute x6, starting transfers between devices, everyone_max(): copies.append(lax.ppermute(value, axis, pairs))  6.35 us
    ppermute x6, waiting for transfers between devices, everyone_max(): copies.append(lax.ppermute(value, axis, pairs))  3.53 us
    pallas_call x1, Pallas kernels, second_stage(): pl.pallas_call(second_kernel, out_shape=jax.ShapeDtypeStruct((FIELDS, BLO...  3.16 us
    pallas_call x1, Pallas kernels, pack(): pl.pallas_call(functools.partial(pack_kernel, size, cap, per_dev), out_sh...  2.93 us
  transfers between devices with their start and end apart: 11, of which 3 were waited for; matrix products, arithmetic and copies ran while one was open for 1% of the time, Pallas kernels for 10%

profile of v12, /device:TPU:0, one launch (start us, length us, event | category | flops | bytes accessed | tf_op | source)
XLA Modules:
  0.0 78.3 jit_solution(12081006649606506086)
XLA Ops:
  0.0 2.9 %pack.1 = f32[16,161,1,128]{3,2,1,0:T(1,128)} custom-call(s32[1024]{0:T(1024)} %owner_hbm.1, f32[1280,128]{1,0:T(8,128)} %bitcast.7), custom_call_target="tpu_custom_call" | custom-call | flops 1000000 | bytes 3000000 | tf_op jit(solution)/shard_map/pack/pallas_call | solution.py:122
  3.0 7.5 %all-to-all-start = ((f32[16,161,1,128]{3,2,1,0:T(1,128)}), f32[16,161,1,128]{3,2,1,0:T(1,128)S(1)}, u32[]{:S(2)}, u32[]{:S(2)}) async-start(f32[16,161,1,128]{3,2,1,0:T(1,128)} %pack.1), calls=%async_computation | async-start | bytes 2637824 | tf_op jit(solution)/shard_map/all_to_all | solution.py:549
  10.5 0.1 eq.33
  10.6 0.3 convert_reduce_fusion
  11.0 0.1 broadcast_add_fusion
  11.1 0.1 add.17
  11.1 0.1 select_reduce_fusion.table
  11.3 31.5 %all-to-all-done = f32[16,161,1,128]{3,2,1,0:T(1,128)S(1)} async-done(((f32[16,161,1,128]{3,2,1,0:T(1,128)}), f32[16,161,1,128]{3,2,1,0:T(1,128)S(1)}, u32[]{:S(2)}, u32[]{:S(2)}) %all-to-all-start) | async-done | bytes 1318944 | tf_op jit(solution)/shard_map/all_to_all | solution.py:549
  42.8 2.8 %unpack.1 = (f32[5,8,32,128]{3,2,1,0:T(8,128)S(1)}, f32[5,3,32,128]{3,2,1,0:T(8,128)S(1)}, f32[5,3,32,128]{3,2,1,0:T(8,128)S(1)}, f32[8,128]{1,0:T(8,128)S(1)}) custom-call(s32[64]{0:T(128)S(1)} %select_reduce_fusion.table, f32[2576,128]{1,0:T(8,128)S(1)} %bitcast.6), custom_call_target="tpu_custom_call" | custom-call | flops 5000000 | bytes 2000000 | tf_op jit(solution)/shard_map/unpack/pallas_call | solution.py:216
  45.7 4.4 %collective-permute-start.1 = (f32[5,3,32,128]{3,2,1,0:T(8,128)S(1)}, f32[5,3,32,128]{3,2,1,0:T(8,128)S(1)}, u32[]{:S(2)}, u32[]{:S(2)}) collective-permute-start(f32[5,3,32,128]{3,2,1,0:T(8,128)S(1)} %get-tuple-element.22), channel_id=1, source_target_pairs={{1,0},{2,1},{3,2},{4,3},{5,4},{6,5},{7,6},{8,7},{9,8},{10,9},{11,1... | collective-permute-start | bytes 737288 | tf_op jit(solution)/shard_map/ppermute | solution.py:560
  50.1 4.1 %planes.2.sides = f32[5,8,32,128]{3,2,1,0:T(8,128)S(1)} custom-call(f32[5,8,32,128]{3,2,1,0:T(8,128)S(1)} %get-tuple-element.19.state.start, f32[8,128]{1,0:T(8,128)S(1)} %get-tuple-element.20.speed.first_speed), custom_call_target="tpu_custom_call" | custom-call | flops 20000000 | bytes 1000000 | tf_op jit(solution)/shard_map/planes/pallas_call | solution.py:402
  54.2 2.5 %first_stage.1 = (f32[5,8,32,128]{3,2,1,0:T(8,128)S(1)}, f32[5,3,32,128]{3,2,1,0:T(8,128)S(1)}, f32[5,3,32,128]{3,2,1,0:T(8,128)S(1)}, f32[8,128]{1,0:T(8,128)S(1)}) custom-call(f32[5,8,32,128]{3,2,1,0:T(8,128)S(1)} %get-tuple-element.19.state.start, f32[5,8,32,128]{3,2,1,0:T(8,128)S(1)} %planes.2.sides, f32[5,3,32,128]{3,2,1,0:T(8,128)S(1)} %collective-permute-done.below, ...), custom_call_target="tpu_custom_call" | custom-call | flops 30000000 | bytes 3000000 | tf_op jit(solution)/shard_map/first_stage/pallas_call | solution.py:473
  56.7 0.1 collective-permute-start.4
  56.8 0.1 collective-permute-start.3
  56.8 4.3 %collective-permute-start.2 = (f32[8,128]{1,0:T(8,128)S(1)}, f32[8,128]{1,0:T(8,128)S(1)}, u32[]{:S(2)}, u32[]{:S(2)}) collective-permute-start(f32[8,128]{1,0:T(8,128)S(1)} %get-tuple-element.24), channel_id=1, source_target_pairs={{0,4},{1,5},{2,6},{3,7},{4,0},{5,1},{6,2},{7,3},{8,12},{9,13},{10,... | collective-permute-start | bytes 12296 | tf_op jit(solution)/shard_map/ppermute | solution.py:533
  61.1 0.5 collective-permute-start.8
  61.6 4.0 %collective-permute-start.9 = (f32[5,3,32,128]{3,2,1,0:T(8,128)S(1)}, f32[5,3,32,128]{3,2,1,0:T(8,128)S(1)}, u32[]{:S(2)}, u32[]{:S(2)}) collective-permute-start(f32[5,3,32,128]{3,2,1,0:T(8,128)S(1)} %get-tuple-element.26), channel_id=1, source_target_pairs={{1,0},{2,1},{3,2},{4,3},{5,4},{6,5},{7,6},{8,7},{9,8},{10,9},{11,1... | collective-permute-start | bytes 737288 | tf_op jit(solution)/shard_map/ppermute | solution.py:565
  65.6 0.1 collective-permute-start.7
  65.7 0.1 collective-permute-start.6
  65.8 1.8 %collective-permute-start.5 = (f32[8,128]{1,0:T(8,128)S(1)}, f32[8,128]{1,0:T(8,128)S(1)}, u32[]{:S(2)}, u32[]{:S(2)}) collective-permute-start(f32[8,128]{1,0:T(8,128)S(1)} %maximum_maximum_fusion.1), channel_id=1, source_target_pairs={{0,1},{1,0},{2,3},{3,2},{4,5},{5,4},{6,7},{7,6},{8,9},{9,8},{10,11... | collective-permute-start | bytes 12296 | tf_op jit(solution)/shard_map/ppermute | solution.py:533
  67.5 2.2 %collective-permute-done.7 = f32[8,128]{1,0:T(8,128)S(1)} collective-permute-done((f32[8,128]{1,0:T(8,128)S(1)}, f32[8,128]{1,0:T(8,128)S(1)}, u32[]{:S(2)}, u32[]{:S(2)}) %collective-permute-start.7) | collective-permute-done | bytes 4128 | tf_op jit(solution)/shard_map/ppermute | solution.py:533
  69.7 1.3 %collective-permute-done.6 = f32[8,128]{1,0:T(8,128)S(1)} collective-permute-done((f32[8,128]{1,0:T(8,128)S(1)}, f32[8,128]{1,0:T(8,128)S(1)}, u32[]{:S(2)}, u32[]{:S(2)}) %collective-permute-start.6) | collective-permute-done | bytes 4128 | tf_op jit(solution)/shard_map/ppermute | solution.py:533
  71.1 4.1 %planes.3.sides = f32[5,8,32,128]{3,2,1,0:T(8,128)S(1)} custom-call(f32[5,8,32,128]{3,2,1,0:T(8,128)S(1)} %get-tuple-element.23.state.middle, f32[8,128]{1,0:T(8,128)S(1)} %maximum_maximum_fusion.speed), custom_call_target="tpu_custom_call" | custom-call | flops 20000000 | bytes 1000000 | tf_op jit(solution)/shard_map/planes/pallas_call | solution.py:402
  75.2 3.2 %second_stage.1 = f32[5,8,32,128]{3,2,1,0:T(8,128)} custom-call(f32[5,8,32,128]{3,2,1,0:T(8,128)S(1)} %get-tuple-element.19.state.start, f32[5,8,32,128]{3,2,1,0:T(8,128)S(1)} %get-tuple-element.23.state.middle, f32[5,8,32,128]{3,2,1,0:T(8,128)S(1)} %planes.3.sides, f32[5,3,32,128]{3,2,1,0:T(8,128)S(1)} %collective-permute-done.8.below, ...), custom_call_target="tpu_custom_call" | custom-call | flops 30000000 | bytes 3000000 | tf_op jit(solution)/shard_map/second_stage/pallas_call | solution.py:512
  (19 shorter events, 0.1 us)
Async XLA Ops:
  2.9 7.6 %copy-start = (s32[1024]{0:T(1024)S(1)}, s32[1024]{0:T(1024)}, u32[]{:S(2)}) copy-start(s32[1024]{0:T(1024)} %owner_hbm.1) | copy-start | bytes 12292
  3.0 7.5 %copy-start.1 = (s32[1024]{0:T(1024)S(1)}, s32[1024]{0:T(1024)}, u32[]{:S(2)}) copy-start(s32[1024]{0:T(1024)} %param.6) | copy-start | bytes 12292
  3.0 8.0 %copy-start.2 = (s32[16]{0:T(128)S(1)}, s32[16]{0:T(128)}, u32[]{:S(2)}) copy-start(s32[16]{0:T(128)} %constant.15) | copy-start | bytes 196
  3.0 39.8 %all-to-all-start = ((f32[16,161,1,128]{3,2,1,0:T(1,128)}), f32[16,161,1,128]{3,2,1,0:T(1,128)S(1)}, u32[]{:S(2)}, u32[]{:S(2)}) async-start(f32[16,161,1,128]{3,2,1,0:T(1,128)} %pack.1), calls=%async_computation | async-start | bytes 2637824 | tf_op jit(solution)/shard_map/all_to_all | solution.py:549
  45.6 8.6 %collective-permute-start = (f32[5,3,32,128]{3,2,1,0:T(8,128)S(1)}, f32[5,3,32,128]{3,2,1,0:T(8,128)S(1)}, u32[]{:S(2)}, u32[]{:S(2)}) collective-permute-start(f32[5,3,32,128]{3,2,1,0:T(8,128)S(1)} %get-tuple-element.21), channel_id=1, source_target_pairs={{0,1},{1,2},{2,3},{3,4},{4,5},{5,6},{6,7},{7,8},{8,9},{9,10},{10,1... | collective-permute-start | bytes 737288 | tf_op jit(solution)/shard_map/ppermute | solution.py:559
  45.7 8.5 %collective-permute-start.1 = (f32[5,3,32,128]{3,2,1,0:T(8,128)S(1)}, f32[5,3,32,128]{3,2,1,0:T(8,128)S(1)}, u32[]{:S(2)}, u32[]{:S(2)}) collective-permute-start(f32[5,3,32,128]{3,2,1,0:T(8,128)S(1)} %get-tuple-element.22), channel_id=1, source_target_pairs={{1,0},{2,1},{3,2},{4,3},{5,4},{6,5},{7,6},{8,7},{9,8},{10,9},{11,1... | collective-permute-start | bytes 737288 | tf_op jit(solution)/shard_map/ppermute | solution.py:560
  56.7 8.9 %collective-permute-start.4 = (f32[8,128]{1,0:T(8,128)S(1)}, f32[8,128]{1,0:T(8,128)S(1)}, u32[]{:S(2)}, u32[]{:S(2)}) collective-permute-start(f32[8,128]{1,0:T(8,128)S(1)} %get-tuple-element.24), channel_id=1, source_target_pairs={{0,12},{1,13},{2,14},{3,15},{4,8},{5,9},{6,10},{7,11},{8,4},{9,5},... | collective-permute-start | bytes 12296 | tf_op jit(solution)/shard_map/ppermute | solution.py:533
  56.8 8.8 %collective-permute-start.3 = (f32[8,128]{1,0:T(8,128)S(1)}, f32[8,128]{1,0:T(8,128)S(1)}, u32[]{:S(2)}, u32[]{:S(2)}) collective-permute-start(f32[8,128]{1,0:T(8,128)S(1)} %get-tuple-element.24), channel_id=1, source_target_pairs={{0,8},{1,9},{2,10},{3,11},{4,12},{5,13},{6,14},{7,15},{8,0},{9,1},... | collective-permute-start | bytes 12296 | tf_op jit(solution)/shard_map/ppermute | solution.py:533
  56.8 8.7 %collective-permute-start.2 = (f32[8,128]{1,0:T(8,128)S(1)}, f32[8,128]{1,0:T(8,128)S(1)}, u32[]{:S(2)}, u32[]{:S(2)}) collective-permute-start(f32[8,128]{1,0:T(8,128)S(1)} %get-tuple-element.24), channel_id=1, source_target_pairs={{0,4},{1,5},{2,6},{3,7},{4,0},{5,1},{6,2},{7,3},{8,12},{9,13},{10,... | collective-permute-start | bytes 12296 | tf_op jit(solution)/shard_map/ppermute | solution.py:533
  61.1 14.0 %collective-permute-start.8 = (f32[5,3,32,128]{3,2,1,0:T(8,128)S(1)}, f32[5,3,32,128]{3,2,1,0:T(8,128)S(1)}, u32[]{:S(2)}, u32[]{:S(2)}) collective-permute-start(f32[5,3,32,128]{3,2,1,0:T(8,128)S(1)} %get-tuple-element.25), channel_id=1, source_target_pairs={{0,1},{1,2},{2,3},{3,4},{4,5},{5,6},{6,7},{7,8},{8,9},{9,10},{10,1... | collective-permute-start | bytes 737288 | tf_op jit(solution)/shard_map/ppermute | solution.py:564
  61.6 13.6 %collective-permute-start.9 = (f32[5,3,32,128]{3,2,1,0:T(8,128)S(1)}, f32[5,3,32,128]{3,2,1,0:T(8,128)S(1)}, u32[]{:S(2)}, u32[]{:S(2)}) collective-permute-start(f32[5,3,32,128]{3,2,1,0:T(8,128)S(1)} %get-tuple-element.26), channel_id=1, source_target_pairs={{1,0},{2,1},{3,2},{4,3},{5,4},{6,5},{7,6},{8,7},{9,8},{10,9},{11,1... | collective-permute-start | bytes 737288 | tf_op jit(solution)/shard_map/ppermute | solution.py:565
  65.6 4.1 %collective-permute-start.7 = (f32[8,128]{1,0:T(8,128)S(1)}, f32[8,128]{1,0:T(8,128)S(1)}, u32[]{:S(2)}, u32[]{:S(2)}) collective-permute-start(f32[8,128]{1,0:T(8,128)S(1)} %maximum_maximum_fusion.1), channel_id=1, source_target_pairs={{0,3},{1,2},{2,1},{3,0},{4,7},{5,6},{6,5},{7,4},{8,11},{9,10},{10,... | collective-permute-start | bytes 12296 | tf_op jit(solution)/shard_map/ppermute | solution.py:533
  65.7 5.4 %collective-permute-start.6 = (f32[8,128]{1,0:T(8,128)S(1)}, f32[8,128]{1,0:T(8,128)S(1)}, u32[]{:S(2)}, u32[]{:S(2)}) collective-permute-start(f32[8,128]{1,0:T(8,128)S(1)} %maximum_maximum_fusion.1), channel_id=1, source_target_pairs={{0,2},{1,3},{2,0},{3,1},{4,6},{5,7},{6,4},{7,5},{8,10},{9,11},{10,... | collective-permute-start | bytes 12296 | tf_op jit(solution)/shard_map/ppermute | solution.py:533
  65.8 5.3 %collective-permute-start.5 = (f32[8,128]{1,0:T(8,128)S(1)}, f32[8,128]{1,0:T(8,128)S(1)}, u32[]{:S(2)}, u32[]{:S(2)}) collective-permute-start(f32[8,128]{1,0:T(8,128)S(1)} %maximum_maximum_fusion.1), channel_id=1, source_target_pairs={{0,1},{1,0},{2,3},{3,2},{4,5},{5,4},{6,7},{7,6},{8,9},{9,8},{10,11... | collective-permute-start | bytes 12296 | tf_op jit(solution)/shard_map/ppermute | solution.py:533

commit v13 on v11

--- a/solution.py
+++ b/solution.py
@@ -154,62 +154,60 @@
     return rows
 
 
-def unpack_kernel(size, cap, table, come, state, low_halo, high_halo, speed, scratch):
+def unpack_kernel(size, cap, couple, table, come, state, halo, *refs):
     message = TILES * cap + 1
-    best = come[message - 1 : message, :]
-    for source in range(1, size):
-        best = jnp.maximum(best, come[(source + 1) * message - 1 : (source + 1) * message, :])
-    speed[...] = jnp.broadcast_to(best, speed.shape)
+    scratch = refs[-1]
+    if couple == 0:
+        best = come[message - 1 : message, :]
+        for source in range(1, size):
+            best = jnp.maximum(best, come[(source + 1) * message - 1 : (source + 1) * message, :])
+        refs[0][...] = jnp.broadcast_to(best, refs[0].shape)
     for slot in range(BY * BZ):
         p, q = divmod(slot, BZ)
         where = table[slot]
         source = lax.div(where, cap)
         rank = lax.rem(where, cap)
-        for pair in range(PAIRS):
-            couple, h = divmod(pair, 2)
-            base = source * message + rank + pair * (FIELDS * cap)
+        for h in range(2):
+            base = source * message + rank + (2 * couple + h) * (FIELDS * cap)
             value = come[pl.ds(base, FIELDS, stride=cap), :]
-            row = (couple * BZ + q) * 8 + 2 * p + h
-            scratch[pl.ds(row, FIELDS, stride=PAIRS // 2 * BZ * 8), :] = value
+            scratch[pl.ds(q * 8 + 2 * p + h, FIELDS, stride=BZ * 8), :] = value
     group = lax.broadcasted_iota(jnp.int32, (8, LANES), 1) // BLOCK
     even = lax.broadcasted_iota(jnp.int32, (8, LANES), 0) % 2 == 0
 
     for f in range(FIELDS):
-        for couple in range(PAIRS // 2):
-            first = (f * (PAIRS // 2) + couple) * BZ * 8
-            rows = [scratch[first + q * 8 : first + q * 8 + 8, :] for q in range(BZ)]
-            moved = exchanged_bits(rows, group)
-            for second in range(2):
-                for j in range(4):
-                    lower = moved[second * BLOCK + j]
-                    upper = moved[second * BLOCK + j + 4]
-                    planes = (
-                        jnp.where(even, lower, pltpu.roll(upper, 1, 0)),
-                        jnp.where(even, pltpu.roll(lower, 7, 0), upper),
-                    )
-                    rows = slice(j * 8, j * 8 + 8)
-                    for h in range(2):
-                        plane = 4 * couple + 2 * h + second
-                        state[f, plane, rows, :] = planes[h]
-                        if plane < 3:
-                            low_halo[f, plane, rows, :] = planes[h]
-                        if plane >= 5:
-                            high_halo[f, plane - 5, rows, :] = planes[h]
-
-
-def unpack(table, come, size, cap):
-    halo = jax.ShapeDtypeStruct((FIELDS, 3, ROWS, LANES), jnp.float32)
+        first = f * BZ * 8
+        rows = [scratch[first + q * 8 : first + q * 8 + 8, :] for q in range(BZ)]
+        moved = exchanged_bits(rows, group)
+        for second in range(2):
+            for j in range(4):
+                lower = moved[second * BLOCK + j]
+                upper = moved[second * BLOCK + j + 4]
+                planes = (
+                    jnp.where(even, lower, pltpu.roll(upper, 1, 0)),
+                    jnp.where(even, pltpu.roll(lower, 7, 0), upper),
+                )
+                rows = slice(j * 8, j * 8 + 8)
+                for h in range(2):
+                    plane = 2 * h + second
+                    state[f, plane, rows, :] = planes[h]
+                    at = plane - couple
+                    if 0 <= at < 3:
+                        halo[f, at, rows, :] = planes[h]
+
+
+def unpack(table, come, couple, size, cap):
+    shapes = [
+        jax.ShapeDtypeStruct((FIELDS, 4, ROWS, LANES), jnp.float32),
+        jax.ShapeDtypeStruct((FIELDS, 3, ROWS, LANES), jnp.float32),
+    ]
+    if couple == 0:
+        shapes.append(jax.ShapeDtypeStruct((8, LANES), jnp.float32))
     return pl.pallas_call(
-        functools.partial(unpack_kernel, size, cap),
-        out_shape=(
-            jax.ShapeDtypeStruct((FIELDS, BLOCK, ROWS, LANES), jnp.float32),
-            halo,
-            halo,
-            jax.ShapeDtypeStruct((8, LANES), jnp.float32),
-        ),
+        functools.partial(unpack_kernel, size, cap, couple),
+        out_shape=shapes,
         in_specs=[SMEM, VMEM],
-        out_specs=(VMEM,) * 4,
-        scratch_shapes=[pltpu.VMEM((FIELDS * (PAIRS // 2) * BZ * 8, LANES), jnp.float32)],
+        out_specs=[VMEM] * len(shapes),
+        scratch_shapes=[pltpu.VMEM((FIELDS * BZ * 8, LANES), jnp.float32)],
         compiler_params=params(),
         cost_estimate=cost(5_000_000, 2_000_000),
         name="unpack",
@@ -344,19 +342,18 @@
     return flux + 0.5 * pressure if field == 1 + direction else flux
 
 
-def plane_kernel(state, speed, out, turned):
+def plane_kernel(state_low, state_high, speed, out, turned):
     half_speed = 0.5 * speed[0:1, :]
     lane = lax.broadcasted_iota(jnp.int32, (LANES, LANES), 1)
     to_turned = (lane % 8) * 16 + lane // 8
     to_plain = (lane % 16) * 8 + lane // 16
 
-    def four_planes(part, carry):
-        planes = pl.ds(part * 4, 4)
+    for part, state in enumerate((state_low, state_high)):
         for f in range(FIELDS):
-            plain = state[f, planes].reshape(LANES, LANES)
+            plain = state[f].reshape(LANES, LANES)
             turned[f] = jnp.take_along_axis(plain, to_turned, axis=1).T
         for place in range(4):
-            fields = [state[f, part * 4 + place] for f in range(FIELDS)]
+            fields = [state[f, place] for f in range(FIELDS)]
             vel, pressure = half_velocities(fields)
             for field in range(FIELDS):
                 out[field, part * 4 + place] = periodic_divergence(
@@ -378,23 +375,20 @@
             scaled = [half_speed * value for value in columns[field]]
             total = jnp.concatenate(ring_divergence(fluxes, scaled), axis=0)
             plain = jnp.take_along_axis(total.T, to_plain, axis=1)
-            out[field, planes] += plain.reshape(4, ROWS, LANES)
-        return carry
-
-    lax.fori_loop(0, state.shape[1] // 4, four_planes, 0)
-
-
-def along_planes(state, speed):
+            out[field, part * 4 : part * 4 + 4] += plain.reshape(4, ROWS, LANES)
+
+
+def along_planes(state_low, state_high, speed):
     return pl.pallas_call(
         plane_kernel,
-        out_shape=jax.ShapeDtypeStruct(state.shape, jnp.float32),
-        in_specs=[VMEM, VMEM],
+        out_shape=jax.ShapeDtypeStruct((FIELDS, BLOCK, ROWS, LANES), jnp.float32),
+        in_specs=[VMEM] * 3,
         out_specs=VMEM,
         scratch_shapes=[pltpu.VMEM((FIELDS, LANES, LANES), jnp.float32)],
         compiler_params=params(),
         cost_estimate=cost(20_000_000, 1_000_000),
         name="planes",
-    )(state, speed)
+    )(state_low, state_high, speed)
 
 
 def across(get, half_speed):
@@ -420,45 +414,47 @@
         yield field, open_divergence(fluxes, scaled)
 
 
-def first_kernel(state, sides, below, above, speed, middle, low, high, top):
+def slab(state_low, state_high, below, above, rows):
+    def get(f, plane):
+        if plane < 0:
+            return below[f, plane + 3, rows, :]
+        if plane >= BLOCK:
+            return above[f, plane - BLOCK, rows, :]
+        return (state_low, state_high)[plane // 4][f, plane % 4, rows, :]
+
+    return get
+
+
+def first_kernel(
+    state_low, state_high, sides, below, above, speed, middle_low, middle_high, low, high
+):
     half_speed = 0.5 * speed[0:1, :]
     factor = (courant / 6.0) / speed[0:1, :]
-
-    def group(j, best):
+    middle = (middle_low, middle_high)
+
+    def group(j, carry):
         rows = pl.ds(pl.multiple_of(j * 8, 8), 8)
-
-        def get(f, plane):
-            if plane < 0:
-                return below[f, plane + 3, rows, :]
-            if plane >= BLOCK:
-                return above[f, plane - BLOCK, rows, :]
-            return state[f, plane, rows, :]
-
+        get = slab(state_low, state_high, below, above, rows)
         for field, along_x in across(get, half_speed):
             for plane in range(BLOCK):
                 total = along_x[plane] + sides[field, plane, rows, :]
                 value = get(field, plane) - factor * total
-                middle[field, plane, rows, :] = value
+                middle[plane // 4][field, plane % 4, rows, :] = value
                 if plane < 3:
                     low[field, plane, rows, :] = value
                 if plane >= 5:
                     high[field, plane - 5, rows, :] = value
-        for plane in range(BLOCK):
-            best = jnp.maximum(
-                best, wave_speed([middle[f, plane, rows, :] for f in range(FIELDS)])
-            )
-        return best
-
-    best = lax.fori_loop(0, 4, group, jnp.zeros((8, LANES), jnp.float32))
-    top[...] = jnp.full((8, LANES), jnp.max(best), jnp.float32)
+        return carry
+
+    lax.fori_loop(0, 4, group, 0)
 
 
 def first_stage(*operands):
-    whole = jax.ShapeDtypeStruct((FIELDS, BLOCK, ROWS, LANES), jnp.float32)
+    part = jax.ShapeDtypeStruct((FIELDS, 4, ROWS, LANES), jnp.float32)
     halo = jax.ShapeDtypeStruct((FIELDS, 3, ROWS, LANES), jnp.float32)
     return pl.pallas_call(
         first_kernel,
-        out_shape=(whole, halo, halo, jax.ShapeDtypeStruct((8, LANES), jnp.float32)),
+        out_shape=(part, part, halo, halo),
         in_specs=[VMEM] * len(operands),
         out_specs=(VMEM,) * 4,
         compiler_params=params(),
@@ -467,7 +463,31 @@
     )(*operands)
 
 
-def second_kernel(start, middle, sides, below, above, first_speed, speed, out):
+def fastest_kernel(middle_low, middle_high, top):
+    best = jnp.zeros((8, LANES), jnp.float32)
+    for part in (middle_low, middle_high):
+        for plane in range(4):
+            for row in range(0, ROWS, 8):
+                fields = [part[f, plane, row : row + 8, :] for f in range(FIELDS)]
+                best = jnp.maximum(best, wave_speed(fields))
+    top[...] = jnp.full(top.shape, jnp.max(best), jnp.float32)
+
+
+def fastest(*parts):
+    return pl.pallas_call(
+        fastest_kernel,
+        out_shape=jax.ShapeDtypeStruct((8, LANES), jnp.float32),
+        in_specs=[VMEM] * 2,
+        out_specs=VMEM,
+        compiler_params=params(),
+        cost_estimate=cost(1_000_000_000, 100_000_000),
+        name="fastest",
+    )(*parts)
+
+
+def second_kernel(
+    state_low, state_high, middle_low, middle_high, sides, below, above, first_speed, speed, out
+):
     half_speed = 0.5 * speed[0:1, :]
     factor = (courant / 12.0) / first_speed[0:1, :]
 
@@ -475,19 +495,12 @@
         rows = pl.ds(pl.multiple_of(j * 8, 8), 8)
         spread = pl.ds(j, 8, stride=4)
 
-        def get(f, plane):
-            if plane < 0:
-                return below[f, plane + 3, rows, :]
-            if plane >= BLOCK:
-                return above[f, plane - BLOCK, rows, :]
-            return middle[f, plane, rows, :]
-
+        get = slab(middle_low, middle_high, below, above, rows)
         for field, along_x in across(get, half_speed):
             for plane in range(BLOCK):
                 total = along_x[plane] + sides[field, plane, rows, :]
-                value = 0.5 * start[field, plane, rows, :] + (
-                    0.5 * get(field, plane) - factor * total
-                )
+                start = (state_low, state_high)[plane // 4][field, plane % 4, rows, :]
+                value = 0.5 * start + (0.5 * get(field, plane) - factor * total)
                 out[field, plane, spread, :] = value
         return carry
 
@@ -534,16 +547,19 @@
     parts, owner_list, slot_list = lax.optimization_barrier((parts, owner_list, slot_list))
     come = lax.all_to_all(parts, "gx", split_axis=0, concat_axis=0, tiled=True)
     table = arrival_spots(owner_list, slot_list, own, per_dev, size, cap)
-    state, low, high, speed = unpack(table, come.reshape(-1, LANES), size, cap)
+    come = come.reshape(-1, LANES)
+    state_low, low, speed = unpack(table, come, 0, size, cap)
+    above = lax.ppermute(low, "gx", down)
+    state_high, high = unpack(table, come, 1, size, cap)
+    below = lax.ppermute(high, "gx", up)
+    state = (state_low, state_high)
+    sides = along_planes(*state, speed)
+    *middle, low, high = first_stage(*state, sides, below, above, speed)
     below = lax.ppermute(high, "gx", up)
     above = lax.ppermute(low, "gx", down)
-    sides = along_planes(state, speed)
-    middle, low, high, top = first_stage(state, sides, below, above, speed)
-    second = everyone_max(top, "gx", size)
-    below = lax.ppermute(high, "gx", up)
-    above = lax.ppermute(low, "gx", down)
-    sides = along_planes(middle, second)
-    return second_stage(state, middle, sides, below, above, speed, second)
+    second = everyone_max(fastest(*middle), "gx", size)
+    sides = along_planes(*middle, second)
+    return second_stage(*state, *middle, sides, below, above, speed, second)
 
 
 def solution(mesh):

time: 74.1 us -> 74.1 us (level)
    pallas_call x4 -> x6, Pallas kernels: 13.4 us -> 13.3 us  [the longest x2 7.94 us: along_planes(): pl.pallas_call(plane_kernel, out_shape=jax.ShapeDtypeStruct((FIELDS, BLOC...]
  transfers between devices with their start and end apart: 11 -> 11, of which waited for: 3 -> 2; matrix products, arithmetic and copies ran while one was open for 1% -> 1% of each run, Pallas kernels for 11% -> 11%
where the time goes in v13:
time: 74.1 us; the launch traced here: 73.9 us
  waiting for transfers between devices  28.9 us (39%)
  starting transfers between devices  24.9 us (34%)
  Pallas kernels  19.2 us (26%)
    all_to_all x1, waiting for transfers between devices, per_device(): come = lax.all_to_all(parts, 'gx', split_axis=0, concat_axis=0, tiled=True)  26.8 us
    ppermute x2, starting transfers between devices, per_device(): above = lax.ppermute(low, 'gx', down)  10.3 us
    pallas_call x2, Pallas kernels, along_planes(): pl.pallas_call(plane_kernel, out_shape=jax.ShapeDtypeStruct((FIELDS, BLOC...  7.94 us
    all_to_all x1, starting transfers between devices, per_device(): come = lax.all_to_all(parts, 'gx', split_axis=0, concat_axis=0, tiled=True)  7.37 us
    ppermute x6, starting transfers between devices, everyone_max(): copies.append(lax.ppermute(value, axis, pairs))  6.36 us
    pallas_call x1, Pallas kernels, second_stage(): pl.pallas_call(second_kernel, out_shape=jax.ShapeDtypeStruct((FIELDS, BLO...  3.16 us
    pallas_call x2, Pallas kernels, unpack(): pl.pallas_call(functools.partial(unpack_kernel, size, cap, couple), out_s...  2.89 us
    pallas_call x1, Pallas kernels, pack(): pl.pallas_call(functools.partial(pack_kernel, size, cap, per_dev), out_sh...  2.73 us
  transfers between devices with their start and end apart: 11, of which 2 were waited for; matrix products, arithmetic and copies ran while one was open for 1% of the time, Pallas kernels for 11%

profile of v13, /device:TPU:0, one launch (start us, length us, event | category | flops | bytes accessed | tf_op | source)
XLA Modules:
  0.0 73.9 jit_solution(11530199030389827402)
XLA Ops:
  0.0 2.7 %pack.1 = f32[16,161,1,128]{3,2,1,0:T(1,128)} custom-call(s32[1024]{0:T(1024)} %owner_hbm.1, f32[1280,128]{1,0:T(8,128)} %bitcast.8), custom_call_target="tpu_custom_call" | custom-call | flops 1000000 | bytes 3000000 | tf_op jit(solution)/shard_map/pack/pallas_call | solution.py:110
  2.8 7.4 %all-to-all-start = ((f32[16,161,1,128]{3,2,1,0:T(1,128)}), f32[16,161,1,128]{3,2,1,0:T(1,128)S(1)}, u32[]{:S(2)}, u32[]{:S(2)}) async-start(f32[16,161,1,128]{3,2,1,0:T(1,128)} %pack.1), calls=%async_computation | async-start | bytes 2637824 | tf_op jit(solution)/shard_map/all_to_all | solution.py:548
  10.2 0.1 eq.33
  10.3 0.3 convert_reduce_fusion
  10.6 0.1 broadcast_add_fusion
  10.7 0.1 add.17
  10.8 0.1 select_reduce_fusion.table
  10.9 26.8 %all-to-all-done = f32[16,161,1,128]{3,2,1,0:T(1,128)S(1)} async-done(((f32[16,161,1,128]{3,2,1,0:T(1,128)}), f32[16,161,1,128]{3,2,1,0:T(1,128)S(1)}, u32[]{:S(2)}, u32[]{:S(2)}) %all-to-all-start) | async-done | bytes 1318944 | tf_op jit(solution)/shard_map/all_to_all | solution.py:548
  37.7 1.4 %unpack.3 = (f32[5,4,32,128]{3,2,1,0:T(8,128)S(1)}, f32[5,3,32,128]{3,2,1,0:T(8,128)S(1)}) custom-call(s32[64]{0:T(128)S(1)} %select_reduce_fusion.table, f32[2576,128]{1,0:T(8,128)S(1)} %bitcast.6), custom_call_target="tpu_custom_call" | custom-call | flops 5000000 | bytes 2000000 | tf_op jit(solution)/shard_map/unpack/pallas_call | solution.py:205
  39.1 1.4 %unpack.2 = (f32[5,4,32,128]{3,2,1,0:T(8,128)S(1)}, f32[5,3,32,128]{3,2,1,0:T(8,128)S(1)}, f32[8,128]{1,0:T(8,128)S(1)}) custom-call(s32[64]{0:T(128)S(1)} %select_reduce_fusion.table, f32[2576,128]{1,0:T(8,128)S(1)} %bitcast.7), custom_call_target="tpu_custom_call" | custom-call | flops 5000000 | bytes 2000000 | tf_op jit(solution)/shard_map/unpack/pallas_call | solution.py:205
  40.6 0.8 %collective-permute-start = (f32[5,3,32,128]{3,2,1,0:T(8,128)S(1)}, f32[5,3,32,128]{3,2,1,0:T(8,128)S(1)}, u32[]{:S(2)}, u32[]{:S(2)}) collective-permute-start(f32[5,3,32,128]{3,2,1,0:T(8,128)S(1)} %get-tuple-element.23), channel_id=1, source_target_pairs={{0,1},{1,2},{2,3},{3,4},{4,5},{5,6},{6,7},{7,8},{8,9},{9,10},{10,1... | collective-permute-start | bytes 737288 | tf_op jit(solution)/shard_map/ppermute | solution.py:554
  41.4 5.9 %collective-permute-start.1 = (f32[5,3,32,128]{3,2,1,0:T(8,128)S(1)}, f32[5,3,32,128]{3,2,1,0:T(8,128)S(1)}, u32[]{:S(2)}, u32[]{:S(2)}) collective-permute-start(f32[5,3,32,128]{3,2,1,0:T(8,128)S(1)} %get-tuple-element.24), channel_id=1, source_target_pairs={{1,0},{2,1},{3,2},{4,3},{5,4},{6,5},{7,6},{8,7},{9,8},{10,9},{11,1... | collective-permute-start | bytes 737288 | tf_op jit(solution)/shard_map/ppermute | solution.py:552
  47.3 4.0 %planes.2.sides = f32[5,8,32,128]{3,2,1,0:T(8,128)S(1)} custom-call(f32[5,4,32,128]{3,2,1,0:T(8,128)S(1)} %get-tuple-element.20.state_low, f32[5,4,32,128]{3,2,1,0:T(8,128)S(1)} %get-tuple-element.21.state_high, f32[8,128]{1,0:T(8,128)S(1)} %get-tuple-element.22.speed.first_speed), custom_call_target="tpu_custom_call" | custom-call | flops 20000000 | bytes 1000000 | tf_op jit(solution)/shard_map/planes/pallas_call | solution.py:382
  51.3 2.3 %first_stage.1 = (f32[5,4,32,128]{3,2,1,0:T(8,128)S(1)}, f32[5,4,32,128]{3,2,1,0:T(8,128)S(1)}, f32[5,3,32,128]{3,2,1,0:T(8,128)S(1)}, f32[5,3,32,128]{3,2,1,0:T(8,128)S(1)}) custom-call(f32[5,4,32,128]{3,2,1,0:T(8,128)S(1)} %get-tuple-element.20.state_low, f32[5,4,32,128]{3,2,1,0:T(8,128)S(1)} %get-tuple-element.21.state_high, ...), custom_call_target="tpu_custom_call" | custom-call | flops 30000000 | bytes 3000000 | tf_op jit(solution)/shard_map/first_stage/pallas_call | solution.py:455
  53.5 0.2 fastest.1
  53.8 0.1 collective-permute-start.4
  53.9 2.3 %collective-permute-start.3 = (f32[8,128]{1,0:T(8,128)S(1)}, f32[8,128]{1,0:T(8,128)S(1)}, u32[]{:S(2)}, u32[]{:S(2)}) collective-permute-start(f32[8,128]{1,0:T(8,128)S(1)} %fastest.1), channel_id=1, source_target_pairs={{0,8},{1,9},{2,10},{3,11},{4,12},{5,13},{6,14},{7,15},{8,0},{9,1},... | collective-permute-start | bytes 12296 | tf_op jit(solution)/shard_map/ppermute | solution.py:532
  56.2 2.1 %collective-permute-start.2 = (f32[8,128]{1,0:T(8,128)S(1)}, f32[8,128]{1,0:T(8,128)S(1)}, u32[]{:S(2)}, u32[]{:S(2)}) collective-permute-start(f32[8,128]{1,0:T(8,128)S(1)} %fastest.1), channel_id=1, source_target_pairs={{0,4},{1,5},{2,6},{3,7},{4,0},{5,1},{6,2},{7,3},{8,12},{9,13},{10,... | collective-permute-start | bytes 12296 | tf_op jit(solution)/shard_map/ppermute | solution.py:532
  58.2 4.4 %collective-permute-start.9 = (f32[5,3,32,128]{3,2,1,0:T(8,128)S(1)}, f32[5,3,32,128]{3,2,1,0:T(8,128)S(1)}, u32[]{:S(2)}, u32[]{:S(2)}) collective-permute-start(f32[5,3,32,128]{3,2,1,0:T(8,128)S(1)} %get-tuple-element.28), channel_id=1, source_target_pairs={{1,0},{2,1},{3,2},{4,3},{5,4},{6,5},{7,6},{8,7},{9,8},{10,9},{11,1... | collective-permute-start | bytes 737288 | tf_op jit(solution)/shard_map/ppermute | solution.py:559
  62.7 0.1 collective-permute-start.7
  62.9 1.8 %collective-permute-start.5 = (f32[8,128]{1,0:T(8,128)S(1)}, f32[8,128]{1,0:T(8,128)S(1)}, u32[]{:S(2)}, u32[]{:S(2)}) collective-permute-start(f32[8,128]{1,0:T(8,128)S(1)} %maximum_maximum_fusion.1), channel_id=1, source_target_pairs={{0,1},{1,0},{2,3},{3,2},{4,5},{5,4},{6,7},{7,6},{8,9},{9,8},{10,11... | collective-permute-start | bytes 12296 | tf_op jit(solution)/shard_map/ppermute | solution.py:532
  64.6 2.1 %collective-permute-done.7 = f32[8,128]{1,0:T(8,128)S(1)} collective-permute-done((f32[8,128]{1,0:T(8,128)S(1)}, f32[8,128]{1,0:T(8,128)S(1)}, u32[]{:S(2)}, u32[]{:S(2)}) %collective-permute-start.7) | collective-permute-done | bytes 4128 | tf_op jit(solution)/shard_map/ppermute | solution.py:532
  66.8 4.0 %planes.3.sides = f32[5,8,32,128]{3,2,1,0:T(8,128)S(1)} custom-call(f32[5,4,32,128]{3,2,1,0:T(8,128)S(1)} %get-tuple-element.25.middle_low.state_low, f32[5,4,32,128]{3,2,1,0:T(8,128)S(1)} %get-tuple-element.26.middle_high.state_high, f32[8,128]{1,0:T(8,128)S(1)} %maximum_maximum_fusion.speed), custom_call_target="tpu_custom_call" | custom-call | flops 20000000 | bytes 1000000 | tf_op jit(solution)/shard_map/planes/pallas_call | solution.py:382
  70.8 3.2 %second_stage.1 = f32[5,8,32,128]{3,2,1,0:T(8,128)} custom-call(f32[5,4,32,128]{3,2,1,0:T(8,128)S(1)} %get-tuple-element.20.state_low, f32[5,4,32,128]{3,2,1,0:T(8,128)S(1)} %get-tuple-element.21.state_high, f32[5,4,32,128]{3,2,1,0:T(8,128)S(1)} %get-tuple-element.25.middle_low.state_low, f32[5,4,32,128]{3,2,1,0:T(8,128)S(1)} %get-tuple-element.26.middle_high.state_high, ...), custom_call_target="tpu_custom_call" | custom-call | flops 30000000 | bytes 3000000 | tf_op jit(solution)/shard_map/second_stage/pallas_call | solution.py:511
  (20 shorter events, 0.1 us)
Async XLA Ops:
  2.7 7.4 %copy-start = (s32[1024]{0:T(1024)S(1)}, s32[1024]{0:T(1024)}, u32[]{:S(2)}) copy-start(s32[1024]{0:T(1024)} %owner_hbm.1) | copy-start | bytes 12292
  2.7 7.4 %copy-start.1 = (s32[1024]{0:T(1024)S(1)}, s32[1024]{0:T(1024)}, u32[]{:S(2)}) copy-start(s32[1024]{0:T(1024)} %param.5) | copy-start | bytes 12292
  2.8 34.9 %all-to-all-start = ((f32[16,161,1,128]{3,2,1,0:T(1,128)}), f32[16,161,1,128]{3,2,1,0:T(1,128)S(1)}, u32[]{:S(2)}, u32[]{:S(2)}) async-start(f32[16,161,1,128]{3,2,1,0:T(1,128)} %pack.1), calls=%async_computation | async-start | bytes 2637824 | tf_op jit(solution)/shard_map/all_to_all | solution.py:548
  40.6 10.7 %collective-permute-start = (f32[5,3,32,128]{3,2,1,0:T(8,128)S(1)}, f32[5,3,32,128]{3,2,1,0:T(8,128)S(1)}, u32[]{:S(2)}, u32[]{:S(2)}) collective-permute-start(f32[5,3,32,128]{3,2,1,0:T(8,128)S(1)} %get-tuple-element.23), channel_id=1, source_target_pairs={{0,1},{1,2},{2,3},{3,4},{4,5},{5,6},{6,7},{7,8},{8,9},{9,10},{10,1... | collective-permute-start | bytes 737288 | tf_op jit(solution)/shard_map/ppermute | solution.py:554
  41.4 9.8 %collective-permute-start.1 = (f32[5,3,32,128]{3,2,1,0:T(8,128)S(1)}, f32[5,3,32,128]{3,2,1,0:T(8,128)S(1)}, u32[]{:S(2)}, u32[]{:S(2)}) collective-permute-start(f32[5,3,32,128]{3,2,1,0:T(8,128)S(1)} %get-tuple-element.24), channel_id=1, source_target_pairs={{1,0},{2,1},{3,2},{4,3},{5,4},{6,5},{7,6},{8,7},{9,8},{10,9},{11,1... | collective-permute-start | bytes 737288 | tf_op jit(solution)/shard_map/ppermute | solution.py:552
  53.8 8.9 %collective-permute-start.4 = (f32[8,128]{1,0:T(8,128)S(1)}, f32[8,128]{1,0:T(8,128)S(1)}, u32[]{:S(2)}, u32[]{:S(2)}) collective-permute-start(f32[8,128]{1,0:T(8,128)S(1)} %fastest.1), channel_id=1, source_target_pairs={{0,12},{1,13},{2,14},{3,15},{4,8},{5,9},{6,10},{7,11},{8,4},{9,5},... | collective-permute-start | bytes 12296 | tf_op jit(solution)/shard_map/ppermute | solution.py:532
  53.9 8.8 %collective-permute-start.3 = (f32[8,128]{1,0:T(8,128)S(1)}, f32[8,128]{1,0:T(8,128)S(1)}, u32[]{:S(2)}, u32[]{:S(2)}) collective-permute-start(f32[8,128]{1,0:T(8,128)S(1)} %fastest.1), channel_id=1, source_target_pairs={{0,8},{1,9},{2,10},{3,11},{4,12},{5,13},{6,14},{7,15},{8,0},{9,1},... | collective-permute-start | bytes 12296 | tf_op jit(solution)/shard_map/ppermute | solution.py:532
  56.2 6.5 %collective-permute-start.2 = (f32[8,128]{1,0:T(8,128)S(1)}, f32[8,128]{1,0:T(8,128)S(1)}, u32[]{:S(2)}, u32[]{:S(2)}) collective-permute-start(f32[8,128]{1,0:T(8,128)S(1)} %fastest.1), channel_id=1, source_target_pairs={{0,4},{1,5},{2,6},{3,7},{4,0},{5,1},{6,2},{7,3},{8,12},{9,13},{10,... | collective-permute-start | bytes 12296 | tf_op jit(solution)/shard_map/ppermute | solution.py:532
  58.2 12.5 %collective-permute-start.8 = (f32[5,3,32,128]{3,2,1,0:T(8,128)S(1)}, f32[5,3,32,128]{3,2,1,0:T(8,128)S(1)}, u32[]{:S(2)}, u32[]{:S(2)}) collective-permute-start(f32[5,3,32,128]{3,2,1,0:T(8,128)S(1)} %get-tuple-element.27), channel_id=1, source_target_pairs={{0,1},{1,2},{2,3},{3,4},{4,5},{5,6},{6,7},{7,8},{8,9},{9,10},{10,1... | collective-permute-start | bytes 737288 | tf_op jit(solution)/shard_map/ppermute | solution.py:558
  58.2 12.5 %collective-permute-start.9 = (f32[5,3,32,128]{3,2,1,0:T(8,128)S(1)}, f32[5,3,32,128]{3,2,1,0:T(8,128)S(1)}, u32[]{:S(2)}, u32[]{:S(2)}) collective-permute-start(f32[5,3,32,128]{3,2,1,0:T(8,128)S(1)} %get-tuple-element.28), channel_id=1, source_target_pairs={{1,0},{2,1},{3,2},{4,3},{5,4},{6,5},{7,6},{8,7},{9,8},{10,9},{11,1... | collective-permute-start | bytes 737288 | tf_op jit(solution)/shard_map/ppermute | solution.py:559
  62.7 4.0 %collective-permute-start.7 = (f32[8,128]{1,0:T(8,128)S(1)}, f32[8,128]{1,0:T(8,128)S(1)}, u32[]{:S(2)}, u32[]{:S(2)}) collective-permute-start(f32[8,128]{1,0:T(8,128)S(1)} %maximum_maximum_fusion.1), channel_id=1, source_target_pairs={{0,3},{1,2},{2,1},{3,0},{4,7},{5,6},{6,5},{7,4},{8,11},{9,10},{10,... | collective-permute-start | bytes 12296 | tf_op jit(solution)/shard_map/ppermute | solution.py:532
  62.8 4.0 %collective-permute-start.6 = (f32[8,128]{1,0:T(8,128)S(1)}, f32[8,128]{1,0:T(8,128)S(1)}, u32[]{:S(2)}, u32[]{:S(2)}) collective-permute-start(f32[8,128]{1,0:T(8,128)S(1)} %maximum_maximum_fusion.1), channel_id=1, source_target_pairs={{0,2},{1,3},{2,0},{3,1},{4,6},{5,7},{6,4},{7,5},{8,10},{9,11},{10,... | collective-permute-start | bytes 12296 | tf_op jit(solution)/shard_map/ppermute | solution.py:532
  62.9 3.9 %collective-permute-start.5 = (f32[8,128]{1,0:T(8,128)S(1)}, f32[8,128]{1,0:T(8,128)S(1)}, u32[]{:S(2)}, u32[]{:S(2)}) collective-permute-start(f32[8,128]{1,0:T(8,128)S(1)} %maximum_maximum_fusion.1), channel_id=1, source_target_pairs={{0,1},{1,0},{2,3},{3,2},{4,5},{5,4},{6,7},{7,6},{8,9},{9,8},{10,11... | collective-permute-start | bytes 12296 | tf_op jit(solution)/shard_map/ppermute | solution.py:532

commit v14 on v13

--- a/solution.py
+++ b/solution.py
@@ -209,7 +209,7 @@
         out_specs=[VMEM] * len(shapes),
         scratch_shapes=[pltpu.VMEM((FIELDS * BZ * 8, LANES), jnp.float32)],
         compiler_params=params(),
-        cost_estimate=cost(5_000_000, 2_000_000),
+        cost_estimate=cost(1_000_000_000, 100_000_000),
         name="unpack",
     )(table, come)
 
@@ -386,7 +386,7 @@
         out_specs=VMEM,
         scratch_shapes=[pltpu.VMEM((FIELDS, LANES, LANES), jnp.float32)],
         compiler_params=params(),
-        cost_estimate=cost(20_000_000, 1_000_000),
+        cost_estimate=cost(1, 1),
         name="planes",
     )(state_low, state_high, speed)
 

time: 74.1 us -> 74.1 us (level)
  no operation moved by 1% of the time
where the time goes in v14:
time: 74.1 us; the launch traced here: 73.9 us
  waiting for transfers between devices  28.9 us (39%)
  starting transfers between devices  24.9 us (34%)
  Pallas kernels  19.2 us (26%)
    all_to_all x1, waiting for transfers between devices, per_device(): come = lax.all_to_all(parts, 'gx', split_axis=0, concat_axis=0, tiled=True)  26.8 us
    ppermute x2, starting transfers between devices, per_device(): above = lax.ppermute(low, 'gx', down)  10.3 us
    pallas_call x2, Pallas kernels, along_planes(): pl.pallas_call(plane_kernel, out_shape=jax.ShapeDtypeStruct((FIELDS, BLOC...  7.94 us
    all_to_all x1, starting transfers between devices, per_device(): come = lax.all_to_all(parts, 'gx', split_axis=0, concat_axis=0, tiled=True)  7.37 us
    ppermute x6, starting transfers between devices, everyone_max(): copies.append(lax.ppermute(value, axis, pairs))  6.36 us
    pallas_call x1, Pallas kernels, second_stage(): pl.pallas_call(second_kernel, out_shape=jax.ShapeDtypeStruct((FIELDS, BLO...  3.16 us
    pallas_call x2, Pallas kernels, unpack(): pl.pallas_call(functools.partial(unpack_kernel, size, cap, couple), out_s...  2.89 us
    pallas_call x1, Pallas kernels, pack(): pl.pallas_call(functools.partial(pack_kernel, size, cap, per_dev), out_sh...  2.73 us
  transfers between devices with their start and end apart: 11, of which 2 were waited for; matrix products, arithmetic and copies ran while one was open for 1% of the time, Pallas kernels for 11%

profile of v14, /device:TPU:0, one launch (start us, length us, event | category | flops | bytes accessed | tf_op | source)
XLA Modules:
  0.0 73.9 jit_solution(11530199030389827402)
XLA Ops:
  0.0 2.7 %pack.1 = f32[16,161,1,128]{3,2,1,0:T(1,128)} custom-call(s32[1024]{0:T(1024)} %owner_hbm.1, f32[1280,128]{1,0:T(8,128)} %bitcast.8), custom_call_target="tpu_custom_call" | custom-call | flops 1000000 | bytes 3000000 | tf_op jit(solution)/shard_map/pack/pallas_call | solution.py:110
  2.8 7.4 %all-to-all-start = ((f32[16,161,1,128]{3,2,1,0:T(1,128)}), f32[16,161,1,128]{3,2,1,0:T(1,128)S(1)}, u32[]{:S(2)}, u32[]{:S(2)}) async-start(f32[16,161,1,128]{3,2,1,0:T(1,128)} %pack.1), calls=%async_computation | async-start | bytes 2637824 | tf_op jit(solution)/shard_map/all_to_all | solution.py:548
  10.2 0.1 eq.33
  10.3 0.3 convert_reduce_fusion
  10.6 0.1 broadcast_add_fusion
  10.7 0.1 add.17
  10.8 0.1 select_reduce_fusion.table
  10.9 26.8 %all-to-all-done = f32[16,161,1,128]{3,2,1,0:T(1,128)S(1)} async-done(((f32[16,161,1,128]{3,2,1,0:T(1,128)}), f32[16,161,1,128]{3,2,1,0:T(1,128)S(1)}, u32[]{:S(2)}, u32[]{:S(2)}) %all-to-all-start) | async-done | bytes 1318944 | tf_op jit(solution)/shard_map/all_to_all | solution.py:548
  37.7 1.4 %unpack.3 = (f32[5,4,32,128]{3,2,1,0:T(8,128)S(1)}, f32[5,3,32,128]{3,2,1,0:T(8,128)S(1)}) custom-call(s32[64]{0:T(128)S(1)} %select_reduce_fusion.table, f32[2576,128]{1,0:T(8,128)S(1)} %bitcast.6), custom_call_target="tpu_custom_call" | custom-call | flops 1000000000 | bytes 100000000 | tf_op jit(solution)/shard_map/unpack/pallas_call | solution.py:205
  39.1 1.4 %unpack.2 = (f32[5,4,32,128]{3,2,1,0:T(8,128)S(1)}, f32[5,3,32,128]{3,2,1,0:T(8,128)S(1)}, f32[8,128]{1,0:T(8,128)S(1)}) custom-call(s32[64]{0:T(128)S(1)} %select_reduce_fusion.table, f32[2576,128]{1,0:T(8,128)S(1)} %bitcast.7), custom_call_target="tpu_custom_call" | custom-call | flops 1000000000 | bytes 100000000 | tf_op jit(solution)/shard_map/unpack/pallas_call | solution.py:205
  40.6 0.8 %collective-permute-start = (f32[5,3,32,128]{3,2,1,0:T(8,128)S(1)}, f32[5,3,32,128]{3,2,1,0:T(8,128)S(1)}, u32[]{:S(2)}, u32[]{:S(2)}) collective-permute-start(f32[5,3,32,128]{3,2,1,0:T(8,128)S(1)} %get-tuple-element.23), channel_id=1, source_target_pairs={{0,1},{1,2},{2,3},{3,4},{4,5},{5,6},{6,7},{7,8},{8,9},{9,10},{10,1... | collective-permute-start | bytes 737288 | tf_op jit(solution)/shard_map/ppermute | solution.py:554
  41.4 5.9 %collective-permute-start.1 = (f32[5,3,32,128]{3,2,1,0:T(8,128)S(1)}, f32[5,3,32,128]{3,2,1,0:T(8,128)S(1)}, u32[]{:S(2)}, u32[]{:S(2)}) collective-permute-start(f32[5,3,32,128]{3,2,1,0:T(8,128)S(1)} %get-tuple-element.24), channel_id=1, source_target_pairs={{1,0},{2,1},{3,2},{4,3},{5,4},{6,5},{7,6},{8,7},{9,8},{10,9},{11,1... | collective-permute-start | bytes 737288 | tf_op jit(solution)/shard_map/ppermute | solution.py:552
  47.3 4.0 %planes.2.sides = f32[5,8,32,128]{3,2,1,0:T(8,128)S(1)} custom-call(f32[5,4,32,128]{3,2,1,0:T(8,128)S(1)} %get-tuple-element.20.state_low, f32[5,4,32,128]{3,2,1,0:T(8,128)S(1)} %get-tuple-element.21.state_high, f32[8,128]{1,0:T(8,128)S(1)} %get-tuple-element.22.speed.first_speed), custom_call_target="tpu_custom_call" | custom-call | flops 1 | bytes 1 | tf_op jit(solution)/shard_map/planes/pallas_call | solution.py:382
  51.3 2.3 %first_stage.1 = (f32[5,4,32,128]{3,2,1,0:T(8,128)S(1)}, f32[5,4,32,128]{3,2,1,0:T(8,128)S(1)}, f32[5,3,32,128]{3,2,1,0:T(8,128)S(1)}, f32[5,3,32,128]{3,2,1,0:T(8,128)S(1)}) custom-call(f32[5,4,32,128]{3,2,1,0:T(8,128)S(1)} %get-tuple-element.20.state_low, f32[5,4,32,128]{3,2,1,0:T(8,128)S(1)} %get-tuple-element.21.state_high, ...), custom_call_target="tpu_custom_call" | custom-call | flops 30000000 | bytes 3000000 | tf_op jit(solution)/shard_map/first_stage/pallas_call | solution.py:455
  53.5 0.2 fastest.1
  53.8 0.1 collective-permute-start.4
  53.9 2.3 %collective-permute-start.3 = (f32[8,128]{1,0:T(8,128)S(1)}, f32[8,128]{1,0:T(8,128)S(1)}, u32[]{:S(2)}, u32[]{:S(2)}) collective-permute-start(f32[8,128]{1,0:T(8,128)S(1)} %fastest.1), channel_id=1, source_target_pairs={{0,8},{1,9},{2,10},{3,11},{4,12},{5,13},{6,14},{7,15},{8,0},{9,1},... | collective-permute-start | bytes 12296 | tf_op jit(solution)/shard_map/ppermute | solution.py:532
  56.2 2.1 %collective-permute-start.2 = (f32[8,128]{1,0:T(8,128)S(1)}, f32[8,128]{1,0:T(8,128)S(1)}, u32[]{:S(2)}, u32[]{:S(2)}) collective-permute-start(f32[8,128]{1,0:T(8,128)S(1)} %fastest.1), channel_id=1, source_target_pairs={{0,4},{1,5},{2,6},{3,7},{4,0},{5,1},{6,2},{7,3},{8,12},{9,13},{10,... | collective-permute-start | bytes 12296 | tf_op jit(solution)/shard_map/ppermute | solution.py:532
  58.2 4.4 %collective-permute-start.9 = (f32[5,3,32,128]{3,2,1,0:T(8,128)S(1)}, f32[5,3,32,128]{3,2,1,0:T(8,128)S(1)}, u32[]{:S(2)}, u32[]{:S(2)}) collective-permute-start(f32[5,3,32,128]{3,2,1,0:T(8,128)S(1)} %get-tuple-element.28), channel_id=1, source_target_pairs={{1,0},{2,1},{3,2},{4,3},{5,4},{6,5},{7,6},{8,7},{9,8},{10,9},{11,1... | collective-permute-start | bytes 737288 | tf_op jit(solution)/shard_map/ppermute | solution.py:559
  62.8 0.1 collective-permute-start.6
  62.9 1.8 %collective-permute-start.5 = (f32[8,128]{1,0:T(8,128)S(1)}, f32[8,128]{1,0:T(8,128)S(1)}, u32[]{:S(2)}, u32[]{:S(2)}) collective-permute-start(f32[8,128]{1,0:T(8,128)S(1)} %maximum_maximum_fusion.1), channel_id=1, source_target_pairs={{0,1},{1,0},{2,3},{3,2},{4,5},{5,4},{6,7},{7,6},{8,9},{9,8},{10,11... | collective-permute-start | bytes 12296 | tf_op jit(solution)/shard_map/ppermute | solution.py:532
  64.6 2.1 %collective-permute-done.7 = f32[8,128]{1,0:T(8,128)S(1)} collective-permute-done((f32[8,128]{1,0:T(8,128)S(1)}, f32[8,128]{1,0:T(8,128)S(1)}, u32[]{:S(2)}, u32[]{:S(2)}) %collective-permute-start.7) | collective-permute-done | bytes 4128 | tf_op jit(solution)/shard_map/ppermute | solution.py:532
  66.8 4.0 %planes.3.sides = f32[5,8,32,128]{3,2,1,0:T(8,128)S(1)} custom-call(f32[5,4,32,128]{3,2,1,0:T(8,128)S(1)} %get-tuple-element.25.middle_low.state_low, f32[5,4,32,128]{3,2,1,0:T(8,128)S(1)} %get-tuple-element.26.middle_high.state_high, f32[8,128]{1,0:T(8,128)S(1)} %maximum_maximum_fusion.speed), custom_call_target="tpu_custom_call" | custom-call | flops 1 | bytes 1 | tf_op jit(solution)/shard_map/planes/pallas_call | solution.py:382
  70.8 3.2 %second_stage.1 = f32[5,8,32,128]{3,2,1,0:T(8,128)} custom-call(f32[5,4,32,128]{3,2,1,0:T(8,128)S(1)} %get-tuple-element.20.state_low, f32[5,4,32,128]{3,2,1,0:T(8,128)S(1)} %get-tuple-element.21.state_high, f32[5,4,32,128]{3,2,1,0:T(8,128)S(1)} %get-tuple-element.25.middle_low.state_low, f32[5,4,32,128]{3,2,1,0:T(8,128)S(1)} %get-tuple-element.26.middle_high.state_high, ...), custom_call_target="tpu_custom_call" | custom-call | flops 30000000 | bytes 3000000 | tf_op jit(solution)/shard_map/second_stage/pallas_call | solution.py:511
  (20 shorter events, 0.1 us)
Async XLA Ops:
  2.7 7.4 %copy-start = (s32[1024]{0:T(1024)S(1)}, s32[1024]{0:T(1024)}, u32[]{:S(2)}) copy-start(s32[1024]{0:T(1024)} %owner_hbm.1) | copy-start | bytes 12292
  2.7 7.4 %copy-start.1 = (s32[1024]{0:T(1024)S(1)}, s32[1024]{0:T(1024)}, u32[]{:S(2)}) copy-start(s32[1024]{0:T(1024)} %param.5) | copy-start | bytes 12292
  2.8 34.9 %all-to-all-start = ((f32[16,161,1,128]{3,2,1,0:T(1,128)}), f32[16,161,1,128]{3,2,1,0:T(1,128)S(1)}, u32[]{:S(2)}, u32[]{:S(2)}) async-start(f32[16,161,1,128]{3,2,1,0:T(1,128)} %pack.1), calls=%async_computation | async-start | bytes 2637824 | tf_op jit(solution)/shard_map/all_to_all | solution.py:548
  40.6 10.7 %collective-permute-start = (f32[5,3,32,128]{3,2,1,0:T(8,128)S(1)}, f32[5,3,32,128]{3,2,1,0:T(8,128)S(1)}, u32[]{:S(2)}, u32[]{:S(2)}) collective-permute-start(f32[5,3,32,128]{3,2,1,0:T(8,128)S(1)} %get-tuple-element.23), channel_id=1, source_target_pairs={{0,1},{1,2},{2,3},{3,4},{4,5},{5,6},{6,7},{7,8},{8,9},{9,10},{10,1... | collective-permute-start | bytes 737288 | tf_op jit(solution)/shard_map/ppermute | solution.py:554
  41.4 9.8 %collective-permute-start.1 = (f32[5,3,32,128]{3,2,1,0:T(8,128)S(1)}, f32[5,3,32,128]{3,2,1,0:T(8,128)S(1)}, u32[]{:S(2)}, u32[]{:S(2)}) collective-permute-start(f32[5,3,32,128]{3,2,1,0:T(8,128)S(1)} %get-tuple-element.24), channel_id=1, source_target_pairs={{1,0},{2,1},{3,2},{4,3},{5,4},{6,5},{7,6},{8,7},{9,8},{10,9},{11,1... | collective-permute-start | bytes 737288 | tf_op jit(solution)/shard_map/ppermute | solution.py:552
  53.8 8.9 %collective-permute-start.4 = (f32[8,128]{1,0:T(8,128)S(1)}, f32[8,128]{1,0:T(8,128)S(1)}, u32[]{:S(2)}, u32[]{:S(2)}) collective-permute-start(f32[8,128]{1,0:T(8,128)S(1)} %fastest.1), channel_id=1, source_target_pairs={{0,12},{1,13},{2,14},{3,15},{4,8},{5,9},{6,10},{7,11},{8,4},{9,5},... | collective-permute-start | bytes 12296 | tf_op jit(solution)/shard_map/ppermute | solution.py:532
  53.9 8.8 %collective-permute-start.3 = (f32[8,128]{1,0:T(8,128)S(1)}, f32[8,128]{1,0:T(8,128)S(1)}, u32[]{:S(2)}, u32[]{:S(2)}) collective-permute-start(f32[8,128]{1,0:T(8,128)S(1)} %fastest.1), channel_id=1, source_target_pairs={{0,8},{1,9},{2,10},{3,11},{4,12},{5,13},{6,14},{7,15},{8,0},{9,1},... | collective-permute-start | bytes 12296 | tf_op jit(solution)/shard_map/ppermute | solution.py:532
  56.2 6.5 %collective-permute-start.2 = (f32[8,128]{1,0:T(8,128)S(1)}, f32[8,128]{1,0:T(8,128)S(1)}, u32[]{:S(2)}, u32[]{:S(2)}) collective-permute-start(f32[8,128]{1,0:T(8,128)S(1)} %fastest.1), channel_id=1, source_target_pairs={{0,4},{1,5},{2,6},{3,7},{4,0},{5,1},{6,2},{7,3},{8,12},{9,13},{10,... | collective-permute-start | bytes 12296 | tf_op jit(solution)/shard_map/ppermute | solution.py:532
  58.2 12.5 %collective-permute-start.8 = (f32[5,3,32,128]{3,2,1,0:T(8,128)S(1)}, f32[5,3,32,128]{3,2,1,0:T(8,128)S(1)}, u32[]{:S(2)}, u32[]{:S(2)}) collective-permute-start(f32[5,3,32,128]{3,2,1,0:T(8,128)S(1)} %get-tuple-element.27), channel_id=1, source_target_pairs={{0,1},{1,2},{2,3},{3,4},{4,5},{5,6},{6,7},{7,8},{8,9},{9,10},{10,1... | collective-permute-start | bytes 737288 | tf_op jit(solution)/shard_map/ppermute | solution.py:558
  58.2 12.5 %collective-permute-start.9 = (f32[5,3,32,128]{3,2,1,0:T(8,128)S(1)}, f32[5,3,32,128]{3,2,1,0:T(8,128)S(1)}, u32[]{:S(2)}, u32[]{:S(2)}) collective-permute-start(f32[5,3,32,128]{3,2,1,0:T(8,128)S(1)} %get-tuple-element.28), channel_id=1, source_target_pairs={{1,0},{2,1},{3,2},{4,3},{5,4},{6,5},{7,6},{8,7},{9,8},{10,9},{11,1... | collective-permute-start | bytes 737288 | tf_op jit(solution)/shard_map/ppermute | solution.py:559
  62.7 4.0 %collective-permute-start.7 = (f32[8,128]{1,0:T(8,128)S(1)}, f32[8,128]{1,0:T(8,128)S(1)}, u32[]{:S(2)}, u32[]{:S(2)}) collective-permute-start(f32[8,128]{1,0:T(8,128)S(1)} %maximum_maximum_fusion.1), channel_id=1, source_target_pairs={{0,3},{1,2},{2,1},{3,0},{4,7},{5,6},{6,5},{7,4},{8,11},{9,10},{10,... | collective-permute-start | bytes 12296 | tf_op jit(solution)/shard_map/ppermute | solution.py:532
  62.8 4.0 %collective-permute-start.6 = (f32[8,128]{1,0:T(8,128)S(1)}, f32[8,128]{1,0:T(8,128)S(1)}, u32[]{:S(2)}, u32[]{:S(2)}) collective-permute-start(f32[8,128]{1,0:T(8,128)S(1)} %maximum_maximum_fusion.1), channel_id=1, source_target_pairs={{0,2},{1,3},{2,0},{3,1},{4,6},{5,7},{6,4},{7,5},{8,10},{9,11},{10,... | collective-permute-start | bytes 12296 | tf_op jit(solution)/shard_map/ppermute | solution.py:532
  62.9 3.9 %collective-permute-start.5 = (f32[8,128]{1,0:T(8,128)S(1)}, f32[8,128]{1,0:T(8,128)S(1)}, u32[]{:S(2)}, u32[]{:S(2)}) collective-permute-start(f32[8,128]{1,0:T(8,128)S(1)} %maximum_maximum_fusion.1), channel_id=1, source_target_pairs={{0,1},{1,0},{2,3},{3,2},{4,5},{5,4},{6,7},{7,6},{8,9},{9,8},{10,11... | collective-permute-start | bytes 12296 | tf_op jit(solution)/shard_map/ppermute | solution.py:532

commit v15 on v11

--- a/solution.py
+++ b/solution.py
@@ -127,6 +127,28 @@
     )(owner_list, rows)
 
 
+def own_is_even():
+    return lax.axis_index("gx") % 2 == 0
+
+
+def swapped(far_side, near_side, size):
+    apart = [(i, (i - 1 if i % 2 == 0 else i + 1) % size) for i in range(size)]
+    chip = [(i, i ^ 1) for i in range(size)]
+    return lax.ppermute(far_side, "gx", apart), lax.ppermute(near_side, "gx", chip)
+
+
+def sort_halos(far, near, below, above):
+    lower_first = own_is_even()
+    for f in range(FIELDS):
+        for plane in range(3):
+            one, two = far[f, plane], near[f, plane]
+            below[f, plane] = jnp.where(lower_first, one, two)
+            above[f, plane] = jnp.where(lower_first, two, one)
+
+
+HALO = (FIELDS, 3, ROWS, LANES)
+
+
 def arrival_spots(owner_list, slot_list, own, per_dev, size, cap):
     owners = owner_list.reshape(size, per_dev)
     slots = slot_list.reshape(size, per_dev)
@@ -154,7 +176,7 @@
     return rows
 
 
-def unpack_kernel(size, cap, table, come, state, low_halo, high_halo, speed, scratch):
+def unpack_kernel(size, cap, table, come, state, far_side, near_side, speed, scratch):
     message = TILES * cap + 1
     best = come[message - 1 : message, :]
     for source in range(1, size):
@@ -191,14 +213,16 @@
                     for h in range(2):
                         plane = 4 * couple + 2 * h + second
                         state[f, plane, rows, :] = planes[h]
-                        if plane < 3:
-                            low_halo[f, plane, rows, :] = planes[h]
-                        if plane >= 5:
-                            high_halo[f, plane - 5, rows, :] = planes[h]
+    lower_first = own_is_even()
+    for f in range(FIELDS):
+        for plane in range(3):
+            low, high = state[f, plane], state[f, BLOCK - 3 + plane]
+            far_side[f, plane] = jnp.where(lower_first, low, high)
+            near_side[f, plane] = jnp.where(lower_first, high, low)
 
 
 def unpack(table, come, size, cap):
-    halo = jax.ShapeDtypeStruct((FIELDS, 3, ROWS, LANES), jnp.float32)
+    halo = jax.ShapeDtypeStruct(HALO, jnp.float32)
     return pl.pallas_call(
         functools.partial(unpack_kernel, size, cap),
         out_shape=(
@@ -420,7 +444,11 @@
         yield field, open_divergence(fluxes, scaled)
 
 
-def first_kernel(state, sides, below, above, speed, middle, low, high, top):
+def first_kernel(
+    state, sides, far, near, speed, middle, far_side, near_side, top, below, above
+):
+    sort_halos(far, near, below, above)
+    lower_first = own_is_even()
     half_speed = 0.5 * speed[0:1, :]
     factor = (courant / 6.0) / speed[0:1, :]
 
@@ -435,14 +463,15 @@
             return state[f, plane, rows, :]
 
         for field, along_x in across(get, half_speed):
+            values = []
             for plane in range(BLOCK):
                 total = along_x[plane] + sides[field, plane, rows, :]
-                value = get(field, plane) - factor * total
-                middle[field, plane, rows, :] = value
-                if plane < 3:
-                    low[field, plane, rows, :] = value
-                if plane >= 5:
-                    high[field, plane - 5, rows, :] = value
+                values.append(get(field, plane) - factor * total)
+                middle[field, plane, rows, :] = values[plane]
+            for plane in range(3):
+                low, high = values[plane], values[BLOCK - 3 + plane]
+                far_side[field, plane, rows, :] = jnp.where(lower_first, low, high)
+                near_side[field, plane, rows, :] = jnp.where(lower_first, high, low)
         for plane in range(BLOCK):
             best = jnp.maximum(
                 best, wave_speed([middle[f, plane, rows, :] for f in range(FIELDS)])
@@ -455,19 +484,21 @@
 
 def first_stage(*operands):
     whole = jax.ShapeDtypeStruct((FIELDS, BLOCK, ROWS, LANES), jnp.float32)
-    halo = jax.ShapeDtypeStruct((FIELDS, 3, ROWS, LANES), jnp.float32)
+    halo = jax.ShapeDtypeStruct(HALO, jnp.float32)
     return pl.pallas_call(
         first_kernel,
         out_shape=(whole, halo, halo, jax.ShapeDtypeStruct((8, LANES), jnp.float32)),
         in_specs=[VMEM] * len(operands),
         out_specs=(VMEM,) * 4,
+        scratch_shapes=[pltpu.VMEM(HALO, jnp.float32)] * 2,
         compiler_params=params(),
         cost_estimate=cost(30_000_000, 3_000_000),
         name="first_stage",
     )(*operands)
 
 
-def second_kernel(start, middle, sides, below, above, first_speed, speed, out):
+def second_kernel(start, middle, sides, far, near, first_speed, speed, out, below, above):
+    sort_halos(far, near, below, above)
     half_speed = 0.5 * speed[0:1, :]
     factor = (courant / 12.0) / first_speed[0:1, :]
 
@@ -500,6 +531,7 @@
         out_shape=jax.ShapeDtypeStruct((FIELDS, BLOCK, ROWS, LANES), jnp.float32),
         in_specs=[VMEM] * len(operands),
         out_specs=VMEM,
+        scratch_shapes=[pltpu.VMEM(HALO, jnp.float32)] * 2,
         compiler_params=params(),
         cost_estimate=cost(30_000_000, 3_000_000),
         name="second_stage",
@@ -527,23 +559,19 @@
     own = lax.axis_index("gx")
     per_dev = blocks.shape[0]
     cap = max(2, 2 * per_dev // size)
-    up = [(i, (i + 1) % size) for i in range(size)]
-    down = [(j, i) for i, j in up]
 
     parts = pack(tiled_rows(blocks), owner_list, size, cap, per_dev)
     parts, owner_list, slot_list = lax.optimization_barrier((parts, owner_list, slot_list))
     come = lax.all_to_all(parts, "gx", split_axis=0, concat_axis=0, tiled=True)
     table = arrival_spots(owner_list, slot_list, own, per_dev, size, cap)
-    state, low, high, speed = unpack(table, come.reshape(-1, LANES), size, cap)
-    below = lax.ppermute(high, "gx", up)
-    above = lax.ppermute(low, "gx", down)
+    state, far_side, near_side, speed = unpack(table, come.reshape(-1, LANES), size, cap)
+    far, near = swapped(far_side, near_side, size)
     sides = along_planes(state, speed)
-    middle, low, high, top = first_stage(state, sides, below, above, speed)
+    middle, far_side, near_side, top = first_stage(state, sides, far, near, speed)
+    far, near = swapped(far_side, near_side, size)
     second = everyone_max(top, "gx", size)
-    below = lax.ppermute(high, "gx", up)
-    above = lax.ppermute(low, "gx", down)
     sides = along_planes(middle, second)
-    return second_stage(state, middle, sides, below, above, speed, second)
+    return second_stage(state, middle, sides, far, near, speed, second)
 
 
 def solution(mesh):

time: 74.1 us -> 74.2 us (level)
  starting transfers between devices: 24.9 us -> 24.1 us
    ppermute x4, starting transfers between devices: 11.1 us -> 10 us  [the longest x2 10 us: swapped(): lax.ppermute(far_side, 'gx', apart)]
    ppermute x6, waiting for transfers between devices: 2.09 us -> 2.85 us  [everyone_max(): copies.append(lax.ppermute(value, axis, pairs))]
where the time goes in v15:
time: 74.2 us; the launch traced here: 74 us
  waiting for transfers between devices  29.6 us (40%)
  starting transfers between devices  24.1 us (32%)
  Pallas kernels  19.4 us (26%)
    all_to_all x1, waiting for transfers between devices, per_device(): come = lax.all_to_all(parts, 'gx', split_axis=0, concat_axis=0, tiled=True)  26.8 us
    ppermute x2, starting transfers between devices, swapped(): lax.ppermute(far_side, 'gx', apart)  10 us
    pallas_call x2, Pallas kernels, along_planes(): pl.pallas_call(plane_kernel, out_shape=jax.ShapeDtypeStruct(state.shape,...  8.11 us
    all_to_all x1, starting transfers between devices, per_device(): come = lax.all_to_all(parts, 'gx', split_axis=0, concat_axis=0, tiled=True)  7.37 us
    ppermute x6, starting transfers between devices, everyone_max(): copies.append(lax.ppermute(value, axis, pairs))  6.67 us
    pallas_call x1, Pallas kernels, second_stage(): pl.pallas_call(second_kernel, out_shape=jax.ShapeDtypeStruct((FIELDS, BLO...  3.2 us
    ppermute x6, waiting for transfers between devices, everyone_max(): copies.append(lax.ppermute(value, axis, pairs))  2.85 us
    pallas_call x1, Pallas kernels, unpack(): pl.pallas_call(functools.partial(unpack_kernel, size, cap), out_shape=(ja...  2.79 us
  transfers between devices with their start and end apart: 11, of which 3 were waited for; matrix products, arithmetic and copies ran while one was open for 1% of the time, Pallas kernels for 11%

profile of v15, /device:TPU:0, one launch (start us, length us, event | category | flops | bytes accessed | tf_op | source)
XLA Modules:
  0.0 74.0 jit_solution(11209408321304822674)
XLA Ops:
  0.0 2.7 %pack.1 = f32[16,161,1,128]{3,2,1,0:T(1,128)} custom-call(s32[1024]{0:T(1024)} %owner_hbm.1, f32[1280,128]{1,0:T(8,128)} %bitcast.7), custom_call_target="tpu_custom_call" | custom-call | flops 1000000 | bytes 3000000 | tf_op jit(solution)/shard_map/pack/pallas_call | solution.py:110
  2.7 0.0 copy-start
  2.8 0.0 copy-start.1
  2.8 7.4 %all-to-all-start = ((f32[16,161,1,128]{3,2,1,0:T(1,128)}), f32[16,161,1,128]{3,2,1,0:T(1,128)S(1)}, u32[]{:S(2)}, u32[]{:S(2)}) async-start(f32[16,161,1,128]{3,2,1,0:T(1,128)} %pack.1), calls=%async_computation | async-start | bytes 2637824 | tf_op jit(solution)/shard_map/all_to_all | solution.py:565
  10.2 0.1 eq.33
  10.3 0.3 convert_reduce_fusion
  10.6 0.1 broadcast_add_fusion
  10.7 0.1 add.17
  10.8 0.1 select_reduce_fusion.table
  10.9 26.8 %all-to-all-done = f32[16,161,1,128]{3,2,1,0:T(1,128)S(1)} async-done(((f32[16,161,1,128]{3,2,1,0:T(1,128)}), f32[16,161,1,128]{3,2,1,0:T(1,128)S(1)}, u32[]{:S(2)}, u32[]{:S(2)}) %all-to-all-start) | async-done | bytes 1318944 | tf_op jit(solution)/shard_map/all_to_all | solution.py:565
  37.7 2.8 %unpack.1 = (f32[5,8,32,128]{3,2,1,0:T(8,128)S(1)}, f32[5,3,32,128]{3,2,1,0:T(8,128)S(1)}, f32[5,3,32,128]{3,2,1,0:T(8,128)S(1)}, f32[8,128]{1,0:T(8,128)S(1)}) custom-call(s32[64]{0:T(128)S(1)} %select_reduce_fusion.table, f32[2576,128]{1,0:T(8,128)S(1)} %bitcast.6), custom_call_target="tpu_custom_call" | custom-call | flops 5000000 | bytes 2000000 | tf_op jit(solution)/shard_map/unpack/pallas_call | solution.py:226
  40.5 6.6 %collective-permute-start = (f32[5,3,32,128]{3,2,1,0:T(8,128)S(1)}, f32[5,3,32,128]{3,2,1,0:T(8,128)S(1)}, u32[]{:S(2)}, u32[]{:S(2)}) collective-permute-start(f32[5,3,32,128]{3,2,1,0:T(8,128)S(1)} %get-tuple-element.21), channel_id=1, source_target_pairs={{0,15},{1,2},{2,1},{3,4},{4,3},{5,6},{6,5},{7,8},{8,7},{9,10},{10,... | collective-permute-start | bytes 737288 | tf_op jit(solution)/shard_map/ppermute | solution.py:137
  47.1 4.0 %planes.2.sides = f32[5,8,32,128]{3,2,1,0:T(8,128)S(1)} custom-call(f32[5,8,32,128]{3,2,1,0:T(8,128)S(1)} %get-tuple-element.19.state.start, f32[8,128]{1,0:T(8,128)S(1)} %get-tuple-element.20.speed.first_speed), custom_call_target="tpu_custom_call" | custom-call | flops 20000000 | bytes 1000000 | tf_op jit(solution)/shard_map/planes/pallas_call | solution.py:412
  51.2 2.5 %first_stage.1 = (f32[5,8,32,128]{3,2,1,0:T(8,128)S(1)}, f32[5,3,32,128]{3,2,1,0:T(8,128)S(1)}, f32[5,3,32,128]{3,2,1,0:T(8,128)S(1)}, f32[8,128]{1,0:T(8,128)S(1)}) custom-call(f32[5,8,32,128]{3,2,1,0:T(8,128)S(1)} %get-tuple-element.19.state.start, f32[5,8,32,128]{3,2,1,0:T(8,128)S(1)} %planes.2.sides, f32[5,3,32,128]{3,2,1,0:T(8,128)S(1)} %collective-permute-done.far, ...), custom_call_target="tpu_custom_call" | custom-call | flops 30000000 | bytes 3000000 | tf_op jit(solution)/shard_map/first_stage/pallas_call | solution.py:488
  53.7 0.8 %collective-permute-start.4 = (f32[8,128]{1,0:T(8,128)S(1)}, f32[8,128]{1,0:T(8,128)S(1)}, u32[]{:S(2)}, u32[]{:S(2)}) collective-permute-start(f32[8,128]{1,0:T(8,128)S(1)} %get-tuple-element.24), channel_id=1, source_target_pairs={{0,12},{1,13},{2,14},{3,15},{4,8},{5,9},{6,10},{7,11},{8,4},{9,5},... | collective-permute-start | bytes 12296 | tf_op jit(solution)/shard_map/ppermute | solution.py:551
  54.6 1.5 %collective-permute-start.3 = (f32[8,128]{1,0:T(8,128)S(1)}, f32[8,128]{1,0:T(8,128)S(1)}, u32[]{:S(2)}, u32[]{:S(2)}) collective-permute-start(f32[8,128]{1,0:T(8,128)S(1)} %get-tuple-element.24), channel_id=1, source_target_pairs={{0,8},{1,9},{2,10},{3,11},{4,12},{5,13},{6,14},{7,15},{8,0},{9,1},... | collective-permute-start | bytes 12296 | tf_op jit(solution)/shard_map/ppermute | solution.py:551
  56.1 2.1 %collective-permute-start.2 = (f32[8,128]{1,0:T(8,128)S(1)}, f32[8,128]{1,0:T(8,128)S(1)}, u32[]{:S(2)}, u32[]{:S(2)}) collective-permute-start(f32[8,128]{1,0:T(8,128)S(1)} %get-tuple-element.24), channel_id=1, source_target_pairs={{0,4},{1,5},{2,6},{3,7},{4,0},{5,1},{6,2},{7,3},{8,12},{9,13},{10,... | collective-permute-start | bytes 12296 | tf_op jit(solution)/shard_map/ppermute | solution.py:551
  58.2 3.4 %collective-permute-start.8 = (f32[5,3,32,128]{3,2,1,0:T(8,128)S(1)}, f32[5,3,32,128]{3,2,1,0:T(8,128)S(1)}, u32[]{:S(2)}, u32[]{:S(2)}) collective-permute-start(f32[5,3,32,128]{3,2,1,0:T(8,128)S(1)} %get-tuple-element.25), channel_id=1, source_target_pairs={{0,15},{1,2},{2,1},{3,4},{4,3},{5,6},{6,5},{7,8},{8,7},{9,10},{10,... | collective-permute-start | bytes 737288 | tf_op jit(solution)/shard_map/ppermute | solution.py:137
  61.6 0.1 collective-permute-start.7
  61.8 2.1 %collective-permute-start.6 = (f32[8,128]{1,0:T(8,128)S(1)}, f32[8,128]{1,0:T(8,128)S(1)}, u32[]{:S(2)}, u32[]{:S(2)}) collective-permute-start(f32[8,128]{1,0:T(8,128)S(1)} %maximum_maximum_fusion.1), channel_id=1, source_target_pairs={{0,2},{1,3},{2,0},{3,1},{4,6},{5,7},{6,4},{7,5},{8,10},{9,11},{10,... | collective-permute-start | bytes 12296 | tf_op jit(solution)/shard_map/ppermute | solution.py:551
  63.8 1.3 %collective-permute-done.7 = f32[8,128]{1,0:T(8,128)S(1)} collective-permute-done((f32[8,128]{1,0:T(8,128)S(1)}, f32[8,128]{1,0:T(8,128)S(1)}, u32[]{:S(2)}, u32[]{:S(2)}) %collective-permute-start.7) | collective-permute-done | bytes 4128 | tf_op jit(solution)/shard_map/ppermute | solution.py:551
  65.1 1.6 %collective-permute-done.6 = f32[8,128]{1,0:T(8,128)S(1)} collective-permute-done((f32[8,128]{1,0:T(8,128)S(1)}, f32[8,128]{1,0:T(8,128)S(1)}, u32[]{:S(2)}, u32[]{:S(2)}) %collective-permute-start.6) | collective-permute-done | bytes 4128 | tf_op jit(solution)/shard_map/ppermute | solution.py:551
  66.7 4.1 %planes.3.sides = f32[5,8,32,128]{3,2,1,0:T(8,128)S(1)} custom-call(f32[5,8,32,128]{3,2,1,0:T(8,128)S(1)} %get-tuple-element.23.state.middle, f32[8,128]{1,0:T(8,128)S(1)} %maximum_maximum_fusion.speed), custom_call_target="tpu_custom_call" | custom-call | flops 20000000 | bytes 1000000 | tf_op jit(solution)/shard_map/planes/pallas_call | solution.py:412
  70.8 3.2 %second_stage.1 = f32[5,8,32,128]{3,2,1,0:T(8,128)} custom-call(f32[5,8,32,128]{3,2,1,0:T(8,128)S(1)} %get-tuple-element.19.state.start, f32[5,8,32,128]{3,2,1,0:T(8,128)S(1)} %get-tuple-element.23.state.middle, f32[5,8,32,128]{3,2,1,0:T(8,128)S(1)} %planes.3.sides, f32[5,3,32,128]{3,2,1,0:T(8,128)S(1)} %collective-permute-done.8.far, ...), custom_call_target="tpu_custom_call" | custom-call | flops 30000000 | bytes 3000000 | tf_op jit(solution)/shard_map/second_stage/pallas_call | solution.py:529
  (18 shorter events, 0.1 us)
Async XLA Ops:
  2.7 7.4 %copy-start = (s32[1024]{0:T(1024)S(1)}, s32[1024]{0:T(1024)}, u32[]{:S(2)}) copy-start(s32[1024]{0:T(1024)} %owner_hbm.1) | copy-start | bytes 12292
  2.8 7.4 %copy-start.1 = (s32[1024]{0:T(1024)S(1)}, s32[1024]{0:T(1024)}, u32[]{:S(2)}) copy-start(s32[1024]{0:T(1024)} %param.5) | copy-start | bytes 12292
  2.8 34.9 %all-to-all-start = ((f32[16,161,1,128]{3,2,1,0:T(1,128)}), f32[16,161,1,128]{3,2,1,0:T(1,128)S(1)}, u32[]{:S(2)}, u32[]{:S(2)}) async-start(f32[16,161,1,128]{3,2,1,0:T(1,128)} %pack.1), calls=%async_computation | async-start | bytes 2637824 | tf_op jit(solution)/shard_map/all_to_all | solution.py:565
  40.5 10.7 %collective-permute-start = (f32[5,3,32,128]{3,2,1,0:T(8,128)S(1)}, f32[5,3,32,128]{3,2,1,0:T(8,128)S(1)}, u32[]{:S(2)}, u32[]{:S(2)}) collective-permute-start(f32[5,3,32,128]{3,2,1,0:T(8,128)S(1)} %get-tuple-element.21), channel_id=1, source_target_pairs={{0,15},{1,2},{2,1},{3,4},{4,3},{5,6},{6,5},{7,8},{8,7},{9,10},{10,... | collective-permute-start | bytes 737288 | tf_op jit(solution)/shard_map/ppermute | solution.py:137
  47.1 4.1 %collective-permute-start.1 = (f32[5,3,32,128]{3,2,1,0:T(8,128)S(1)}, f32[5,3,32,128]{3,2,1,0:T(8,128)S(1)}, u32[]{:S(2)}, u32[]{:S(2)}) collective-permute-start(f32[5,3,32,128]{3,2,1,0:T(8,128)S(1)} %get-tuple-element.22), channel_id=1, source_target_pairs={{0,1},{1,0},{2,3},{3,2},{4,5},{5,4},{6,7},{7,6},{8,9},{9,8},{10,11... | collective-permute-start | bytes 737288 | tf_op jit(solution)/shard_map/ppermute | solution.py:137
  53.7 7.9 %collective-permute-start.4 = (f32[8,128]{1,0:T(8,128)S(1)}, f32[8,128]{1,0:T(8,128)S(1)}, u32[]{:S(2)}, u32[]{:S(2)}) collective-permute-start(f32[8,128]{1,0:T(8,128)S(1)} %get-tuple-element.24), channel_id=1, source_target_pairs={{0,12},{1,13},{2,14},{3,15},{4,8},{5,9},{6,10},{7,11},{8,4},{9,5},... | collective-permute-start | bytes 12296 | tf_op jit(solution)/shard_map/ppermute | solution.py:551
  54.6 7.0 %collective-permute-start.3 = (f32[8,128]{1,0:T(8,128)S(1)}, f32[8,128]{1,0:T(8,128)S(1)}, u32[]{:S(2)}, u32[]{:S(2)}) collective-permute-start(f32[8,128]{1,0:T(8,128)S(1)} %get-tuple-element.24), channel_id=1, source_target_pairs={{0,8},{1,9},{2,10},{3,11},{4,12},{5,13},{6,14},{7,15},{8,0},{9,1},... | collective-permute-start | bytes 12296 | tf_op jit(solution)/shard_map/ppermute | solution.py:551
  56.1 5.5 %collective-permute-start.2 = (f32[8,128]{1,0:T(8,128)S(1)}, f32[8,128]{1,0:T(8,128)S(1)}, u32[]{:S(2)}, u32[]{:S(2)}) collective-permute-start(f32[8,128]{1,0:T(8,128)S(1)} %get-tuple-element.24), channel_id=1, source_target_pairs={{0,4},{1,5},{2,6},{3,7},{4,0},{5,1},{6,2},{7,3},{8,12},{9,13},{10,... | collective-permute-start | bytes 12296 | tf_op jit(solution)/shard_map/ppermute | solution.py:551
  58.2 12.6 %collective-permute-start.8 = (f32[5,3,32,128]{3,2,1,0:T(8,128)S(1)}, f32[5,3,32,128]{3,2,1,0:T(8,128)S(1)}, u32[]{:S(2)}, u32[]{:S(2)}) collective-permute-start(f32[5,3,32,128]{3,2,1,0:T(8,128)S(1)} %get-tuple-element.25), channel_id=1, source_target_pairs={{0,15},{1,2},{2,1},{3,4},{4,3},{5,6},{6,5},{7,8},{8,7},{9,10},{10,... | collective-permute-start | bytes 737288 | tf_op jit(solution)/shard_map/ppermute | solution.py:137
  61.6 9.2 %collective-permute-start.9 = (f32[5,3,32,128]{3,2,1,0:T(8,128)S(1)}, f32[5,3,32,128]{3,2,1,0:T(8,128)S(1)}, u32[]{:S(2)}, u32[]{:S(2)}) collective-permute-start(f32[5,3,32,128]{3,2,1,0:T(8,128)S(1)} %get-tuple-element.26), channel_id=1, source_target_pairs={{0,1},{1,0},{2,3},{3,2},{4,5},{5,4},{6,7},{7,6},{8,9},{9,8},{10,11... | collective-permute-start | bytes 737288 | tf_op jit(solution)/shard_map/ppermute | solution.py:137
  61.6 3.5 %collective-permute-start.7 = (f32[8,128]{1,0:T(8,128)S(1)}, f32[8,128]{1,0:T(8,128)S(1)}, u32[]{:S(2)}, u32[]{:S(2)}) collective-permute-start(f32[8,128]{1,0:T(8,128)S(1)} %maximum_maximum_fusion.1), channel_id=1, source_target_pairs={{0,3},{1,2},{2,1},{3,0},{4,7},{5,6},{6,5},{7,4},{8,11},{9,10},{10,... | collective-permute-start | bytes 12296 | tf_op jit(solution)/shard_map/ppermute | solution.py:551
  61.8 4.9 %collective-permute-start.6 = (f32[8,128]{1,0:T(8,128)S(1)}, f32[8,128]{1,0:T(8,128)S(1)}, u32[]{:S(2)}, u32[]{:S(2)}) collective-permute-start(f32[8,128]{1,0:T(8,128)S(1)} %maximum_maximum_fusion.1), channel_id=1, source_target_pairs={{0,2},{1,3},{2,0},{3,1},{4,6},{5,7},{6,4},{7,5},{8,10},{9,11},{10,... | collective-permute-start | bytes 12296 | tf_op jit(solution)/shard_map/ppermute | solution.py:551
  63.8 2.9 %collective-permute-start.5 = (f32[8,128]{1,0:T(8,128)S(1)}, f32[8,128]{1,0:T(8,128)S(1)}, u32[]{:S(2)}, u32[]{:S(2)}) collective-permute-start(f32[8,128]{1,0:T(8,128)S(1)} %maximum_maximum_fusion.1), channel_id=1, source_target_pairs={{0,1},{1,0},{2,3},{3,2},{4,5},{5,4},{6,7},{7,6},{8,9},{9,8},{10,11... | collective-permute-start | bytes 12296 | tf_op jit(solution)/shard_map/ppermute | solution.py:551

commit v16 on v15

--- a/solution.py
+++ b/solution.py
@@ -321,6 +321,70 @@
     return [here - below for here, below in zip(face, down(face))]
 
 
+def x_divergence(half_flux, scaled, plus_at, minus_at, centre_at):
+    faces = {i: 6.0 * (half_flux[i] + half_flux[i + 1]) for i in centre_at}
+
+    def add(i, value):
+        faces[i] = faces[i] + value if i in faces else value
+
+    def side(sign):
+        values = {i: half_flux[i] + sign * scaled[i] for i in half_flux}
+        steps = {i: values[i + 1] - values[i] for i in values if i + 1 in values}
+        return {i: smoothness(steps[i - 1], steps[i]) for i in steps if i - 1 in steps}
+
+    parts = side(1)
+    for i in plus_at:
+        curve, left, centre, right = zip(parts[i - 1], parts[i], parts[i + 1])
+        term = upwind_term(left[0], centre[1], right[2], curve[1] - curve[0], curve[2] - curve[1])
+        add(i, -(curve[1] + term))
+    parts = side(-1)
+    for i in minus_at:
+        curve, left, centre, right = zip(parts[i - 1], parts[i], parts[i + 1])
+        term = upwind_term(right[2], centre[1], left[0], curve[2] - curve[1], curve[1] - curve[0])
+        add(i - 1, term - curve[1])
+    total = {}
+    for i in range(BLOCK):
+        if i in faces:
+            total[i] = faces[i]
+        if i - 1 in faces:
+            total[i] = total[i] - faces[i - 1] if i in total else -faces[i - 1]
+    return total
+
+
+INNER = (range(2, 6), range(2, 6), range(0, 7))
+OUTER = ((-1, 0, 1, 6, 7), (0, 1, 6, 7, 8), (-1, 7))
+EVERY = (range(-1, 8), range(0, 9), range(-1, 8))
+
+
+def ring_divergence(half_flux, scaled):
+    count = len(half_flux)
+
+    def up(values):
+        return values[1:] + [pltpu.roll(values[0], 7, 0)]
+
+    def down(values):
+        return [pltpu.roll(values[-1], 1, 0)] + values[:-1]
+
+    def side(values):
+        after = [above - value for above, value in zip(up(values), values)]
+        parts = [smoothness(before, step) for before, step in zip(down(after), after)]
+        curve, left, centre, right = (list(part) for part in zip(*parts))
+        jump = [above - value for above, value in zip(up(curve), curve)]
+        return curve, left, centre, right, jump
+
+    curve, left, centre, right, jump = side([a + b for a, b in zip(half_flux, scaled)])
+    terms = zip(down(left), centre, up(right), down(jump), jump)
+    face = [
+        6.0 * (here + above) - bend - upwind_term(*term)
+        for here, above, bend, term in zip(half_flux, up(half_flux), curve, terms)
+    ]
+    curve, left, centre, right, jump = side([a - b for a, b in zip(half_flux, scaled)])
+    terms = zip(up(right), centre, down(left), jump, down(jump))
+    other = [upwind_term(*term) - bend for bend, term in zip(curve, terms)]
+    face = [one + two for one, two in zip(face, up(other))]
+    return [here - below for here, below in zip(face, down(face))]
+
+
 def open_divergence(half_flux, scaled):
     count = len(half_flux)
     plus = [a + b for a, b in zip(half_flux, scaled)]
@@ -368,7 +432,7 @@
     return flux + 0.5 * pressure if field == 1 + direction else flux
 
 
-def plane_kernel(state, speed, out, turned):
+def plane_kernel(with_inner, state, speed, out, turned):
     half_speed = 0.5 * speed[0:1, :]
     lane = lax.broadcasted_iota(jnp.int32, (LANES, LANES), 1)
     to_turned = (lane % 8) * 16 + lane // 8
@@ -407,10 +471,24 @@
 
     lax.fori_loop(0, state.shape[1] // 4, four_planes, 0)
 
-
-def along_planes(state, speed):
+    def group(j, carry):
+        rows = pl.ds(pl.multiple_of(j * 8, 8), 8)
+
+        def get(f, plane):
+            return state[f, plane, rows, :]
+
+        for field, along_x in across(get, half_speed, range(BLOCK), INNER):
+            for plane in range(BLOCK):
+                out[field, plane, rows, :] += along_x[plane]
+        return carry
+
+    if with_inner:
+        lax.fori_loop(0, 4, group, 0)
+
+
+def along_planes(state, speed, with_inner):
     return pl.pallas_call(
-        plane_kernel,
+        functools.partial(plane_kernel, with_inner),
         out_shape=jax.ShapeDtypeStruct(state.shape, jnp.float32),
         in_specs=[VMEM, VMEM],
         out_specs=VMEM,
@@ -421,27 +499,29 @@
     )(state, speed)
 
 
-def across(get, half_speed):
-    span = range(-3, BLOCK + 3)
-    speeds, pressures = [], []
+def across(get, half_speed, span, parts):
+    speeds, pressures = {}, {}
     for plane in span:
         vel, pressure = half_velocities([get(f, plane) for f in range(FIELDS)])
-        speeds.append(vel[0])
-        pressures.append(pressure)
+        speeds[plane] = vel[0]
+        pressures[plane] = pressure
     for field in range(FIELDS):
-        fluxes, scaled = [], []
-        for i, plane in enumerate(span):
+        fluxes, scaled = {}, {}
+        for plane in span:
             if field == 0:
                 flux = 0.5 * get(1, plane)
             elif field == 4:
-                flux = (get(4, plane) + pressures[i]) * speeds[i]
+                flux = (get(4, plane) + pressures[plane]) * speeds[plane]
             else:
-                flux = get(field, plane) * speeds[i]
+                flux = get(field, plane) * speeds[plane]
                 if field == 1:
-                    flux = flux + 0.5 * pressures[i]
-            fluxes.append(flux)
-            scaled.append(half_speed * get(field, plane))
-        yield field, open_divergence(fluxes, scaled)
+                    flux = flux + 0.5 * pressures[plane]
+            fluxes[plane] = flux
+            scaled[plane] = half_speed * get(field, plane)
+        yield field, x_divergence(fluxes, scaled, *parts)
+
+
+WITH_HALOS = range(-3, BLOCK + 3)
 
 
 def first_kernel(
@@ -462,10 +542,12 @@
                 return above[f, plane - BLOCK, rows, :]
             return state[f, plane, rows, :]
 
-        for field, along_x in across(get, half_speed):
+        for field, along_x in across(get, half_speed, WITH_HALOS, OUTER):
             values = []
             for plane in range(BLOCK):
-                total = along_x[plane] + sides[field, plane, rows, :]
+                total = sides[field, plane, rows, :]
+                if plane in along_x:
+                    total = total + along_x[plane]
                 values.append(get(field, plane) - factor * total)
                 middle[field, plane, rows, :] = values[plane]
             for plane in range(3):
@@ -513,7 +595,7 @@
                 return above[f, plane - BLOCK, rows, :]
             return middle[f, plane, rows, :]
 
-        for field, along_x in across(get, half_speed):
+        for field, along_x in across(get, half_speed, WITH_HALOS, EVERY):
             for plane in range(BLOCK):
                 total = along_x[plane] + sides[field, plane, rows, :]
                 value = 0.5 * start[field, plane, rows, :] + (
@@ -566,11 +648,11 @@
     table = arrival_spots(owner_list, slot_list, own, per_dev, size, cap)
     state, far_side, near_side, speed = unpack(table, come.reshape(-1, LANES), size, cap)
     far, near = swapped(far_side, near_side, size)
-    sides = along_planes(state, speed)
+    sides = along_planes(state, speed, True)
     middle, far_side, near_side, top = first_stage(state, sides, far, near, speed)
     far, near = swapped(far_side, near_side, size)
     second = everyone_max(top, "gx", size)
-    sides = along_planes(middle, second)
+    sides = along_planes(middle, second, False)
     return second_stage(state, middle, sides, far, near, speed, second)
 
 

time: 74.2 us -> 74.7 us (level)
  starting transfers between devices: 24.1 us -> 22.9 us
  waiting for transfers between devices: 29.6 us -> 30.7 us
    pallas_call x2, Pallas kernels: 8.11 us -> 9.26 us  [along_planes(): pl.pallas_call(functools.partial(plane_kernel, with_inner), out_shape=jax...]
    ppermute x2, starting transfers between devices: 10 us -> 8.89 us  [swapped(): lax.ppermute(far_side, 'gx', apart)]
    ppermute x6, waiting for transfers between devices: 2.85 us -> 3.95 us  [everyone_max(): copies.append(lax.ppermute(value, axis, pairs))]
  transfers between devices with their start and end apart: 11 -> 11, of which waited for: 3 -> 3; matrix products, arithmetic and copies ran while one was open for 1% -> 1% of each run, Pallas kernels for 11% -> 12%
where the time goes in v16:
time: 74.7 us; the launch traced here: 74.5 us
  waiting for transfers between devices  30.7 us (41%)
  starting transfers between devices  22.9 us (31%)
  Pallas kernels  19.9 us (27%)
    all_to_all x1, waiting for transfers between devices, per_device(): come = lax.all_to_all(parts, 'gx', split_axis=0, concat_axis=0, tiled=True)  26.8 us
    pallas_call x2, Pallas kernels, along_planes(): pl.pallas_call(functools.partial(plane_kernel, with_inner), out_shape=jax...  9.26 us
    ppermute x2, starting transfers between devices, swapped(): lax.ppermute(far_side, 'gx', apart)  8.89 us
    all_to_all x1, starting transfers between devices, per_device(): come = lax.all_to_all(parts, 'gx', split_axis=0, concat_axis=0, tiled=True)  7.37 us
    ppermute x6, starting transfers between devices, everyone_max(): copies.append(lax.ppermute(value, axis, pairs))  6.67 us
    ppermute x6, waiting for transfers between devices, everyone_max(): copies.append(lax.ppermute(value, axis, pairs))  3.95 us
    pallas_call x1, Pallas kernels, second_stage(): pl.pallas_call(second_kernel, out_shape=jax.ShapeDtypeStruct((FIELDS, BLO...  3.25 us
    pallas_call x1, Pallas kernels, unpack(): pl.pallas_call(functools.partial(unpack_kernel, size, cap), out_shape=(ja...  2.79 us
  transfers between devices with their start and end apart: 11, of which 3 were waited for; matrix products, arithmetic and copies ran while one was open for 1% of the time, Pallas kernels for 12%

profile of v16, /device:TPU:0, one launch (start us, length us, event | category | flops | bytes accessed | tf_op | source)
XLA Modules:
  0.0 74.5 jit_solution(10429313787913963872)
XLA Ops:
  0.0 2.7 %pack.1 = f32[16,161,1,128]{3,2,1,0:T(1,128)} custom-call(s32[1024]{0:T(1024)} %owner_hbm.1, f32[1280,128]{1,0:T(8,128)} %bitcast.7), custom_call_target="tpu_custom_call" | custom-call | flops 1000000 | bytes 3000000 | tf_op jit(solution)/shard_map/pack/pallas_call | solution.py:110
  2.7 0.0 copy-start
  2.8 0.0 copy-start.1
  2.8 7.4 %all-to-all-start = ((f32[16,161,1,128]{3,2,1,0:T(1,128)}), f32[16,161,1,128]{3,2,1,0:T(1,128)S(1)}, u32[]{:S(2)}, u32[]{:S(2)}) async-start(f32[16,161,1,128]{3,2,1,0:T(1,128)} %pack.1), calls=%async_computation | async-start | bytes 2637824 | tf_op jit(solution)/shard_map/all_to_all | solution.py:647
  10.2 0.1 eq.33
  10.3 0.3 convert_reduce_fusion
  10.6 0.1 broadcast_add_fusion
  10.7 0.1 add.17
  10.8 0.1 select_reduce_fusion.table
  10.9 26.8 %all-to-all-done = f32[16,161,1,128]{3,2,1,0:T(1,128)S(1)} async-done(((f32[16,161,1,128]{3,2,1,0:T(1,128)}), f32[16,161,1,128]{3,2,1,0:T(1,128)S(1)}, u32[]{:S(2)}, u32[]{:S(2)}) %all-to-all-start) | async-done | bytes 1318944 | tf_op jit(solution)/shard_map/all_to_all | solution.py:647
  37.7 2.8 %unpack.1 = (f32[5,8,32,128]{3,2,1,0:T(8,128)S(1)}, f32[5,3,32,128]{3,2,1,0:T(8,128)S(1)}, f32[5,3,32,128]{3,2,1,0:T(8,128)S(1)}, f32[8,128]{1,0:T(8,128)S(1)}) custom-call(s32[64]{0:T(128)S(1)} %select_reduce_fusion.table, f32[2576,128]{1,0:T(8,128)S(1)} %bitcast.6), custom_call_target="tpu_custom_call" | custom-call | flops 5000000 | bytes 2000000 | tf_op jit(solution)/shard_map/unpack/pallas_call | solution.py:226
  40.5 6.6 %collective-permute-start = (f32[5,3,32,128]{3,2,1,0:T(8,128)S(1)}, f32[5,3,32,128]{3,2,1,0:T(8,128)S(1)}, u32[]{:S(2)}, u32[]{:S(2)}) collective-permute-start(f32[5,3,32,128]{3,2,1,0:T(8,128)S(1)} %get-tuple-element.21), channel_id=1, source_target_pairs={{0,15},{1,2},{2,1},{3,4},{4,3},{5,6},{6,5},{7,8},{8,7},{9,10},{10,... | collective-permute-start | bytes 737288 | tf_op jit(solution)/shard_map/ppermute | solution.py:137
  47.1 5.2 %planes.2.sides = f32[5,8,32,128]{3,2,1,0:T(8,128)S(1)} custom-call(f32[5,8,32,128]{3,2,1,0:T(8,128)S(1)} %get-tuple-element.19.state.start, f32[8,128]{1,0:T(8,128)S(1)} %get-tuple-element.20.speed.first_speed), custom_call_target="tpu_custom_call" | custom-call | flops 20000000 | bytes 1000000 | tf_op jit(solution)/shard_map/planes/pallas_call | solution.py:490
  52.3 1.8 %first_stage.1 = (f32[5,8,32,128]{3,2,1,0:T(8,128)S(1)}, f32[5,3,32,128]{3,2,1,0:T(8,128)S(1)}, f32[5,3,32,128]{3,2,1,0:T(8,128)S(1)}, f32[8,128]{1,0:T(8,128)S(1)}) custom-call(f32[5,8,32,128]{3,2,1,0:T(8,128)S(1)} %get-tuple-element.19.state.start, f32[5,8,32,128]{3,2,1,0:T(8,128)S(1)} %planes.2.sides, f32[5,3,32,128]{3,2,1,0:T(8,128)S(1)} %collective-permute-done.far, ...), custom_call_target="tpu_custom_call" | custom-call | flops 30000000 | bytes 3000000 | tf_op jit(solution)/shard_map/first_stage/pallas_call | solution.py:570
  54.2 0.8 %collective-permute-start.4 = (f32[8,128]{1,0:T(8,128)S(1)}, f32[8,128]{1,0:T(8,128)S(1)}, u32[]{:S(2)}, u32[]{:S(2)}) collective-permute-start(f32[8,128]{1,0:T(8,128)S(1)} %get-tuple-element.24), channel_id=1, source_target_pairs={{0,12},{1,13},{2,14},{3,15},{4,8},{5,9},{6,10},{7,11},{8,4},{9,5},... | collective-permute-start | bytes 12296 | tf_op jit(solution)/shard_map/ppermute | solution.py:633
  55.0 0.7 collective-permute-start.3
  55.7 3.0 %collective-permute-start.2 = (f32[8,128]{1,0:T(8,128)S(1)}, f32[8,128]{1,0:T(8,128)S(1)}, u32[]{:S(2)}, u32[]{:S(2)}) collective-permute-start(f32[8,128]{1,0:T(8,128)S(1)} %get-tuple-element.24), channel_id=1, source_target_pairs={{0,4},{1,5},{2,6},{3,7},{4,0},{5,1},{6,2},{7,3},{8,12},{9,13},{10,... | collective-permute-start | bytes 12296 | tf_op jit(solution)/shard_map/ppermute | solution.py:633
  58.7 2.3 %collective-permute-start.8 = (f32[5,3,32,128]{3,2,1,0:T(8,128)S(1)}, f32[5,3,32,128]{3,2,1,0:T(8,128)S(1)}, u32[]{:S(2)}, u32[]{:S(2)}) collective-permute-start(f32[5,3,32,128]{3,2,1,0:T(8,128)S(1)} %get-tuple-element.25), channel_id=1, source_target_pairs={{0,15},{1,2},{2,1},{3,4},{4,3},{5,6},{6,5},{7,8},{8,7},{9,10},{10,... | collective-permute-start | bytes 737288 | tf_op jit(solution)/shard_map/ppermute | solution.py:137
  60.9 0.1 collective-permute-start.7
  61.1 2.1 %collective-permute-start.6 = (f32[8,128]{1,0:T(8,128)S(1)}, f32[8,128]{1,0:T(8,128)S(1)}, u32[]{:S(2)}, u32[]{:S(2)}) collective-permute-start(f32[8,128]{1,0:T(8,128)S(1)} %maximum_maximum_fusion.1), channel_id=1, source_target_pairs={{0,2},{1,3},{2,0},{3,1},{4,6},{5,7},{6,4},{7,5},{8,10},{9,11},{10,... | collective-permute-start | bytes 12296 | tf_op jit(solution)/shard_map/ppermute | solution.py:633
  63.2 1.0 %collective-permute-done.7 = f32[8,128]{1,0:T(8,128)S(1)} collective-permute-done((f32[8,128]{1,0:T(8,128)S(1)}, f32[8,128]{1,0:T(8,128)S(1)}, u32[]{:S(2)}, u32[]{:S(2)}) %collective-permute-start.7) | collective-permute-done | bytes 4128 | tf_op jit(solution)/shard_map/ppermute | solution.py:633
  64.2 2.9 %collective-permute-done.6 = f32[8,128]{1,0:T(8,128)S(1)} collective-permute-done((f32[8,128]{1,0:T(8,128)S(1)}, f32[8,128]{1,0:T(8,128)S(1)}, u32[]{:S(2)}, u32[]{:S(2)}) %collective-permute-start.6) | collective-permute-done | bytes 4128 | tf_op jit(solution)/shard_map/ppermute | solution.py:633
  67.1 4.1 %planes.3.sides = f32[5,8,32,128]{3,2,1,0:T(8,128)S(1)} custom-call(f32[5,8,32,128]{3,2,1,0:T(8,128)S(1)} %get-tuple-element.23.state.middle, f32[8,128]{1,0:T(8,128)S(1)} %maximum_maximum_fusion.speed), custom_call_target="tpu_custom_call" | custom-call | flops 20000000 | bytes 1000000 | tf_op jit(solution)/shard_map/planes/pallas_call | solution.py:490
  71.2 3.3 %second_stage.1 = f32[5,8,32,128]{3,2,1,0:T(8,128)} custom-call(f32[5,8,32,128]{3,2,1,0:T(8,128)S(1)} %get-tuple-element.19.state.start, f32[5,8,32,128]{3,2,1,0:T(8,128)S(1)} %get-tuple-element.23.state.middle, f32[5,8,32,128]{3,2,1,0:T(8,128)S(1)} %planes.3.sides, f32[5,3,32,128]{3,2,1,0:T(8,128)S(1)} %collective-permute-done.8.far, ...), custom_call_target="tpu_custom_call" | custom-call | flops 30000000 | bytes 3000000 | tf_op jit(solution)/shard_map/second_stage/pallas_call | solution.py:611
  (18 shorter events, 0.1 us)
Async XLA Ops:
  2.7 7.4 %copy-start = (s32[1024]{0:T(1024)S(1)}, s32[1024]{0:T(1024)}, u32[]{:S(2)}) copy-start(s32[1024]{0:T(1024)} %owner_hbm.1) | copy-start | bytes 12292
  2.8 7.4 %copy-start.1 = (s32[1024]{0:T(1024)S(1)}, s32[1024]{0:T(1024)}, u32[]{:S(2)}) copy-start(s32[1024]{0:T(1024)} %param.5) | copy-start | bytes 12292
  2.8 34.9 %all-to-all-start = ((f32[16,161,1,128]{3,2,1,0:T(1,128)}), f32[16,161,1,128]{3,2,1,0:T(1,128)S(1)}, u32[]{:S(2)}, u32[]{:S(2)}) async-start(f32[16,161,1,128]{3,2,1,0:T(1,128)} %pack.1), calls=%async_computation | async-start | bytes 2637824 | tf_op jit(solution)/shard_map/all_to_all | solution.py:647
  40.5 11.8 %collective-permute-start = (f32[5,3,32,128]{3,2,1,0:T(8,128)S(1)}, f32[5,3,32,128]{3,2,1,0:T(8,128)S(1)}, u32[]{:S(2)}, u32[]{:S(2)}) collective-permute-start(f32[5,3,32,128]{3,2,1,0:T(8,128)S(1)} %get-tuple-element.21), channel_id=1, source_target_pairs={{0,15},{1,2},{2,1},{3,4},{4,3},{5,6},{6,5},{7,8},{8,7},{9,10},{10,... | collective-permute-start | bytes 737288 | tf_op jit(solution)/shard_map/ppermute | solution.py:137
  47.1 5.2 %collective-permute-start.1 = (f32[5,3,32,128]{3,2,1,0:T(8,128)S(1)}, f32[5,3,32,128]{3,2,1,0:T(8,128)S(1)}, u32[]{:S(2)}, u32[]{:S(2)}) collective-permute-start(f32[5,3,32,128]{3,2,1,0:T(8,128)S(1)} %get-tuple-element.22), channel_id=1, source_target_pairs={{0,1},{1,0},{2,3},{3,2},{4,5},{5,4},{6,7},{7,6},{8,9},{9,8},{10,11... | collective-permute-start | bytes 737288 | tf_op jit(solution)/shard_map/ppermute | solution.py:137
  54.2 6.7 %collective-permute-start.4 = (f32[8,128]{1,0:T(8,128)S(1)}, f32[8,128]{1,0:T(8,128)S(1)}, u32[]{:S(2)}, u32[]{:S(2)}) collective-permute-start(f32[8,128]{1,0:T(8,128)S(1)} %get-tuple-element.24), channel_id=1, source_target_pairs={{0,12},{1,13},{2,14},{3,15},{4,8},{5,9},{6,10},{7,11},{8,4},{9,5},... | collective-permute-start | bytes 12296 | tf_op jit(solution)/shard_map/ppermute | solution.py:633
  55.0 5.9 %collective-permute-start.3 = (f32[8,128]{1,0:T(8,128)S(1)}, f32[8,128]{1,0:T(8,128)S(1)}, u32[]{:S(2)}, u32[]{:S(2)}) collective-permute-start(f32[8,128]{1,0:T(8,128)S(1)} %get-tuple-element.24), channel_id=1, source_target_pairs={{0,8},{1,9},{2,10},{3,11},{4,12},{5,13},{6,14},{7,15},{8,0},{9,1},... | collective-permute-start | bytes 12296 | tf_op jit(solution)/shard_map/ppermute | solution.py:633
  55.7 5.2 %collective-permute-start.2 = (f32[8,128]{1,0:T(8,128)S(1)}, f32[8,128]{1,0:T(8,128)S(1)}, u32[]{:S(2)}, u32[]{:S(2)}) collective-permute-start(f32[8,128]{1,0:T(8,128)S(1)} %get-tuple-element.24), channel_id=1, source_target_pairs={{0,4},{1,5},{2,6},{3,7},{4,0},{5,1},{6,2},{7,3},{8,12},{9,13},{10,... | collective-permute-start | bytes 12296 | tf_op jit(solution)/shard_map/ppermute | solution.py:633
  58.7 12.5 %collective-permute-start.8 = (f32[5,3,32,128]{3,2,1,0:T(8,128)S(1)}, f32[5,3,32,128]{3,2,1,0:T(8,128)S(1)}, u32[]{:S(2)}, u32[]{:S(2)}) collective-permute-start(f32[5,3,32,128]{3,2,1,0:T(8,128)S(1)} %get-tuple-element.25), channel_id=1, source_target_pairs={{0,15},{1,2},{2,1},{3,4},{4,3},{5,6},{6,5},{7,8},{8,7},{9,10},{10,... | collective-permute-start | bytes 737288 | tf_op jit(solution)/shard_map/ppermute | solution.py:137
  60.9 10.3 %collective-permute-start.9 = (f32[5,3,32,128]{3,2,1,0:T(8,128)S(1)}, f32[5,3,32,128]{3,2,1,0:T(8,128)S(1)}, u32[]{:S(2)}, u32[]{:S(2)}) collective-permute-start(f32[5,3,32,128]{3,2,1,0:T(8,128)S(1)} %get-tuple-element.26), channel_id=1, source_target_pairs={{0,1},{1,0},{2,3},{3,2},{4,5},{5,4},{6,7},{7,6},{8,9},{9,8},{10,11... | collective-permute-start | bytes 737288 | tf_op jit(solution)/shard_map/ppermute | solution.py:137
  60.9 3.2 %collective-permute-start.7 = (f32[8,128]{1,0:T(8,128)S(1)}, f32[8,128]{1,0:T(8,128)S(1)}, u32[]{:S(2)}, u32[]{:S(2)}) collective-permute-start(f32[8,128]{1,0:T(8,128)S(1)} %maximum_maximum_fusion.1), channel_id=1, source_target_pairs={{0,3},{1,2},{2,1},{3,0},{4,7},{5,6},{6,5},{7,4},{8,11},{9,10},{10,... | collective-permute-start | bytes 12296 | tf_op jit(solution)/shard_map/ppermute | solution.py:633
  61.1 6.0 %collective-permute-start.6 = (f32[8,128]{1,0:T(8,128)S(1)}, f32[8,128]{1,0:T(8,128)S(1)}, u32[]{:S(2)}, u32[]{:S(2)}) collective-permute-start(f32[8,128]{1,0:T(8,128)S(1)} %maximum_maximum_fusion.1), channel_id=1, source_target_pairs={{0,2},{1,3},{2,0},{3,1},{4,6},{5,7},{6,4},{7,5},{8,10},{9,11},{10,... | collective-permute-start | bytes 12296 | tf_op jit(solution)/shard_map/ppermute | solution.py:633
  63.2 3.9 %collective-permute-start.5 = (f32[8,128]{1,0:T(8,128)S(1)}, f32[8,128]{1,0:T(8,128)S(1)}, u32[]{:S(2)}, u32[]{:S(2)}) collective-permute-start(f32[8,128]{1,0:T(8,128)S(1)} %maximum_maximum_fusion.1), channel_id=1, source_target_pairs={{0,1},{1,0},{2,3},{3,2},{4,5},{5,4},{6,7},{7,6},{8,9},{9,8},{10,11... | collective-permute-start | bytes 12296 | tf_op jit(solution)/shard_map/ppermute | solution.py:633

commit v17 on v16

--- a/solution.py
+++ b/solution.py
@@ -620,19 +620,22 @@
     )(*operands)
 
 
+def max_rounds(size):
+    rounds = []
+    while size > 4:
+        width = 4 if size >= 16 else 2
+        size //= width
+        rounds.append([size * times for times in range(1, width)])
+    return rounds + [[size // 2]] * (size == 4) + [[1]] * (size > 1)
+
+
 def everyone_max(value, axis, size):
-    reach = 1
-    while reach * 4 < size:
-        reach *= 4
-    while reach:
+    for turns in max_rounds(size):
         copies = [value]
-        for times in range(1, 4):
-            turn = reach * times
-            if turn < size:
-                pairs = [(i, i ^ turn) for i in range(size)]
-                copies.append(lax.ppermute(value, axis, pairs))
+        for turn in turns:
+            pairs = [(i, i ^ turn) for i in range(size)]
+            copies.append(lax.ppermute(value, axis, pairs))
         value = functools.reduce(jnp.maximum, copies)
-        reach //= 4
     return value
 
 

time: 74.7 us -> 75.7 us (1.013)
  waiting for transfers between devices: 30.7 us -> 32.2 us
    ppermute x6 -> x5, waiting for transfers between devices: 3.95 us -> 5.45 us  [everyone_max(): copies.append(lax.ppermute(value, axis, pairs))]
    ppermute x6 -> x5, starting transfers between devices: 6.67 us -> 5.3 us  [everyone_max(): copies.append(lax.ppermute(value, axis, pairs))]
    ppermute x2, starting transfers between devices: 8.89 us -> 9.79 us  [swapped(): lax.ppermute(far_side, 'gx', apart)]
  transfers between devices with their start and end apart: 11 -> 10, of which waited for: 3 -> 5; matrix products, arithmetic and copies ran while one was open for 1% -> 1% of each run, Pallas kernels for 12% -> 12%
where the time goes in v17:
time: 75.7 us; the launch traced here: 75.5 us
  waiting for transfers between devices  32.2 us (43%)
  starting transfers between devices  22.5 us (30%)
  Pallas kernels  19.9 us (26%)
    all_to_all x1, waiting for transfers between devices, per_device(): come = lax.all_to_all(parts, 'gx', split_axis=0, concat_axis=0, tiled=True)  26.8 us
    ppermute x2, starting transfers between devices, swapped(): lax.ppermute(far_side, 'gx', apart)  9.79 us
    pallas_call x2, Pallas kernels, along_planes(): pl.pallas_call(functools.partial(plane_kernel, with_inner), out_shape=jax...  9.26 us
    all_to_all x1, starting transfers between devices, per_device(): come = lax.all_to_all(parts, 'gx', split_axis=0, concat_axis=0, tiled=True)  7.37 us
    ppermute x5, waiting for transfers between devices, everyone_max(): copies.append(lax.ppermute(value, axis, pairs))  5.45 us
    ppermute x5, starting transfers between devices, everyone_max(): copies.append(lax.ppermute(value, axis, pairs))  5.3 us
    pallas_call x1, Pallas kernels, second_stage(): pl.pallas_call(second_kernel, out_shape=jax.ShapeDtypeStruct((FIELDS, BLO...  3.25 us
    pallas_call x1, Pallas kernels, unpack(): pl.pallas_call(functools.partial(unpack_kernel, size, cap), out_shape=(ja...  2.79 us
  transfers between devices with their start and end apart: 10, of which 5 were waited for; matrix products, arithmetic and copies ran while one was open for 1% of the time, Pallas kernels for 12%

profile of v17, /device:TPU:0, one launch (start us, length us, event | category | flops | bytes accessed | tf_op | source)
XLA Modules:
  0.0 75.5 jit_solution(10521882551732672666)
XLA Ops:
  0.0 2.7 %pack.1 = f32[16,161,1,128]{3,2,1,0:T(1,128)} custom-call(s32[1024]{0:T(1024)} %owner_hbm.1, f32[1280,128]{1,0:T(8,128)} %bitcast.7), custom_call_target="tpu_custom_call" | custom-call | flops 1000000 | bytes 3000000 | tf_op jit(solution)/shard_map/pack/pallas_call | solution.py:110
  2.7 0.0 copy-start
  2.8 0.0 copy-start.1
  2.8 7.4 %all-to-all-start = ((f32[16,161,1,128]{3,2,1,0:T(1,128)}), f32[16,161,1,128]{3,2,1,0:T(1,128)S(1)}, u32[]{:S(2)}, u32[]{:S(2)}) async-start(f32[16,161,1,128]{3,2,1,0:T(1,128)} %pack.1), calls=%async_computation | async-start | bytes 2637824 | tf_op jit(solution)/shard_map/all_to_all | solution.py:650
  10.2 0.1 eq.33
  10.3 0.3 convert_reduce_fusion
  10.6 0.1 broadcast_add_fusion
  10.7 0.1 add.17
  10.8 0.1 select_reduce_fusion.table
  10.9 26.8 %all-to-all-done = f32[16,161,1,128]{3,2,1,0:T(1,128)S(1)} async-done(((f32[16,161,1,128]{3,2,1,0:T(1,128)}), f32[16,161,1,128]{3,2,1,0:T(1,128)S(1)}, u32[]{:S(2)}, u32[]{:S(2)}) %all-to-all-start) | async-done | bytes 1318944 | tf_op jit(solution)/shard_map/all_to_all | solution.py:650
  37.7 2.8 %unpack.1 = (f32[5,8,32,128]{3,2,1,0:T(8,128)S(1)}, f32[5,3,32,128]{3,2,1,0:T(8,128)S(1)}, f32[5,3,32,128]{3,2,1,0:T(8,128)S(1)}, f32[8,128]{1,0:T(8,128)S(1)}) custom-call(s32[64]{0:T(128)S(1)} %select_reduce_fusion.table, f32[2576,128]{1,0:T(8,128)S(1)} %bitcast.6), custom_call_target="tpu_custom_call" | custom-call | flops 5000000 | bytes 2000000 | tf_op jit(solution)/shard_map/unpack/pallas_call | solution.py:226
  40.5 6.6 %collective-permute-start = (f32[5,3,32,128]{3,2,1,0:T(8,128)S(1)}, f32[5,3,32,128]{3,2,1,0:T(8,128)S(1)}, u32[]{:S(2)}, u32[]{:S(2)}) collective-permute-start(f32[5,3,32,128]{3,2,1,0:T(8,128)S(1)} %get-tuple-element.21), channel_id=1, source_target_pairs={{0,15},{1,2},{2,1},{3,4},{4,3},{5,6},{6,5},{7,8},{8,7},{9,10},{10,... | collective-permute-start | bytes 737288 | tf_op jit(solution)/shard_map/ppermute | solution.py:137
  47.1 5.2 %planes.2.sides = f32[5,8,32,128]{3,2,1,0:T(8,128)S(1)} custom-call(f32[5,8,32,128]{3,2,1,0:T(8,128)S(1)} %get-tuple-element.19.state.start, f32[8,128]{1,0:T(8,128)S(1)} %get-tuple-element.20.speed.first_speed), custom_call_target="tpu_custom_call" | custom-call | flops 20000000 | bytes 1000000 | tf_op jit(solution)/shard_map/planes/pallas_call | solution.py:490
  52.3 1.8 %first_stage.1 = (f32[5,8,32,128]{3,2,1,0:T(8,128)S(1)}, f32[5,3,32,128]{3,2,1,0:T(8,128)S(1)}, f32[5,3,32,128]{3,2,1,0:T(8,128)S(1)}, f32[8,128]{1,0:T(8,128)S(1)}) custom-call(f32[5,8,32,128]{3,2,1,0:T(8,128)S(1)} %get-tuple-element.19.state.start, f32[5,8,32,128]{3,2,1,0:T(8,128)S(1)} %planes.2.sides, f32[5,3,32,128]{3,2,1,0:T(8,128)S(1)} %collective-permute-done.far, ...), custom_call_target="tpu_custom_call" | custom-call | flops 30000000 | bytes 3000000 | tf_op jit(solution)/shard_map/first_stage/pallas_call | solution.py:570
  54.2 3.2 %collective-permute-start.7 = (f32[5,3,32,128]{3,2,1,0:T(8,128)S(1)}, f32[5,3,32,128]{3,2,1,0:T(8,128)S(1)}, u32[]{:S(2)}, u32[]{:S(2)}) collective-permute-start(f32[5,3,32,128]{3,2,1,0:T(8,128)S(1)} %get-tuple-element.25), channel_id=1, source_target_pairs={{0,15},{1,2},{2,1},{3,4},{4,3},{5,6},{6,5},{7,8},{8,7},{9,10},{10,... | collective-permute-start | bytes 737288 | tf_op jit(solution)/shard_map/ppermute | solution.py:137
  57.4 1.4 %collective-permute-start.3 = (f32[8,128]{1,0:T(8,128)S(1)}, f32[8,128]{1,0:T(8,128)S(1)}, u32[]{:S(2)}, u32[]{:S(2)}) collective-permute-start(f32[8,128]{1,0:T(8,128)S(1)} %get-tuple-element.24), channel_id=1, source_target_pairs={{0,8},{1,9},{2,10},{3,11},{4,12},{5,13},{6,14},{7,15},{8,0},{9,1},... | collective-permute-start | bytes 12296 | tf_op jit(solution)/shard_map/ppermute | solution.py:637
  58.7 3.0 %collective-permute-start.2 = (f32[8,128]{1,0:T(8,128)S(1)}, f32[8,128]{1,0:T(8,128)S(1)}, u32[]{:S(2)}, u32[]{:S(2)}) collective-permute-start(f32[8,128]{1,0:T(8,128)S(1)} %get-tuple-element.24), channel_id=1, source_target_pairs={{0,4},{1,5},{2,6},{3,7},{4,0},{5,1},{6,2},{7,3},{8,12},{9,13},{10,... | collective-permute-start | bytes 12296 | tf_op jit(solution)/shard_map/ppermute | solution.py:637
  61.8 1.0 %collective-permute-done.4 = f32[8,128]{1,0:T(8,128)S(1)} collective-permute-done((f32[8,128]{1,0:T(8,128)S(1)}, f32[8,128]{1,0:T(8,128)S(1)}, u32[]{:S(2)}, u32[]{:S(2)}) %collective-permute-start.4) | collective-permute-done | bytes 4128 | tf_op jit(solution)/shard_map/ppermute | solution.py:637
  62.8 0.6 collective-permute-done.2
  63.3 0.9 %collective-permute-start.5 = (f32[8,128]{1,0:T(8,128)S(1)}, f32[8,128]{1,0:T(8,128)S(1)}, u32[]{:S(2)}, u32[]{:S(2)}) collective-permute-start(f32[8,128]{1,0:T(8,128)S(1)} %maximum_maximum_fusion), channel_id=1, source_target_pairs={{0,2},{1,3},{2,0},{3,1},{4,6},{5,7},{6,4},{7,5},{8,10},{9,11},{10,... | collective-permute-start | bytes 12296 | tf_op jit(solution)/shard_map/ppermute | solution.py:637
  64.2 2.7 %collective-permute-done.5 = f32[8,128]{1,0:T(8,128)S(1)} collective-permute-done((f32[8,128]{1,0:T(8,128)S(1)}, f32[8,128]{1,0:T(8,128)S(1)}, u32[]{:S(2)}, u32[]{:S(2)}) %collective-permute-start.5) | collective-permute-done | bytes 4128 | tf_op jit(solution)/shard_map/ppermute | solution.py:637
  67.0 1.2 %collective-permute-done.6 = f32[8,128]{1,0:T(8,128)S(1)} collective-permute-done((f32[8,128]{1,0:T(8,128)S(1)}, f32[8,128]{1,0:T(8,128)S(1)}, u32[]{:S(2)}, u32[]{:S(2)}) %collective-permute-start.6) | collective-permute-done | bytes 4128 | tf_op jit(solution)/shard_map/ppermute | solution.py:637
  68.1 4.1 %planes.3.sides = f32[5,8,32,128]{3,2,1,0:T(8,128)S(1)} custom-call(f32[5,8,32,128]{3,2,1,0:T(8,128)S(1)} %get-tuple-element.23.state.middle, f32[8,128]{1,0:T(8,128)S(1)} %max.19.speed), custom_call_target="tpu_custom_call" | custom-call | flops 20000000 | bytes 1000000 | tf_op jit(solution)/shard_map/planes/pallas_call | solution.py:490
  72.2 3.3 %second_stage.1 = f32[5,8,32,128]{3,2,1,0:T(8,128)} custom-call(f32[5,8,32,128]{3,2,1,0:T(8,128)S(1)} %get-tuple-element.19.state.start, f32[5,8,32,128]{3,2,1,0:T(8,128)S(1)} %get-tuple-element.23.state.middle, f32[5,8,32,128]{3,2,1,0:T(8,128)S(1)} %planes.3.sides, f32[5,3,32,128]{3,2,1,0:T(8,128)S(1)} %collective-permute-done.7.far, ...), custom_call_target="tpu_custom_call" | custom-call | flops 30000000 | bytes 3000000 | tf_op jit(solution)/shard_map/second_stage/pallas_call | solution.py:611
  (17 shorter events, 0.1 us)
Async XLA Ops:
  2.7 7.4 %copy-start = (s32[1024]{0:T(1024)S(1)}, s32[1024]{0:T(1024)}, u32[]{:S(2)}) copy-start(s32[1024]{0:T(1024)} %owner_hbm.1) | copy-start | bytes 12292
  2.8 7.4 %copy-start.1 = (s32[1024]{0:T(1024)S(1)}, s32[1024]{0:T(1024)}, u32[]{:S(2)}) copy-start(s32[1024]{0:T(1024)} %param.5) | copy-start | bytes 12292
  2.8 34.9 %all-to-all-start = ((f32[16,161,1,128]{3,2,1,0:T(1,128)}), f32[16,161,1,128]{3,2,1,0:T(1,128)S(1)}, u32[]{:S(2)}, u32[]{:S(2)}) async-start(f32[16,161,1,128]{3,2,1,0:T(1,128)} %pack.1), calls=%async_computation | async-start | bytes 2637824 | tf_op jit(solution)/shard_map/all_to_all | solution.py:650
  40.5 11.8 %collective-permute-start = (f32[5,3,32,128]{3,2,1,0:T(8,128)S(1)}, f32[5,3,32,128]{3,2,1,0:T(8,128)S(1)}, u32[]{:S(2)}, u32[]{:S(2)}) collective-permute-start(f32[5,3,32,128]{3,2,1,0:T(8,128)S(1)} %get-tuple-element.21), channel_id=1, source_target_pairs={{0,15},{1,2},{2,1},{3,4},{4,3},{5,6},{6,5},{7,8},{8,7},{9,10},{10,... | collective-permute-start | bytes 737288 | tf_op jit(solution)/shard_map/ppermute | solution.py:137
  47.1 5.2 %collective-permute-start.1 = (f32[5,3,32,128]{3,2,1,0:T(8,128)S(1)}, f32[5,3,32,128]{3,2,1,0:T(8,128)S(1)}, u32[]{:S(2)}, u32[]{:S(2)}) collective-permute-start(f32[5,3,32,128]{3,2,1,0:T(8,128)S(1)} %get-tuple-element.22), channel_id=1, source_target_pairs={{0,1},{1,0},{2,3},{3,2},{4,5},{5,4},{6,7},{7,6},{8,9},{9,8},{10,11... | collective-permute-start | bytes 737288 | tf_op jit(solution)/shard_map/ppermute | solution.py:137
  54.2 18.0 %collective-permute-start.7 = (f32[5,3,32,128]{3,2,1,0:T(8,128)S(1)}, f32[5,3,32,128]{3,2,1,0:T(8,128)S(1)}, u32[]{:S(2)}, u32[]{:S(2)}) collective-permute-start(f32[5,3,32,128]{3,2,1,0:T(8,128)S(1)} %get-tuple-element.25), channel_id=1, source_target_pairs={{0,15},{1,2},{2,1},{3,4},{4,3},{5,6},{6,5},{7,8},{8,7},{9,10},{10,... | collective-permute-start | bytes 737288 | tf_op jit(solution)/shard_map/ppermute | solution.py:137
  57.4 14.9 %collective-permute-start.8 = (f32[5,3,32,128]{3,2,1,0:T(8,128)S(1)}, f32[5,3,32,128]{3,2,1,0:T(8,128)S(1)}, u32[]{:S(2)}, u32[]{:S(2)}) collective-permute-start(f32[5,3,32,128]{3,2,1,0:T(8,128)S(1)} %get-tuple-element.26), channel_id=1, source_target_pairs={{0,1},{1,0},{2,3},{3,2},{4,5},{5,4},{6,7},{7,6},{8,9},{9,8},{10,11... | collective-permute-start | bytes 737288 | tf_op jit(solution)/shard_map/ppermute | solution.py:137
  57.4 5.4 %collective-permute-start.4 = (f32[8,128]{1,0:T(8,128)S(1)}, f32[8,128]{1,0:T(8,128)S(1)}, u32[]{:S(2)}, u32[]{:S(2)}) collective-permute-start(f32[8,128]{1,0:T(8,128)S(1)} %get-tuple-element.24), channel_id=1, source_target_pairs={{0,12},{1,13},{2,14},{3,15},{4,8},{5,9},{6,10},{7,11},{8,4},{9,5},... | collective-permute-start | bytes 12296 | tf_op jit(solution)/shard_map/ppermute | solution.py:637
  57.4 5.4 %collective-permute-start.3 = (f32[8,128]{1,0:T(8,128)S(1)}, f32[8,128]{1,0:T(8,128)S(1)}, u32[]{:S(2)}, u32[]{:S(2)}) collective-permute-start(f32[8,128]{1,0:T(8,128)S(1)} %get-tuple-element.24), channel_id=1, source_target_pairs={{0,8},{1,9},{2,10},{3,11},{4,12},{5,13},{6,14},{7,15},{8,0},{9,1},... | collective-permute-start | bytes 12296 | tf_op jit(solution)/shard_map/ppermute | solution.py:637
  58.7 4.6 %collective-permute-start.2 = (f32[8,128]{1,0:T(8,128)S(1)}, f32[8,128]{1,0:T(8,128)S(1)}, u32[]{:S(2)}, u32[]{:S(2)}) collective-permute-start(f32[8,128]{1,0:T(8,128)S(1)} %get-tuple-element.24), channel_id=1, source_target_pairs={{0,4},{1,5},{2,6},{3,7},{4,0},{5,1},{6,2},{7,3},{8,12},{9,13},{10,... | collective-permute-start | bytes 12296 | tf_op jit(solution)/shard_map/ppermute | solution.py:637
  63.3 3.6 %collective-permute-start.5 = (f32[8,128]{1,0:T(8,128)S(1)}, f32[8,128]{1,0:T(8,128)S(1)}, u32[]{:S(2)}, u32[]{:S(2)}) collective-permute-start(f32[8,128]{1,0:T(8,128)S(1)} %maximum_maximum_fusion), channel_id=1, source_target_pairs={{0,2},{1,3},{2,0},{3,1},{4,6},{5,7},{6,4},{7,5},{8,10},{9,11},{10,... | collective-permute-start | bytes 12296 | tf_op jit(solution)/shard_map/ppermute | solution.py:637
  67.0 1.2 %collective-permute-start.6 = (f32[8,128]{1,0:T(8,128)S(1)}, f32[8,128]{1,0:T(8,128)S(1)}, u32[]{:S(2)}, u32[]{:S(2)}) collective-permute-start(f32[8,128]{1,0:T(8,128)S(1)} %max.18), channel_id=1, source_target_pairs={{0,1},{1,0},{2,3},{3,2},{4,5},{5,4},{6,7},{7,6},{8,9},{9,8},{10,11... | collective-permute-start | bytes 12296 | tf_op jit(solution)/shard_map/ppermute | solution.py:637

commit v18 on v16

--- a/solution.py
+++ b/solution.py
@@ -156,7 +156,7 @@
     spot = jnp.arange(per_dev, dtype=jnp.int32)
     earlier = spot[None, :] < spot[:, None]
     rank = jnp.sum((mine[:, None, :] & earlier[None]).astype(jnp.int32), axis=2)
-    row = jnp.arange(size, dtype=jnp.int32)[:, None] * cap + rank
+    row = jnp.arange(size, dtype=jnp.int32)[:, None] * (TILES * cap + 1) + rank
     key = jnp.where(mine, slots, -1)
     hit = key.reshape(1, -1) == spot[:, None]
     return jnp.max(jnp.where(hit, row.reshape(1, -1), 0), axis=1)
@@ -182,37 +182,41 @@
     for source in range(1, size):
         best = jnp.maximum(best, come[(source + 1) * message - 1 : (source + 1) * message, :])
     speed[...] = jnp.broadcast_to(best, speed.shape)
-    for slot in range(BY * BZ):
-        p, q = divmod(slot, BZ)
-        where = table[slot]
-        source = lax.div(where, cap)
-        rank = lax.rem(where, cap)
-        for pair in range(PAIRS):
-            couple, h = divmod(pair, 2)
-            base = source * message + rank + pair * (FIELDS * cap)
-            value = come[pl.ds(base, FIELDS, stride=cap), :]
-            row = (couple * BZ + q) * 8 + 2 * p + h
-            scratch[pl.ds(row, FIELDS, stride=PAIRS // 2 * BZ * 8), :] = value
     group = lax.broadcasted_iota(jnp.int32, (8, LANES), 1) // BLOCK
     even = lax.broadcasted_iota(jnp.int32, (8, LANES), 0) % 2 == 0
-
+    half = FIELDS * BZ * 8
+
+    def gather(couple, slot):
+        p, q = divmod(slot, BZ)
+        for h in range(2):
+            base = table[slot] + (2 * couple + h) * (FIELDS * cap)
+            value = come[pl.ds(base, FIELDS, stride=cap), :]
+            scratch[pl.ds(couple * half + q * 8 + 2 * p + h, FIELDS, stride=BZ * 8), :] = value
+
+    def arrange(couple, f):
+        first = couple * half + f * BZ * 8
+        moved = exchanged_bits(
+            [scratch[first + q * 8 : first + q * 8 + 8, :] for q in range(BZ)], group
+        )
+        for second in range(2):
+            for j in range(4):
+                lower = moved[second * BLOCK + j]
+                upper = moved[second * BLOCK + j + 4]
+                planes = (
+                    jnp.where(even, lower, pltpu.roll(upper, 1, 0)),
+                    jnp.where(even, pltpu.roll(lower, 7, 0), upper),
+                )
+                for h in range(2):
+                    state[f, 4 * couple + 2 * h + second, j * 8 : j * 8 + 8, :] = planes[h]
+
+    for slot in range(BY * BZ):
+        gather(0, slot)
     for f in range(FIELDS):
-        for couple in range(PAIRS // 2):
-            first = (f * (PAIRS // 2) + couple) * BZ * 8
-            rows = [scratch[first + q * 8 : first + q * 8 + 8, :] for q in range(BZ)]
-            moved = exchanged_bits(rows, group)
-            for second in range(2):
-                for j in range(4):
-                    lower = moved[second * BLOCK + j]
-                    upper = moved[second * BLOCK + j + 4]
-                    planes = (
-                        jnp.where(even, lower, pltpu.roll(upper, 1, 0)),
-                        jnp.where(even, pltpu.roll(lower, 7, 0), upper),
-                    )
-                    rows = slice(j * 8, j * 8 + 8)
-                    for h in range(2):
-                        plane = 4 * couple + 2 * h + second
-                        state[f, plane, rows, :] = planes[h]
+        for slot in range(f, BY * BZ, FIELDS):
+            gather(1, slot)
+        arrange(0, f)
+    for f in range(FIELDS):
+        arrange(1, f)
     lower_first = own_is_even()
     for f in range(FIELDS):
         for plane in range(3):

time: 74.7 us -> 74.6 us (level)
  no operation moved by 1% of the time
where the time goes in v18:
time: 74.6 us; the launch traced here: 74.4 us
  waiting for transfers between devices  30.7 us (41%)
  starting transfers between devices  22.9 us (31%)
  Pallas kernels  19.8 us (27%)
    all_to_all x1, waiting for transfers between devices, per_device(): come = lax.all_to_all(parts, 'gx', split_axis=0, concat_axis=0, tiled=True)  26.8 us
    pallas_call x2, Pallas kernels, along_planes(): pl.pallas_call(functools.partial(plane_kernel, with_inner), out_shape=jax...  9.26 us
    ppermute x2, starting transfers between devices, swapped(): lax.ppermute(far_side, 'gx', apart)  8.89 us
    all_to_all x1, starting transfers between devices, per_device(): come = lax.all_to_all(parts, 'gx', split_axis=0, concat_axis=0, tiled=True)  7.37 us
    ppermute x6, starting transfers between devices, everyone_max(): copies.append(lax.ppermute(value, axis, pairs))  6.67 us
    ppermute x6, waiting for transfers between devices, everyone_max(): copies.append(lax.ppermute(value, axis, pairs))  3.95 us
    pallas_call x1, Pallas kernels, second_stage(): pl.pallas_call(second_kernel, out_shape=jax.ShapeDtypeStruct((FIELDS, BLO...  3.25 us
    pallas_call x1, Pallas kernels, pack(): pl.pallas_call(functools.partial(pack_kernel, size, cap, per_dev), out_sh...  2.74 us
  transfers between devices with their start and end apart: 11, of which 3 were waited for; matrix products, arithmetic and copies ran while one was open for 1% of the time, Pallas kernels for 12%

profile of v18, /device:TPU:0, one launch (start us, length us, event | category | flops | bytes accessed | tf_op | source)
XLA Modules:
  0.0 74.4 jit_solution(13685628961698540087)
XLA Ops:
  0.0 2.7 %pack.1 = f32[16,161,1,128]{3,2,1,0:T(1,128)} custom-call(s32[1024]{0:T(1024)} %owner_hbm.1, f32[1280,128]{1,0:T(8,128)} %bitcast.7), custom_call_target="tpu_custom_call" | custom-call | flops 1000000 | bytes 3000000 | tf_op jit(solution)/shard_map/pack/pallas_call | solution.py:110
  2.7 0.0 copy-start
  2.8 0.0 copy-start.1
  2.8 7.4 %all-to-all-start = ((f32[16,161,1,128]{3,2,1,0:T(1,128)}), f32[16,161,1,128]{3,2,1,0:T(1,128)S(1)}, u32[]{:S(2)}, u32[]{:S(2)}) async-start(f32[16,161,1,128]{3,2,1,0:T(1,128)} %pack.1), calls=%async_computation | async-start | bytes 2637824 | tf_op jit(solution)/shard_map/all_to_all | solution.py:651
  10.2 0.1 eq.33
  10.3 0.3 convert_reduce_fusion
  10.6 0.1 broadcast_add_fusion
  10.7 0.1 add.17
  10.8 0.1 select_reduce_fusion.table
  10.9 26.8 %all-to-all-done = f32[16,161,1,128]{3,2,1,0:T(1,128)S(1)} async-done(((f32[16,161,1,128]{3,2,1,0:T(1,128)}), f32[16,161,1,128]{3,2,1,0:T(1,128)S(1)}, u32[]{:S(2)}, u32[]{:S(2)}) %all-to-all-start) | async-done | bytes 1318944 | tf_op jit(solution)/shard_map/all_to_all | solution.py:651
  37.7 2.7 %unpack.1 = (f32[5,8,32,128]{3,2,1,0:T(8,128)S(1)}, f32[5,3,32,128]{3,2,1,0:T(8,128)S(1)}, f32[5,3,32,128]{3,2,1,0:T(8,128)S(1)}, f32[8,128]{1,0:T(8,128)S(1)}) custom-call(s32[64]{0:T(128)S(1)} %select_reduce_fusion.table, f32[2576,128]{1,0:T(8,128)S(1)} %bitcast.6), custom_call_target="tpu_custom_call" | custom-call | flops 5000000 | bytes 2000000 | tf_op jit(solution)/shard_map/unpack/pallas_call | solution.py:230
  40.4 6.6 %collective-permute-start = (f32[5,3,32,128]{3,2,1,0:T(8,128)S(1)}, f32[5,3,32,128]{3,2,1,0:T(8,128)S(1)}, u32[]{:S(2)}, u32[]{:S(2)}) collective-permute-start(f32[5,3,32,128]{3,2,1,0:T(8,128)S(1)} %get-tuple-element.21), channel_id=1, source_target_pairs={{0,15},{1,2},{2,1},{3,4},{4,3},{5,6},{6,5},{7,8},{8,7},{9,10},{10,... | collective-permute-start | bytes 737288 | tf_op jit(solution)/shard_map/ppermute | solution.py:137
  47.1 5.2 %planes.2.sides = f32[5,8,32,128]{3,2,1,0:T(8,128)S(1)} custom-call(f32[5,8,32,128]{3,2,1,0:T(8,128)S(1)} %get-tuple-element.19.state.start, f32[8,128]{1,0:T(8,128)S(1)} %get-tuple-element.20.speed.first_speed), custom_call_target="tpu_custom_call" | custom-call | flops 20000000 | bytes 1000000 | tf_op jit(solution)/shard_map/planes/pallas_call | solution.py:494
  52.3 1.8 %first_stage.1 = (f32[5,8,32,128]{3,2,1,0:T(8,128)S(1)}, f32[5,3,32,128]{3,2,1,0:T(8,128)S(1)}, f32[5,3,32,128]{3,2,1,0:T(8,128)S(1)}, f32[8,128]{1,0:T(8,128)S(1)}) custom-call(f32[5,8,32,128]{3,2,1,0:T(8,128)S(1)} %get-tuple-element.19.state.start, f32[5,8,32,128]{3,2,1,0:T(8,128)S(1)} %planes.2.sides, f32[5,3,32,128]{3,2,1,0:T(8,128)S(1)} %collective-permute-done.far, ...), custom_call_target="tpu_custom_call" | custom-call | flops 30000000 | bytes 3000000 | tf_op jit(solution)/shard_map/first_stage/pallas_call | solution.py:574
  54.1 0.8 %collective-permute-start.4 = (f32[8,128]{1,0:T(8,128)S(1)}, f32[8,128]{1,0:T(8,128)S(1)}, u32[]{:S(2)}, u32[]{:S(2)}) collective-permute-start(f32[8,128]{1,0:T(8,128)S(1)} %get-tuple-element.24), channel_id=1, source_target_pairs={{0,12},{1,13},{2,14},{3,15},{4,8},{5,9},{6,10},{7,11},{8,4},{9,5},... | collective-permute-start | bytes 12296 | tf_op jit(solution)/shard_map/ppermute | solution.py:637
  55.0 0.7 collective-permute-start.3
  55.6 3.0 %collective-permute-start.2 = (f32[8,128]{1,0:T(8,128)S(1)}, f32[8,128]{1,0:T(8,128)S(1)}, u32[]{:S(2)}, u32[]{:S(2)}) collective-permute-start(f32[8,128]{1,0:T(8,128)S(1)} %get-tuple-element.24), channel_id=1, source_target_pairs={{0,4},{1,5},{2,6},{3,7},{4,0},{5,1},{6,2},{7,3},{8,12},{9,13},{10,... | collective-permute-start | bytes 12296 | tf_op jit(solution)/shard_map/ppermute | solution.py:637
  58.6 2.3 %collective-permute-start.8 = (f32[5,3,32,128]{3,2,1,0:T(8,128)S(1)}, f32[5,3,32,128]{3,2,1,0:T(8,128)S(1)}, u32[]{:S(2)}, u32[]{:S(2)}) collective-permute-start(f32[5,3,32,128]{3,2,1,0:T(8,128)S(1)} %get-tuple-element.25), channel_id=1, source_target_pairs={{0,15},{1,2},{2,1},{3,4},{4,3},{5,6},{6,5},{7,8},{8,7},{9,10},{10,... | collective-permute-start | bytes 737288 | tf_op jit(solution)/shard_map/ppermute | solution.py:137
  60.9 0.1 collective-permute-start.7
  61.0 2.1 %collective-permute-start.6 = (f32[8,128]{1,0:T(8,128)S(1)}, f32[8,128]{1,0:T(8,128)S(1)}, u32[]{:S(2)}, u32[]{:S(2)}) collective-permute-start(f32[8,128]{1,0:T(8,128)S(1)} %maximum_maximum_fusion.1), channel_id=1, source_target_pairs={{0,2},{1,3},{2,0},{3,1},{4,6},{5,7},{6,4},{7,5},{8,10},{9,11},{10,... | collective-permute-start | bytes 12296 | tf_op jit(solution)/shard_map/ppermute | solution.py:637
  63.1 1.0 %collective-permute-done.7 = f32[8,128]{1,0:T(8,128)S(1)} collective-permute-done((f32[8,128]{1,0:T(8,128)S(1)}, f32[8,128]{1,0:T(8,128)S(1)}, u32[]{:S(2)}, u32[]{:S(2)}) %collective-permute-start.7) | collective-permute-done | bytes 4128 | tf_op jit(solution)/shard_map/ppermute | solution.py:637
  64.1 2.9 %collective-permute-done.6 = f32[8,128]{1,0:T(8,128)S(1)} collective-permute-done((f32[8,128]{1,0:T(8,128)S(1)}, f32[8,128]{1,0:T(8,128)S(1)}, u32[]{:S(2)}, u32[]{:S(2)}) %collective-permute-start.6) | collective-permute-done | bytes 4128 | tf_op jit(solution)/shard_map/ppermute | solution.py:637
  67.0 4.1 %planes.3.sides = f32[5,8,32,128]{3,2,1,0:T(8,128)S(1)} custom-call(f32[5,8,32,128]{3,2,1,0:T(8,128)S(1)} %get-tuple-element.23.state.middle, f32[8,128]{1,0:T(8,128)S(1)} %maximum_maximum_fusion.speed), custom_call_target="tpu_custom_call" | custom-call | flops 20000000 | bytes 1000000 | tf_op jit(solution)/shard_map/planes/pallas_call | solution.py:494
  71.1 3.3 %second_stage.1 = f32[5,8,32,128]{3,2,1,0:T(8,128)} custom-call(f32[5,8,32,128]{3,2,1,0:T(8,128)S(1)} %get-tuple-element.19.state.start, f32[5,8,32,128]{3,2,1,0:T(8,128)S(1)} %get-tuple-element.23.state.middle, f32[5,8,32,128]{3,2,1,0:T(8,128)S(1)} %planes.3.sides, f32[5,3,32,128]{3,2,1,0:T(8,128)S(1)} %collective-permute-done.8.far, ...), custom_call_target="tpu_custom_call" | custom-call | flops 30000000 | bytes 3000000 | tf_op jit(solution)/shard_map/second_stage/pallas_call | solution.py:615
  (18 shorter events, 0.1 us)
Async XLA Ops:
  2.7 7.4 %copy-start = (s32[1024]{0:T(1024)S(1)}, s32[1024]{0:T(1024)}, u32[]{:S(2)}) copy-start(s32[1024]{0:T(1024)} %owner_hbm.1) | copy-start | bytes 12292
  2.8 7.4 %copy-start.1 = (s32[1024]{0:T(1024)S(1)}, s32[1024]{0:T(1024)}, u32[]{:S(2)}) copy-start(s32[1024]{0:T(1024)} %param.5) | copy-start | bytes 12292
  2.8 34.9 %all-to-all-start = ((f32[16,161,1,128]{3,2,1,0:T(1,128)}), f32[16,161,1,128]{3,2,1,0:T(1,128)S(1)}, u32[]{:S(2)}, u32[]{:S(2)}) async-start(f32[16,161,1,128]{3,2,1,0:T(1,128)} %pack.1), calls=%async_computation | async-start | bytes 2637824 | tf_op jit(solution)/shard_map/all_to_all | solution.py:651
  40.4 11.8 %collective-permute-start = (f32[5,3,32,128]{3,2,1,0:T(8,128)S(1)}, f32[5,3,32,128]{3,2,1,0:T(8,128)S(1)}, u32[]{:S(2)}, u32[]{:S(2)}) collective-permute-start(f32[5,3,32,128]{3,2,1,0:T(8,128)S(1)} %get-tuple-element.21), channel_id=1, source_target_pairs={{0,15},{1,2},{2,1},{3,4},{4,3},{5,6},{6,5},{7,8},{8,7},{9,10},{10,... | collective-permute-start | bytes 737288 | tf_op jit(solution)/shard_map/ppermute | solution.py:137
  47.1 5.2 %collective-permute-start.1 = (f32[5,3,32,128]{3,2,1,0:T(8,128)S(1)}, f32[5,3,32,128]{3,2,1,0:T(8,128)S(1)}, u32[]{:S(2)}, u32[]{:S(2)}) collective-permute-start(f32[5,3,32,128]{3,2,1,0:T(8,128)S(1)} %get-tuple-element.22), channel_id=1, source_target_pairs={{0,1},{1,0},{2,3},{3,2},{4,5},{5,4},{6,7},{7,6},{8,9},{9,8},{10,11... | collective-permute-start | bytes 737288 | tf_op jit(solution)/shard_map/ppermute | solution.py:137
  54.1 6.7 %collective-permute-start.4 = (f32[8,128]{1,0:T(8,128)S(1)}, f32[8,128]{1,0:T(8,128)S(1)}, u32[]{:S(2)}, u32[]{:S(2)}) collective-permute-start(f32[8,128]{1,0:T(8,128)S(1)} %get-tuple-element.24), channel_id=1, source_target_pairs={{0,12},{1,13},{2,14},{3,15},{4,8},{5,9},{6,10},{7,11},{8,4},{9,5},... | collective-permute-start | bytes 12296 | tf_op jit(solution)/shard_map/ppermute | solution.py:637
  55.0 5.9 %collective-permute-start.3 = (f32[8,128]{1,0:T(8,128)S(1)}, f32[8,128]{1,0:T(8,128)S(1)}, u32[]{:S(2)}, u32[]{:S(2)}) collective-permute-start(f32[8,128]{1,0:T(8,128)S(1)} %get-tuple-element.24), channel_id=1, source_target_pairs={{0,8},{1,9},{2,10},{3,11},{4,12},{5,13},{6,14},{7,15},{8,0},{9,1},... | collective-permute-start | bytes 12296 | tf_op jit(solution)/shard_map/ppermute | solution.py:637
  55.6 5.2 %collective-permute-start.2 = (f32[8,128]{1,0:T(8,128)S(1)}, f32[8,128]{1,0:T(8,128)S(1)}, u32[]{:S(2)}, u32[]{:S(2)}) collective-permute-start(f32[8,128]{1,0:T(8,128)S(1)} %get-tuple-element.24), channel_id=1, source_target_pairs={{0,4},{1,5},{2,6},{3,7},{4,0},{5,1},{6,2},{7,3},{8,12},{9,13},{10,... | collective-permute-start | bytes 12296 | tf_op jit(solution)/shard_map/ppermute | solution.py:637
  58.6 12.5 %collective-permute-start.8 = (f32[5,3,32,128]{3,2,1,0:T(8,128)S(1)}, f32[5,3,32,128]{3,2,1,0:T(8,128)S(1)}, u32[]{:S(2)}, u32[]{:S(2)}) collective-permute-start(f32[5,3,32,128]{3,2,1,0:T(8,128)S(1)} %get-tuple-element.25), channel_id=1, source_target_pairs={{0,15},{1,2},{2,1},{3,4},{4,3},{5,6},{6,5},{7,8},{8,7},{9,10},{10,... | collective-permute-start | bytes 737288 | tf_op jit(solution)/shard_map/ppermute | solution.py:137
  60.8 10.3 %collective-permute-start.9 = (f32[5,3,32,128]{3,2,1,0:T(8,128)S(1)}, f32[5,3,32,128]{3,2,1,0:T(8,128)S(1)}, u32[]{:S(2)}, u32[]{:S(2)}) collective-permute-start(f32[5,3,32,128]{3,2,1,0:T(8,128)S(1)} %get-tuple-element.26), channel_id=1, source_target_pairs={{0,1},{1,0},{2,3},{3,2},{4,5},{5,4},{6,7},{7,6},{8,9},{9,8},{10,11... | collective-permute-start | bytes 737288 | tf_op jit(solution)/shard_map/ppermute | solution.py:137
  60.9 3.2 %collective-permute-start.7 = (f32[8,128]{1,0:T(8,128)S(1)}, f32[8,128]{1,0:T(8,128)S(1)}, u32[]{:S(2)}, u32[]{:S(2)}) collective-permute-start(f32[8,128]{1,0:T(8,128)S(1)} %maximum_maximum_fusion.1), channel_id=1, source_target_pairs={{0,3},{1,2},{2,1},{3,0},{4,7},{5,6},{6,5},{7,4},{8,11},{9,10},{10,... | collective-permute-start | bytes 12296 | tf_op jit(solution)/shard_map/ppermute | solution.py:637
  61.0 6.0 %collective-permute-start.6 = (f32[8,128]{1,0:T(8,128)S(1)}, f32[8,128]{1,0:T(8,128)S(1)}, u32[]{:S(2)}, u32[]{:S(2)}) collective-permute-start(f32[8,128]{1,0:T(8,128)S(1)} %maximum_maximum_fusion.1), channel_id=1, source_target_pairs={{0,2},{1,3},{2,0},{3,1},{4,6},{5,7},{6,4},{7,5},{8,10},{9,11},{10,... | collective-permute-start | bytes 12296 | tf_op jit(solution)/shard_map/ppermute | solution.py:637
  63.1 3.9 %collective-permute-start.5 = (f32[8,128]{1,0:T(8,128)S(1)}, f32[8,128]{1,0:T(8,128)S(1)}, u32[]{:S(2)}, u32[]{:S(2)}) collective-permute-start(f32[8,128]{1,0:T(8,128)S(1)} %maximum_maximum_fusion.1), channel_id=1, source_target_pairs={{0,1},{1,0},{2,3},{3,2},{4,5},{5,4},{6,7},{7,6},{8,9},{9,8},{10,11... | collective-permute-start | bytes 12296 | tf_op jit(solution)/shard_map/ppermute | solution.py:637

commit v19 on v18

--- a/solution.py
+++ b/solution.py
@@ -46,17 +46,19 @@
 def tiled_rows(blocks):
     count = blocks.shape[0] // 8
     groups = blocks.reshape(count, 8, FIELDS, PAIRS, LANES).transpose(2, 0, 3, 1, 4)
-    return groups.reshape(FIELDS * count * PAIRS * 8, LANES)
+    return groups.reshape(FIELDS * count * PAIRS * 8, 1, LANES)
 
 
 def pack_kernel(
-    size, cap, per_dev, owner_hbm, rows_hbm, out_hbm, owner, rows, out, top, count, member, sems
+    size, cap, per_dev, owner_hbm, rows_hbm, out_hbm, owner, rows, tiled, out, top, count, member, sems
 ):
     own = lax.axis_index("gx")
     fetch_owner = pltpu.make_async_copy(owner_hbm, owner, sems.at[0])
     fetch_rows = pltpu.make_async_copy(rows_hbm, rows, sems.at[1])
+    fetch_tiled = pltpu.make_async_copy(rows_hbm.at[:, 0], tiled, sems.at[4])
     fetch_owner.start()
     fetch_rows.start()
+    fetch_tiled.start()
 
     def clear(dest, carry):
         count[dest] = 0
@@ -82,19 +84,20 @@
             for rank in range(cap):
                 first = member[dest * cap + rank]
                 for pair in range(PAIRS):
-                    source = pl.ds(first + pair * 8, FIELDS, stride=per_dev * PAIRS)
-                    to = dest * tiles + pair * (FIELDS * cap) + rank
-                    out[pl.ds(to, FIELDS, stride=cap), :] = rows[source, :]
-            part = out.at[pl.ds(pl.multiple_of(dest * tiles, tiles), tiles)]
-            pltpu.make_async_copy(part, out_hbm.at[dest, pl.ds(0, tiles), 0], sems.at[2]).start()
+                    for f in range(FIELDS):
+                        to = dest * tiles + (pair * FIELDS + f) * cap + rank
+                        out[to] = rows[first + f * (per_dev * PAIRS) + pair * 8]
+            part = out.at[pl.ds(dest * tiles, tiles)]
+            pltpu.make_async_copy(part, out_hbm.at[dest, pl.ds(0, tiles)], sems.at[2]).start()
 
         return carry
 
     lax.fori_loop(0, size, message, 0)
+    fetch_tiled.wait()
     best = jnp.zeros((8, LANES), jnp.float32)
     step = per_dev * PAIRS
     for first in range(0, step, 8):
-        fields = [rows[f * step + first : f * step + first + 8, :] for f in range(FIELDS)]
+        fields = [tiled[f * step + first : f * step + first + 8, :] for f in range(FIELDS)]
         best = jnp.maximum(best, wave_speed(fields))
     top[...] = jnp.full(top.shape, jnp.max(best), jnp.float32)
     for dest in range(size):
@@ -115,11 +118,12 @@
         scratch_shapes=[
             pltpu.SMEM(owner_list.shape, jnp.int32),
             pltpu.VMEM(rows.shape, jnp.float32),
-            pltpu.VMEM((size * TILES * cap, LANES), jnp.float32),
+            pltpu.VMEM((rows.shape[0], LANES), jnp.float32),
+            pltpu.VMEM((size * TILES * cap, 1, LANES), jnp.float32),
             pltpu.VMEM((size, LANES), jnp.float32),
             pltpu.SMEM((size,), jnp.int32),
             pltpu.SMEM((size * cap,), jnp.int32),
-            pltpu.SemaphoreType.DMA((4,)),
+            pltpu.SemaphoreType.DMA((5,)),
         ],
         compiler_params=params(62),
         cost_estimate=cost(1_000_000, 3_000_000),
@@ -178,9 +182,9 @@
 
 def unpack_kernel(size, cap, table, come, state, far_side, near_side, speed, scratch):
     message = TILES * cap + 1
-    best = come[message - 1 : message, :]
+    best = come[message - 1]
     for source in range(1, size):
-        best = jnp.maximum(best, come[(source + 1) * message - 1 : (source + 1) * message, :])
+        best = jnp.maximum(best, come[(source + 1) * message - 1])
     speed[...] = jnp.broadcast_to(best, speed.shape)
     group = lax.broadcasted_iota(jnp.int32, (8, LANES), 1) // BLOCK
     even = lax.broadcasted_iota(jnp.int32, (8, LANES), 0) % 2 == 0
@@ -188,10 +192,12 @@
 
     def gather(couple, slot):
         p, q = divmod(slot, BZ)
+        first = table[slot]
         for h in range(2):
-            base = table[slot] + (2 * couple + h) * (FIELDS * cap)
-            value = come[pl.ds(base, FIELDS, stride=cap), :]
-            scratch[pl.ds(couple * half + q * 8 + 2 * p + h, FIELDS, stride=BZ * 8), :] = value
+            for f in range(FIELDS):
+                row = couple * half + (f * BZ + q) * 8 + 2 * p + h
+                value = come[first + ((2 * couple + h) * FIELDS + f) * cap]
+                scratch[row : row + 1, :] = value
 
     def arrange(couple, f):
         first = couple * half + f * BZ * 8
@@ -650,7 +656,7 @@
     parts, owner_list, slot_list = lax.optimization_barrier((parts, owner_list, slot_list))
     come = lax.all_to_all(parts, "gx", split_axis=0, concat_axis=0, tiled=True)
     table = arrival_spots(owner_list, slot_list, own, per_dev, size, cap)
-    state, far_side, near_side, speed = unpack(table, come.reshape(-1, LANES), size, cap)
+    state, far_side, near_side, speed = unpack(table, come.reshape(-1, 1, LANES), size, cap)
     far, near = swapped(far_side, near_side, size)
     sides = along_planes(state, speed, True)
     middle, far_side, near_side, top = first_stage(state, sides, far, near, speed)

time: 74.6 us -> 74.4 us (level)
  no operation moved by 1% of the time
where the time goes in v19:
time: 74.4 us; the launch traced here: 74.1 us
  waiting for transfers between devices  30.7 us (41%)
  starting transfers between devices  22.9 us (31%)
  Pallas kernels  19.6 us (26%)
    all_to_all x1, waiting for transfers between devices, per_device(): come = lax.all_to_all(parts, 'gx', split_axis=0, concat_axis=0, tiled=True)  26.8 us
    pallas_call x2, Pallas kernels, along_planes(): pl.pallas_call(functools.partial(plane_kernel, with_inner), out_shape=jax...  9.26 us
    ppermute x2, starting transfers between devices, swapped(): lax.ppermute(far_side, 'gx', apart)  8.89 us
    all_to_all x1, starting transfers between devices, per_device(): come = lax.all_to_all(parts, 'gx', split_axis=0, concat_axis=0, tiled=True)  7.37 us
    ppermute x6, starting transfers between devices, everyone_max(): copies.append(lax.ppermute(value, axis, pairs))  6.67 us
    ppermute x6, waiting for transfers between devices, everyone_max(): copies.append(lax.ppermute(value, axis, pairs))  3.95 us
    pallas_call x1, Pallas kernels, second_stage(): pl.pallas_call(second_kernel, out_shape=jax.ShapeDtypeStruct((FIELDS, BLO...  3.25 us
    pallas_call x1, Pallas kernels, pack(): pl.pallas_call(functools.partial(pack_kernel, size, cap, per_dev), out_sh...  2.74 us
  transfers between devices with their start and end apart: 11, of which 3 were waited for; matrix products, arithmetic and copies ran while one was open for 1% of the time, Pallas kernels for 12%

profile of v19, /device:TPU:0, one launch (start us, length us, event | category | flops | bytes accessed | tf_op | source)
XLA Modules:
  0.0 74.1 jit_solution(10271828657016556960)
XLA Ops:
  0.0 2.7 %pack.1 = f32[16,161,1,128]{3,2,1,0:T(1,128)} custom-call(s32[1024]{0:T(1024)} %owner_hbm.1, f32[1280,1,128]{2,1,0:T(1,128)} %bitcast.7), custom_call_target="tpu_custom_call" | custom-call | flops 1000000 | bytes 3000000 | tf_op jit(solution)/shard_map/pack/pallas_call | solution.py:113
  2.7 0.0 copy-start
  2.8 0.0 copy-start.1
  2.8 7.4 %all-to-all-start = ((f32[16,161,1,128]{3,2,1,0:T(1,128)}), f32[16,161,1,128]{3,2,1,0:T(1,128)S(1)}, u32[]{:S(2)}, u32[]{:S(2)}) async-start(f32[16,161,1,128]{3,2,1,0:T(1,128)} %pack.1), calls=%async_computation | async-start | bytes 2637824 | tf_op jit(solution)/shard_map/all_to_all | solution.py:657
  10.2 0.1 eq.33
  10.3 0.3 convert_reduce_fusion
  10.6 0.1 broadcast_add_fusion
  10.7 0.1 add.17
  10.8 0.1 select_reduce_fusion.table
  10.9 26.8 %all-to-all-done = f32[16,161,1,128]{3,2,1,0:T(1,128)S(1)} async-done(((f32[16,161,1,128]{3,2,1,0:T(1,128)}), f32[16,161,1,128]{3,2,1,0:T(1,128)S(1)}, u32[]{:S(2)}, u32[]{:S(2)}) %all-to-all-start) | async-done | bytes 1318944 | tf_op jit(solution)/shard_map/all_to_all | solution.py:657
  37.7 2.5 %unpack.1 = (f32[5,8,32,128]{3,2,1,0:T(8,128)S(1)}, f32[5,3,32,128]{3,2,1,0:T(8,128)S(1)}, f32[5,3,32,128]{3,2,1,0:T(8,128)S(1)}, f32[8,128]{1,0:T(8,128)S(1)}) custom-call(s32[64]{0:T(128)S(1)} %select_reduce_fusion.table, f32[2576,1,128]{2,1,0:T(1,128)S(1)} %bitcast.6), custom_call_target="tpu_custom_call" | custom-call | flops 5000000 | bytes 2000000 | tf_op jit(solution)/shard_map/unpack/pallas_call | solution.py:236
  40.2 6.6 %collective-permute-start = (f32[5,3,32,128]{3,2,1,0:T(8,128)S(1)}, f32[5,3,32,128]{3,2,1,0:T(8,128)S(1)}, u32[]{:S(2)}, u32[]{:S(2)}) collective-permute-start(f32[5,3,32,128]{3,2,1,0:T(8,128)S(1)} %get-tuple-element.21), channel_id=1, source_target_pairs={{0,15},{1,2},{2,1},{3,4},{4,3},{5,6},{6,5},{7,8},{8,7},{9,10},{10,... | collective-permute-start | bytes 737288 | tf_op jit(solution)/shard_map/ppermute | solution.py:141
  46.8 5.2 %planes.2.sides = f32[5,8,32,128]{3,2,1,0:T(8,128)S(1)} custom-call(f32[5,8,32,128]{3,2,1,0:T(8,128)S(1)} %get-tuple-element.19.state.start, f32[8,128]{1,0:T(8,128)S(1)} %get-tuple-element.20.speed.first_speed), custom_call_target="tpu_custom_call" | custom-call | flops 20000000 | bytes 1000000 | tf_op jit(solution)/shard_map/planes/pallas_call | solution.py:500
  52.0 1.8 %first_stage.1 = (f32[5,8,32,128]{3,2,1,0:T(8,128)S(1)}, f32[5,3,32,128]{3,2,1,0:T(8,128)S(1)}, f32[5,3,32,128]{3,2,1,0:T(8,128)S(1)}, f32[8,128]{1,0:T(8,128)S(1)}) custom-call(f32[5,8,32,128]{3,2,1,0:T(8,128)S(1)} %get-tuple-element.19.state.start, f32[5,8,32,128]{3,2,1,0:T(8,128)S(1)} %planes.2.sides, f32[5,3,32,128]{3,2,1,0:T(8,128)S(1)} %collective-permute-done.far, ...), custom_call_target="tpu_custom_call" | custom-call | flops 30000000 | bytes 3000000 | tf_op jit(solution)/shard_map/first_stage/pallas_call | solution.py:580
  53.9 0.8 %collective-permute-start.4 = (f32[8,128]{1,0:T(8,128)S(1)}, f32[8,128]{1,0:T(8,128)S(1)}, u32[]{:S(2)}, u32[]{:S(2)}) collective-permute-start(f32[8,128]{1,0:T(8,128)S(1)} %get-tuple-element.24), channel_id=1, source_target_pairs={{0,12},{1,13},{2,14},{3,15},{4,8},{5,9},{6,10},{7,11},{8,4},{9,5},... | collective-permute-start | bytes 12296 | tf_op jit(solution)/shard_map/ppermute | solution.py:643
  54.7 0.7 collective-permute-start.3
  55.4 3.0 %collective-permute-start.2 = (f32[8,128]{1,0:T(8,128)S(1)}, f32[8,128]{1,0:T(8,128)S(1)}, u32[]{:S(2)}, u32[]{:S(2)}) collective-permute-start(f32[8,128]{1,0:T(8,128)S(1)} %get-tuple-element.24), channel_id=1, source_target_pairs={{0,4},{1,5},{2,6},{3,7},{4,0},{5,1},{6,2},{7,3},{8,12},{9,13},{10,... | collective-permute-start | bytes 12296 | tf_op jit(solution)/shard_map/ppermute | solution.py:643
  58.3 2.3 %collective-permute-start.8 = (f32[5,3,32,128]{3,2,1,0:T(8,128)S(1)}, f32[5,3,32,128]{3,2,1,0:T(8,128)S(1)}, u32[]{:S(2)}, u32[]{:S(2)}) collective-permute-start(f32[5,3,32,128]{3,2,1,0:T(8,128)S(1)} %get-tuple-element.25), channel_id=1, source_target_pairs={{0,15},{1,2},{2,1},{3,4},{4,3},{5,6},{6,5},{7,8},{8,7},{9,10},{10,... | collective-permute-start | bytes 737288 | tf_op jit(solution)/shard_map/ppermute | solution.py:141
  60.6 0.1 collective-permute-start.7
  60.8 2.1 %collective-permute-start.6 = (f32[8,128]{1,0:T(8,128)S(1)}, f32[8,128]{1,0:T(8,128)S(1)}, u32[]{:S(2)}, u32[]{:S(2)}) collective-permute-start(f32[8,128]{1,0:T(8,128)S(1)} %maximum_maximum_fusion.1), channel_id=1, source_target_pairs={{0,2},{1,3},{2,0},{3,1},{4,6},{5,7},{6,4},{7,5},{8,10},{9,11},{10,... | collective-permute-start | bytes 12296 | tf_op jit(solution)/shard_map/ppermute | solution.py:643
  62.8 1.0 %collective-permute-done.7 = f32[8,128]{1,0:T(8,128)S(1)} collective-permute-done((f32[8,128]{1,0:T(8,128)S(1)}, f32[8,128]{1,0:T(8,128)S(1)}, u32[]{:S(2)}, u32[]{:S(2)}) %collective-permute-start.7) | collective-permute-done | bytes 4128 | tf_op jit(solution)/shard_map/ppermute | solution.py:643
  63.8 2.9 %collective-permute-done.6 = f32[8,128]{1,0:T(8,128)S(1)} collective-permute-done((f32[8,128]{1,0:T(8,128)S(1)}, f32[8,128]{1,0:T(8,128)S(1)}, u32[]{:S(2)}, u32[]{:S(2)}) %collective-permute-start.6) | collective-permute-done | bytes 4128 | tf_op jit(solution)/shard_map/ppermute | solution.py:643
  66.8 4.1 %planes.3.sides = f32[5,8,32,128]{3,2,1,0:T(8,128)S(1)} custom-call(f32[5,8,32,128]{3,2,1,0:T(8,128)S(1)} %get-tuple-element.23.state.middle, f32[8,128]{1,0:T(8,128)S(1)} %maximum_maximum_fusion.speed), custom_call_target="tpu_custom_call" | custom-call | flops 20000000 | bytes 1000000 | tf_op jit(solution)/shard_map/planes/pallas_call | solution.py:500
  70.9 3.3 %second_stage.1 = f32[5,8,32,128]{3,2,1,0:T(8,128)} custom-call(f32[5,8,32,128]{3,2,1,0:T(8,128)S(1)} %get-tuple-element.19.state.start, f32[5,8,32,128]{3,2,1,0:T(8,128)S(1)} %get-tuple-element.23.state.middle, f32[5,8,32,128]{3,2,1,0:T(8,128)S(1)} %planes.3.sides, f32[5,3,32,128]{3,2,1,0:T(8,128)S(1)} %collective-permute-done.8.far, ...), custom_call_target="tpu_custom_call" | custom-call | flops 30000000 | bytes 3000000 | tf_op jit(solution)/shard_map/second_stage/pallas_call | solution.py:621
  (18 shorter events, 0.1 us)
Async XLA Ops:
  2.7 7.4 %copy-start = (s32[1024]{0:T(1024)S(1)}, s32[1024]{0:T(1024)}, u32[]{:S(2)}) copy-start(s32[1024]{0:T(1024)} %owner_hbm.1) | copy-start | bytes 12292
  2.8 7.4 %copy-start.1 = (s32[1024]{0:T(1024)S(1)}, s32[1024]{0:T(1024)}, u32[]{:S(2)}) copy-start(s32[1024]{0:T(1024)} %param.5) | copy-start | bytes 12292
  2.8 34.9 %all-to-all-start = ((f32[16,161,1,128]{3,2,1,0:T(1,128)}), f32[16,161,1,128]{3,2,1,0:T(1,128)S(1)}, u32[]{:S(2)}, u32[]{:S(2)}) async-start(f32[16,161,1,128]{3,2,1,0:T(1,128)} %pack.1), calls=%async_computation | async-start | bytes 2637824 | tf_op jit(solution)/shard_map/all_to_all | solution.py:657
  40.2 11.8 %collective-permute-start = (f32[5,3,32,128]{3,2,1,0:T(8,128)S(1)}, f32[5,3,32,128]{3,2,1,0:T(8,128)S(1)}, u32[]{:S(2)}, u32[]{:S(2)}) collective-permute-start(f32[5,3,32,128]{3,2,1,0:T(8,128)S(1)} %get-tuple-element.21), channel_id=1, source_target_pairs={{0,15},{1,2},{2,1},{3,4},{4,3},{5,6},{6,5},{7,8},{8,7},{9,10},{10,... | collective-permute-start | bytes 737288 | tf_op jit(solution)/shard_map/ppermute | solution.py:141
  46.8 5.2 %collective-permute-start.1 = (f32[5,3,32,128]{3,2,1,0:T(8,128)S(1)}, f32[5,3,32,128]{3,2,1,0:T(8,128)S(1)}, u32[]{:S(2)}, u32[]{:S(2)}) collective-permute-start(f32[5,3,32,128]{3,2,1,0:T(8,128)S(1)} %get-tuple-element.22), channel_id=1, source_target_pairs={{0,1},{1,0},{2,3},{3,2},{4,5},{5,4},{6,7},{7,6},{8,9},{9,8},{10,11... | collective-permute-start | bytes 737288 | tf_op jit(solution)/shard_map/ppermute | solution.py:141
  53.9 6.7 %collective-permute-start.4 = (f32[8,128]{1,0:T(8,128)S(1)}, f32[8,128]{1,0:T(8,128)S(1)}, u32[]{:S(2)}, u32[]{:S(2)}) collective-permute-start(f32[8,128]{1,0:T(8,128)S(1)} %get-tuple-element.24), channel_id=1, source_target_pairs={{0,12},{1,13},{2,14},{3,15},{4,8},{5,9},{6,10},{7,11},{8,4},{9,5},... | collective-permute-start | bytes 12296 | tf_op jit(solution)/shard_map/ppermute | solution.py:643
  54.7 5.9 %collective-permute-start.3 = (f32[8,128]{1,0:T(8,128)S(1)}, f32[8,128]{1,0:T(8,128)S(1)}, u32[]{:S(2)}, u32[]{:S(2)}) collective-permute-start(f32[8,128]{1,0:T(8,128)S(1)} %get-tuple-element.24), channel_id=1, source_target_pairs={{0,8},{1,9},{2,10},{3,11},{4,12},{5,13},{6,14},{7,15},{8,0},{9,1},... | collective-permute-start | bytes 12296 | tf_op jit(solution)/shard_map/ppermute | solution.py:643
  55.4 5.2 %collective-permute-start.2 = (f32[8,128]{1,0:T(8,128)S(1)}, f32[8,128]{1,0:T(8,128)S(1)}, u32[]{:S(2)}, u32[]{:S(2)}) collective-permute-start(f32[8,128]{1,0:T(8,128)S(1)} %get-tuple-element.24), channel_id=1, source_target_pairs={{0,4},{1,5},{2,6},{3,7},{4,0},{5,1},{6,2},{7,3},{8,12},{9,13},{10,... | collective-permute-start | bytes 12296 | tf_op jit(solution)/shard_map/ppermute | solution.py:643
  58.3 12.5 %collective-permute-start.8 = (f32[5,3,32,128]{3,2,1,0:T(8,128)S(1)}, f32[5,3,32,128]{3,2,1,0:T(8,128)S(1)}, u32[]{:S(2)}, u32[]{:S(2)}) collective-permute-start(f32[5,3,32,128]{3,2,1,0:T(8,128)S(1)} %get-tuple-element.25), channel_id=1, source_target_pairs={{0,15},{1,2},{2,1},{3,4},{4,3},{5,6},{6,5},{7,8},{8,7},{9,10},{10,... | collective-permute-start | bytes 737288 | tf_op jit(solution)/shard_map/ppermute | solution.py:141
  60.6 10.3 %collective-permute-start.9 = (f32[5,3,32,128]{3,2,1,0:T(8,128)S(1)}, f32[5,3,32,128]{3,2,1,0:T(8,128)S(1)}, u32[]{:S(2)}, u32[]{:S(2)}) collective-permute-start(f32[5,3,32,128]{3,2,1,0:T(8,128)S(1)} %get-tuple-element.26), channel_id=1, source_target_pairs={{0,1},{1,0},{2,3},{3,2},{4,5},{5,4},{6,7},{7,6},{8,9},{9,8},{10,11... | collective-permute-start | bytes 737288 | tf_op jit(solution)/shard_map/ppermute | solution.py:141
  60.6 3.2 %collective-permute-start.7 = (f32[8,128]{1,0:T(8,128)S(1)}, f32[8,128]{1,0:T(8,128)S(1)}, u32[]{:S(2)}, u32[]{:S(2)}) collective-permute-start(f32[8,128]{1,0:T(8,128)S(1)} %maximum_maximum_fusion.1), channel_id=1, source_target_pairs={{0,3},{1,2},{2,1},{3,0},{4,7},{5,6},{6,5},{7,4},{8,11},{9,10},{10,... | collective-permute-start | bytes 12296 | tf_op jit(solution)/shard_map/ppermute | solution.py:643
  60.8 6.0 %collective-permute-start.6 = (f32[8,128]{1,0:T(8,128)S(1)}, f32[8,128]{1,0:T(8,128)S(1)}, u32[]{:S(2)}, u32[]{:S(2)}) collective-permute-start(f32[8,128]{1,0:T(8,128)S(1)} %maximum_maximum_fusion.1), channel_id=1, source_target_pairs={{0,2},{1,3},{2,0},{3,1},{4,6},{5,7},{6,4},{7,5},{8,10},{9,11},{10,... | collective-permute-start | bytes 12296 | tf_op jit(solution)/shard_map/ppermute | solution.py:643
  62.8 3.9 %collective-permute-start.5 = (f32[8,128]{1,0:T(8,128)S(1)}, f32[8,128]{1,0:T(8,128)S(1)}, u32[]{:S(2)}, u32[]{:S(2)}) collective-permute-start(f32[8,128]{1,0:T(8,128)S(1)} %maximum_maximum_fusion.1), channel_id=1, source_target_pairs={{0,1},{1,0},{2,3},{3,2},{4,5},{5,4},{6,7},{7,6},{8,9},{9,8},{10,11... | collective-permute-start | bytes 12296 | tf_op jit(solution)/shard_map/ppermute | solution.py:643

commit v20 on v19

--- a/solution.py
+++ b/solution.py
@@ -67,14 +67,22 @@
     lax.fori_loop(0, size, clear, 0, unroll=8)
     fetch_owner.wait()
 
-    def note(block, carry):
+    fetch_tiled.wait()
+    best = jnp.zeros((8, LANES), jnp.float32)
+    step = per_dev * PAIRS
+    for first in range(0, step, 8):
+        fields = [tiled[f * step + first : f * step + first + 8, :] for f in range(FIELDS)]
+        best = jnp.maximum(best, wave_speed(fields))
+    for block in range(per_dev):
         dest = owner[own * per_dev + block]
         rank = count[dest]
         count[dest] = rank + 1
-        member[dest * cap + rank] = lax.div(block, 8) * (PAIRS * 8) + lax.rem(block, 8)
-        return carry
-
-    lax.fori_loop(0, per_dev, note, 0, unroll=8)
+        member[dest * cap + rank] = block // 8 * (PAIRS * 8) + block % 8
+    most = jnp.full((1, LANES), jnp.max(best), jnp.float32)
+    for dest in range(size):
+        top[dest] = most
+    send_top = pltpu.make_async_copy(top, out_hbm.at[:, TILES * cap], sems.at[3])
+    send_top.start()
     fetch_rows.wait()
     tiles = TILES * cap
 
@@ -93,20 +101,9 @@
         return carry
 
     lax.fori_loop(0, size, message, 0)
-    fetch_tiled.wait()
-    best = jnp.zeros((8, LANES), jnp.float32)
-    step = per_dev * PAIRS
-    for first in range(0, step, 8):
-        fields = [tiled[f * step + first : f * step + first + 8, :] for f in range(FIELDS)]
-        best = jnp.maximum(best, wave_speed(fields))
-    top[...] = jnp.full(top.shape, jnp.max(best), jnp.float32)
-    for dest in range(size):
-        pltpu.make_async_copy(
-            top.at[pl.ds(dest, 1)], out_hbm.at[dest, tiles], sems.at[3]
-        ).start()
     half = out.at[pl.ds(0, per_dev * TILES)]
     pltpu.make_async_copy(half, half, sems.at[2]).wait()
-    pltpu.make_async_copy(top, top, sems.at[3]).wait()
+    send_top.wait()
 
 
 def pack(rows, owner_list, size, cap, per_dev):
@@ -120,7 +117,7 @@
             pltpu.VMEM(rows.shape, jnp.float32),
             pltpu.VMEM((rows.shape[0], LANES), jnp.float32),
             pltpu.VMEM((size * TILES * cap, 1, LANES), jnp.float32),
-            pltpu.VMEM((size, LANES), jnp.float32),
+            pltpu.VMEM((size, 1, LANES), jnp.float32),
             pltpu.SMEM((size,), jnp.int32),
             pltpu.SMEM((size * cap,), jnp.int32),
             pltpu.SemaphoreType.DMA((5,)),
@@ -131,23 +128,25 @@
     )(owner_list, rows)
 
 
-def own_is_even():
-    return lax.axis_index("gx") % 2 == 0
-
-
-def swapped(far_side, near_side, size):
-    apart = [(i, (i - 1 if i % 2 == 0 else i + 1) % size) for i in range(size)]
-    chip = [(i, i ^ 1) for i in range(size)]
-    return lax.ppermute(far_side, "gx", apart), lax.ppermute(near_side, "gx", chip)
-
-
-def sort_halos(far, near, below, above):
-    lower_first = own_is_even()
-    for f in range(FIELDS):
-        for plane in range(3):
-            one, two = far[f, plane], near[f, plane]
-            below[f, plane] = jnp.where(lower_first, one, two)
-            above[f, plane] = jnp.where(lower_first, two, one)
+def turned_round():
+    return lax.axis_index("gx") % 2
+
+
+def place_of(plane):
+    return jnp.where(turned_round() == 0, plane, BLOCK - 1 - plane)
+
+
+def sign_of_x():
+    return jnp.where(turned_round() == 0, 1.0, -1.0).astype(jnp.float32)
+
+
+def from_far(far_side, size):
+    pairs = [(i, (i - 1 if i % 2 == 0 else i + 1) % size) for i in range(size)]
+    return lax.ppermute(far_side, "gx", pairs)
+
+
+def from_near(near_side, size):
+    return lax.ppermute(near_side, "gx", [(i, i ^ 1) for i in range(size)])
 
 
 HALO = (FIELDS, 3, ROWS, LANES)
@@ -189,6 +188,7 @@
     group = lax.broadcasted_iota(jnp.int32, (8, LANES), 1) // BLOCK
     even = lax.broadcasted_iota(jnp.int32, (8, LANES), 0) % 2 == 0
     half = FIELDS * BZ * 8
+    places = [place_of(plane) for plane in range(BLOCK)]
 
     def gather(couple, slot):
         p, q = divmod(slot, BZ)
@@ -213,7 +213,7 @@
                     jnp.where(even, pltpu.roll(lower, 7, 0), upper),
                 )
                 for h in range(2):
-                    state[f, 4 * couple + 2 * h + second, j * 8 : j * 8 + 8, :] = planes[h]
+                    state[f, places[4 * couple + 2 * h + second], j * 8 : j * 8 + 8, :] = planes[h]
 
     for slot in range(BY * BZ):
         gather(0, slot)
@@ -223,12 +223,10 @@
         arrange(0, f)
     for f in range(FIELDS):
         arrange(1, f)
-    lower_first = own_is_even()
     for f in range(FIELDS):
-        for plane in range(3):
-            low, high = state[f, plane], state[f, BLOCK - 3 + plane]
-            far_side[f, plane] = jnp.where(lower_first, low, high)
-            near_side[f, plane] = jnp.where(lower_first, high, low)
+        for place in range(3):
+            far_side[f, place] = state[f, place]
+            near_side[f, place] = state[f, BLOCK - 3 + place]
 
 
 def unpack(table, come, size, cap):
@@ -362,7 +360,8 @@
 
 
 INNER = (range(2, 6), range(2, 6), range(0, 7))
-OUTER = ((-1, 0, 1, 6, 7), (0, 1, 6, 7, 8), (-1, 7))
+FAR = ((-1, 0, 1), (0, 1), (-1,))
+NEAR = ((6, 7), (6, 7, 8), (7,))
 EVERY = (range(-1, 8), range(0, 9), range(-1, 8))
 
 
@@ -442,19 +441,20 @@
     return flux + 0.5 * pressure if field == 1 + direction else flux
 
 
-def plane_kernel(with_inner, state, speed, out, turned):
+def plane_kernel(with_inner, *refs):
+    *states, speed, out, turned = refs
     half_speed = 0.5 * speed[0:1, :]
     lane = lax.broadcasted_iota(jnp.int32, (LANES, LANES), 1)
     to_turned = (lane % 8) * 16 + lane // 8
     to_plain = (lane % 16) * 8 + lane // 16
 
-    def four_planes(part, carry):
-        planes = pl.ds(part * 4, 4)
+    for part in range(2):
+        state, first = (states[0], 4 * part) if len(states) == 1 else (states[part], 0)
         for f in range(FIELDS):
-            plain = state[f, planes].reshape(LANES, LANES)
+            plain = state[f, first : first + 4].reshape(LANES, LANES)
             turned[f] = jnp.take_along_axis(plain, to_turned, axis=1).T
         for place in range(4):
-            fields = [state[f, part * 4 + place] for f in range(FIELDS)]
+            fields = [state[f, first + place] for f in range(FIELDS)]
             vel, pressure = half_velocities(fields)
             for field in range(FIELDS):
                 out[field, part * 4 + place] = periodic_divergence(
@@ -476,142 +476,144 @@
             scaled = [half_speed * value for value in columns[field]]
             total = jnp.concatenate(ring_divergence(fluxes, scaled), axis=0)
             plain = jnp.take_along_axis(total.T, to_plain, axis=1)
-            out[field, planes] += plain.reshape(4, ROWS, LANES)
-        return carry
-
-    lax.fori_loop(0, state.shape[1] // 4, four_planes, 0)
+            out[field, part * 4 : part * 4 + 4] += plain.reshape(4, ROWS, LANES)
 
     def group(j, carry):
         rows = pl.ds(pl.multiple_of(j * 8, 8), 8)
 
-        def get(f, plane):
-            return state[f, plane, rows, :]
+        def get(f, place):
+            return states[0][f, place, rows, :]
 
         for field, along_x in across(get, half_speed, range(BLOCK), INNER):
-            for plane in range(BLOCK):
-                out[field, plane, rows, :] += along_x[plane]
+            for place in range(BLOCK):
+                out[field, place, rows, :] += along_x[place]
         return carry
 
     if with_inner:
         lax.fori_loop(0, 4, group, 0)
 
 
-def along_planes(state, speed, with_inner):
+def along_planes(states, speed, with_inner):
     return pl.pallas_call(
         functools.partial(plane_kernel, with_inner),
-        out_shape=jax.ShapeDtypeStruct(state.shape, jnp.float32),
-        in_specs=[VMEM, VMEM],
+        out_shape=jax.ShapeDtypeStruct((FIELDS, BLOCK, ROWS, LANES), jnp.float32),
+        in_specs=[VMEM] * (len(states) + 1),
         out_specs=VMEM,
         scratch_shapes=[pltpu.VMEM((FIELDS, LANES, LANES), jnp.float32)],
         compiler_params=params(),
         cost_estimate=cost(20_000_000, 1_000_000),
         name="planes",
-    )(state, speed)
+    )(*states, speed)
 
 
 def across(get, half_speed, span, parts):
+    sign = sign_of_x()
     speeds, pressures = {}, {}
-    for plane in span:
-        vel, pressure = half_velocities([get(f, plane) for f in range(FIELDS)])
-        speeds[plane] = vel[0]
-        pressures[plane] = pressure
+    for place in span:
+        vel, pressure = half_velocities([get(f, place) for f in range(FIELDS)])
+        speeds[place] = sign * vel[0]
+        pressures[place] = pressure
     for field in range(FIELDS):
         fluxes, scaled = {}, {}
-        for plane in span:
+        for place in span:
             if field == 0:
-                flux = 0.5 * get(1, plane)
+                flux = (0.5 * sign) * get(1, place)
             elif field == 4:
-                flux = (get(4, plane) + pressures[plane]) * speeds[plane]
+                flux = (get(4, place) + pressures[place]) * speeds[place]
             else:
-                flux = get(field, plane) * speeds[plane]
+                flux = get(field, place) * speeds[place]
                 if field == 1:
-                    flux = flux + 0.5 * pressures[plane]
-            fluxes[plane] = flux
-            scaled[plane] = half_speed * get(field, plane)
+                    flux = flux + (0.5 * sign) * pressures[place]
+            fluxes[place] = flux
+            scaled[place] = half_speed * get(field, place)
         yield field, x_divergence(fluxes, scaled, *parts)
 
 
 WITH_HALOS = range(-3, BLOCK + 3)
 
 
-def first_kernel(
-    state, sides, far, near, speed, middle, far_side, near_side, top, below, above
-):
-    sort_halos(far, near, below, above)
-    lower_first = own_is_even()
+def with_halos(far, near, inside, rows):
+    def get(f, place):
+        if place < 0:
+            return far[f, -1 - place, rows, :]
+        if place >= BLOCK:
+            return near[f, BLOCK + 2 - place, rows, :]
+        return inside(f, place)
+
+    return get
+
+
+def first_kernel(is_far, *refs):
+    if is_far:
+        state, sides, halo, speed, other, middle, side, top = refs
+    else:
+        state, sides, halo, speed, middle, side, top = refs
+    first, parts, span = (0, FAR, range(-3, 4)) if is_far else (4, NEAR, range(4, 11))
     half_speed = 0.5 * speed[0:1, :]
     factor = (courant / 6.0) / speed[0:1, :]
 
     def group(j, best):
         rows = pl.ds(pl.multiple_of(j * 8, 8), 8)
 
-        def get(f, plane):
-            if plane < 0:
-                return below[f, plane + 3, rows, :]
-            if plane >= BLOCK:
-                return above[f, plane - BLOCK, rows, :]
-            return state[f, plane, rows, :]
-
-        for field, along_x in across(get, half_speed, WITH_HALOS, OUTER):
-            values = []
-            for plane in range(BLOCK):
-                total = sides[field, plane, rows, :]
-                if plane in along_x:
-                    total = total + along_x[plane]
-                values.append(get(field, plane) - factor * total)
-                middle[field, plane, rows, :] = values[plane]
-            for plane in range(3):
-                low, high = values[plane], values[BLOCK - 3 + plane]
-                far_side[field, plane, rows, :] = jnp.where(lower_first, low, high)
-                near_side[field, plane, rows, :] = jnp.where(lower_first, high, low)
-        for plane in range(BLOCK):
-            best = jnp.maximum(
-                best, wave_speed([middle[f, plane, rows, :] for f in range(FIELDS)])
-            )
+        def inside(f, place):
+            return state[f, place, rows, :]
+
+        get = with_halos(halo, halo, inside, rows)
+        for field, along_x in across(get, half_speed, span, parts):
+            for k in range(4):
+                total = sides[field, first + k, rows, :]
+                if first + k in along_x:
+                    total = total + along_x[first + k]
+                value = get(field, first + k) - factor * total
+                middle[field, k, rows, :] = value
+                at = k if is_far else k - 1
+                if 0 <= at < 3:
+                    side[field, at, rows, :] = value
+        for k in range(4):
+            best = jnp.maximum(best, wave_speed([middle[f, k, rows, :] for f in range(FIELDS)]))
         return best
 
-    best = lax.fori_loop(0, 4, group, jnp.zeros((8, LANES), jnp.float32))
-    top[...] = jnp.full((8, LANES), jnp.max(best), jnp.float32)
-
-
-def first_stage(*operands):
-    whole = jax.ShapeDtypeStruct((FIELDS, BLOCK, ROWS, LANES), jnp.float32)
-    halo = jax.ShapeDtypeStruct(HALO, jnp.float32)
+    start = other[...] if is_far else jnp.zeros((8, LANES), jnp.float32)
+    best = lax.fori_loop(0, 4, group, start)
+    top[...] = jnp.full((8, LANES), jnp.max(best), jnp.float32) if is_far else best
+
+
+def first_stage(is_far, *operands):
     return pl.pallas_call(
-        first_kernel,
-        out_shape=(whole, halo, halo, jax.ShapeDtypeStruct((8, LANES), jnp.float32)),
+        functools.partial(first_kernel, is_far),
+        out_shape=(
+            jax.ShapeDtypeStruct((FIELDS, 4, ROWS, LANES), jnp.float32),
+            jax.ShapeDtypeStruct(HALO, jnp.float32),
+            jax.ShapeDtypeStruct((8, LANES), jnp.float32),
+        ),
         in_specs=[VMEM] * len(operands),
-        out_specs=(VMEM,) * 4,
-        scratch_shapes=[pltpu.VMEM(HALO, jnp.float32)] * 2,
+        out_specs=(VMEM,) * 3,
         compiler_params=params(),
-        cost_estimate=cost(30_000_000, 3_000_000),
-        name="first_stage",
+        cost_estimate=cost(15_000_000, 2_000_000),
+        name="first_far" if is_far else "first_near",
     )(*operands)
 
 
-def second_kernel(start, middle, sides, far, near, first_speed, speed, out, below, above):
-    sort_halos(far, near, below, above)
+def second_kernel(state, middle_far, middle_near, sides, far, near, first_speed, speed, out):
     half_speed = 0.5 * speed[0:1, :]
     factor = (courant / 12.0) / first_speed[0:1, :]
+    planes = [place_of(place) for place in range(BLOCK)]
 
     def group(j, carry):
         rows = pl.ds(pl.multiple_of(j * 8, 8), 8)
         spread = pl.ds(j, 8, stride=4)
 
-        def get(f, plane):
-            if plane < 0:
-                return below[f, plane + 3, rows, :]
-            if plane >= BLOCK:
-                return above[f, plane - BLOCK, rows, :]
-            return middle[f, plane, rows, :]
-
+        def inside(f, place):
+            return (middle_far, middle_near)[place // 4][f, place % 4, rows, :]
+
+        get = with_halos(far, near, inside, rows)
         for field, along_x in across(get, half_speed, WITH_HALOS, EVERY):
-            for plane in range(BLOCK):
-                total = along_x[plane] + sides[field, plane, rows, :]
-                value = 0.5 * start[field, plane, rows, :] + (
-                    0.5 * get(field, plane) - factor * total
+            for place in range(BLOCK):
+                total = along_x[place] + sides[field, place, rows, :]
+                value = 0.5 * state[field, place, rows, :] + (
+                    0.5 * get(field, place) - factor * total
                 )
-                out[field, plane, spread, :] = value
+                out[field, planes[place], spread, :] = value
         return carry
 
     lax.fori_loop(0, 4, group, 0)
@@ -623,7 +625,6 @@
         out_shape=jax.ShapeDtypeStruct((FIELDS, BLOCK, ROWS, LANES), jnp.float32),
         in_specs=[VMEM] * len(operands),
         out_specs=VMEM,
-        scratch_shapes=[pltpu.VMEM(HALO, jnp.float32)] * 2,
         compiler_params=params(),
         cost_estimate=cost(30_000_000, 3_000_000),
         name="second_stage",
@@ -657,13 +658,16 @@
     come = lax.all_to_all(parts, "gx", split_axis=0, concat_axis=0, tiled=True)
     table = arrival_spots(owner_list, slot_list, own, per_dev, size, cap)
     state, far_side, near_side, speed = unpack(table, come.reshape(-1, 1, LANES), size, cap)
-    far, near = swapped(far_side, near_side, size)
-    sides = along_planes(state, speed, True)
-    middle, far_side, near_side, top = first_stage(state, sides, far, near, speed)
-    far, near = swapped(far_side, near_side, size)
+    far = from_far(far_side, size)
+    near = from_near(near_side, size)
+    sides = along_planes((state,), speed, True)
+    middle_near, near_side, top = first_stage(False, state, sides, near, speed)
+    middle_far, far_side, top = first_stage(True, state, sides, far, speed, top)
+    far = from_far(far_side, size)
+    near = from_near(near_side, size)
     second = everyone_max(top, "gx", size)
-    sides = along_planes(middle, second, False)
-    return second_stage(state, middle, sides, far, near, speed, second)
+    sides = along_planes((middle_far, middle_near), second, False)
+    return second_stage(state, middle_far, middle_near, sides, far, near, speed, second)
 
 
 def solution(mesh):

time: 74.4 us -> 71.8 us (0.965)
  waiting for transfers between devices: 30.7 us -> 28.6 us
    ppermute x6, waiting for transfers between devices: 3.95 us -> 1.77 us  [everyone_max(): copies.append(lax.ppermute(value, axis, pairs))]
    pallas_call x1 -> x2, Pallas kernels: 1.84 us -> 1.89 us  [first_stage(): pl.pallas_call(functools.partial(first_kernel, is_far), out_shape=(jax.Sh...]
  transfers between devices with their start and end apart: 11 -> 11, of which waited for: 3 -> 4; matrix products, arithmetic and copies ran while one was open for 1% -> 1% of each run, Pallas kernels for 12% -> 14%
where the time goes in v20:
time: 71.8 us; the launch traced here: 71.4 us
  waiting for transfers between devices  28.6 us (40%)
  starting transfers between devices  22.2 us (31%)
  Pallas kernels  19.8 us (28%)
    all_to_all x1, waiting for transfers between devices, per_device(): come = lax.all_to_all(parts, 'gx', split_axis=0, concat_axis=0, tiled=True)  26.8 us
    pallas_call x2, Pallas kernels, along_planes(): pl.pallas_call(functools.partial(plane_kernel, with_inner), out_shape=jax...  9.11 us
    ppermute x2, starting transfers between devices, from_far(): return lax.ppermute(far_side, 'gx', pairs)  7.44 us
    all_to_all x1, starting transfers between devices, per_device(): come = lax.all_to_all(parts, 'gx', split_axis=0, concat_axis=0, tiled=True)  7.39 us
    ppermute x6, starting transfers between devices, everyone_max(): copies.append(lax.ppermute(value, axis, pairs))  6.53 us
    pallas_call x1, Pallas kernels, second_stage(): pl.pallas_call(second_kernel, out_shape=jax.ShapeDtypeStruct((FIELDS, BLO...  3.27 us
    pallas_call x1, Pallas kernels, pack(): pl.pallas_call(functools.partial(pack_kernel, size, cap, per_dev), out_sh...  2.98 us
    pallas_call x1, Pallas kernels, unpack(): pl.pallas_call(functools.partial(unpack_kernel, size, cap), out_shape=(ja...  2.52 us
  transfers between devices with their start and end apart: 11, of which 4 were waited for; matrix products, arithmetic and copies ran while one was open for 1% of the time, Pallas kernels for 14%

profile of v20, /device:TPU:0, one launch (start us, length us, event | category | flops | bytes accessed | tf_op | source)
XLA Modules:
  0.0 71.4 jit_solution(14460508252971715717)
XLA Ops:
  0.0 3.0 %pack.1 = f32[16,161,1,128]{3,2,1,0:T(1,128)} custom-call(s32[1024]{0:T(1024)} %owner_hbm.1, f32[1280,1,128]{2,1,0:T(1,128)} %bitcast.7), custom_call_target="tpu_custom_call" | custom-call | flops 1000000 | bytes 3000000 | tf_op jit(solution)/shard_map/pack/pallas_call | solution.py:110
  3.0 7.4 %all-to-all-start = ((f32[16,161,1,128]{3,2,1,0:T(1,128)}), f32[16,161,1,128]{3,2,1,0:T(1,128)S(1)}, u32[]{:S(2)}, u32[]{:S(2)}) async-start(f32[16,161,1,128]{3,2,1,0:T(1,128)} %pack.1), calls=%async_computation | async-start | bytes 2637824 | tf_op jit(solution)/shard_map/all_to_all | solution.py:658
  10.5 0.1 eq.33
  10.5 0.3 convert_reduce_fusion
  10.9 0.1 broadcast_add_fusion
  11.0 0.1 add.17
  11.0 0.1 select_reduce_fusion.table
  11.2 26.8 %all-to-all-done = f32[16,161,1,128]{3,2,1,0:T(1,128)S(1)} async-done(((f32[16,161,1,128]{3,2,1,0:T(1,128)}), f32[16,161,1,128]{3,2,1,0:T(1,128)S(1)}, u32[]{:S(2)}, u32[]{:S(2)}) %all-to-all-start) | async-done | bytes 1318944 | tf_op jit(solution)/shard_map/all_to_all | solution.py:658
  38.0 2.5 %unpack.1 = (f32[5,8,32,128]{3,2,1,0:T(8,128)S(1)}, f32[5,3,32,128]{3,2,1,0:T(8,128)S(1)}, f32[5,3,32,128]{3,2,1,0:T(8,128)S(1)}, f32[8,128]{1,0:T(8,128)S(1)}) custom-call(s32[64]{0:T(128)S(1)} %select_reduce_fusion.table, f32[2576,1,128]{2,1,0:T(1,128)S(1)} %bitcast.6), custom_call_target="tpu_custom_call" | custom-call | flops 5000000 | bytes 2000000 | tf_op jit(solution)/shard_map/unpack/pallas_call | solution.py:234
  40.5 0.8 %collective-permute-start.1 = (f32[5,3,32,128]{3,2,1,0:T(8,128)S(1)}, f32[5,3,32,128]{3,2,1,0:T(8,128)S(1)}, u32[]{:S(2)}, u32[]{:S(2)}) collective-permute-start(f32[5,3,32,128]{3,2,1,0:T(8,128)S(1)} %get-tuple-element.24), channel_id=1, source_target_pairs={{0,1},{1,0},{2,3},{3,2},{4,5},{5,4},{6,7},{7,6},{8,9},{9,8},{10,11... | collective-permute-start | bytes 737288 | tf_op jit(solution)/shard_map/ppermute | solution.py:149
  41.3 6.0 %collective-permute-start = (f32[5,3,32,128]{3,2,1,0:T(8,128)S(1)}, f32[5,3,32,128]{3,2,1,0:T(8,128)S(1)}, u32[]{:S(2)}, u32[]{:S(2)}) collective-permute-start(f32[5,3,32,128]{3,2,1,0:T(8,128)S(1)} %get-tuple-element.23), channel_id=1, source_target_pairs={{0,15},{1,2},{2,1},{3,4},{4,3},{5,6},{6,5},{7,8},{8,7},{9,10},{10,... | collective-permute-start | bytes 737288 | tf_op jit(solution)/shard_map/ppermute | solution.py:145
  47.3 5.1 %planes.2.refs_1_ = f32[5,8,32,128]{3,2,1,0:T(8,128)S(1)} custom-call(f32[5,8,32,128]{3,2,1,0:T(8,128)S(1)} %get-tuple-element.21.refs_0_.state, f32[8,128]{1,0:T(8,128)S(1)} %get-tuple-element.22.refs_1_.refs_3_.first_speed), custom_call_target="tpu_custom_call" | custom-call | flops 20000000 | bytes 1000000 | tf_op jit(solution)/shard_map/planes/pallas_call | solution.py:497
  52.5 0.9 %first_near.1 = (f32[5,4,32,128]{3,2,1,0:T(8,128)S(1)}, f32[5,3,32,128]{3,2,1,0:T(8,128)S(1)}, f32[8,128]{1,0:T(8,128)S(1)}) custom-call(f32[5,8,32,128]{3,2,1,0:T(8,128)S(1)} %get-tuple-element.21.refs_0_.state, f32[5,8,32,128]{3,2,1,0:T(8,128)S(1)} %planes.2.refs_1_, f32[5,3,32,128]{3,2,1,0:T(8,128)S(1)} %collective-permute-done.1.refs_2_, ...), custom_call_target="tpu_custom_call" | custom-call | flops 15000000 | bytes 2000000 | tf_op jit(solution)/shard_map/first_near/pallas_call | solution.py:582
  53.4 1.0 %first_far.1 = (f32[5,4,32,128]{3,2,1,0:T(8,128)S(1)}, f32[5,3,32,128]{3,2,1,0:T(8,128)S(1)}, f32[8,128]{1,0:T(8,128)S(1)}) custom-call(f32[5,8,32,128]{3,2,1,0:T(8,128)S(1)} %get-tuple-element.21.refs_0_.state, f32[5,8,32,128]{3,2,1,0:T(8,128)S(1)} %planes.2.refs_1_, f32[5,3,32,128]{3,2,1,0:T(8,128)S(1)} %collective-permute-done.refs_2_, ...), custom_call_target="tpu_custom_call" | custom-call | flops 15000000 | bytes 2000000 | tf_op jit(solution)/shard_map/first_far/pallas_call | solution.py:582
  54.4 0.3 collective-permute-start.4
  54.7 0.5 collective-permute-start.3
  55.2 3.6 %collective-permute-start.2 = (f32[8,128]{1,0:T(8,128)S(1)}, f32[8,128]{1,0:T(8,128)S(1)}, u32[]{:S(2)}, u32[]{:S(2)}) collective-permute-start(f32[8,128]{1,0:T(8,128)S(1)} %get-tuple-element.28), channel_id=1, source_target_pairs={{0,4},{1,5},{2,6},{3,7},{4,0},{5,1},{6,2},{7,3},{8,12},{9,13},{10,... | collective-permute-start | bytes 12296 | tf_op jit(solution)/shard_map/ppermute | solution.py:644
  58.9 1.4 %collective-permute-start.8 = (f32[5,3,32,128]{3,2,1,0:T(8,128)S(1)}, f32[5,3,32,128]{3,2,1,0:T(8,128)S(1)}, u32[]{:S(2)}, u32[]{:S(2)}) collective-permute-start(f32[5,3,32,128]{3,2,1,0:T(8,128)S(1)} %get-tuple-element.29), channel_id=1, source_target_pairs={{0,15},{1,2},{2,1},{3,4},{4,3},{5,6},{6,5},{7,8},{8,7},{9,10},{10,... | collective-permute-start | bytes 737288 | tf_op jit(solution)/shard_map/ppermute | solution.py:145
  60.3 0.1 collective-permute-done.2
  60.5 2.1 %collective-permute-start.6 = (f32[8,128]{1,0:T(8,128)S(1)}, f32[8,128]{1,0:T(8,128)S(1)}, u32[]{:S(2)}, u32[]{:S(2)}) collective-permute-start(f32[8,128]{1,0:T(8,128)S(1)} %maximum_maximum_fusion.1), channel_id=1, source_target_pairs={{0,2},{1,3},{2,0},{3,1},{4,6},{5,7},{6,4},{7,5},{8,10},{9,11},{10,... | collective-permute-start | bytes 12296 | tf_op jit(solution)/shard_map/ppermute | solution.py:644
  62.5 1.0 %collective-permute-done.7 = f32[8,128]{1,0:T(8,128)S(1)} collective-permute-done((f32[8,128]{1,0:T(8,128)S(1)}, f32[8,128]{1,0:T(8,128)S(1)}, u32[]{:S(2)}, u32[]{:S(2)}) %collective-permute-start.7) | collective-permute-done | bytes 4128 | tf_op jit(solution)/shard_map/ppermute | solution.py:644
  63.5 0.7 collective-permute-done.6
  64.2 4.0 %planes.3.sides = f32[5,8,32,128]{3,2,1,0:T(8,128)S(1)} custom-call(f32[5,4,32,128]{3,2,1,0:T(8,128)S(1)} %get-tuple-element.26.refs_0_.middle_far, f32[5,4,32,128]{3,2,1,0:T(8,128)S(1)} %get-tuple-element.27.refs_1_.middle_near, f32[8,128]{1,0:T(8,128)S(1)} %maximum_maximum_fusion.refs_2_.speed), custom_call_target="tpu_custom_call" | custom-call | flops 20000000 | bytes 1000000 | tf_op jit(solution)/shard_map/planes/pallas_call | solution.py:497
  68.2 3.3 %second_stage.1 = f32[5,8,32,128]{3,2,1,0:T(8,128)} custom-call(f32[5,8,32,128]{3,2,1,0:T(8,128)S(1)} %get-tuple-element.21.refs_0_.state, f32[5,4,32,128]{3,2,1,0:T(8,128)S(1)} %get-tuple-element.26.refs_0_.middle_far, f32[5,4,32,128]{3,2,1,0:T(8,128)S(1)} %get-tuple-element.27.refs_1_.middle_near, f32[5,8,32,128]{3,2,1,0:T(8,128)S(1)} %planes.3.sides, ...), custom_call_target="tpu_custom_call" | custom-call | flops 30000000 | bytes 3000000 | tf_op jit(solution)/shard_map/second_stage/pallas_call | solution.py:623
  (19 shorter events, 0.1 us)
Async XLA Ops:
  3.0 7.4 %copy-start = (s32[1024]{0:T(1024)S(1)}, s32[1024]{0:T(1024)}, u32[]{:S(2)}) copy-start(s32[1024]{0:T(1024)} %owner_hbm.1) | copy-start | bytes 12292
  3.0 7.4 %copy-start.1 = (s32[1024]{0:T(1024)S(1)}, s32[1024]{0:T(1024)}, u32[]{:S(2)}) copy-start(s32[1024]{0:T(1024)} %param.5) | copy-start | bytes 12292
  3.0 35.0 %all-to-all-start = ((f32[16,161,1,128]{3,2,1,0:T(1,128)}), f32[16,161,1,128]{3,2,1,0:T(1,128)S(1)}, u32[]{:S(2)}, u32[]{:S(2)}) async-start(f32[16,161,1,128]{3,2,1,0:T(1,128)} %pack.1), calls=%async_computation | async-start | bytes 2637824 | tf_op jit(solution)/shard_map/all_to_all | solution.py:658
  40.5 12.0 %collective-permute-start.1 = (f32[5,3,32,128]{3,2,1,0:T(8,128)S(1)}, f32[5,3,32,128]{3,2,1,0:T(8,128)S(1)}, u32[]{:S(2)}, u32[]{:S(2)}) collective-permute-start(f32[5,3,32,128]{3,2,1,0:T(8,128)S(1)} %get-tuple-element.24), channel_id=1, source_target_pairs={{0,1},{1,0},{2,3},{3,2},{4,5},{5,4},{6,7},{7,6},{8,9},{9,8},{10,11... | collective-permute-start | bytes 737288 | tf_op jit(solution)/shard_map/ppermute | solution.py:149
  41.3 12.0 %collective-permute-start = (f32[5,3,32,128]{3,2,1,0:T(8,128)S(1)}, f32[5,3,32,128]{3,2,1,0:T(8,128)S(1)}, u32[]{:S(2)}, u32[]{:S(2)}) collective-permute-start(f32[5,3,32,128]{3,2,1,0:T(8,128)S(1)} %get-tuple-element.23), channel_id=1, source_target_pairs={{0,15},{1,2},{2,1},{3,4},{4,3},{5,6},{6,5},{7,8},{8,7},{9,10},{10,... | collective-permute-start | bytes 737288 | tf_op jit(solution)/shard_map/ppermute | solution.py:145
  54.4 5.9 %collective-permute-start.4 = (f32[8,128]{1,0:T(8,128)S(1)}, f32[8,128]{1,0:T(8,128)S(1)}, u32[]{:S(2)}, u32[]{:S(2)}) collective-permute-start(f32[8,128]{1,0:T(8,128)S(1)} %get-tuple-element.28), channel_id=1, source_target_pairs={{0,12},{1,13},{2,14},{3,15},{4,8},{5,9},{6,10},{7,11},{8,4},{9,5},... | collective-permute-start | bytes 12296 | tf_op jit(solution)/shard_map/ppermute | solution.py:644
  54.7 5.6 %collective-permute-start.3 = (f32[8,128]{1,0:T(8,128)S(1)}, f32[8,128]{1,0:T(8,128)S(1)}, u32[]{:S(2)}, u32[]{:S(2)}) collective-permute-start(f32[8,128]{1,0:T(8,128)S(1)} %get-tuple-element.28), channel_id=1, source_target_pairs={{0,8},{1,9},{2,10},{3,11},{4,12},{5,13},{6,14},{7,15},{8,0},{9,1},... | collective-permute-start | bytes 12296 | tf_op jit(solution)/shard_map/ppermute | solution.py:644
  55.2 5.2 %collective-permute-start.2 = (f32[8,128]{1,0:T(8,128)S(1)}, f32[8,128]{1,0:T(8,128)S(1)}, u32[]{:S(2)}, u32[]{:S(2)}) collective-permute-start(f32[8,128]{1,0:T(8,128)S(1)} %get-tuple-element.28), channel_id=1, source_target_pairs={{0,4},{1,5},{2,6},{3,7},{4,0},{5,1},{6,2},{7,3},{8,12},{9,13},{10,... | collective-permute-start | bytes 12296 | tf_op jit(solution)/shard_map/ppermute | solution.py:644
  58.9 9.3 %collective-permute-start.8 = (f32[5,3,32,128]{3,2,1,0:T(8,128)S(1)}, f32[5,3,32,128]{3,2,1,0:T(8,128)S(1)}, u32[]{:S(2)}, u32[]{:S(2)}) collective-permute-start(f32[5,3,32,128]{3,2,1,0:T(8,128)S(1)} %get-tuple-element.29), channel_id=1, source_target_pairs={{0,15},{1,2},{2,1},{3,4},{4,3},{5,6},{6,5},{7,8},{8,7},{9,10},{10,... | collective-permute-start | bytes 737288 | tf_op jit(solution)/shard_map/ppermute | solution.py:145
  60.3 7.9 %collective-permute-start.9 = (f32[5,3,32,128]{3,2,1,0:T(8,128)S(1)}, f32[5,3,32,128]{3,2,1,0:T(8,128)S(1)}, u32[]{:S(2)}, u32[]{:S(2)}) collective-permute-start(f32[5,3,32,128]{3,2,1,0:T(8,128)S(1)} %get-tuple-element.30), channel_id=1, source_target_pairs={{0,1},{1,0},{2,3},{3,2},{4,5},{5,4},{6,7},{7,6},{8,9},{9,8},{10,11... | collective-permute-start | bytes 737288 | tf_op jit(solution)/shard_map/ppermute | solution.py:149
  60.4 3.0 %collective-permute-start.7 = (f32[8,128]{1,0:T(8,128)S(1)}, f32[8,128]{1,0:T(8,128)S(1)}, u32[]{:S(2)}, u32[]{:S(2)}) collective-permute-start(f32[8,128]{1,0:T(8,128)S(1)} %maximum_maximum_fusion.1), channel_id=1, source_target_pairs={{0,3},{1,2},{2,1},{3,0},{4,7},{5,6},{6,5},{7,4},{8,11},{9,10},{10,... | collective-permute-start | bytes 12296 | tf_op jit(solution)/shard_map/ppermute | solution.py:644
  60.5 3.7 %collective-permute-start.6 = (f32[8,128]{1,0:T(8,128)S(1)}, f32[8,128]{1,0:T(8,128)S(1)}, u32[]{:S(2)}, u32[]{:S(2)}) collective-permute-start(f32[8,128]{1,0:T(8,128)S(1)} %maximum_maximum_fusion.1), channel_id=1, source_target_pairs={{0,2},{1,3},{2,0},{3,1},{4,6},{5,7},{6,4},{7,5},{8,10},{9,11},{10,... | collective-permute-start | bytes 12296 | tf_op jit(solution)/shard_map/ppermute | solution.py:644
  62.5 1.6 %collective-permute-start.5 = (f32[8,128]{1,0:T(8,128)S(1)}, f32[8,128]{1,0:T(8,128)S(1)}, u32[]{:S(2)}, u32[]{:S(2)}) collective-permute-start(f32[8,128]{1,0:T(8,128)S(1)} %maximum_maximum_fusion.1), channel_id=1, source_target_pairs={{0,1},{1,0},{2,3},{3,2},{4,5},{5,4},{6,7},{7,6},{8,9},{9,8},{10,11... | collective-permute-start | bytes 12296 | tf_op jit(solution)/shard_map/ppermute | solution.py:644

commit v21 on v20

--- a/solution.py
+++ b/solution.py
@@ -67,22 +67,14 @@
     lax.fori_loop(0, size, clear, 0, unroll=8)
     fetch_owner.wait()
 
-    fetch_tiled.wait()
-    best = jnp.zeros((8, LANES), jnp.float32)
-    step = per_dev * PAIRS
-    for first in range(0, step, 8):
-        fields = [tiled[f * step + first : f * step + first + 8, :] for f in range(FIELDS)]
-        best = jnp.maximum(best, wave_speed(fields))
-    for block in range(per_dev):
+    def note(block, carry):
         dest = owner[own * per_dev + block]
         rank = count[dest]
         count[dest] = rank + 1
-        member[dest * cap + rank] = block // 8 * (PAIRS * 8) + block % 8
-    most = jnp.full((1, LANES), jnp.max(best), jnp.float32)
-    for dest in range(size):
-        top[dest] = most
-    send_top = pltpu.make_async_copy(top, out_hbm.at[:, TILES * cap], sems.at[3])
-    send_top.start()
+        member[dest * cap + rank] = lax.div(block, 8) * (PAIRS * 8) + lax.rem(block, 8)
+        return carry
+
+    lax.fori_loop(0, per_dev, note, 0, unroll=8)
     fetch_rows.wait()
     tiles = TILES * cap
 
@@ -101,6 +93,17 @@
         return carry
 
     lax.fori_loop(0, size, message, 0)
+    fetch_tiled.wait()
+    best = jnp.zeros((8, LANES), jnp.float32)
+    step = per_dev * PAIRS
+    for first in range(0, step, 8):
+        fields = [tiled[f * step + first : f * step + first + 8, :] for f in range(FIELDS)]
+        best = jnp.maximum(best, wave_speed(fields))
+    most = jnp.full((1, LANES), jnp.max(best), jnp.float32)
+    for dest in range(size):
+        top[dest] = most
+    send_top = pltpu.make_async_copy(top, out_hbm.at[:, tiles], sems.at[3])
+    send_top.start()
     half = out.at[pl.ds(0, per_dev * TILES)]
     pltpu.make_async_copy(half, half, sems.at[2]).wait()
     send_top.wait()
@@ -362,7 +365,6 @@
 INNER = (range(2, 6), range(2, 6), range(0, 7))
 FAR = ((-1, 0, 1), (0, 1), (-1,))
 NEAR = ((6, 7), (6, 7, 8), (7,))
-EVERY = (range(-1, 8), range(0, 9), range(-1, 8))
 
 
 def ring_divergence(half_flux, scaled):
@@ -441,7 +443,7 @@
     return flux + 0.5 * pressure if field == 1 + direction else flux
 
 
-def plane_kernel(with_inner, *refs):
+def plane_kernel(*refs):
     *states, speed, out, turned = refs
     half_speed = 0.5 * speed[0:1, :]
     lane = lax.broadcasted_iota(jnp.int32, (LANES, LANES), 1)
@@ -482,20 +484,21 @@
         rows = pl.ds(pl.multiple_of(j * 8, 8), 8)
 
         def get(f, place):
-            return states[0][f, place, rows, :]
+            if len(states) == 1:
+                return states[0][f, place, rows, :]
+            return states[place // 4][f, place % 4, rows, :]
 
         for field, along_x in across(get, half_speed, range(BLOCK), INNER):
             for place in range(BLOCK):
                 out[field, place, rows, :] += along_x[place]
         return carry
 
-    if with_inner:
-        lax.fori_loop(0, 4, group, 0)
-
-
-def along_planes(states, speed, with_inner):
+    lax.fori_loop(0, 4, group, 0)
+
+
+def along_planes(states, speed):
     return pl.pallas_call(
-        functools.partial(plane_kernel, with_inner),
+        plane_kernel,
         out_shape=jax.ShapeDtypeStruct((FIELDS, BLOCK, ROWS, LANES), jnp.float32),
         in_specs=[VMEM] * (len(states) + 1),
         out_specs=VMEM,
@@ -529,18 +532,19 @@
         yield field, x_divergence(fluxes, scaled, *parts)
 
 
-WITH_HALOS = range(-3, BLOCK + 3)
-
-
-def with_halos(far, near, inside, rows):
+def with_halo(halo, inside, rows):
     def get(f, place):
         if place < 0:
-            return far[f, -1 - place, rows, :]
+            return halo[f, -1 - place, rows, :]
         if place >= BLOCK:
-            return near[f, BLOCK + 2 - place, rows, :]
+            return halo[f, BLOCK + 2 - place, rows, :]
         return inside(f, place)
 
     return get
+
+
+def half_of(is_far):
+    return (0, FAR, range(-3, 4)) if is_far else (4, NEAR, range(4, 11))
 
 
 def first_kernel(is_far, *refs):
@@ -548,7 +552,7 @@
         state, sides, halo, speed, other, middle, side, top = refs
     else:
         state, sides, halo, speed, middle, side, top = refs
-    first, parts, span = (0, FAR, range(-3, 4)) if is_far else (4, NEAR, range(4, 11))
+    first, parts, span = half_of(is_far)
     half_speed = 0.5 * speed[0:1, :]
     factor = (courant / 6.0) / speed[0:1, :]
 
@@ -558,7 +562,7 @@
         def inside(f, place):
             return state[f, place, rows, :]
 
-        get = with_halos(halo, halo, inside, rows)
+        get = with_halo(halo, inside, rows)
         for field, along_x in across(get, half_speed, span, parts):
             for k in range(4):
                 total = sides[field, first + k, rows, :]
@@ -594,40 +598,52 @@
     )(*operands)
 
 
-def second_kernel(state, middle_far, middle_near, sides, far, near, first_speed, speed, out):
+def second_kernel(is_far, *refs):
+    if is_far:
+        state, middle, sides, halo, first_speed, speed, other, out = refs
+    else:
+        state, middle, sides, halo, first_speed, speed, out = refs
+    first, parts, span = half_of(is_far)
     half_speed = 0.5 * speed[0:1, :]
     factor = (courant / 12.0) / first_speed[0:1, :]
-    planes = [place_of(place) for place in range(BLOCK)]
+    if is_far:
+        for k in range(4):
+            plane = place_of(4 + k)
+            for f in range(FIELDS):
+                out[f, plane] = other[f, k]
 
     def group(j, carry):
         rows = pl.ds(pl.multiple_of(j * 8, 8), 8)
         spread = pl.ds(j, 8, stride=4)
 
         def inside(f, place):
-            return (middle_far, middle_near)[place // 4][f, place % 4, rows, :]
-
-        get = with_halos(far, near, inside, rows)
-        for field, along_x in across(get, half_speed, WITH_HALOS, EVERY):
-            for place in range(BLOCK):
-                total = along_x[place] + sides[field, place, rows, :]
-                value = 0.5 * state[field, place, rows, :] + (
-                    0.5 * get(field, place) - factor * total
+            return middle[f, place - first, rows, :]
+
+        get = with_halo(halo, inside, rows)
+        for field, along_x in across(get, half_speed, span, parts):
+            for k in range(4):
+                total = sides[field, first + k, rows, :]
+                if first + k in along_x:
+                    total = total + along_x[first + k]
+                value = 0.5 * state[field, first + k, rows, :] + (
+                    0.5 * get(field, first + k) - factor * total
                 )
-                out[field, planes[place], spread, :] = value
+                out[field, place_of(k) if is_far else k, spread, :] = value
         return carry
 
     lax.fori_loop(0, 4, group, 0)
 
 
-def second_stage(*operands):
+def second_stage(is_far, *operands):
+    places = BLOCK if is_far else 4
     return pl.pallas_call(
-        second_kernel,
-        out_shape=jax.ShapeDtypeStruct((FIELDS, BLOCK, ROWS, LANES), jnp.float32),
+        functools.partial(second_kernel, is_far),
+        out_shape=jax.ShapeDtypeStruct((FIELDS, places, ROWS, LANES), jnp.float32),
         in_specs=[VMEM] * len(operands),
         out_specs=VMEM,
         compiler_params=params(),
-        cost_estimate=cost(30_000_000, 3_000_000),
-        name="second_stage",
+        cost_estimate=cost(15_000_000, 2_000_000),
+        name="second_far" if is_far else "second_near",
     )(*operands)
 
 
@@ -660,14 +676,16 @@
     state, far_side, near_side, speed = unpack(table, come.reshape(-1, 1, LANES), size, cap)
     far = from_far(far_side, size)
     near = from_near(near_side, size)
-    sides = along_planes((state,), speed, True)
+    sides = along_planes((state,), speed)
     middle_near, near_side, top = first_stage(False, state, sides, near, speed)
     middle_far, far_side, top = first_stage(True, state, sides, far, speed, top)
-    far = from_far(far_side, size)
     near = from_near(near_side, size)
     second = everyone_max(top, "gx", size)
-    sides = along_planes((middle_far, middle_near), second, False)
-    return second_stage(state, middle_far, middle_near, sides, far, near, speed, second)
+    far_side, second = lax.optimization_barrier((far_side, second))
+    far = from_far(far_side, size)
+    sides = along_planes((middle_far, middle_near), second)
+    part = second_stage(False, state, middle_near, sides, near, speed, second)
+    return second_stage(True, state, middle_far, sides, far, speed, second, part)
 
 
 def solution(mesh):

time: 71.8 us -> 74.3 us (1.035)
  waiting for transfers between devices: 28.6 us -> 30.2 us
  starting transfers between devices: 22.2 us -> 23 us
    ppermute x6, waiting for transfers between devices: 1.77 us -> 3.4 us  [everyone_max(): copies.append(lax.ppermute(value, axis, pairs))]
    ppermute x2, starting transfers between devices: 7.44 us -> 8.47 us  [from_far(): return lax.ppermute(far_side, 'gx', pairs)]
    pallas_call x3 -> x4, Pallas kernels: 12.4 us -> 12.9 us  [the longest x2 10.3 us: along_planes(): pl.pallas_call(plane_kernel, out_shape=jax.ShapeDtypeStruct((FIELDS, BLOC...]
  transfers between devices with their start and end apart: 11 -> 11, of which waited for: 4 -> 5; matrix products, arithmetic and copies ran while one was open for 1% -> 1% of each run, Pallas kernels for 14% -> 16%
where the time goes in v21:
time: 74.3 us; the launch traced here: 74.1 us
  waiting for transfers between devices  30.2 us (41%)
  starting transfers between devices  23 us (31%)
  Pallas kernels  20 us (27%)
    all_to_all x1, waiting for transfers between devices, per_device(): come = lax.all_to_all(parts, 'gx', split_axis=0, concat_axis=0, tiled=True)  26.8 us
    pallas_call x2, Pallas kernels, along_planes(): pl.pallas_call(plane_kernel, out_shape=jax.ShapeDtypeStruct((FIELDS, BLOC...  10.3 us
    ppermute x2, starting transfers between devices, from_far(): return lax.ppermute(far_side, 'gx', pairs)  8.47 us
    all_to_all x1, starting transfers between devices, per_device(): come = lax.all_to_all(parts, 'gx', split_axis=0, concat_axis=0, tiled=True)  7.37 us
    ppermute x6, starting transfers between devices, everyone_max(): copies.append(lax.ppermute(value, axis, pairs))  6.31 us
    ppermute x6, waiting for transfers between devices, everyone_max(): copies.append(lax.ppermute(value, axis, pairs))  3.4 us
    pallas_call x1, Pallas kernels, pack(): pl.pallas_call(functools.partial(pack_kernel, size, cap, per_dev), out_sh...  2.7 us
    pallas_call x2, Pallas kernels, second_stage(): pl.pallas_call(functools.partial(second_kernel, is_far), out_shape=jax.Sh...  2.59 us
  transfers between devices with their start and end apart: 11, of which 5 were waited for; matrix products, arithmetic and copies ran while one was open for 1% of the time, Pallas kernels for 16%

profile of v21, /device:TPU:0, one launch (start us, length us, event | category | flops | bytes accessed | tf_op | source)
XLA Modules:
  0.0 74.1 jit_solution(8992712273639236709)
XLA Ops:
  0.0 2.7 %pack.1 = f32[16,161,1,128]{3,2,1,0:T(1,128)} custom-call(s32[1024]{0:T(1024)} %owner_hbm.1, f32[1280,1,128]{2,1,0:T(1,128)} %bitcast.7), custom_call_target="tpu_custom_call" | custom-call | flops 1000000 | bytes 3000000 | tf_op jit(solution)/shard_map/pack/pallas_call | solution.py:113
  2.7 7.4 %all-to-all-start = ((f32[16,161,1,128]{3,2,1,0:T(1,128)}), f32[16,161,1,128]{3,2,1,0:T(1,128)S(1)}, u32[]{:S(2)}, u32[]{:S(2)}) async-start(f32[16,161,1,128]{3,2,1,0:T(1,128)} %pack.1), calls=%async_computation | async-start | bytes 2637824 | tf_op jit(solution)/shard_map/all_to_all | solution.py:674
  10.2 0.3 convert_reduce_fusion
  10.7 0.1 select_reduce_fusion.table
  10.9 26.8 %all-to-all-done = f32[16,161,1,128]{3,2,1,0:T(1,128)S(1)} async-done(((f32[16,161,1,128]{3,2,1,0:T(1,128)}), f32[16,161,1,128]{3,2,1,0:T(1,128)S(1)}, u32[]{:S(2)}, u32[]{:S(2)}) %all-to-all-start) | async-done | bytes 1318944 | tf_op jit(solution)/shard_map/all_to_all | solution.py:674
  37.7 2.5 %unpack.1 = (f32[5,8,32,128]{3,2,1,0:T(8,128)S(1)}, f32[5,3,32,128]{3,2,1,0:T(8,128)S(1)}, f32[5,3,32,128]{3,2,1,0:T(8,128)S(1)}, f32[8,128]{1,0:T(8,128)S(1)}) custom-call(s32[64]{0:T(128)S(1)} %select_reduce_fusion.table, f32[2576,1,128]{2,1,0:T(1,128)S(1)} %bitcast.6), custom_call_target="tpu_custom_call" | custom-call | flops 5000000 | bytes 2000000 | tf_op jit(solution)/shard_map/unpack/pallas_call | solution.py:237
  40.2 0.8 %collective-permute-start.1 = (f32[5,3,32,128]{3,2,1,0:T(8,128)S(1)}, f32[5,3,32,128]{3,2,1,0:T(8,128)S(1)}, u32[]{:S(2)}, u32[]{:S(2)}) collective-permute-start(f32[5,3,32,128]{3,2,1,0:T(8,128)S(1)} %get-tuple-element.26), channel_id=1, source_target_pairs={{0,1},{1,0},{2,3},{3,2},{4,5},{5,4},{6,7},{7,6},{8,9},{9,8},{10,11... | collective-permute-start | bytes 737288 | tf_op jit(solution)/shard_map/ppermute | solution.py:152
  41.0 6.0 %collective-permute-start = (f32[5,3,32,128]{3,2,1,0:T(8,128)S(1)}, f32[5,3,32,128]{3,2,1,0:T(8,128)S(1)}, u32[]{:S(2)}, u32[]{:S(2)}) collective-permute-start(f32[5,3,32,128]{3,2,1,0:T(8,128)S(1)} %get-tuple-element.25), channel_id=1, source_target_pairs={{0,15},{1,2},{2,1},{3,4},{4,3},{5,6},{6,5},{7,8},{8,7},{9,10},{10,... | collective-permute-start | bytes 737288 | tf_op jit(solution)/shard_map/ppermute | solution.py:148
  47.0 5.1 %planes.2.refs_1_ = f32[5,8,32,128]{3,2,1,0:T(8,128)S(1)} custom-call(f32[5,8,32,128]{3,2,1,0:T(8,128)S(1)} %get-tuple-element.23.refs_0_, f32[8,128]{1,0:T(8,128)S(1)} %get-tuple-element.24.refs_1_.refs_3_.refs_4_), custom_call_target="tpu_custom_call" | custom-call | flops 20000000 | bytes 1000000 | tf_op jit(solution)/shard_map/planes/pallas_call | solution.py:500
  52.2 0.9 %first_near.1 = (f32[5,4,32,128]{3,2,1,0:T(8,128)S(1)}, f32[5,3,32,128]{3,2,1,0:T(8,128)S(1)}, f32[8,128]{1,0:T(8,128)S(1)}) custom-call(f32[5,8,32,128]{3,2,1,0:T(8,128)S(1)} %get-tuple-element.23.refs_0_, f32[5,8,32,128]{3,2,1,0:T(8,128)S(1)} %planes.2.refs_1_, f32[5,3,32,128]{3,2,1,0:T(8,128)S(1)} %collective-permute-done.1.refs_2_, ...), custom_call_target="tpu_custom_call" | custom-call | flops 15000000 | bytes 2000000 | tf_op jit(solution)/shard_map/first_near/pallas_call | solution.py:586
  53.1 1.0 %first_far.1 = (f32[5,4,32,128]{3,2,1,0:T(8,128)S(1)}, f32[5,3,32,128]{3,2,1,0:T(8,128)S(1)}, f32[8,128]{1,0:T(8,128)S(1)}) custom-call(f32[5,8,32,128]{3,2,1,0:T(8,128)S(1)} %get-tuple-element.23.refs_0_, f32[5,8,32,128]{3,2,1,0:T(8,128)S(1)} %planes.2.refs_1_, f32[5,3,32,128]{3,2,1,0:T(8,128)S(1)} %collective-permute-done.refs_2_, ...), custom_call_target="tpu_custom_call" | custom-call | flops 15000000 | bytes 2000000 | tf_op jit(solution)/shard_map/first_far/pallas_call | solution.py:586
  54.1 0.3 collective-permute-start.4
  54.4 0.5 collective-permute-start.3
  54.9 3.6 %collective-permute-start.2 = (f32[8,128]{1,0:T(8,128)S(1)}, f32[8,128]{1,0:T(8,128)S(1)}, u32[]{:S(2)}, u32[]{:S(2)}) collective-permute-start(f32[8,128]{1,0:T(8,128)S(1)} %get-tuple-element.31), channel_id=1, source_target_pairs={{0,4},{1,5},{2,6},{3,7},{4,0},{5,1},{6,2},{7,3},{8,12},{9,13},{10,... | collective-permute-start | bytes 12296 | tf_op jit(solution)/shard_map/ppermute | solution.py:660
  58.5 1.0 %collective-permute-done.4 = f32[8,128]{1,0:T(8,128)S(1)} collective-permute-done((f32[8,128]{1,0:T(8,128)S(1)}, f32[8,128]{1,0:T(8,128)S(1)}, u32[]{:S(2)}, u32[]{:S(2)}) %collective-permute-start.4) | collective-permute-done | bytes 4128 | tf_op jit(solution)/shard_map/ppermute | solution.py:660
  59.6 0.6 collective-permute-done.2
  60.2 1.3 %collective-permute-start.6 = (f32[8,128]{1,0:T(8,128)S(1)}, f32[8,128]{1,0:T(8,128)S(1)}, u32[]{:S(2)}, u32[]{:S(2)}) collective-permute-start(f32[8,128]{1,0:T(8,128)S(1)} %maximum_maximum_fusion.1), channel_id=1, source_target_pairs={{0,2},{1,3},{2,0},{3,1},{4,6},{5,7},{6,4},{7,5},{8,10},{9,11},{10,... | collective-permute-start | bytes 12296 | tf_op jit(solution)/shard_map/ppermute | solution.py:660
  61.5 0.5 collective-permute-start.5
  62.0 1.2 %collective-permute-done.7 = f32[8,128]{1,0:T(8,128)S(1)} collective-permute-done((f32[8,128]{1,0:T(8,128)S(1)}, f32[8,128]{1,0:T(8,128)S(1)}, u32[]{:S(2)}, u32[]{:S(2)}) %collective-permute-start.7) | collective-permute-done | bytes 4128 | tf_op jit(solution)/shard_map/ppermute | solution.py:660
  63.2 0.6 collective-permute-done.6
  63.8 2.5 %collective-permute-start.8 = (f32[5,3,32,128]{3,2,1,0:T(8,128)S(1)}, f32[5,3,32,128]{3,2,1,0:T(8,128)S(1)}, u32[]{:S(2)}, u32[]{:S(2)}) collective-permute-start(f32[5,3,32,128]{3,2,1,0:T(8,128)S(1)} %get-tuple-element.33), channel_id=1, source_target_pairs={{0,15},{1,2},{2,1},{3,4},{4,3},{5,6},{6,5},{7,8},{8,7},{9,10},{10,... | collective-permute-start | bytes 737288 | tf_op jit(solution)/shard_map/ppermute | solution.py:148
  66.3 5.2 %planes.3.refs_2_ = f32[5,8,32,128]{3,2,1,0:T(8,128)S(1)} custom-call(f32[5,4,32,128]{3,2,1,0:T(8,128)S(1)} %get-tuple-element.28.refs_0_.refs_1_, f32[5,4,32,128]{3,2,1,0:T(8,128)S(1)} %get-tuple-element.29.refs_1_, f32[8,128]{1,0:T(8,128)S(1)} %maximum_maximum_fusion.refs_2_.refs_5_), custom_call_target="tpu_custom_call" | custom-call | flops 20000000 | bytes 1000000 | tf_op jit(solution)/shard_map/planes/pallas_call | solution.py:500
  71.4 0.9 %second_near.1.refs_6_ = f32[5,4,32,128]{3,2,1,0:T(8,128)S(1)} custom-call(f32[5,8,32,128]{3,2,1,0:T(8,128)S(1)} %get-tuple-element.23.refs_0_, f32[5,4,32,128]{3,2,1,0:T(8,128)S(1)} %get-tuple-element.29.refs_1_, f32[5,8,32,128]{3,2,1,0:T(8,128)S(1)} %planes.3.refs_2_, f32[5,3,32,128]{3,2,1,0:T(8,128)S(1)} %collective-permute-done.9.refs_3_, ...), custom_call_target="tpu_custom_call" | custom-call | flops 15000000 | bytes 2000000 | tf_op jit(solution)/shard_map/second_near/pallas_call | solution.py:639
  72.3 1.7 %second_far.1 = f32[5,8,32,128]{3,2,1,0:T(8,128)} custom-call(f32[5,8,32,128]{3,2,1,0:T(8,128)S(1)} %get-tuple-element.23.refs_0_, f32[5,4,32,128]{3,2,1,0:T(8,128)S(1)} %get-tuple-element.28.refs_0_.refs_1_, f32[5,8,32,128]{3,2,1,0:T(8,128)S(1)} %planes.3.refs_2_, f32[5,3,32,128]{3,2,1,0:T(8,128)S(1)} %collective-permute-done.8.refs_3_, ...), custom_call_target="tpu_custom_call" | custom-call | flops 15000000 | bytes 2000000 | tf_op jit(solution)/shard_map/second_far/pallas_call | solution.py:639
  (20 shorter events, 0.3 us)
Async XLA Ops:
  2.7 7.4 %copy-start = (s32[1024]{0:T(1024)S(1)}, s32[1024]{0:T(1024)}, u32[]{:S(2)}) copy-start(s32[1024]{0:T(1024)} %owner_hbm.1) | copy-start | bytes 12292
  2.7 7.4 %copy-start.1 = (s32[1024]{0:T(1024)S(1)}, s32[1024]{0:T(1024)}, u32[]{:S(2)}) copy-start(s32[1024]{0:T(1024)} %param.5) | copy-start | bytes 12292
  2.7 34.9 %all-to-all-start = ((f32[16,161,1,128]{3,2,1,0:T(1,128)}), f32[16,161,1,128]{3,2,1,0:T(1,128)S(1)}, u32[]{:S(2)}, u32[]{:S(2)}) async-start(f32[16,161,1,128]{3,2,1,0:T(1,128)} %pack.1), calls=%async_computation | async-start | bytes 2637824 | tf_op jit(solution)/shard_map/all_to_all | solution.py:674
  40.2 12.0 %collective-permute-start.1 = (f32[5,3,32,128]{3,2,1,0:T(8,128)S(1)}, f32[5,3,32,128]{3,2,1,0:T(8,128)S(1)}, u32[]{:S(2)}, u32[]{:S(2)}) collective-permute-start(f32[5,3,32,128]{3,2,1,0:T(8,128)S(1)} %get-tuple-element.26), channel_id=1, source_target_pairs={{0,1},{1,0},{2,3},{3,2},{4,5},{5,4},{6,7},{7,6},{8,9},{9,8},{10,11... | collective-permute-start | bytes 737288 | tf_op jit(solution)/shard_map/ppermute | solution.py:152
  41.0 12.0 %collective-permute-start = (f32[5,3,32,128]{3,2,1,0:T(8,128)S(1)}, f32[5,3,32,128]{3,2,1,0:T(8,128)S(1)}, u32[]{:S(2)}, u32[]{:S(2)}) collective-permute-start(f32[5,3,32,128]{3,2,1,0:T(8,128)S(1)} %get-tuple-element.25), channel_id=1, source_target_pairs={{0,15},{1,2},{2,1},{3,4},{4,3},{5,6},{6,5},{7,8},{8,7},{9,10},{10,... | collective-permute-start | bytes 737288 | tf_op jit(solution)/shard_map/ppermute | solution.py:148
  54.1 5.5 %collective-permute-start.4 = (f32[8,128]{1,0:T(8,128)S(1)}, f32[8,128]{1,0:T(8,128)S(1)}, u32[]{:S(2)}, u32[]{:S(2)}) collective-permute-start(f32[8,128]{1,0:T(8,128)S(1)} %get-tuple-element.31), channel_id=1, source_target_pairs={{0,12},{1,13},{2,14},{3,15},{4,8},{5,9},{6,10},{7,11},{8,4},{9,5},... | collective-permute-start | bytes 12296 | tf_op jit(solution)/shard_map/ppermute | solution.py:660
  54.4 5.2 %collective-permute-start.3 = (f32[8,128]{1,0:T(8,128)S(1)}, f32[8,128]{1,0:T(8,128)S(1)}, u32[]{:S(2)}, u32[]{:S(2)}) collective-permute-start(f32[8,128]{1,0:T(8,128)S(1)} %get-tuple-element.31), channel_id=1, source_target_pairs={{0,8},{1,9},{2,10},{3,11},{4,12},{5,13},{6,14},{7,15},{8,0},{9,1},... | collective-permute-start | bytes 12296 | tf_op jit(solution)/shard_map/ppermute | solution.py:660
  54.9 5.2 %collective-permute-start.2 = (f32[8,128]{1,0:T(8,128)S(1)}, f32[8,128]{1,0:T(8,128)S(1)}, u32[]{:S(2)}, u32[]{:S(2)}) collective-permute-start(f32[8,128]{1,0:T(8,128)S(1)} %get-tuple-element.31), channel_id=1, source_target_pairs={{0,4},{1,5},{2,6},{3,7},{4,0},{5,1},{6,2},{7,3},{8,12},{9,13},{10,... | collective-permute-start | bytes 12296 | tf_op jit(solution)/shard_map/ppermute | solution.py:660
  60.1 3.0 %collective-permute-start.7 = (f32[8,128]{1,0:T(8,128)S(1)}, f32[8,128]{1,0:T(8,128)S(1)}, u32[]{:S(2)}, u32[]{:S(2)}) collective-permute-start(f32[8,128]{1,0:T(8,128)S(1)} %maximum_maximum_fusion.1), channel_id=1, source_target_pairs={{0,3},{1,2},{2,1},{3,0},{4,7},{5,6},{6,5},{7,4},{8,11},{9,10},{10,... | collective-permute-start | bytes 12296 | tf_op jit(solution)/shard_map/ppermute | solution.py:660
  60.2 3.7 %collective-permute-start.6 = (f32[8,128]{1,0:T(8,128)S(1)}, f32[8,128]{1,0:T(8,128)S(1)}, u32[]{:S(2)}, u32[]{:S(2)}) collective-permute-start(f32[8,128]{1,0:T(8,128)S(1)} %maximum_maximum_fusion.1), channel_id=1, source_target_pairs={{0,2},{1,3},{2,0},{3,1},{4,6},{5,7},{6,4},{7,5},{8,10},{9,11},{10,... | collective-permute-start | bytes 12296 | tf_op jit(solution)/shard_map/ppermute | solution.py:660
  61.5 2.4 %collective-permute-start.5 = (f32[8,128]{1,0:T(8,128)S(1)}, f32[8,128]{1,0:T(8,128)S(1)}, u32[]{:S(2)}, u32[]{:S(2)}) collective-permute-start(f32[8,128]{1,0:T(8,128)S(1)} %maximum_maximum_fusion.1), channel_id=1, source_target_pairs={{0,1},{1,0},{2,3},{3,2},{4,5},{5,4},{6,7},{7,6},{8,9},{9,8},{10,11... | collective-permute-start | bytes 12296 | tf_op jit(solution)/shard_map/ppermute | solution.py:660
  62.0 9.4 %collective-permute-start.9 = (f32[5,3,32,128]{3,2,1,0:T(8,128)S(1)}, f32[5,3,32,128]{3,2,1,0:T(8,128)S(1)}, u32[]{:S(2)}, u32[]{:S(2)}) collective-permute-start(f32[5,3,32,128]{3,2,1,0:T(8,128)S(1)} %get-tuple-element.34), channel_id=1, source_target_pairs={{0,1},{1,0},{2,3},{3,2},{4,5},{5,4},{6,7},{7,6},{8,9},{9,8},{10,11... | collective-permute-start | bytes 737288 | tf_op jit(solution)/shard_map/ppermute | solution.py:152
  63.8 8.5 %collective-permute-start.8 = (f32[5,3,32,128]{3,2,1,0:T(8,128)S(1)}, f32[5,3,32,128]{3,2,1,0:T(8,128)S(1)}, u32[]{:S(2)}, u32[]{:S(2)}) collective-permute-start(f32[5,3,32,128]{3,2,1,0:T(8,128)S(1)} %get-tuple-element.33), channel_id=1, source_target_pairs={{0,15},{1,2},{2,1},{3,4},{4,3},{5,6},{6,5},{7,8},{8,7},{9,10},{10,... | collective-permute-start | bytes 737288 | tf_op jit(solution)/shard_map/ppermute | solution.py:148

commit v22 on v20

--- a/solution.py
+++ b/solution.py
@@ -67,22 +67,14 @@
     lax.fori_loop(0, size, clear, 0, unroll=8)
     fetch_owner.wait()
 
-    fetch_tiled.wait()
-    best = jnp.zeros((8, LANES), jnp.float32)
-    step = per_dev * PAIRS
-    for first in range(0, step, 8):
-        fields = [tiled[f * step + first : f * step + first + 8, :] for f in range(FIELDS)]
-        best = jnp.maximum(best, wave_speed(fields))
-    for block in range(per_dev):
+    def note(block, carry):
         dest = owner[own * per_dev + block]
         rank = count[dest]
         count[dest] = rank + 1
-        member[dest * cap + rank] = block // 8 * (PAIRS * 8) + block % 8
-    most = jnp.full((1, LANES), jnp.max(best), jnp.float32)
-    for dest in range(size):
-        top[dest] = most
-    send_top = pltpu.make_async_copy(top, out_hbm.at[:, TILES * cap], sems.at[3])
-    send_top.start()
+        member[dest * cap + rank] = lax.div(block, 8) * (PAIRS * 8) + lax.rem(block, 8)
+        return carry
+
+    lax.fori_loop(0, per_dev, note, 0, unroll=8)
     fetch_rows.wait()
     tiles = TILES * cap
 
@@ -101,6 +93,17 @@
         return carry
 
     lax.fori_loop(0, size, message, 0)
+    fetch_tiled.wait()
+    best = jnp.zeros((8, LANES), jnp.float32)
+    step = per_dev * PAIRS
+    for first in range(0, step, 8):
+        fields = [tiled[f * step + first : f * step + first + 8, :] for f in range(FIELDS)]
+        best = jnp.maximum(best, wave_speed(fields))
+    most = jnp.full((1, LANES), jnp.max(best), jnp.float32)
+    for dest in range(size):
+        top[dest] = most
+    send_top = pltpu.make_async_copy(top, out_hbm.at[:, tiles], sems.at[3])
+    send_top.start()
     half = out.at[pl.ds(0, per_dev * TILES)]
     pltpu.make_async_copy(half, half, sems.at[2]).wait()
     send_top.wait()
@@ -637,7 +640,7 @@
         reach *= 4
     while reach:
         copies = [value]
-        for times in range(1, 4):
+        for times in range(3, 0, -1):
             turn = reach * times
             if turn < size:
                 pairs = [(i, i ^ turn) for i in range(size)]

time: 71.8 us -> 73 us (1.017)
  waiting for transfers between devices: 28.6 us -> 30.5 us
    ppermute x6, waiting for transfers between devices: 1.77 us -> 3.68 us  [everyone_max(): copies.append(lax.ppermute(value, axis, pairs))]
where the time goes in v22:
time: 73 us; the launch traced here: 72.8 us
  waiting for transfers between devices  30.5 us (42%)
  starting transfers between devices  22 us (30%)
  Pallas kernels  19.5 us (27%)
    all_to_all x1, waiting for transfers between devices, per_device(): come = lax.all_to_all(parts, 'gx', split_axis=0, concat_axis=0, tiled=True)  26.8 us
    pallas_call x2, Pallas kernels, along_planes(): pl.pallas_call(functools.partial(plane_kernel, with_inner), out_shape=jax...  9.11 us
    ppermute x2, starting transfers between devices, from_far(): return lax.ppermute(far_side, 'gx', pairs)  7.44 us
    all_to_all x1, starting transfers between devices, per_device(): come = lax.all_to_all(parts, 'gx', split_axis=0, concat_axis=0, tiled=True)  7.37 us
    ppermute x6, starting transfers between devices, everyone_max(): copies.append(lax.ppermute(value, axis, pairs))  6.31 us
    ppermute x6, waiting for transfers between devices, everyone_max(): copies.append(lax.ppermute(value, axis, pairs))  3.68 us
    pallas_call x1, Pallas kernels, second_stage(): pl.pallas_call(second_kernel, out_shape=jax.ShapeDtypeStruct((FIELDS, BLO...  3.27 us
    pallas_call x1, Pallas kernels, pack(): pl.pallas_call(functools.partial(pack_kernel, size, cap, per_dev), out_sh...  2.7 us
  transfers between devices with their start and end apart: 11, of which 4 were waited for; matrix products, arithmetic and copies ran while one was open for 1% of the time, Pallas kernels for 14%

profile of v22, /device:TPU:0, one launch (start us, length us, event | category | flops | bytes accessed | tf_op | source)
XLA Modules:
  0.0 72.8 jit_solution(7703536218274546928)
XLA Ops:
  0.0 2.7 %pack.1 = f32[16,161,1,128]{3,2,1,0:T(1,128)} custom-call(s32[1024]{0:T(1024)} %owner_hbm.1, f32[1280,1,128]{2,1,0:T(1,128)} %bitcast.7), custom_call_target="tpu_custom_call" | custom-call | flops 1000000 | bytes 3000000 | tf_op jit(solution)/shard_map/pack/pallas_call | solution.py:113
  2.7 7.4 %all-to-all-start = ((f32[16,161,1,128]{3,2,1,0:T(1,128)}), f32[16,161,1,128]{3,2,1,0:T(1,128)S(1)}, u32[]{:S(2)}, u32[]{:S(2)}) async-start(f32[16,161,1,128]{3,2,1,0:T(1,128)} %pack.1), calls=%async_computation | async-start | bytes 2637824 | tf_op jit(solution)/shard_map/all_to_all | solution.py:661
  10.1 0.1 eq.33
  10.2 0.3 convert_reduce_fusion
  10.7 0.1 add.17
  10.7 0.1 select_reduce_fusion.table
  10.9 26.8 %all-to-all-done = f32[16,161,1,128]{3,2,1,0:T(1,128)S(1)} async-done(((f32[16,161,1,128]{3,2,1,0:T(1,128)}), f32[16,161,1,128]{3,2,1,0:T(1,128)S(1)}, u32[]{:S(2)}, u32[]{:S(2)}) %all-to-all-start) | async-done | bytes 1318944 | tf_op jit(solution)/shard_map/all_to_all | solution.py:661
  37.7 2.5 %unpack.1 = (f32[5,8,32,128]{3,2,1,0:T(8,128)S(1)}, f32[5,3,32,128]{3,2,1,0:T(8,128)S(1)}, f32[5,3,32,128]{3,2,1,0:T(8,128)S(1)}, f32[8,128]{1,0:T(8,128)S(1)}) custom-call(s32[64]{0:T(128)S(1)} %select_reduce_fusion.table, f32[2576,1,128]{2,1,0:T(1,128)S(1)} %bitcast.6), custom_call_target="tpu_custom_call" | custom-call | flops 5000000 | bytes 2000000 | tf_op jit(solution)/shard_map/unpack/pallas_call | solution.py:237
  40.2 0.8 %collective-permute-start.1 = (f32[5,3,32,128]{3,2,1,0:T(8,128)S(1)}, f32[5,3,32,128]{3,2,1,0:T(8,128)S(1)}, u32[]{:S(2)}, u32[]{:S(2)}) collective-permute-start(f32[5,3,32,128]{3,2,1,0:T(8,128)S(1)} %get-tuple-element.24), channel_id=1, source_target_pairs={{0,1},{1,0},{2,3},{3,2},{4,5},{5,4},{6,7},{7,6},{8,9},{9,8},{10,11... | collective-permute-start | bytes 737288 | tf_op jit(solution)/shard_map/ppermute | solution.py:152
  41.0 6.0 %collective-permute-start = (f32[5,3,32,128]{3,2,1,0:T(8,128)S(1)}, f32[5,3,32,128]{3,2,1,0:T(8,128)S(1)}, u32[]{:S(2)}, u32[]{:S(2)}) collective-permute-start(f32[5,3,32,128]{3,2,1,0:T(8,128)S(1)} %get-tuple-element.23), channel_id=1, source_target_pairs={{0,15},{1,2},{2,1},{3,4},{4,3},{5,6},{6,5},{7,8},{8,7},{9,10},{10,... | collective-permute-start | bytes 737288 | tf_op jit(solution)/shard_map/ppermute | solution.py:148
  47.0 5.1 %planes.2.refs_1_ = f32[5,8,32,128]{3,2,1,0:T(8,128)S(1)} custom-call(f32[5,8,32,128]{3,2,1,0:T(8,128)S(1)} %get-tuple-element.21.refs_0_.state, f32[8,128]{1,0:T(8,128)S(1)} %get-tuple-element.22.refs_1_.refs_3_.first_speed), custom_call_target="tpu_custom_call" | custom-call | flops 20000000 | bytes 1000000 | tf_op jit(solution)/shard_map/planes/pallas_call | solution.py:500
  52.2 0.9 %first_near.1 = (f32[5,4,32,128]{3,2,1,0:T(8,128)S(1)}, f32[5,3,32,128]{3,2,1,0:T(8,128)S(1)}, f32[8,128]{1,0:T(8,128)S(1)}) custom-call(f32[5,8,32,128]{3,2,1,0:T(8,128)S(1)} %get-tuple-element.21.refs_0_.state, f32[5,8,32,128]{3,2,1,0:T(8,128)S(1)} %planes.2.refs_1_, f32[5,3,32,128]{3,2,1,0:T(8,128)S(1)} %collective-permute-done.1.refs_2_, ...), custom_call_target="tpu_custom_call" | custom-call | flops 15000000 | bytes 2000000 | tf_op jit(solution)/shard_map/first_near/pallas_call | solution.py:585
  53.1 1.0 %first_far.1 = (f32[5,4,32,128]{3,2,1,0:T(8,128)S(1)}, f32[5,3,32,128]{3,2,1,0:T(8,128)S(1)}, f32[8,128]{1,0:T(8,128)S(1)}) custom-call(f32[5,8,32,128]{3,2,1,0:T(8,128)S(1)} %get-tuple-element.21.refs_0_.state, f32[5,8,32,128]{3,2,1,0:T(8,128)S(1)} %planes.2.refs_1_, f32[5,3,32,128]{3,2,1,0:T(8,128)S(1)} %collective-permute-done.refs_2_, ...), custom_call_target="tpu_custom_call" | custom-call | flops 15000000 | bytes 2000000 | tf_op jit(solution)/shard_map/first_far/pallas_call | solution.py:585
  54.2 0.8 %collective-permute-start.3 = (f32[8,128]{1,0:T(8,128)S(1)}, f32[8,128]{1,0:T(8,128)S(1)}, u32[]{:S(2)}, u32[]{:S(2)}) collective-permute-start(f32[8,128]{1,0:T(8,128)S(1)} %get-tuple-element.28), channel_id=1, source_target_pairs={{0,8},{1,9},{2,10},{3,11},{4,12},{5,13},{6,14},{7,15},{8,0},{9,1},... | collective-permute-start | bytes 12296 | tf_op jit(solution)/shard_map/ppermute | solution.py:647
  55.0 3.6 %collective-permute-start.2 = (f32[8,128]{1,0:T(8,128)S(1)}, f32[8,128]{1,0:T(8,128)S(1)}, u32[]{:S(2)}, u32[]{:S(2)}) collective-permute-start(f32[8,128]{1,0:T(8,128)S(1)} %get-tuple-element.28), channel_id=1, source_target_pairs={{0,12},{1,13},{2,14},{3,15},{4,8},{5,9},{6,10},{7,11},{8,4},{9,5},... | collective-permute-start | bytes 12296 | tf_op jit(solution)/shard_map/ppermute | solution.py:647
  58.5 1.4 %collective-permute-start.8 = (f32[5,3,32,128]{3,2,1,0:T(8,128)S(1)}, f32[5,3,32,128]{3,2,1,0:T(8,128)S(1)}, u32[]{:S(2)}, u32[]{:S(2)}) collective-permute-start(f32[5,3,32,128]{3,2,1,0:T(8,128)S(1)} %get-tuple-element.29), channel_id=1, source_target_pairs={{0,15},{1,2},{2,1},{3,4},{4,3},{5,6},{6,5},{7,8},{8,7},{9,10},{10,... | collective-permute-start | bytes 737288 | tf_op jit(solution)/shard_map/ppermute | solution.py:148
  60.0 0.4 collective-permute-done.2
  60.4 0.2 collective-permute-start.7
  60.6 1.3 %collective-permute-start.6 = (f32[8,128]{1,0:T(8,128)S(1)}, f32[8,128]{1,0:T(8,128)S(1)}, u32[]{:S(2)}, u32[]{:S(2)}) collective-permute-start(f32[8,128]{1,0:T(8,128)S(1)} %maximum_maximum_fusion.1), channel_id=1, source_target_pairs={{0,2},{1,3},{2,0},{3,1},{4,6},{5,7},{6,4},{7,5},{8,10},{9,11},{10,... | collective-permute-start | bytes 12296 | tf_op jit(solution)/shard_map/ppermute | solution.py:647
  61.9 0.3 collective-permute-start.5
  62.2 2.0 %collective-permute-done.6 = f32[8,128]{1,0:T(8,128)S(1)} collective-permute-done((f32[8,128]{1,0:T(8,128)S(1)}, f32[8,128]{1,0:T(8,128)S(1)}, u32[]{:S(2)}, u32[]{:S(2)}) %collective-permute-start.6) | collective-permute-done | bytes 4128 | tf_op jit(solution)/shard_map/ppermute | solution.py:647
  64.2 1.3 %collective-permute-done.5 = f32[8,128]{1,0:T(8,128)S(1)} collective-permute-done((f32[8,128]{1,0:T(8,128)S(1)}, f32[8,128]{1,0:T(8,128)S(1)}, u32[]{:S(2)}, u32[]{:S(2)}) %collective-permute-start.5) | collective-permute-done | bytes 4128 | tf_op jit(solution)/shard_map/ppermute | solution.py:647
  65.5 4.0 %planes.3.sides = f32[5,8,32,128]{3,2,1,0:T(8,128)S(1)} custom-call(f32[5,4,32,128]{3,2,1,0:T(8,128)S(1)} %get-tuple-element.26.refs_0_.middle_far, f32[5,4,32,128]{3,2,1,0:T(8,128)S(1)} %get-tuple-element.27.refs_1_.middle_near, f32[8,128]{1,0:T(8,128)S(1)} %maximum_maximum_fusion.refs_2_.speed), custom_call_target="tpu_custom_call" | custom-call | flops 20000000 | bytes 1000000 | tf_op jit(solution)/shard_map/planes/pallas_call | solution.py:500
  69.6 3.3 %second_stage.1 = f32[5,8,32,128]{3,2,1,0:T(8,128)} custom-call(f32[5,8,32,128]{3,2,1,0:T(8,128)S(1)} %get-tuple-element.21.refs_0_.state, f32[5,4,32,128]{3,2,1,0:T(8,128)S(1)} %get-tuple-element.26.refs_0_.middle_far, f32[5,4,32,128]{3,2,1,0:T(8,128)S(1)} %get-tuple-element.27.refs_1_.middle_near, f32[5,8,32,128]{3,2,1,0:T(8,128)S(1)} %planes.3.sides, ...), custom_call_target="tpu_custom_call" | custom-call | flops 30000000 | bytes 3000000 | tf_op jit(solution)/shard_map/second_stage/pallas_call | solution.py:626
  (19 shorter events, 0.2 us)
Async XLA Ops:
  2.7 7.4 %copy-start = (s32[1024]{0:T(1024)S(1)}, s32[1024]{0:T(1024)}, u32[]{:S(2)}) copy-start(s32[1024]{0:T(1024)} %owner_hbm.1) | copy-start | bytes 12292
  2.7 7.4 %copy-start.1 = (s32[1024]{0:T(1024)S(1)}, s32[1024]{0:T(1024)}, u32[]{:S(2)}) copy-start(s32[1024]{0:T(1024)} %param.5) | copy-start | bytes 12292
  2.7 34.9 %all-to-all-start = ((f32[16,161,1,128]{3,2,1,0:T(1,128)}), f32[16,161,1,128]{3,2,1,0:T(1,128)S(1)}, u32[]{:S(2)}, u32[]{:S(2)}) async-start(f32[16,161,1,128]{3,2,1,0:T(1,128)} %pack.1), calls=%async_computation | async-start | bytes 2637824 | tf_op jit(solution)/shard_map/all_to_all | solution.py:661
  40.2 12.0 %collective-permute-start.1 = (f32[5,3,32,128]{3,2,1,0:T(8,128)S(1)}, f32[5,3,32,128]{3,2,1,0:T(8,128)S(1)}, u32[]{:S(2)}, u32[]{:S(2)}) collective-permute-start(f32[5,3,32,128]{3,2,1,0:T(8,128)S(1)} %get-tuple-element.24), channel_id=1, source_target_pairs={{0,1},{1,0},{2,3},{3,2},{4,5},{5,4},{6,7},{7,6},{8,9},{9,8},{10,11... | collective-permute-start | bytes 737288 | tf_op jit(solution)/shard_map/ppermute | solution.py:152
  41.0 12.0 %collective-permute-start = (f32[5,3,32,128]{3,2,1,0:T(8,128)S(1)}, f32[5,3,32,128]{3,2,1,0:T(8,128)S(1)}, u32[]{:S(2)}, u32[]{:S(2)}) collective-permute-start(f32[5,3,32,128]{3,2,1,0:T(8,128)S(1)} %get-tuple-element.23), channel_id=1, source_target_pairs={{0,15},{1,2},{2,1},{3,4},{4,3},{5,6},{6,5},{7,8},{8,7},{9,10},{10,... | collective-permute-start | bytes 737288 | tf_op jit(solution)/shard_map/ppermute | solution.py:148
  54.1 5.9 %collective-permute-start.4 = (f32[8,128]{1,0:T(8,128)S(1)}, f32[8,128]{1,0:T(8,128)S(1)}, u32[]{:S(2)}, u32[]{:S(2)}) collective-permute-start(f32[8,128]{1,0:T(8,128)S(1)} %get-tuple-element.28), channel_id=1, source_target_pairs={{0,4},{1,5},{2,6},{3,7},{4,0},{5,1},{6,2},{7,3},{8,12},{9,13},{10,... | collective-permute-start | bytes 12296 | tf_op jit(solution)/shard_map/ppermute | solution.py:647
  54.2 5.8 %collective-permute-start.3 = (f32[8,128]{1,0:T(8,128)S(1)}, f32[8,128]{1,0:T(8,128)S(1)}, u32[]{:S(2)}, u32[]{:S(2)}) collective-permute-start(f32[8,128]{1,0:T(8,128)S(1)} %get-tuple-element.28), channel_id=1, source_target_pairs={{0,8},{1,9},{2,10},{3,11},{4,12},{5,13},{6,14},{7,15},{8,0},{9,1},... | collective-permute-start | bytes 12296 | tf_op jit(solution)/shard_map/ppermute | solution.py:647
  55.0 5.4 %collective-permute-start.2 = (f32[8,128]{1,0:T(8,128)S(1)}, f32[8,128]{1,0:T(8,128)S(1)}, u32[]{:S(2)}, u32[]{:S(2)}) collective-permute-start(f32[8,128]{1,0:T(8,128)S(1)} %get-tuple-element.28), channel_id=1, source_target_pairs={{0,12},{1,13},{2,14},{3,15},{4,8},{5,9},{6,10},{7,11},{8,4},{9,5},... | collective-permute-start | bytes 12296 | tf_op jit(solution)/shard_map/ppermute | solution.py:647
  58.5 11.0 %collective-permute-start.8 = (f32[5,3,32,128]{3,2,1,0:T(8,128)S(1)}, f32[5,3,32,128]{3,2,1,0:T(8,128)S(1)}, u32[]{:S(2)}, u32[]{:S(2)}) collective-permute-start(f32[5,3,32,128]{3,2,1,0:T(8,128)S(1)} %get-tuple-element.29), channel_id=1, source_target_pairs={{0,15},{1,2},{2,1},{3,4},{4,3},{5,6},{6,5},{7,8},{8,7},{9,10},{10,... | collective-permute-start | bytes 737288 | tf_op jit(solution)/shard_map/ppermute | solution.py:148
  60.0 9.6 %collective-permute-start.9 = (f32[5,3,32,128]{3,2,1,0:T(8,128)S(1)}, f32[5,3,32,128]{3,2,1,0:T(8,128)S(1)}, u32[]{:S(2)}, u32[]{:S(2)}) collective-permute-start(f32[5,3,32,128]{3,2,1,0:T(8,128)S(1)} %get-tuple-element.30), channel_id=1, source_target_pairs={{0,1},{1,0},{2,3},{3,2},{4,5},{5,4},{6,7},{7,6},{8,9},{9,8},{10,11... | collective-permute-start | bytes 737288 | tf_op jit(solution)/shard_map/ppermute | solution.py:152
  60.4 1.9 %collective-permute-start.7 = (f32[8,128]{1,0:T(8,128)S(1)}, f32[8,128]{1,0:T(8,128)S(1)}, u32[]{:S(2)}, u32[]{:S(2)}) collective-permute-start(f32[8,128]{1,0:T(8,128)S(1)} %maximum_maximum_fusion.1), channel_id=1, source_target_pairs={{0,1},{1,0},{2,3},{3,2},{4,5},{5,4},{6,7},{7,6},{8,9},{9,8},{10,11... | collective-permute-start | bytes 12296 | tf_op jit(solution)/shard_map/ppermute | solution.py:647
  60.6 3.6 %collective-permute-start.6 = (f32[8,128]{1,0:T(8,128)S(1)}, f32[8,128]{1,0:T(8,128)S(1)}, u32[]{:S(2)}, u32[]{:S(2)}) collective-permute-start(f32[8,128]{1,0:T(8,128)S(1)} %maximum_maximum_fusion.1), channel_id=1, source_target_pairs={{0,2},{1,3},{2,0},{3,1},{4,6},{5,7},{6,4},{7,5},{8,10},{9,11},{10,... | collective-permute-start | bytes 12296 | tf_op jit(solution)/shard_map/ppermute | solution.py:647
  61.9 3.7 %collective-permute-start.5 = (f32[8,128]{1,0:T(8,128)S(1)}, f32[8,128]{1,0:T(8,128)S(1)}, u32[]{:S(2)}, u32[]{:S(2)}) collective-permute-start(f32[8,128]{1,0:T(8,128)S(1)} %maximum_maximum_fusion.1), channel_id=1, source_target_pairs={{0,3},{1,2},{2,1},{3,0},{4,7},{5,6},{6,5},{7,4},{8,11},{9,10},{10,... | collective-permute-start | bytes 12296 | tf_op jit(solution)/shard_map/ppermute | solution.py:647

commit v23 on v22

--- a/solution.py
+++ b/solution.py
@@ -509,6 +509,23 @@
     )(*states, speed)
 
 
+def along_one_field(field, get, speeds, pressures, half_speed, span, parts):
+    sign = sign_of_x()
+    fluxes, scaled = {}, {}
+    for place in span:
+        if field == 0:
+            flux = (0.5 * sign) * get(1, place)
+        elif field == 4:
+            flux = (get(4, place) + pressures[place]) * speeds[place]
+        else:
+            flux = get(field, place) * speeds[place]
+            if field == 1:
+                flux = flux + (0.5 * sign) * pressures[place]
+        fluxes[place] = flux
+        scaled[place] = half_speed * get(field, place)
+    return x_divergence(fluxes, scaled, *parts)
+
+
 def across(get, half_speed, span, parts):
     sign = sign_of_x()
     speeds, pressures = {}, {}
@@ -517,19 +534,7 @@
         speeds[place] = sign * vel[0]
         pressures[place] = pressure
     for field in range(FIELDS):
-        fluxes, scaled = {}, {}
-        for place in span:
-            if field == 0:
-                flux = (0.5 * sign) * get(1, place)
-            elif field == 4:
-                flux = (get(4, place) + pressures[place]) * speeds[place]
-            else:
-                flux = get(field, place) * speeds[place]
-                if field == 1:
-                    flux = flux + (0.5 * sign) * pressures[place]
-            fluxes[place] = flux
-            scaled[place] = half_speed * get(field, place)
-        yield field, x_divergence(fluxes, scaled, *parts)
+        yield field, along_one_field(field, get, speeds, pressures, half_speed, span, parts)
 
 
 WITH_HALOS = range(-3, BLOCK + 3)
@@ -597,37 +602,79 @@
     )(*operands)
 
 
-def second_kernel(state, middle_far, middle_near, sides, far, near, first_speed, speed, out):
+def second_kernel(
+    state, middle_far, middle_near, sides, far, near, first_speed, speed,
+    out_hbm, out, speeds, pressures, sems,
+):
     half_speed = 0.5 * speed[0:1, :]
     factor = (courant / 12.0) / first_speed[0:1, :]
     planes = [place_of(place) for place in range(BLOCK)]
-
-    def group(j, carry):
+    sign = sign_of_x()
+
+    def rows_and_get(j):
         rows = pl.ds(pl.multiple_of(j * 8, 8), 8)
-        spread = pl.ds(j, 8, stride=4)
 
         def inside(f, place):
             return (middle_far, middle_near)[place // 4][f, place % 4, rows, :]
 
-        get = with_halos(far, near, inside, rows)
-        for field, along_x in across(get, half_speed, WITH_HALOS, EVERY):
-            for place in range(BLOCK):
-                total = along_x[place] + sides[field, place, rows, :]
-                value = 0.5 * state[field, place, rows, :] + (
-                    0.5 * get(field, place) - factor * total
-                )
-                out[field, planes[place], spread, :] = value
+        return rows, with_halos(far, near, inside, rows)
+
+    def primitives(j, carry):
+        rows, get = rows_and_get(j)
+        for place in WITH_HALOS:
+            vel, pressure = half_velocities([get(f, place) for f in range(FIELDS)])
+            speeds[place + 3, rows, :] = sign * vel[0]
+            pressures[place + 3, rows, :] = pressure
         return carry
 
-    lax.fori_loop(0, 4, group, 0)
+    lax.fori_loop(0, 4, primitives, 0)
+
+    def one_field(field, j):
+        rows, get = rows_and_get(j)
+        along_x = along_one_field(
+            field,
+            get,
+            {place: speeds[place + 3, rows, :] for place in WITH_HALOS},
+            {place: pressures[place + 3, rows, :] for place in WITH_HALOS},
+            half_speed,
+            WITH_HALOS,
+            EVERY,
+        )
+        for place in range(BLOCK):
+            total = along_x[place] + sides[field, place, rows, :]
+            value = 0.5 * state[field, place, rows, :] + (
+                0.5 * get(field, place) - factor * total
+            )
+            out[field, planes[place], pl.ds(j, 8, stride=4), :] = value
+
+    copies = []
+    for field in range(FIELDS):
+
+        def group(j, carry, field=field):
+            one_field(field, j)
+            return carry
+
+        lax.fori_loop(0, 4, group, 0)
+        copies.append(pltpu.make_async_copy(out.at[field], out_hbm.at[field], sems.at[field]))
+        copies[-1].start()
+    for copy in copies:
+        copy.wait()
 
 
 def second_stage(*operands):
+    whole = (FIELDS, BLOCK, ROWS, LANES)
+    kept = pltpu.VMEM((BLOCK + 6, ROWS, LANES), jnp.float32)
     return pl.pallas_call(
         second_kernel,
-        out_shape=jax.ShapeDtypeStruct((FIELDS, BLOCK, ROWS, LANES), jnp.float32),
+        out_shape=jax.ShapeDtypeStruct(whole, jnp.float32),
         in_specs=[VMEM] * len(operands),
-        out_specs=VMEM,
+        out_specs=pl.BlockSpec(memory_space=pltpu.HBM),
+        scratch_shapes=[
+            pltpu.VMEM(whole, jnp.float32),
+            kept,
+            kept,
+            pltpu.SemaphoreType.DMA((FIELDS,)),
+        ],
         compiler_params=params(),
         cost_estimate=cost(30_000_000, 3_000_000),
         name="second_stage",
@@ -640,7 +687,7 @@
         reach *= 4
     while reach:
         copies = [value]
-        for times in range(3, 0, -1):
+        for times in range(1, 4):
             turn = reach * times
             if turn < size:
                 pairs = [(i, i ^ turn) for i in range(size)]

time: 73 us -> 71.6 us (0.981)
  waiting for transfers between devices: 30.5 us -> 28.6 us
    ppermute x6, waiting for transfers between devices: 3.68 us -> 1.77 us  [everyone_max(): copies.append(lax.ppermute(value, axis, pairs))]
where the time goes in v23:
time: 71.6 us; the launch traced here: 71.3 us
  waiting for transfers between devices  28.6 us (40%)
  starting transfers between devices  22.2 us (31%)
  Pallas kernels  19.6 us (27%)
    all_to_all x1, waiting for transfers between devices, per_device(): come = lax.all_to_all(parts, 'gx', split_axis=0, concat_axis=0, tiled=True)  26.8 us
    pallas_call x2, Pallas kernels, along_planes(): pl.pallas_call(functools.partial(plane_kernel, with_inner), out_shape=jax...  9.11 us
    ppermute x2, starting transfers between devices, from_far(): return lax.ppermute(far_side, 'gx', pairs)  7.44 us
    all_to_all x1, starting transfers between devices, per_device(): come = lax.all_to_all(parts, 'gx', split_axis=0, concat_axis=0, tiled=True)  7.37 us
    ppermute x6, starting transfers between devices, everyone_max(): copies.append(lax.ppermute(value, axis, pairs))  6.53 us
    pallas_call x1, Pallas kernels, second_stage(): pl.pallas_call(second_kernel, out_shape=jax.ShapeDtypeStruct(whole, jnp.f...  3.4 us
    pallas_call x1, Pallas kernels, pack(): pl.pallas_call(functools.partial(pack_kernel, size, cap, per_dev), out_sh...  2.7 us
    pallas_call x1, Pallas kernels, unpack(): pl.pallas_call(functools.partial(unpack_kernel, size, cap), out_shape=(ja...  2.52 us
  transfers between devices with their start and end apart: 11, of which 4 were waited for; matrix products, arithmetic and copies ran while one was open for 1% of the time, Pallas kernels for 14%

profile of v23, /device:TPU:0, one launch (start us, length us, event | category | flops | bytes accessed | tf_op | source)
XLA Modules:
  0.0 71.3 jit_solution(2327003326532894557)
XLA Ops:
  0.0 2.7 %pack.1 = f32[16,161,1,128]{3,2,1,0:T(1,128)} custom-call(s32[1024]{0:T(1024)} %owner_hbm.1, f32[1280,1,128]{2,1,0:T(1,128)} %bitcast.7), custom_call_target="tpu_custom_call" | custom-call | flops 1000000 | bytes 3000000 | tf_op jit(solution)/shard_map/pack/pallas_call | solution.py:113
  2.7 7.4 %all-to-all-start = ((f32[16,161,1,128]{3,2,1,0:T(1,128)}), f32[16,161,1,128]{3,2,1,0:T(1,128)S(1)}, u32[]{:S(2)}, u32[]{:S(2)}) async-start(f32[16,161,1,128]{3,2,1,0:T(1,128)} %pack.1), calls=%async_computation | async-start | bytes 2637824 | tf_op jit(solution)/shard_map/all_to_all | solution.py:708
  10.1 0.1 eq.33
  10.2 0.3 convert_reduce_fusion
  10.6 0.1 broadcast_add_fusion
  10.7 0.1 add.17
  10.7 0.1 select_reduce_fusion.table
  10.9 26.8 %all-to-all-done = f32[16,161,1,128]{3,2,1,0:T(1,128)S(1)} async-done(((f32[16,161,1,128]{3,2,1,0:T(1,128)}), f32[16,161,1,128]{3,2,1,0:T(1,128)S(1)}, u32[]{:S(2)}, u32[]{:S(2)}) %all-to-all-start) | async-done | bytes 1318944 | tf_op jit(solution)/shard_map/all_to_all | solution.py:708
  37.7 2.5 %unpack.1 = (f32[5,8,32,128]{3,2,1,0:T(8,128)S(1)}, f32[5,3,32,128]{3,2,1,0:T(8,128)S(1)}, f32[5,3,32,128]{3,2,1,0:T(8,128)S(1)}, f32[8,128]{1,0:T(8,128)S(1)}) custom-call(s32[64]{0:T(128)S(1)} %select_reduce_fusion.table, f32[2576,1,128]{2,1,0:T(1,128)S(1)} %bitcast.6), custom_call_target="tpu_custom_call" | custom-call | flops 5000000 | bytes 2000000 | tf_op jit(solution)/shard_map/unpack/pallas_call | solution.py:237
  40.2 0.8 %collective-permute-start.1 = (f32[5,3,32,128]{3,2,1,0:T(8,128)S(1)}, f32[5,3,32,128]{3,2,1,0:T(8,128)S(1)}, u32[]{:S(2)}, u32[]{:S(2)}) collective-permute-start(f32[5,3,32,128]{3,2,1,0:T(8,128)S(1)} %get-tuple-element.24), channel_id=1, source_target_pairs={{0,1},{1,0},{2,3},{3,2},{4,5},{5,4},{6,7},{7,6},{8,9},{9,8},{10,11... | collective-permute-start | bytes 737288 | tf_op jit(solution)/shard_map/ppermute | solution.py:152
  41.0 6.0 %collective-permute-start = (f32[5,3,32,128]{3,2,1,0:T(8,128)S(1)}, f32[5,3,32,128]{3,2,1,0:T(8,128)S(1)}, u32[]{:S(2)}, u32[]{:S(2)}) collective-permute-start(f32[5,3,32,128]{3,2,1,0:T(8,128)S(1)} %get-tuple-element.23), channel_id=1, source_target_pairs={{0,15},{1,2},{2,1},{3,4},{4,3},{5,6},{6,5},{7,8},{8,7},{9,10},{10,... | collective-permute-start | bytes 737288 | tf_op jit(solution)/shard_map/ppermute | solution.py:148
  47.0 5.1 %planes.2.refs_1_ = f32[5,8,32,128]{3,2,1,0:T(8,128)S(1)} custom-call(f32[5,8,32,128]{3,2,1,0:T(8,128)S(1)} %get-tuple-element.21.refs_0_.state, f32[8,128]{1,0:T(8,128)S(1)} %get-tuple-element.22.refs_1_.refs_3_.first_speed), custom_call_target="tpu_custom_call" | custom-call | flops 20000000 | bytes 1000000 | tf_op jit(solution)/shard_map/planes/pallas_call | solution.py:500
  52.2 0.9 %first_near.1 = (f32[5,4,32,128]{3,2,1,0:T(8,128)S(1)}, f32[5,3,32,128]{3,2,1,0:T(8,128)S(1)}, f32[8,128]{1,0:T(8,128)S(1)}) custom-call(f32[5,8,32,128]{3,2,1,0:T(8,128)S(1)} %get-tuple-element.21.refs_0_.state, f32[5,8,32,128]{3,2,1,0:T(8,128)S(1)} %planes.2.refs_1_, f32[5,3,32,128]{3,2,1,0:T(8,128)S(1)} %collective-permute-done.1.refs_2_, ...), custom_call_target="tpu_custom_call" | custom-call | flops 15000000 | bytes 2000000 | tf_op jit(solution)/shard_map/first_near/pallas_call | solution.py:590
  53.1 1.0 %first_far.1 = (f32[5,4,32,128]{3,2,1,0:T(8,128)S(1)}, f32[5,3,32,128]{3,2,1,0:T(8,128)S(1)}, f32[8,128]{1,0:T(8,128)S(1)}) custom-call(f32[5,8,32,128]{3,2,1,0:T(8,128)S(1)} %get-tuple-element.21.refs_0_.state, f32[5,8,32,128]{3,2,1,0:T(8,128)S(1)} %planes.2.refs_1_, f32[5,3,32,128]{3,2,1,0:T(8,128)S(1)} %collective-permute-done.refs_2_, ...), custom_call_target="tpu_custom_call" | custom-call | flops 15000000 | bytes 2000000 | tf_op jit(solution)/shard_map/first_far/pallas_call | solution.py:590
  54.1 0.3 collective-permute-start.4
  54.4 0.5 collective-permute-start.3
  54.9 3.6 %collective-permute-start.2 = (f32[8,128]{1,0:T(8,128)S(1)}, f32[8,128]{1,0:T(8,128)S(1)}, u32[]{:S(2)}, u32[]{:S(2)}) collective-permute-start(f32[8,128]{1,0:T(8,128)S(1)} %get-tuple-element.28), channel_id=1, source_target_pairs={{0,4},{1,5},{2,6},{3,7},{4,0},{5,1},{6,2},{7,3},{8,12},{9,13},{10,... | collective-permute-start | bytes 12296 | tf_op jit(solution)/shard_map/ppermute | solution.py:694
  58.5 1.4 %collective-permute-start.8 = (f32[5,3,32,128]{3,2,1,0:T(8,128)S(1)}, f32[5,3,32,128]{3,2,1,0:T(8,128)S(1)}, u32[]{:S(2)}, u32[]{:S(2)}) collective-permute-start(f32[5,3,32,128]{3,2,1,0:T(8,128)S(1)} %get-tuple-element.29), channel_id=1, source_target_pairs={{0,15},{1,2},{2,1},{3,4},{4,3},{5,6},{6,5},{7,8},{8,7},{9,10},{10,... | collective-permute-start | bytes 737288 | tf_op jit(solution)/shard_map/ppermute | solution.py:148
  60.0 0.1 collective-permute-done.2
  60.2 2.1 %collective-permute-start.6 = (f32[8,128]{1,0:T(8,128)S(1)}, f32[8,128]{1,0:T(8,128)S(1)}, u32[]{:S(2)}, u32[]{:S(2)}) collective-permute-start(f32[8,128]{1,0:T(8,128)S(1)} %maximum_maximum_fusion.1), channel_id=1, source_target_pairs={{0,2},{1,3},{2,0},{3,1},{4,6},{5,7},{6,4},{7,5},{8,10},{9,11},{10,... | collective-permute-start | bytes 12296 | tf_op jit(solution)/shard_map/ppermute | solution.py:694
  62.2 1.0 %collective-permute-done.7 = f32[8,128]{1,0:T(8,128)S(1)} collective-permute-done((f32[8,128]{1,0:T(8,128)S(1)}, f32[8,128]{1,0:T(8,128)S(1)}, u32[]{:S(2)}, u32[]{:S(2)}) %collective-permute-start.7) | collective-permute-done | bytes 4128 | tf_op jit(solution)/shard_map/ppermute | solution.py:694
  63.2 0.7 collective-permute-done.6
  63.9 4.0 %planes.3.sides = f32[5,8,32,128]{3,2,1,0:T(8,128)S(1)} custom-call(f32[5,4,32,128]{3,2,1,0:T(8,128)S(1)} %get-tuple-element.26.refs_0_.middle_far, f32[5,4,32,128]{3,2,1,0:T(8,128)S(1)} %get-tuple-element.27.refs_1_.middle_near, f32[8,128]{1,0:T(8,128)S(1)} %maximum_maximum_fusion.refs_2_.speed), custom_call_target="tpu_custom_call" | custom-call | flops 20000000 | bytes 1000000 | tf_op jit(solution)/shard_map/planes/pallas_call | solution.py:500
  67.9 3.4 %second_stage.1 = f32[5,8,32,128]{3,2,1,0:T(8,128)} custom-call(f32[5,8,32,128]{3,2,1,0:T(8,128)S(1)} %get-tuple-element.21.refs_0_.state, f32[5,4,32,128]{3,2,1,0:T(8,128)S(1)} %get-tuple-element.26.refs_0_.middle_far, f32[5,4,32,128]{3,2,1,0:T(8,128)S(1)} %get-tuple-element.27.refs_1_.middle_near, f32[5,8,32,128]{3,2,1,0:T(8,128)S(1)} %planes.3.sides, ...), custom_call_target="tpu_custom_call" | custom-call | flops 30000000 | bytes 3000000 | tf_op jit(solution)/shard_map/second_stage/pallas_call | solution.py:667
  (19 shorter events, 0.1 us)
Async XLA Ops:
  2.7 7.4 %copy-start = (s32[1024]{0:T(1024)S(1)}, s32[1024]{0:T(1024)}, u32[]{:S(2)}) copy-start(s32[1024]{0:T(1024)} %owner_hbm.1) | copy-start | bytes 12292
  2.7 7.4 %copy-start.1 = (s32[1024]{0:T(1024)S(1)}, s32[1024]{0:T(1024)}, u32[]{:S(2)}) copy-start(s32[1024]{0:T(1024)} %param.5) | copy-start | bytes 12292
  2.7 34.9 %all-to-all-start = ((f32[16,161,1,128]{3,2,1,0:T(1,128)}), f32[16,161,1,128]{3,2,1,0:T(1,128)S(1)}, u32[]{:S(2)}, u32[]{:S(2)}) async-start(f32[16,161,1,128]{3,2,1,0:T(1,128)} %pack.1), calls=%async_computation | async-start | bytes 2637824 | tf_op jit(solution)/shard_map/all_to_all | solution.py:708
  40.2 12.0 %collective-permute-start.1 = (f32[5,3,32,128]{3,2,1,0:T(8,128)S(1)}, f32[5,3,32,128]{3,2,1,0:T(8,128)S(1)}, u32[]{:S(2)}, u32[]{:S(2)}) collective-permute-start(f32[5,3,32,128]{3,2,1,0:T(8,128)S(1)} %get-tuple-element.24), channel_id=1, source_target_pairs={{0,1},{1,0},{2,3},{3,2},{4,5},{5,4},{6,7},{7,6},{8,9},{9,8},{10,11... | collective-permute-start | bytes 737288 | tf_op jit(solution)/shard_map/ppermute | solution.py:152
  41.0 12.0 %collective-permute-start = (f32[5,3,32,128]{3,2,1,0:T(8,128)S(1)}, f32[5,3,32,128]{3,2,1,0:T(8,128)S(1)}, u32[]{:S(2)}, u32[]{:S(2)}) collective-permute-start(f32[5,3,32,128]{3,2,1,0:T(8,128)S(1)} %get-tuple-element.23), channel_id=1, source_target_pairs={{0,15},{1,2},{2,1},{3,4},{4,3},{5,6},{6,5},{7,8},{8,7},{9,10},{10,... | collective-permute-start | bytes 737288 | tf_op jit(solution)/shard_map/ppermute | solution.py:148
  54.1 5.9 %collective-permute-start.4 = (f32[8,128]{1,0:T(8,128)S(1)}, f32[8,128]{1,0:T(8,128)S(1)}, u32[]{:S(2)}, u32[]{:S(2)}) collective-permute-start(f32[8,128]{1,0:T(8,128)S(1)} %get-tuple-element.28), channel_id=1, source_target_pairs={{0,12},{1,13},{2,14},{3,15},{4,8},{5,9},{6,10},{7,11},{8,4},{9,5},... | collective-permute-start | bytes 12296 | tf_op jit(solution)/shard_map/ppermute | solution.py:694
  54.4 5.6 %collective-permute-start.3 = (f32[8,128]{1,0:T(8,128)S(1)}, f32[8,128]{1,0:T(8,128)S(1)}, u32[]{:S(2)}, u32[]{:S(2)}) collective-permute-start(f32[8,128]{1,0:T(8,128)S(1)} %get-tuple-element.28), channel_id=1, source_target_pairs={{0,8},{1,9},{2,10},{3,11},{4,12},{5,13},{6,14},{7,15},{8,0},{9,1},... | collective-permute-start | bytes 12296 | tf_op jit(solution)/shard_map/ppermute | solution.py:694
  54.9 5.2 %collective-permute-start.2 = (f32[8,128]{1,0:T(8,128)S(1)}, f32[8,128]{1,0:T(8,128)S(1)}, u32[]{:S(2)}, u32[]{:S(2)}) collective-permute-start(f32[8,128]{1,0:T(8,128)S(1)} %get-tuple-element.28), channel_id=1, source_target_pairs={{0,4},{1,5},{2,6},{3,7},{4,0},{5,1},{6,2},{7,3},{8,12},{9,13},{10,... | collective-permute-start | bytes 12296 | tf_op jit(solution)/shard_map/ppermute | solution.py:694
  58.5 9.3 %collective-permute-start.8 = (f32[5,3,32,128]{3,2,1,0:T(8,128)S(1)}, f32[5,3,32,128]{3,2,1,0:T(8,128)S(1)}, u32[]{:S(2)}, u32[]{:S(2)}) collective-permute-start(f32[5,3,32,128]{3,2,1,0:T(8,128)S(1)} %get-tuple-element.29), channel_id=1, source_target_pairs={{0,15},{1,2},{2,1},{3,4},{4,3},{5,6},{6,5},{7,8},{8,7},{9,10},{10,... | collective-permute-start | bytes 737288 | tf_op jit(solution)/shard_map/ppermute | solution.py:148
  60.0 7.9 %collective-permute-start.9 = (f32[5,3,32,128]{3,2,1,0:T(8,128)S(1)}, f32[5,3,32,128]{3,2,1,0:T(8,128)S(1)}, u32[]{:S(2)}, u32[]{:S(2)}) collective-permute-start(f32[5,3,32,128]{3,2,1,0:T(8,128)S(1)} %get-tuple-element.30), channel_id=1, source_target_pairs={{0,1},{1,0},{2,3},{3,2},{4,5},{5,4},{6,7},{7,6},{8,9},{9,8},{10,11... | collective-permute-start | bytes 737288 | tf_op jit(solution)/shard_map/ppermute | solution.py:152
  60.1 3.0 %collective-permute-start.7 = (f32[8,128]{1,0:T(8,128)S(1)}, f32[8,128]{1,0:T(8,128)S(1)}, u32[]{:S(2)}, u32[]{:S(2)}) collective-permute-start(f32[8,128]{1,0:T(8,128)S(1)} %maximum_maximum_fusion.1), channel_id=1, source_target_pairs={{0,3},{1,2},{2,1},{3,0},{4,7},{5,6},{6,5},{7,4},{8,11},{9,10},{10,... | collective-permute-start | bytes 12296 | tf_op jit(solution)/shard_map/ppermute | solution.py:694
  60.2 3.7 %collective-permute-start.6 = (f32[8,128]{1,0:T(8,128)S(1)}, f32[8,128]{1,0:T(8,128)S(1)}, u32[]{:S(2)}, u32[]{:S(2)}) collective-permute-start(f32[8,128]{1,0:T(8,128)S(1)} %maximum_maximum_fusion.1), channel_id=1, source_target_pairs={{0,2},{1,3},{2,0},{3,1},{4,6},{5,7},{6,4},{7,5},{8,10},{9,11},{10,... | collective-permute-start | bytes 12296 | tf_op jit(solution)/shard_map/ppermute | solution.py:694
  62.2 1.6 %collective-permute-start.5 = (f32[8,128]{1,0:T(8,128)S(1)}, f32[8,128]{1,0:T(8,128)S(1)}, u32[]{:S(2)}, u32[]{:S(2)}) collective-permute-start(f32[8,128]{1,0:T(8,128)S(1)} %maximum_maximum_fusion.1), channel_id=1, source_target_pairs={{0,1},{1,0},{2,3},{3,2},{4,5},{5,4},{6,7},{7,6},{8,9},{9,8},{10,11... | collective-permute-start | bytes 12296 | tf_op jit(solution)/shard_map/ppermute | solution.py:694

commit v24 on v22

--- a/solution.py
+++ b/solution.py
@@ -640,9 +640,10 @@
         reach *= 4
     while reach:
         copies = [value]
-        for times in range(3, 0, -1):
+        for times in range(1, 4):
             turn = reach * times
             if turn < size:
+                turn += 2 if times == 1 and reach > 1 else 0
                 pairs = [(i, i ^ turn) for i in range(size)]
                 copies.append(lax.ppermute(value, axis, pairs))
         value = functools.reduce(jnp.maximum, copies)

time: 73 us -> 74.5 us (1.021)
  waiting for transfers between devices: 30.5 us -> 31.4 us
    ppermute x6, starting transfers between devices: 6.31 us -> 4.68 us  [everyone_max(): copies.append(lax.ppermute(value, axis, pairs))]
    ppermute x2, starting transfers between devices: 7.44 us -> 8.64 us  [from_far(): return lax.ppermute(far_side, 'gx', pairs)]
    ppermute x2, starting transfers between devices: 0.84 us -> 1.81 us  [from_near(): return lax.ppermute(near_side, 'gx', [(i, i ^ 1) for i in range(size)])]
    ppermute x6, waiting for transfers between devices: 3.68 us -> 4.59 us  [everyone_max(): copies.append(lax.ppermute(value, axis, pairs))]
  transfers between devices with their start and end apart: 11 -> 11, of which waited for: 4 -> 3; matrix products, arithmetic and copies ran while one was open for 1% -> 1% of each run, Pallas kernels for 14% -> 13%
where the time goes in v24:
time: 74.5 us; the launch traced here: 74.3 us
  waiting for transfers between devices  31.4 us (42%)
  starting transfers between devices  22.5 us (30%)
  Pallas kernels  19.5 us (26%)
    all_to_all x1, waiting for transfers between devices, per_device(): come = lax.all_to_all(parts, 'gx', split_axis=0, concat_axis=0, tiled=True)  26.8 us
    pallas_call x2, Pallas kernels, along_planes(): pl.pallas_call(functools.partial(plane_kernel, with_inner), out_shape=jax...  9.11 us
    ppermute x2, starting transfers between devices, from_far(): return lax.ppermute(far_side, 'gx', pairs)  8.64 us
    all_to_all x1, starting transfers between devices, per_device(): come = lax.all_to_all(parts, 'gx', split_axis=0, concat_axis=0, tiled=True)  7.37 us
    ppermute x6, starting transfers between devices, everyone_max(): copies.append(lax.ppermute(value, axis, pairs))  4.68 us
    ppermute x6, waiting for transfers between devices, everyone_max(): copies.append(lax.ppermute(value, axis, pairs))  4.59 us
    pallas_call x1, Pallas kernels, second_stage(): pl.pallas_call(second_kernel, out_shape=jax.ShapeDtypeStruct((FIELDS, BLO...  3.27 us
    pallas_call x1, Pallas kernels, pack(): pl.pallas_call(functools.partial(pack_kernel, size, cap, per_dev), out_sh...  2.7 us
  transfers between devices with their start and end apart: 11, of which 3 were waited for; matrix products, arithmetic and copies ran while one was open for 1% of the time, Pallas kernels for 13%

profile of v24, /device:TPU:0, one launch (start us, length us, event | category | flops | bytes accessed | tf_op | source)
XLA Modules:
  0.0 74.3 jit_solution(4742192514340870000)
XLA Ops:
  0.0 2.7 %pack.1 = f32[16,161,1,128]{3,2,1,0:T(1,128)} custom-call(s32[1024]{0:T(1024)} %owner_hbm.1, f32[1280,1,128]{2,1,0:T(1,128)} %bitcast.7), custom_call_target="tpu_custom_call" | custom-call | flops 1000000 | bytes 3000000 | tf_op jit(solution)/shard_map/pack/pallas_call | solution.py:113
  2.7 7.4 %all-to-all-start = ((f32[16,161,1,128]{3,2,1,0:T(1,128)}), f32[16,161,1,128]{3,2,1,0:T(1,128)S(1)}, u32[]{:S(2)}, u32[]{:S(2)}) async-start(f32[16,161,1,128]{3,2,1,0:T(1,128)} %pack.1), calls=%async_computation | async-start | bytes 2637824 | tf_op jit(solution)/shard_map/all_to_all | solution.py:662
  10.1 0.1 eq.33
  10.2 0.3 convert_reduce_fusion
  10.7 0.1 add.17
  10.7 0.1 select_reduce_fusion.table
  10.9 26.8 %all-to-all-done = f32[16,161,1,128]{3,2,1,0:T(1,128)S(1)} async-done(((f32[16,161,1,128]{3,2,1,0:T(1,128)}), f32[16,161,1,128]{3,2,1,0:T(1,128)S(1)}, u32[]{:S(2)}, u32[]{:S(2)}) %all-to-all-start) | async-done | bytes 1318944 | tf_op jit(solution)/shard_map/all_to_all | solution.py:662
  37.7 2.5 %unpack.1 = (f32[5,8,32,128]{3,2,1,0:T(8,128)S(1)}, f32[5,3,32,128]{3,2,1,0:T(8,128)S(1)}, f32[5,3,32,128]{3,2,1,0:T(8,128)S(1)}, f32[8,128]{1,0:T(8,128)S(1)}) custom-call(s32[64]{0:T(128)S(1)} %select_reduce_fusion.table, f32[2576,1,128]{2,1,0:T(1,128)S(1)} %bitcast.6), custom_call_target="tpu_custom_call" | custom-call | flops 5000000 | bytes 2000000 | tf_op jit(solution)/shard_map/unpack/pallas_call | solution.py:237
  40.2 0.8 %collective-permute-start.1 = (f32[5,3,32,128]{3,2,1,0:T(8,128)S(1)}, f32[5,3,32,128]{3,2,1,0:T(8,128)S(1)}, u32[]{:S(2)}, u32[]{:S(2)}) collective-permute-start(f32[5,3,32,128]{3,2,1,0:T(8,128)S(1)} %get-tuple-element.24), channel_id=1, source_target_pairs={{0,1},{1,0},{2,3},{3,2},{4,5},{5,4},{6,7},{7,6},{8,9},{9,8},{10,11... | collective-permute-start | bytes 737288 | tf_op jit(solution)/shard_map/ppermute | solution.py:152
  41.0 6.0 %collective-permute-start = (f32[5,3,32,128]{3,2,1,0:T(8,128)S(1)}, f32[5,3,32,128]{3,2,1,0:T(8,128)S(1)}, u32[]{:S(2)}, u32[]{:S(2)}) collective-permute-start(f32[5,3,32,128]{3,2,1,0:T(8,128)S(1)} %get-tuple-element.23), channel_id=1, source_target_pairs={{0,15},{1,2},{2,1},{3,4},{4,3},{5,6},{6,5},{7,8},{8,7},{9,10},{10,... | collective-permute-start | bytes 737288 | tf_op jit(solution)/shard_map/ppermute | solution.py:148
  47.0 5.1 %planes.2.refs_1_ = f32[5,8,32,128]{3,2,1,0:T(8,128)S(1)} custom-call(f32[5,8,32,128]{3,2,1,0:T(8,128)S(1)} %get-tuple-element.21.refs_0_.state, f32[8,128]{1,0:T(8,128)S(1)} %get-tuple-element.22.refs_1_.refs_3_.first_speed), custom_call_target="tpu_custom_call" | custom-call | flops 20000000 | bytes 1000000 | tf_op jit(solution)/shard_map/planes/pallas_call | solution.py:500
  52.2 0.9 %first_near.1 = (f32[5,4,32,128]{3,2,1,0:T(8,128)S(1)}, f32[5,3,32,128]{3,2,1,0:T(8,128)S(1)}, f32[8,128]{1,0:T(8,128)S(1)}) custom-call(f32[5,8,32,128]{3,2,1,0:T(8,128)S(1)} %get-tuple-element.21.refs_0_.state, f32[5,8,32,128]{3,2,1,0:T(8,128)S(1)} %planes.2.refs_1_, f32[5,3,32,128]{3,2,1,0:T(8,128)S(1)} %collective-permute-done.1.refs_2_, ...), custom_call_target="tpu_custom_call" | custom-call | flops 15000000 | bytes 2000000 | tf_op jit(solution)/shard_map/first_near/pallas_call | solution.py:585
  53.1 1.0 %first_far.1 = (f32[5,4,32,128]{3,2,1,0:T(8,128)S(1)}, f32[5,3,32,128]{3,2,1,0:T(8,128)S(1)}, f32[8,128]{1,0:T(8,128)S(1)}) custom-call(f32[5,8,32,128]{3,2,1,0:T(8,128)S(1)} %get-tuple-element.21.refs_0_.state, f32[5,8,32,128]{3,2,1,0:T(8,128)S(1)} %planes.2.refs_1_, f32[5,3,32,128]{3,2,1,0:T(8,128)S(1)} %collective-permute-done.refs_2_, ...), custom_call_target="tpu_custom_call" | custom-call | flops 15000000 | bytes 2000000 | tf_op jit(solution)/shard_map/first_far/pallas_call | solution.py:585
  54.1 0.3 collective-permute-start.4
  54.4 0.5 collective-permute-start.3
  54.9 1.6 %collective-permute-start.2 = (f32[8,128]{1,0:T(8,128)S(1)}, f32[8,128]{1,0:T(8,128)S(1)}, u32[]{:S(2)}, u32[]{:S(2)}) collective-permute-start(f32[8,128]{1,0:T(8,128)S(1)} %get-tuple-element.28), channel_id=1, source_target_pairs={{0,6},{1,7},{2,4},{3,5},{4,2},{5,3},{6,0},{7,1},{8,14},{9,15},{10,... | collective-permute-start | bytes 12296 | tf_op jit(solution)/shard_map/ppermute | solution.py:648
  56.5 2.6 %collective-permute-start.8 = (f32[5,3,32,128]{3,2,1,0:T(8,128)S(1)}, f32[5,3,32,128]{3,2,1,0:T(8,128)S(1)}, u32[]{:S(2)}, u32[]{:S(2)}) collective-permute-start(f32[5,3,32,128]{3,2,1,0:T(8,128)S(1)} %get-tuple-element.29), channel_id=1, source_target_pairs={{0,15},{1,2},{2,1},{3,4},{4,3},{5,6},{6,5},{7,8},{8,7},{9,10},{10,... | collective-permute-start | bytes 737288 | tf_op jit(solution)/shard_map/ppermute | solution.py:148
  59.1 1.0 %collective-permute-start.9 = (f32[5,3,32,128]{3,2,1,0:T(8,128)S(1)}, f32[5,3,32,128]{3,2,1,0:T(8,128)S(1)}, u32[]{:S(2)}, u32[]{:S(2)}) collective-permute-start(f32[5,3,32,128]{3,2,1,0:T(8,128)S(1)} %get-tuple-element.30), channel_id=1, source_target_pairs={{0,1},{1,0},{2,3},{3,2},{4,5},{5,4},{6,7},{7,6},{8,9},{9,8},{10,11... | collective-permute-start | bytes 737288 | tf_op jit(solution)/shard_map/ppermute | solution.py:152
  60.2 0.4 collective-permute-start.7
  60.5 1.8 %collective-permute-start.6 = (f32[8,128]{1,0:T(8,128)S(1)}, f32[8,128]{1,0:T(8,128)S(1)}, u32[]{:S(2)}, u32[]{:S(2)}) collective-permute-start(f32[8,128]{1,0:T(8,128)S(1)} %maximum_maximum_fusion.1), channel_id=1, source_target_pairs={{0,2},{1,3},{2,0},{3,1},{4,6},{5,7},{6,4},{7,5},{8,10},{9,11},{10,... | collective-permute-start | bytes 12296 | tf_op jit(solution)/shard_map/ppermute | solution.py:648
  62.4 2.7 %collective-permute-done.7 = f32[8,128]{1,0:T(8,128)S(1)} collective-permute-done((f32[8,128]{1,0:T(8,128)S(1)}, f32[8,128]{1,0:T(8,128)S(1)}, u32[]{:S(2)}, u32[]{:S(2)}) %collective-permute-start.7) | collective-permute-done | bytes 4128 | tf_op jit(solution)/shard_map/ppermute | solution.py:648
  65.1 1.9 %collective-permute-done.6 = f32[8,128]{1,0:T(8,128)S(1)} collective-permute-done((f32[8,128]{1,0:T(8,128)S(1)}, f32[8,128]{1,0:T(8,128)S(1)}, u32[]{:S(2)}, u32[]{:S(2)}) %collective-permute-start.6) | collective-permute-done | bytes 4128 | tf_op jit(solution)/shard_map/ppermute | solution.py:648
  67.0 4.0 %planes.3.sides = f32[5,8,32,128]{3,2,1,0:T(8,128)S(1)} custom-call(f32[5,4,32,128]{3,2,1,0:T(8,128)S(1)} %get-tuple-element.26.refs_0_.middle_far, f32[5,4,32,128]{3,2,1,0:T(8,128)S(1)} %get-tuple-element.27.refs_1_.middle_near, f32[8,128]{1,0:T(8,128)S(1)} %maximum_maximum_fusion.refs_2_.speed), custom_call_target="tpu_custom_call" | custom-call | flops 20000000 | bytes 1000000 | tf_op jit(solution)/shard_map/planes/pallas_call | solution.py:500
  71.0 3.3 %second_stage.1 = f32[5,8,32,128]{3,2,1,0:T(8,128)} custom-call(f32[5,8,32,128]{3,2,1,0:T(8,128)S(1)} %get-tuple-element.21.refs_0_.state, f32[5,4,32,128]{3,2,1,0:T(8,128)S(1)} %get-tuple-element.26.refs_0_.middle_far, f32[5,4,32,128]{3,2,1,0:T(8,128)S(1)} %get-tuple-element.27.refs_1_.middle_near, f32[5,8,32,128]{3,2,1,0:T(8,128)S(1)} %planes.3.sides, ...), custom_call_target="tpu_custom_call" | custom-call | flops 30000000 | bytes 3000000 | tf_op jit(solution)/shard_map/second_stage/pallas_call | solution.py:626
  (19 shorter events, 0.2 us)
Async XLA Ops:
  2.7 7.4 %copy-start = (s32[1024]{0:T(1024)S(1)}, s32[1024]{0:T(1024)}, u32[]{:S(2)}) copy-start(s32[1024]{0:T(1024)} %owner_hbm.1) | copy-start | bytes 12292
  2.7 7.4 %copy-start.1 = (s32[1024]{0:T(1024)S(1)}, s32[1024]{0:T(1024)}, u32[]{:S(2)}) copy-start(s32[1024]{0:T(1024)} %param.5) | copy-start | bytes 12292
  2.7 34.9 %all-to-all-start = ((f32[16,161,1,128]{3,2,1,0:T(1,128)}), f32[16,161,1,128]{3,2,1,0:T(1,128)S(1)}, u32[]{:S(2)}, u32[]{:S(2)}) async-start(f32[16,161,1,128]{3,2,1,0:T(1,128)} %pack.1), calls=%async_computation | async-start | bytes 2637824 | tf_op jit(solution)/shard_map/all_to_all | solution.py:662
  40.2 12.0 %collective-permute-start.1 = (f32[5,3,32,128]{3,2,1,0:T(8,128)S(1)}, f32[5,3,32,128]{3,2,1,0:T(8,128)S(1)}, u32[]{:S(2)}, u32[]{:S(2)}) collective-permute-start(f32[5,3,32,128]{3,2,1,0:T(8,128)S(1)} %get-tuple-element.24), channel_id=1, source_target_pairs={{0,1},{1,0},{2,3},{3,2},{4,5},{5,4},{6,7},{7,6},{8,9},{9,8},{10,11... | collective-permute-start | bytes 737288 | tf_op jit(solution)/shard_map/ppermute | solution.py:152
  41.0 12.0 %collective-permute-start = (f32[5,3,32,128]{3,2,1,0:T(8,128)S(1)}, f32[5,3,32,128]{3,2,1,0:T(8,128)S(1)}, u32[]{:S(2)}, u32[]{:S(2)}) collective-permute-start(f32[5,3,32,128]{3,2,1,0:T(8,128)S(1)} %get-tuple-element.23), channel_id=1, source_target_pairs={{0,15},{1,2},{2,1},{3,4},{4,3},{5,6},{6,5},{7,8},{8,7},{9,10},{10,... | collective-permute-start | bytes 737288 | tf_op jit(solution)/shard_map/ppermute | solution.py:148
  54.1 6.0 %collective-permute-start.4 = (f32[8,128]{1,0:T(8,128)S(1)}, f32[8,128]{1,0:T(8,128)S(1)}, u32[]{:S(2)}, u32[]{:S(2)}) collective-permute-start(f32[8,128]{1,0:T(8,128)S(1)} %get-tuple-element.28), channel_id=1, source_target_pairs={{0,12},{1,13},{2,14},{3,15},{4,8},{5,9},{6,10},{7,11},{8,4},{9,5},... | collective-permute-start | bytes 12296 | tf_op jit(solution)/shard_map/ppermute | solution.py:648
  54.4 5.8 %collective-permute-start.3 = (f32[8,128]{1,0:T(8,128)S(1)}, f32[8,128]{1,0:T(8,128)S(1)}, u32[]{:S(2)}, u32[]{:S(2)}) collective-permute-start(f32[8,128]{1,0:T(8,128)S(1)} %get-tuple-element.28), channel_id=1, source_target_pairs={{0,8},{1,9},{2,10},{3,11},{4,12},{5,13},{6,14},{7,15},{8,0},{9,1},... | collective-permute-start | bytes 12296 | tf_op jit(solution)/shard_map/ppermute | solution.py:648
  54.9 5.2 %collective-permute-start.2 = (f32[8,128]{1,0:T(8,128)S(1)}, f32[8,128]{1,0:T(8,128)S(1)}, u32[]{:S(2)}, u32[]{:S(2)}) collective-permute-start(f32[8,128]{1,0:T(8,128)S(1)} %get-tuple-element.28), channel_id=1, source_target_pairs={{0,6},{1,7},{2,4},{3,5},{4,2},{5,3},{6,0},{7,1},{8,14},{9,15},{10,... | collective-permute-start | bytes 12296 | tf_op jit(solution)/shard_map/ppermute | solution.py:648
  56.5 14.5 %collective-permute-start.8 = (f32[5,3,32,128]{3,2,1,0:T(8,128)S(1)}, f32[5,3,32,128]{3,2,1,0:T(8,128)S(1)}, u32[]{:S(2)}, u32[]{:S(2)}) collective-permute-start(f32[5,3,32,128]{3,2,1,0:T(8,128)S(1)} %get-tuple-element.29), channel_id=1, source_target_pairs={{0,15},{1,2},{2,1},{3,4},{4,3},{5,6},{6,5},{7,8},{8,7},{9,10},{10,... | collective-permute-start | bytes 737288 | tf_op jit(solution)/shard_map/ppermute | solution.py:148
  59.1 11.9 %collective-permute-start.9 = (f32[5,3,32,128]{3,2,1,0:T(8,128)S(1)}, f32[5,3,32,128]{3,2,1,0:T(8,128)S(1)}, u32[]{:S(2)}, u32[]{:S(2)}) collective-permute-start(f32[5,3,32,128]{3,2,1,0:T(8,128)S(1)} %get-tuple-element.30), channel_id=1, source_target_pairs={{0,1},{1,0},{2,3},{3,2},{4,5},{5,4},{6,7},{7,6},{8,9},{9,8},{10,11... | collective-permute-start | bytes 737288 | tf_op jit(solution)/shard_map/ppermute | solution.py:152
  60.2 4.9 %collective-permute-start.7 = (f32[8,128]{1,0:T(8,128)S(1)}, f32[8,128]{1,0:T(8,128)S(1)}, u32[]{:S(2)}, u32[]{:S(2)}) collective-permute-start(f32[8,128]{1,0:T(8,128)S(1)} %maximum_maximum_fusion.1), channel_id=1, source_target_pairs={{0,3},{1,2},{2,1},{3,0},{4,7},{5,6},{6,5},{7,4},{8,11},{9,10},{10,... | collective-permute-start | bytes 12296 | tf_op jit(solution)/shard_map/ppermute | solution.py:648
  60.5 6.5 %collective-permute-start.6 = (f32[8,128]{1,0:T(8,128)S(1)}, f32[8,128]{1,0:T(8,128)S(1)}, u32[]{:S(2)}, u32[]{:S(2)}) collective-permute-start(f32[8,128]{1,0:T(8,128)S(1)} %maximum_maximum_fusion.1), channel_id=1, source_target_pairs={{0,2},{1,3},{2,0},{3,1},{4,6},{5,7},{6,4},{7,5},{8,10},{9,11},{10,... | collective-permute-start | bytes 12296 | tf_op jit(solution)/shard_map/ppermute | solution.py:648
  62.4 4.6 %collective-permute-start.5 = (f32[8,128]{1,0:T(8,128)S(1)}, f32[8,128]{1,0:T(8,128)S(1)}, u32[]{:S(2)}, u32[]{:S(2)}) collective-permute-start(f32[8,128]{1,0:T(8,128)S(1)} %maximum_maximum_fusion.1), channel_id=1, source_target_pairs={{0,1},{1,0},{2,3},{3,2},{4,5},{5,4},{6,7},{7,6},{8,9},{9,8},{10,11... | collective-permute-start | bytes 12296 | tf_op jit(solution)/shard_map/ppermute | solution.py:648

commit v25 on v24

--- a/solution.py
+++ b/solution.py
@@ -643,7 +643,6 @@
         for times in range(1, 4):
             turn = reach * times
             if turn < size:
-                turn += 2 if times == 1 and reach > 1 else 0
                 pairs = [(i, i ^ turn) for i in range(size)]
                 copies.append(lax.ppermute(value, axis, pairs))
         value = functools.reduce(jnp.maximum, copies)

time: 74.5 us -> 71.5 us (0.960)
  waiting for transfers between devices: 31.4 us -> 28.6 us
    ppermute x6, waiting for transfers between devices: 4.59 us -> 1.77 us  [everyone_max(): copies.append(lax.ppermute(value, axis, pairs))]
    ppermute x6, starting transfers between devices: 4.68 us -> 6.53 us  [everyone_max(): copies.append(lax.ppermute(value, axis, pairs))]
    ppermute x2, starting transfers between devices: 8.64 us -> 7.44 us  [from_far(): return lax.ppermute(far_side, 'gx', pairs)]
    ppermute x2, starting transfers between devices: 1.81 us -> 0.84 us  [from_near(): return lax.ppermute(near_side, 'gx', [(i, i ^ 1) for i in range(size)])]
  transfers between devices with their start and end apart: 11 -> 11, of which waited for: 3 -> 4; matrix products, arithmetic and copies ran while one was open for 1% -> 1% of each run, Pallas kernels for 13% -> 14%
where the time goes in v25:
time: 71.5 us; the launch traced here: 71.1 us
  waiting for transfers between devices  28.6 us (40%)
  starting transfers between devices  22.2 us (31%)
  Pallas kernels  19.5 us (27%)
    all_to_all x1, waiting for transfers between devices, per_device(): come = lax.all_to_all(parts, 'gx', split_axis=0, concat_axis=0, tiled=True)  26.8 us
    pallas_call x2, Pallas kernels, along_planes(): pl.pallas_call(functools.partial(plane_kernel, with_inner), out_shape=jax...  9.11 us
    ppermute x2, starting transfers between devices, from_far(): return lax.ppermute(far_side, 'gx', pairs)  7.44 us
    all_to_all x1, starting transfers between devices, per_device(): come = lax.all_to_all(parts, 'gx', split_axis=0, concat_axis=0, tiled=True)  7.37 us
    ppermute x6, starting transfers between devices, everyone_max(): copies.append(lax.ppermute(value, axis, pairs))  6.53 us
    pallas_call x1, Pallas kernels, second_stage(): pl.pallas_call(second_kernel, out_shape=jax.ShapeDtypeStruct((FIELDS, BLO...  3.27 us
    pallas_call x1, Pallas kernels, pack(): pl.pallas_call(functools.partial(pack_kernel, size, cap, per_dev), out_sh...  2.7 us
    pallas_call x1, Pallas kernels, unpack(): pl.pallas_call(functools.partial(unpack_kernel, size, cap), out_shape=(ja...  2.52 us
  transfers between devices with their start and end apart: 11, of which 4 were waited for; matrix products, arithmetic and copies ran while one was open for 1% of the time, Pallas kernels for 14%

profile of v25, /device:TPU:0, one launch (start us, length us, event | category | flops | bytes accessed | tf_op | source)
XLA Modules:
  0.0 71.1 jit_solution(16482040343879269526)
XLA Ops:
  0.0 2.7 %pack.1 = f32[16,161,1,128]{3,2,1,0:T(1,128)} custom-call(s32[1024]{0:T(1024)} %owner_hbm.1, f32[1280,1,128]{2,1,0:T(1,128)} %bitcast.7), custom_call_target="tpu_custom_call" | custom-call | flops 1000000 | bytes 3000000 | tf_op jit(solution)/shard_map/pack/pallas_call | solution.py:113
  2.7 7.4 %all-to-all-start = ((f32[16,161,1,128]{3,2,1,0:T(1,128)}), f32[16,161,1,128]{3,2,1,0:T(1,128)S(1)}, u32[]{:S(2)}, u32[]{:S(2)}) async-start(f32[16,161,1,128]{3,2,1,0:T(1,128)} %pack.1), calls=%async_computation | async-start | bytes 2637824 | tf_op jit(solution)/shard_map/all_to_all | solution.py:661
  10.1 0.1 eq.33
  10.2 0.3 convert_reduce_fusion
  10.6 0.1 broadcast_add_fusion
  10.7 0.1 add.17
  10.7 0.1 select_reduce_fusion.table
  10.9 26.8 %all-to-all-done = f32[16,161,1,128]{3,2,1,0:T(1,128)S(1)} async-done(((f32[16,161,1,128]{3,2,1,0:T(1,128)}), f32[16,161,1,128]{3,2,1,0:T(1,128)S(1)}, u32[]{:S(2)}, u32[]{:S(2)}) %all-to-all-start) | async-done | bytes 1318944 | tf_op jit(solution)/shard_map/all_to_all | solution.py:661
  37.7 2.5 %unpack.1 = (f32[5,8,32,128]{3,2,1,0:T(8,128)S(1)}, f32[5,3,32,128]{3,2,1,0:T(8,128)S(1)}, f32[5,3,32,128]{3,2,1,0:T(8,128)S(1)}, f32[8,128]{1,0:T(8,128)S(1)}) custom-call(s32[64]{0:T(128)S(1)} %select_reduce_fusion.table, f32[2576,1,128]{2,1,0:T(1,128)S(1)} %bitcast.6), custom_call_target="tpu_custom_call" | custom-call | flops 5000000 | bytes 2000000 | tf_op jit(solution)/shard_map/unpack/pallas_call | solution.py:237
  40.2 0.8 %collective-permute-start.1 = (f32[5,3,32,128]{3,2,1,0:T(8,128)S(1)}, f32[5,3,32,128]{3,2,1,0:T(8,128)S(1)}, u32[]{:S(2)}, u32[]{:S(2)}) collective-permute-start(f32[5,3,32,128]{3,2,1,0:T(8,128)S(1)} %get-tuple-element.24), channel_id=1, source_target_pairs={{0,1},{1,0},{2,3},{3,2},{4,5},{5,4},{6,7},{7,6},{8,9},{9,8},{10,11... | collective-permute-start | bytes 737288 | tf_op jit(solution)/shard_map/ppermute | solution.py:152
  41.0 6.0 %collective-permute-start = (f32[5,3,32,128]{3,2,1,0:T(8,128)S(1)}, f32[5,3,32,128]{3,2,1,0:T(8,128)S(1)}, u32[]{:S(2)}, u32[]{:S(2)}) collective-permute-start(f32[5,3,32,128]{3,2,1,0:T(8,128)S(1)} %get-tuple-element.23), channel_id=1, source_target_pairs={{0,15},{1,2},{2,1},{3,4},{4,3},{5,6},{6,5},{7,8},{8,7},{9,10},{10,... | collective-permute-start | bytes 737288 | tf_op jit(solution)/shard_map/ppermute | solution.py:148
  47.0 5.1 %planes.2.refs_1_ = f32[5,8,32,128]{3,2,1,0:T(8,128)S(1)} custom-call(f32[5,8,32,128]{3,2,1,0:T(8,128)S(1)} %get-tuple-element.21.refs_0_.state, f32[8,128]{1,0:T(8,128)S(1)} %get-tuple-element.22.refs_1_.refs_3_.first_speed), custom_call_target="tpu_custom_call" | custom-call | flops 20000000 | bytes 1000000 | tf_op jit(solution)/shard_map/planes/pallas_call | solution.py:500
  52.2 0.9 %first_near.1 = (f32[5,4,32,128]{3,2,1,0:T(8,128)S(1)}, f32[5,3,32,128]{3,2,1,0:T(8,128)S(1)}, f32[8,128]{1,0:T(8,128)S(1)}) custom-call(f32[5,8,32,128]{3,2,1,0:T(8,128)S(1)} %get-tuple-element.21.refs_0_.state, f32[5,8,32,128]{3,2,1,0:T(8,128)S(1)} %planes.2.refs_1_, f32[5,3,32,128]{3,2,1,0:T(8,128)S(1)} %collective-permute-done.1.refs_2_, ...), custom_call_target="tpu_custom_call" | custom-call | flops 15000000 | bytes 2000000 | tf_op jit(solution)/shard_map/first_near/pallas_call | solution.py:585
  53.1 1.0 %first_far.1 = (f32[5,4,32,128]{3,2,1,0:T(8,128)S(1)}, f32[5,3,32,128]{3,2,1,0:T(8,128)S(1)}, f32[8,128]{1,0:T(8,128)S(1)}) custom-call(f32[5,8,32,128]{3,2,1,0:T(8,128)S(1)} %get-tuple-element.21.refs_0_.state, f32[5,8,32,128]{3,2,1,0:T(8,128)S(1)} %planes.2.refs_1_, f32[5,3,32,128]{3,2,1,0:T(8,128)S(1)} %collective-permute-done.refs_2_, ...), custom_call_target="tpu_custom_call" | custom-call | flops 15000000 | bytes 2000000 | tf_op jit(solution)/shard_map/first_far/pallas_call | solution.py:585
  54.1 0.3 collective-permute-start.4
  54.4 0.5 collective-permute-start.3
  54.9 3.7 %collective-permute-start.2 = (f32[8,128]{1,0:T(8,128)S(1)}, f32[8,128]{1,0:T(8,128)S(1)}, u32[]{:S(2)}, u32[]{:S(2)}) collective-permute-start(f32[8,128]{1,0:T(8,128)S(1)} %get-tuple-element.28), channel_id=1, source_target_pairs={{0,4},{1,5},{2,6},{3,7},{4,0},{5,1},{6,2},{7,3},{8,12},{9,13},{10,... | collective-permute-start | bytes 12296 | tf_op jit(solution)/shard_map/ppermute | solution.py:647
  58.5 1.4 %collective-permute-start.8 = (f32[5,3,32,128]{3,2,1,0:T(8,128)S(1)}, f32[5,3,32,128]{3,2,1,0:T(8,128)S(1)}, u32[]{:S(2)}, u32[]{:S(2)}) collective-permute-start(f32[5,3,32,128]{3,2,1,0:T(8,128)S(1)} %get-tuple-element.29), channel_id=1, source_target_pairs={{0,15},{1,2},{2,1},{3,4},{4,3},{5,6},{6,5},{7,8},{8,7},{9,10},{10,... | collective-permute-start | bytes 737288 | tf_op jit(solution)/shard_map/ppermute | solution.py:148
  60.0 0.1 collective-permute-done.2
  60.2 2.1 %collective-permute-start.6 = (f32[8,128]{1,0:T(8,128)S(1)}, f32[8,128]{1,0:T(8,128)S(1)}, u32[]{:S(2)}, u32[]{:S(2)}) collective-permute-start(f32[8,128]{1,0:T(8,128)S(1)} %maximum_maximum_fusion.1), channel_id=1, source_target_pairs={{0,2},{1,3},{2,0},{3,1},{4,6},{5,7},{6,4},{7,5},{8,10},{9,11},{10,... | collective-permute-start | bytes 12296 | tf_op jit(solution)/shard_map/ppermute | solution.py:647
  62.2 1.0 %collective-permute-done.7 = f32[8,128]{1,0:T(8,128)S(1)} collective-permute-done((f32[8,128]{1,0:T(8,128)S(1)}, f32[8,128]{1,0:T(8,128)S(1)}, u32[]{:S(2)}, u32[]{:S(2)}) %collective-permute-start.7) | collective-permute-done | bytes 4128 | tf_op jit(solution)/shard_map/ppermute | solution.py:647
  63.2 0.7 collective-permute-done.6
  63.9 4.0 %planes.3.sides = f32[5,8,32,128]{3,2,1,0:T(8,128)S(1)} custom-call(f32[5,4,32,128]{3,2,1,0:T(8,128)S(1)} %get-tuple-element.26.refs_0_.middle_far, f32[5,4,32,128]{3,2,1,0:T(8,128)S(1)} %get-tuple-element.27.refs_1_.middle_near, f32[8,128]{1,0:T(8,128)S(1)} %maximum_maximum_fusion.refs_2_.speed), custom_call_target="tpu_custom_call" | custom-call | flops 20000000 | bytes 1000000 | tf_op jit(solution)/shard_map/planes/pallas_call | solution.py:500
  67.9 3.3 %second_stage.1 = f32[5,8,32,128]{3,2,1,0:T(8,128)} custom-call(f32[5,8,32,128]{3,2,1,0:T(8,128)S(1)} %get-tuple-element.21.refs_0_.state, f32[5,4,32,128]{3,2,1,0:T(8,128)S(1)} %get-tuple-element.26.refs_0_.middle_far, f32[5,4,32,128]{3,2,1,0:T(8,128)S(1)} %get-tuple-element.27.refs_1_.middle_near, f32[5,8,32,128]{3,2,1,0:T(8,128)S(1)} %planes.3.sides, ...), custom_call_target="tpu_custom_call" | custom-call | flops 30000000 | bytes 3000000 | tf_op jit(solution)/shard_map/second_stage/pallas_call | solution.py:626
  (19 shorter events, 0.1 us)
Async XLA Ops:
  2.7 7.4 %copy-start = (s32[1024]{0:T(1024)S(1)}, s32[1024]{0:T(1024)}, u32[]{:S(2)}) copy-start(s32[1024]{0:T(1024)} %owner_hbm.1) | copy-start | bytes 12292
  2.7 7.4 %copy-start.1 = (s32[1024]{0:T(1024)S(1)}, s32[1024]{0:T(1024)}, u32[]{:S(2)}) copy-start(s32[1024]{0:T(1024)} %param.5) | copy-start | bytes 12292
  2.7 34.9 %all-to-all-start = ((f32[16,161,1,128]{3,2,1,0:T(1,128)}), f32[16,161,1,128]{3,2,1,0:T(1,128)S(1)}, u32[]{:S(2)}, u32[]{:S(2)}) async-start(f32[16,161,1,128]{3,2,1,0:T(1,128)} %pack.1), calls=%async_computation | async-start | bytes 2637824 | tf_op jit(solution)/shard_map/all_to_all | solution.py:661
  40.2 12.0 %collective-permute-start.1 = (f32[5,3,32,128]{3,2,1,0:T(8,128)S(1)}, f32[5,3,32,128]{3,2,1,0:T(8,128)S(1)}, u32[]{:S(2)}, u32[]{:S(2)}) collective-permute-start(f32[5,3,32,128]{3,2,1,0:T(8,128)S(1)} %get-tuple-element.24), channel_id=1, source_target_pairs={{0,1},{1,0},{2,3},{3,2},{4,5},{5,4},{6,7},{7,6},{8,9},{9,8},{10,11... | collective-permute-start | bytes 737288 | tf_op jit(solution)/shard_map/ppermute | solution.py:152
  41.0 12.0 %collective-permute-start = (f32[5,3,32,128]{3,2,1,0:T(8,128)S(1)}, f32[5,3,32,128]{3,2,1,0:T(8,128)S(1)}, u32[]{:S(2)}, u32[]{:S(2)}) collective-permute-start(f32[5,3,32,128]{3,2,1,0:T(8,128)S(1)} %get-tuple-element.23), channel_id=1, source_target_pairs={{0,15},{1,2},{2,1},{3,4},{4,3},{5,6},{6,5},{7,8},{8,7},{9,10},{10,... | collective-permute-start | bytes 737288 | tf_op jit(solution)/shard_map/ppermute | solution.py:148
  54.1 5.9 %collective-permute-start.4 = (f32[8,128]{1,0:T(8,128)S(1)}, f32[8,128]{1,0:T(8,128)S(1)}, u32[]{:S(2)}, u32[]{:S(2)}) collective-permute-start(f32[8,128]{1,0:T(8,128)S(1)} %get-tuple-element.28), channel_id=1, source_target_pairs={{0,12},{1,13},{2,14},{3,15},{4,8},{5,9},{6,10},{7,11},{8,4},{9,5},... | collective-permute-start | bytes 12296 | tf_op jit(solution)/shard_map/ppermute | solution.py:647
  54.4 5.6 %collective-permute-start.3 = (f32[8,128]{1,0:T(8,128)S(1)}, f32[8,128]{1,0:T(8,128)S(1)}, u32[]{:S(2)}, u32[]{:S(2)}) collective-permute-start(f32[8,128]{1,0:T(8,128)S(1)} %get-tuple-element.28), channel_id=1, source_target_pairs={{0,8},{1,9},{2,10},{3,11},{4,12},{5,13},{6,14},{7,15},{8,0},{9,1},... | collective-permute-start | bytes 12296 | tf_op jit(solution)/shard_map/ppermute | solution.py:647
  54.9 5.2 %collective-permute-start.2 = (f32[8,128]{1,0:T(8,128)S(1)}, f32[8,128]{1,0:T(8,128)S(1)}, u32[]{:S(2)}, u32[]{:S(2)}) collective-permute-start(f32[8,128]{1,0:T(8,128)S(1)} %get-tuple-element.28), channel_id=1, source_target_pairs={{0,4},{1,5},{2,6},{3,7},{4,0},{5,1},{6,2},{7,3},{8,12},{9,13},{10,... | collective-permute-start | bytes 12296 | tf_op jit(solution)/shard_map/ppermute | solution.py:647
  58.5 9.3 %collective-permute-start.8 = (f32[5,3,32,128]{3,2,1,0:T(8,128)S(1)}, f32[5,3,32,128]{3,2,1,0:T(8,128)S(1)}, u32[]{:S(2)}, u32[]{:S(2)}) collective-permute-start(f32[5,3,32,128]{3,2,1,0:T(8,128)S(1)} %get-tuple-element.29), channel_id=1, source_target_pairs={{0,15},{1,2},{2,1},{3,4},{4,3},{5,6},{6,5},{7,8},{8,7},{9,10},{10,... | collective-permute-start | bytes 737288 | tf_op jit(solution)/shard_map/ppermute | solution.py:148
  60.0 7.9 %collective-permute-start.9 = (f32[5,3,32,128]{3,2,1,0:T(8,128)S(1)}, f32[5,3,32,128]{3,2,1,0:T(8,128)S(1)}, u32[]{:S(2)}, u32[]{:S(2)}) collective-permute-start(f32[5,3,32,128]{3,2,1,0:T(8,128)S(1)} %get-tuple-element.30), channel_id=1, source_target_pairs={{0,1},{1,0},{2,3},{3,2},{4,5},{5,4},{6,7},{7,6},{8,9},{9,8},{10,11... | collective-permute-start | bytes 737288 | tf_op jit(solution)/shard_map/ppermute | solution.py:152
  60.1 3.0 %collective-permute-start.7 = (f32[8,128]{1,0:T(8,128)S(1)}, f32[8,128]{1,0:T(8,128)S(1)}, u32[]{:S(2)}, u32[]{:S(2)}) collective-permute-start(f32[8,128]{1,0:T(8,128)S(1)} %maximum_maximum_fusion.1), channel_id=1, source_target_pairs={{0,3},{1,2},{2,1},{3,0},{4,7},{5,6},{6,5},{7,4},{8,11},{9,10},{10,... | collective-permute-start | bytes 12296 | tf_op jit(solution)/shard_map/ppermute | solution.py:647
  60.2 3.7 %collective-permute-start.6 = (f32[8,128]{1,0:T(8,128)S(1)}, f32[8,128]{1,0:T(8,128)S(1)}, u32[]{:S(2)}, u32[]{:S(2)}) collective-permute-start(f32[8,128]{1,0:T(8,128)S(1)} %maximum_maximum_fusion.1), channel_id=1, source_target_pairs={{0,2},{1,3},{2,0},{3,1},{4,6},{5,7},{6,4},{7,5},{8,10},{9,11},{10,... | collective-permute-start | bytes 12296 | tf_op jit(solution)/shard_map/ppermute | solution.py:647
  62.2 1.6 %collective-permute-start.5 = (f32[8,128]{1,0:T(8,128)S(1)}, f32[8,128]{1,0:T(8,128)S(1)}, u32[]{:S(2)}, u32[]{:S(2)}) collective-permute-start(f32[8,128]{1,0:T(8,128)S(1)} %maximum_maximum_fusion.1), channel_id=1, source_target_pairs={{0,1},{1,0},{2,3},{3,2},{4,5},{5,4},{6,7},{7,6},{8,9},{9,8},{10,11... | collective-permute-start | bytes 12296 | tf_op jit(solution)/shard_map/ppermute | solution.py:647

commit v26 on v25

--- a/solution.py
+++ b/solution.py
@@ -634,19 +634,24 @@
     )(*operands)
 
 
+def max_rounds(size):
+    rounds = [[1]] if size > 1 else []
+    low = 2
+    for width in (8, 4, 4, 4):
+        width = min(width, max(size // low, 1))
+        if width > 1:
+            rounds.insert(0, [low * times for times in range(1, width)])
+        low *= width
+    return rounds
+
+
 def everyone_max(value, axis, size):
-    reach = 1
-    while reach * 4 < size:
-        reach *= 4
-    while reach:
+    for turns in max_rounds(size):
         copies = [value]
-        for times in range(1, 4):
-            turn = reach * times
-            if turn < size:
-                pairs = [(i, i ^ turn) for i in range(size)]
-                copies.append(lax.ppermute(value, axis, pairs))
+        for turn in turns:
+            pairs = [(i, i ^ turn) for i in range(size)]
+            copies.append(lax.ppermute(value, axis, pairs))
         value = functools.reduce(jnp.maximum, copies)
-        reach //= 4
     return value
 
 

time: 71.5 us -> 79.6 us (1.11)
  waiting for transfers between devices: 28.6 us -> 35.7 us
  starting transfers between devices: 22.2 us -> 23.3 us
    ppermute x6 -> x8, waiting for transfers between devices: 1.77 us -> 8.95 us  [everyone_max(): copies.append(lax.ppermute(value, axis, pairs))]
    ppermute x2, starting transfers between devices: 7.44 us -> 8.35 us  [from_far(): return lax.ppermute(far_side, 'gx', pairs)]
    ppermute x6 -> x8, starting transfers between devices: 6.53 us -> 6.7 us  [everyone_max(): copies.append(lax.ppermute(value, axis, pairs))]
  transfers between devices with their start and end apart: 11 -> 13, of which waited for: 4 -> 8; matrix products, arithmetic and copies ran while one was open for 1% -> 1% of each run, Pallas kernels for 14% -> 13%
where the time goes in v26:
time: 79.6 us; the launch traced here: 79.4 us
  waiting for transfers between devices  35.7 us (45%)
  starting transfers between devices  23.3 us (29%)
  Pallas kernels  19.5 us (24%)
    all_to_all x1, waiting for transfers between devices, per_device(): come = lax.all_to_all(parts, 'gx', split_axis=0, concat_axis=0, tiled=True)  26.8 us
    pallas_call x2, Pallas kernels, along_planes(): pl.pallas_call(functools.partial(plane_kernel, with_inner), out_shape=jax...  9.11 us
    ppermute x8, waiting for transfers between devices, everyone_max(): copies.append(lax.ppermute(value, axis, pairs))  8.95 us
    ppermute x2, starting transfers between devices, from_far(): return lax.ppermute(far_side, 'gx', pairs)  8.35 us
    all_to_all x1, starting transfers between devices, per_device(): come = lax.all_to_all(parts, 'gx', split_axis=0, concat_axis=0, tiled=True)  7.37 us
    ppermute x8, starting transfers between devices, everyone_max(): copies.append(lax.ppermute(value, axis, pairs))  6.7 us
    pallas_call x1, Pallas kernels, second_stage(): pl.pallas_call(second_kernel, out_shape=jax.ShapeDtypeStruct((FIELDS, BLO...  3.27 us
    pallas_call x1, Pallas kernels, pack(): pl.pallas_call(functools.partial(pack_kernel, size, cap, per_dev), out_sh...  2.7 us
  transfers between devices with their start and end apart: 13, of which 8 were waited for; matrix products, arithmetic and copies ran while one was open for 1% of the time, Pallas kernels for 13%

profile of v26, /device:TPU:0, one launch (start us, length us, event | category | flops | bytes accessed | tf_op | source)
XLA Modules:
  0.0 79.4 jit_solution(16309039506659031662)
XLA Ops:
  0.0 2.7 %pack.1 = f32[16,161,1,128]{3,2,1,0:T(1,128)} custom-call(s32[1024]{0:T(1024)} %owner_hbm.1, f32[1280,1,128]{2,1,0:T(1,128)} %bitcast.7), custom_call_target="tpu_custom_call" | custom-call | flops 1000000 | bytes 3000000 | tf_op jit(solution)/shard_map/pack/pallas_call | solution.py:113
  2.7 7.4 %all-to-all-start = ((f32[16,161,1,128]{3,2,1,0:T(1,128)}), f32[16,161,1,128]{3,2,1,0:T(1,128)S(1)}, u32[]{:S(2)}, u32[]{:S(2)}) async-start(f32[16,161,1,128]{3,2,1,0:T(1,128)} %pack.1), calls=%async_computation | async-start | bytes 2637824 | tf_op jit(solution)/shard_map/all_to_all | solution.py:666
  10.2 0.3 convert_reduce_fusion
  10.9 26.8 %all-to-all-done = f32[16,161,1,128]{3,2,1,0:T(1,128)S(1)} async-done(((f32[16,161,1,128]{3,2,1,0:T(1,128)}), f32[16,161,1,128]{3,2,1,0:T(1,128)S(1)}, u32[]{:S(2)}, u32[]{:S(2)}) %all-to-all-start) | async-done | bytes 1318944 | tf_op jit(solution)/shard_map/all_to_all | solution.py:666
  37.7 2.5 %unpack.1 = (f32[5,8,32,128]{3,2,1,0:T(8,128)S(1)}, f32[5,3,32,128]{3,2,1,0:T(8,128)S(1)}, f32[5,3,32,128]{3,2,1,0:T(8,128)S(1)}, f32[8,128]{1,0:T(8,128)S(1)}) custom-call(s32[64]{0:T(128)S(1)} %select_reduce_fusion.table, f32[2576,1,128]{2,1,0:T(1,128)S(1)} %bitcast.6), custom_call_target="tpu_custom_call" | custom-call | flops 5000000 | bytes 2000000 | tf_op jit(solution)/shard_map/unpack/pallas_call | solution.py:237
  40.2 0.8 %collective-permute-start.1 = (f32[5,3,32,128]{3,2,1,0:T(8,128)S(1)}, f32[5,3,32,128]{3,2,1,0:T(8,128)S(1)}, u32[]{:S(2)}, u32[]{:S(2)}) collective-permute-start(f32[5,3,32,128]{3,2,1,0:T(8,128)S(1)} %get-tuple-element.24), channel_id=1, source_target_pairs={{0,1},{1,0},{2,3},{3,2},{4,5},{5,4},{6,7},{7,6},{8,9},{9,8},{10,11... | collective-permute-start | bytes 737288 | tf_op jit(solution)/shard_map/ppermute | solution.py:152
  41.0 6.0 %collective-permute-start = (f32[5,3,32,128]{3,2,1,0:T(8,128)S(1)}, f32[5,3,32,128]{3,2,1,0:T(8,128)S(1)}, u32[]{:S(2)}, u32[]{:S(2)}) collective-permute-start(f32[5,3,32,128]{3,2,1,0:T(8,128)S(1)} %get-tuple-element.23), channel_id=1, source_target_pairs={{0,15},{1,2},{2,1},{3,4},{4,3},{5,6},{6,5},{7,8},{8,7},{9,10},{10,... | collective-permute-start | bytes 737288 | tf_op jit(solution)/shard_map/ppermute | solution.py:148
  47.0 5.1 %planes.2.refs_1_ = f32[5,8,32,128]{3,2,1,0:T(8,128)S(1)} custom-call(f32[5,8,32,128]{3,2,1,0:T(8,128)S(1)} %get-tuple-element.21.refs_0_.state, f32[8,128]{1,0:T(8,128)S(1)} %get-tuple-element.22.refs_1_.refs_3_.first_speed), custom_call_target="tpu_custom_call" | custom-call | flops 20000000 | bytes 1000000 | tf_op jit(solution)/shard_map/planes/pallas_call | solution.py:500
  52.2 0.9 %first_near.1 = (f32[5,4,32,128]{3,2,1,0:T(8,128)S(1)}, f32[5,3,32,128]{3,2,1,0:T(8,128)S(1)}, f32[8,128]{1,0:T(8,128)S(1)}) custom-call(f32[5,8,32,128]{3,2,1,0:T(8,128)S(1)} %get-tuple-element.21.refs_0_.state, f32[5,8,32,128]{3,2,1,0:T(8,128)S(1)} %planes.2.refs_1_, f32[5,3,32,128]{3,2,1,0:T(8,128)S(1)} %collective-permute-done.1.refs_2_, ...), custom_call_target="tpu_custom_call" | custom-call | flops 15000000 | bytes 2000000 | tf_op jit(solution)/shard_map/first_near/pallas_call | solution.py:585
  53.1 1.0 %first_far.1 = (f32[5,4,32,128]{3,2,1,0:T(8,128)S(1)}, f32[5,3,32,128]{3,2,1,0:T(8,128)S(1)}, f32[8,128]{1,0:T(8,128)S(1)}) custom-call(f32[5,8,32,128]{3,2,1,0:T(8,128)S(1)} %get-tuple-element.21.refs_0_.state, f32[5,8,32,128]{3,2,1,0:T(8,128)S(1)} %planes.2.refs_1_, f32[5,3,32,128]{3,2,1,0:T(8,128)S(1)} %collective-permute-done.refs_2_, ...), custom_call_target="tpu_custom_call" | custom-call | flops 15000000 | bytes 2000000 | tf_op jit(solution)/shard_map/first_far/pallas_call | solution.py:585
  54.1 2.3 %collective-permute-start.10 = (f32[5,3,32,128]{3,2,1,0:T(8,128)S(1)}, f32[5,3,32,128]{3,2,1,0:T(8,128)S(1)}, u32[]{:S(2)}, u32[]{:S(2)}) collective-permute-start(f32[5,3,32,128]{3,2,1,0:T(8,128)S(1)} %get-tuple-element.29), channel_id=1, source_target_pairs={{0,15},{1,2},{2,1},{3,4},{4,3},{5,6},{6,5},{7,8},{8,7},{9,10},{10,... | collective-permute-start | bytes 737288 | tf_op jit(solution)/shard_map/ppermute | solution.py:148
  56.4 2.6 %collective-permute-start.8 = (f32[8,128]{1,0:T(8,128)S(1)}, f32[8,128]{1,0:T(8,128)S(1)}, u32[]{:S(2)}, u32[]{:S(2)}) collective-permute-start(f32[8,128]{1,0:T(8,128)S(1)} %get-tuple-element.28), channel_id=1, source_target_pairs={{0,14},{1,15},{2,12},{3,13},{4,10},{5,11},{6,8},{7,9},{8,6},{9,7},... | collective-permute-start | bytes 12296 | tf_op jit(solution)/shard_map/ppermute | solution.py:653
  59.0 0.3 collective-permute-start.6
  59.3 3.4 %collective-permute-done.8 = f32[8,128]{1,0:T(8,128)S(1)} collective-permute-done((f32[8,128]{1,0:T(8,128)S(1)}, f32[8,128]{1,0:T(8,128)S(1)}, u32[]{:S(2)}, u32[]{:S(2)}) %collective-permute-start.8) | collective-permute-done | bytes 4128 | tf_op jit(solution)/shard_map/ppermute | solution.py:653
  62.8 1.3 %collective-permute-start.5 = (f32[8,128]{1,0:T(8,128)S(1)}, f32[8,128]{1,0:T(8,128)S(1)}, u32[]{:S(2)}, u32[]{:S(2)}) collective-permute-start(f32[8,128]{1,0:T(8,128)S(1)} %get-tuple-element.28), channel_id=1, source_target_pairs={{0,8},{1,9},{2,10},{3,11},{4,12},{5,13},{6,14},{7,15},{8,0},{9,1},... | collective-permute-start | bytes 12296 | tf_op jit(solution)/shard_map/ppermute | solution.py:653
  64.4 1.8 %collective-permute-start.4 = (f32[8,128]{1,0:T(8,128)S(1)}, f32[8,128]{1,0:T(8,128)S(1)}, u32[]{:S(2)}, u32[]{:S(2)}) collective-permute-start(f32[8,128]{1,0:T(8,128)S(1)} %get-tuple-element.28), channel_id=1, source_target_pairs={{0,6},{1,7},{2,4},{3,5},{4,2},{5,3},{6,0},{7,1},{8,14},{9,15},{10,... | collective-permute-start | bytes 12296 | tf_op jit(solution)/shard_map/ppermute | solution.py:653
  66.2 1.1 %collective-permute-done.5 = f32[8,128]{1,0:T(8,128)S(1)} collective-permute-done((f32[8,128]{1,0:T(8,128)S(1)}, f32[8,128]{1,0:T(8,128)S(1)}, u32[]{:S(2)}, u32[]{:S(2)}) %collective-permute-start.5) | collective-permute-done | bytes 4128 | tf_op jit(solution)/shard_map/ppermute | solution.py:653
  67.3 0.6 collective-permute-start.2
  67.9 1.0 %collective-permute-done.4 = f32[8,128]{1,0:T(8,128)S(1)} collective-permute-done((f32[8,128]{1,0:T(8,128)S(1)}, f32[8,128]{1,0:T(8,128)S(1)}, u32[]{:S(2)}, u32[]{:S(2)}) %collective-permute-start.4) | collective-permute-done | bytes 4128 | tf_op jit(solution)/shard_map/ppermute | solution.py:653
  68.9 0.9 %collective-permute-done.3 = f32[8,128]{1,0:T(8,128)S(1)} collective-permute-done((f32[8,128]{1,0:T(8,128)S(1)}, f32[8,128]{1,0:T(8,128)S(1)}, u32[]{:S(2)}, u32[]{:S(2)}) %collective-permute-start.3) | collective-permute-done | bytes 4128 | tf_op jit(solution)/shard_map/ppermute | solution.py:653
  69.8 1.1 %collective-permute-done.2 = f32[8,128]{1,0:T(8,128)S(1)} collective-permute-done((f32[8,128]{1,0:T(8,128)S(1)}, f32[8,128]{1,0:T(8,128)S(1)}, u32[]{:S(2)}, u32[]{:S(2)}) %collective-permute-start.2) | collective-permute-done | bytes 4128 | tf_op jit(solution)/shard_map/ppermute | solution.py:653
  71.0 1.2 %collective-permute-done.9 = f32[8,128]{1,0:T(8,128)S(1)} collective-permute-done((f32[8,128]{1,0:T(8,128)S(1)}, f32[8,128]{1,0:T(8,128)S(1)}, u32[]{:S(2)}, u32[]{:S(2)}) %collective-permute-start.9) | collective-permute-done | bytes 4128 | tf_op jit(solution)/shard_map/ppermute | solution.py:653
  72.1 4.0 %planes.3.sides = f32[5,8,32,128]{3,2,1,0:T(8,128)S(1)} custom-call(f32[5,4,32,128]{3,2,1,0:T(8,128)S(1)} %get-tuple-element.26.refs_0_.middle_far, f32[5,4,32,128]{3,2,1,0:T(8,128)S(1)} %get-tuple-element.27.refs_1_.middle_near, f32[8,128]{1,0:T(8,128)S(1)} %max.31.refs_2_.speed), custom_call_target="tpu_custom_call" | custom-call | flops 20000000 | bytes 1000000 | tf_op jit(solution)/shard_map/planes/pallas_call | solution.py:500
  76.1 3.3 %second_stage.1 = f32[5,8,32,128]{3,2,1,0:T(8,128)} custom-call(f32[5,8,32,128]{3,2,1,0:T(8,128)S(1)} %get-tuple-element.21.refs_0_.state, f32[5,4,32,128]{3,2,1,0:T(8,128)S(1)} %get-tuple-element.26.refs_0_.middle_far, f32[5,4,32,128]{3,2,1,0:T(8,128)S(1)} %get-tuple-element.27.refs_1_.middle_near, f32[5,8,32,128]{3,2,1,0:T(8,128)S(1)} %planes.3.sides, ...), custom_call_target="tpu_custom_call" | custom-call | flops 30000000 | bytes 3000000 | tf_op jit(solution)/shard_map/second_stage/pallas_call | solution.py:626
  (23 shorter events, 0.8 us)
Async XLA Ops:
  2.7 7.4 %copy-start = (s32[1024]{0:T(1024)S(1)}, s32[1024]{0:T(1024)}, u32[]{:S(2)}) copy-start(s32[1024]{0:T(1024)} %owner_hbm.1) | copy-start | bytes 12292
  2.7 7.4 %copy-start.1 = (s32[1024]{0:T(1024)S(1)}, s32[1024]{0:T(1024)}, u32[]{:S(2)}) copy-start(s32[1024]{0:T(1024)} %param.5) | copy-start | bytes 12292
  2.7 34.9 %all-to-all-start = ((f32[16,161,1,128]{3,2,1,0:T(1,128)}), f32[16,161,1,128]{3,2,1,0:T(1,128)S(1)}, u32[]{:S(2)}, u32[]{:S(2)}) async-start(f32[16,161,1,128]{3,2,1,0:T(1,128)} %pack.1), calls=%async_computation | async-start | bytes 2637824 | tf_op jit(solution)/shard_map/all_to_all | solution.py:666
  40.2 12.0 %collective-permute-start.1 = (f32[5,3,32,128]{3,2,1,0:T(8,128)S(1)}, f32[5,3,32,128]{3,2,1,0:T(8,128)S(1)}, u32[]{:S(2)}, u32[]{:S(2)}) collective-permute-start(f32[5,3,32,128]{3,2,1,0:T(8,128)S(1)} %get-tuple-element.24), channel_id=1, source_target_pairs={{0,1},{1,0},{2,3},{3,2},{4,5},{5,4},{6,7},{7,6},{8,9},{9,8},{10,11... | collective-permute-start | bytes 737288 | tf_op jit(solution)/shard_map/ppermute | solution.py:152
  41.0 12.0 %collective-permute-start = (f32[5,3,32,128]{3,2,1,0:T(8,128)S(1)}, f32[5,3,32,128]{3,2,1,0:T(8,128)S(1)}, u32[]{:S(2)}, u32[]{:S(2)}) collective-permute-start(f32[5,3,32,128]{3,2,1,0:T(8,128)S(1)} %get-tuple-element.23), channel_id=1, source_target_pairs={{0,15},{1,2},{2,1},{3,4},{4,3},{5,6},{6,5},{7,8},{8,7},{9,10},{10,... | collective-permute-start | bytes 737288 | tf_op jit(solution)/shard_map/ppermute | solution.py:148
  54.1 22.0 %collective-permute-start.10 = (f32[5,3,32,128]{3,2,1,0:T(8,128)S(1)}, f32[5,3,32,128]{3,2,1,0:T(8,128)S(1)}, u32[]{:S(2)}, u32[]{:S(2)}) collective-permute-start(f32[5,3,32,128]{3,2,1,0:T(8,128)S(1)} %get-tuple-element.29), channel_id=1, source_target_pairs={{0,15},{1,2},{2,1},{3,4},{4,3},{5,6},{6,5},{7,8},{8,7},{9,10},{10,... | collective-permute-start | bytes 737288 | tf_op jit(solution)/shard_map/ppermute | solution.py:148
  56.4 19.7 %collective-permute-start.11 = (f32[5,3,32,128]{3,2,1,0:T(8,128)S(1)}, f32[5,3,32,128]{3,2,1,0:T(8,128)S(1)}, u32[]{:S(2)}, u32[]{:S(2)}) collective-permute-start(f32[5,3,32,128]{3,2,1,0:T(8,128)S(1)} %get-tuple-element.30), channel_id=1, source_target_pairs={{0,1},{1,0},{2,3},{3,2},{4,5},{5,4},{6,7},{7,6},{8,9},{9,8},{10,11... | collective-permute-start | bytes 737288 | tf_op jit(solution)/shard_map/ppermute | solution.py:152
  56.4 6.3 %collective-permute-start.8 = (f32[8,128]{1,0:T(8,128)S(1)}, f32[8,128]{1,0:T(8,128)S(1)}, u32[]{:S(2)}, u32[]{:S(2)}) collective-permute-start(f32[8,128]{1,0:T(8,128)S(1)} %get-tuple-element.28), channel_id=1, source_target_pairs={{0,14},{1,15},{2,12},{3,13},{4,10},{5,11},{6,8},{7,9},{8,6},{9,7},... | collective-permute-start | bytes 12296 | tf_op jit(solution)/shard_map/ppermute | solution.py:653
  59.0 5.4 %collective-permute-start.7 = (f32[8,128]{1,0:T(8,128)S(1)}, f32[8,128]{1,0:T(8,128)S(1)}, u32[]{:S(2)}, u32[]{:S(2)}) collective-permute-start(f32[8,128]{1,0:T(8,128)S(1)} %get-tuple-element.28), channel_id=1, source_target_pairs={{0,12},{1,13},{2,14},{3,15},{4,8},{5,9},{6,10},{7,11},{8,4},{9,5},... | collective-permute-start | bytes 12296 | tf_op jit(solution)/shard_map/ppermute | solution.py:653
  59.0 7.2 %collective-permute-start.6 = (f32[8,128]{1,0:T(8,128)S(1)}, f32[8,128]{1,0:T(8,128)S(1)}, u32[]{:S(2)}, u32[]{:S(2)}) collective-permute-start(f32[8,128]{1,0:T(8,128)S(1)} %get-tuple-element.28), channel_id=1, source_target_pairs={{0,10},{1,11},{2,8},{3,9},{4,14},{5,15},{6,12},{7,13},{8,2},{9,3},... | collective-permute-start | bytes 12296 | tf_op jit(solution)/shard_map/ppermute | solution.py:653
  62.8 4.5 %collective-permute-start.5 = (f32[8,128]{1,0:T(8,128)S(1)}, f32[8,128]{1,0:T(8,128)S(1)}, u32[]{:S(2)}, u32[]{:S(2)}) collective-permute-start(f32[8,128]{1,0:T(8,128)S(1)} %get-tuple-element.28), channel_id=1, source_target_pairs={{0,8},{1,9},{2,10},{3,11},{4,12},{5,13},{6,14},{7,15},{8,0},{9,1},... | collective-permute-start | bytes 12296 | tf_op jit(solution)/shard_map/ppermute | solution.py:653
  64.4 4.5 %collective-permute-start.4 = (f32[8,128]{1,0:T(8,128)S(1)}, f32[8,128]{1,0:T(8,128)S(1)}, u32[]{:S(2)}, u32[]{:S(2)}) collective-permute-start(f32[8,128]{1,0:T(8,128)S(1)} %get-tuple-element.28), channel_id=1, source_target_pairs={{0,6},{1,7},{2,4},{3,5},{4,2},{5,3},{6,0},{7,1},{8,14},{9,15},{10,... | collective-permute-start | bytes 12296 | tf_op jit(solution)/shard_map/ppermute | solution.py:653
  66.2 3.6 %collective-permute-start.3 = (f32[8,128]{1,0:T(8,128)S(1)}, f32[8,128]{1,0:T(8,128)S(1)}, u32[]{:S(2)}, u32[]{:S(2)}) collective-permute-start(f32[8,128]{1,0:T(8,128)S(1)} %get-tuple-element.28), channel_id=1, source_target_pairs={{0,4},{1,5},{2,6},{3,7},{4,0},{5,1},{6,2},{7,3},{8,12},{9,13},{10,... | collective-permute-start | bytes 12296 | tf_op jit(solution)/shard_map/ppermute | solution.py:653
  67.3 3.6 %collective-permute-start.2 = (f32[8,128]{1,0:T(8,128)S(1)}, f32[8,128]{1,0:T(8,128)S(1)}, u32[]{:S(2)}, u32[]{:S(2)}) collective-permute-start(f32[8,128]{1,0:T(8,128)S(1)} %get-tuple-element.28), channel_id=1, source_target_pairs={{0,2},{1,3},{2,0},{3,1},{4,6},{5,7},{6,4},{7,5},{8,10},{9,11},{10,... | collective-permute-start | bytes 12296 | tf_op jit(solution)/shard_map/ppermute | solution.py:653
  70.9 1.2 %collective-permute-start.9 = (f32[8,128]{1,0:T(8,128)S(1)}, f32[8,128]{1,0:T(8,128)S(1)}, u32[]{:S(2)}, u32[]{:S(2)}) collective-permute-start(f32[8,128]{1,0:T(8,128)S(1)} %maximum_maximum_fusion), channel_id=1, source_target_pairs={{0,1},{1,0},{2,3},{3,2},{4,5},{5,4},{6,7},{7,6},{8,9},{9,8},{10,11... | collective-permute-start | bytes 12296 | tf_op jit(solution)/shard_map/ppermute | solution.py:653

commit v27 on v25

--- a/solution.py
+++ b/solution.py
@@ -640,7 +640,7 @@
         reach *= 4
     while reach:
         copies = [value]
-        for times in range(1, 4):
+        for times in (3, 2, 1) if reach > 1 else (1, 2, 3):
             turn = reach * times
             if turn < size:
                 pairs = [(i, i ^ turn) for i in range(size)]

time: 71.5 us -> 72.9 us (1.020)
  waiting for transfers between devices: 28.6 us -> 30.3 us
    ppermute x6, waiting for transfers between devices: 1.77 us -> 3.55 us  [everyone_max(): copies.append(lax.ppermute(value, axis, pairs))]
where the time goes in v27:
time: 72.9 us; the launch traced here: 72.7 us
  waiting for transfers between devices  30.3 us (42%)
  starting transfers between devices  22 us (30%)
  Pallas kernels  19.5 us (27%)
    all_to_all x1, waiting for transfers between devices, per_device(): come = lax.all_to_all(parts, 'gx', split_axis=0, concat_axis=0, tiled=True)  26.8 us
    pallas_call x2, Pallas kernels, along_planes(): pl.pallas_call(functools.partial(plane_kernel, with_inner), out_shape=jax...  9.11 us
    ppermute x2, starting transfers between devices, from_far(): return lax.ppermute(far_side, 'gx', pairs)  7.44 us
    all_to_all x1, starting transfers between devices, per_device(): come = lax.all_to_all(parts, 'gx', split_axis=0, concat_axis=0, tiled=True)  7.37 us
    ppermute x6, starting transfers between devices, everyone_max(): copies.append(lax.ppermute(value, axis, pairs))  6.31 us
    ppermute x6, waiting for transfers between devices, everyone_max(): copies.append(lax.ppermute(value, axis, pairs))  3.55 us
    pallas_call x1, Pallas kernels, second_stage(): pl.pallas_call(second_kernel, out_shape=jax.ShapeDtypeStruct((FIELDS, BLO...  3.27 us
    pallas_call x1, Pallas kernels, pack(): pl.pallas_call(functools.partial(pack_kernel, size, cap, per_dev), out_sh...  2.7 us
  transfers between devices with their start and end apart: 11, of which 4 were waited for; matrix products, arithmetic and copies ran while one was open for 1% of the time, Pallas kernels for 14%

profile of v27, /device:TPU:0, one launch (start us, length us, event | category | flops | bytes accessed | tf_op | source)
XLA Modules:
  0.0 72.7 jit_solution(872905419300800838)
XLA Ops:
  0.0 2.7 %pack.1 = f32[16,161,1,128]{3,2,1,0:T(1,128)} custom-call(s32[1024]{0:T(1024)} %owner_hbm.1, f32[1280,1,128]{2,1,0:T(1,128)} %bitcast.7), custom_call_target="tpu_custom_call" | custom-call | flops 1000000 | bytes 3000000 | tf_op jit(solution)/shard_map/pack/pallas_call | solution.py:113
  2.7 7.4 %all-to-all-start = ((f32[16,161,1,128]{3,2,1,0:T(1,128)}), f32[16,161,1,128]{3,2,1,0:T(1,128)S(1)}, u32[]{:S(2)}, u32[]{:S(2)}) async-start(f32[16,161,1,128]{3,2,1,0:T(1,128)} %pack.1), calls=%async_computation | async-start | bytes 2637824 | tf_op jit(solution)/shard_map/all_to_all | solution.py:661
  10.1 0.1 eq.33
  10.2 0.3 convert_reduce_fusion
  10.6 0.1 broadcast_add_fusion
  10.7 0.1 add.17
  10.7 0.1 select_reduce_fusion.table
  10.9 26.8 %all-to-all-done = f32[16,161,1,128]{3,2,1,0:T(1,128)S(1)} async-done(((f32[16,161,1,128]{3,2,1,0:T(1,128)}), f32[16,161,1,128]{3,2,1,0:T(1,128)S(1)}, u32[]{:S(2)}, u32[]{:S(2)}) %all-to-all-start) | async-done | bytes 1318944 | tf_op jit(solution)/shard_map/all_to_all | solution.py:661
  37.7 2.5 %unpack.1 = (f32[5,8,32,128]{3,2,1,0:T(8,128)S(1)}, f32[5,3,32,128]{3,2,1,0:T(8,128)S(1)}, f32[5,3,32,128]{3,2,1,0:T(8,128)S(1)}, f32[8,128]{1,0:T(8,128)S(1)}) custom-call(s32[64]{0:T(128)S(1)} %select_reduce_fusion.table, f32[2576,1,128]{2,1,0:T(1,128)S(1)} %bitcast.6), custom_call_target="tpu_custom_call" | custom-call | flops 5000000 | bytes 2000000 | tf_op jit(solution)/shard_map/unpack/pallas_call | solution.py:237
  40.2 0.8 %collective-permute-start.1 = (f32[5,3,32,128]{3,2,1,0:T(8,128)S(1)}, f32[5,3,32,128]{3,2,1,0:T(8,128)S(1)}, u32[]{:S(2)}, u32[]{:S(2)}) collective-permute-start(f32[5,3,32,128]{3,2,1,0:T(8,128)S(1)} %get-tuple-element.24), channel_id=1, source_target_pairs={{0,1},{1,0},{2,3},{3,2},{4,5},{5,4},{6,7},{7,6},{8,9},{9,8},{10,11... | collective-permute-start | bytes 737288 | tf_op jit(solution)/shard_map/ppermute | solution.py:152
  41.0 6.0 %collective-permute-start = (f32[5,3,32,128]{3,2,1,0:T(8,128)S(1)}, f32[5,3,32,128]{3,2,1,0:T(8,128)S(1)}, u32[]{:S(2)}, u32[]{:S(2)}) collective-permute-start(f32[5,3,32,128]{3,2,1,0:T(8,128)S(1)} %get-tuple-element.23), channel_id=1, source_target_pairs={{0,15},{1,2},{2,1},{3,4},{4,3},{5,6},{6,5},{7,8},{8,7},{9,10},{10,... | collective-permute-start | bytes 737288 | tf_op jit(solution)/shard_map/ppermute | solution.py:148
  47.0 5.1 %planes.2.refs_1_ = f32[5,8,32,128]{3,2,1,0:T(8,128)S(1)} custom-call(f32[5,8,32,128]{3,2,1,0:T(8,128)S(1)} %get-tuple-element.21.refs_0_.state, f32[8,128]{1,0:T(8,128)S(1)} %get-tuple-element.22.refs_1_.refs_3_.first_speed), custom_call_target="tpu_custom_call" | custom-call | flops 20000000 | bytes 1000000 | tf_op jit(solution)/shard_map/planes/pallas_call | solution.py:500
  52.2 0.9 %first_near.1 = (f32[5,4,32,128]{3,2,1,0:T(8,128)S(1)}, f32[5,3,32,128]{3,2,1,0:T(8,128)S(1)}, f32[8,128]{1,0:T(8,128)S(1)}) custom-call(f32[5,8,32,128]{3,2,1,0:T(8,128)S(1)} %get-tuple-element.21.refs_0_.state, f32[5,8,32,128]{3,2,1,0:T(8,128)S(1)} %planes.2.refs_1_, f32[5,3,32,128]{3,2,1,0:T(8,128)S(1)} %collective-permute-done.1.refs_2_, ...), custom_call_target="tpu_custom_call" | custom-call | flops 15000000 | bytes 2000000 | tf_op jit(solution)/shard_map/first_near/pallas_call | solution.py:585
  53.1 1.0 %first_far.1 = (f32[5,4,32,128]{3,2,1,0:T(8,128)S(1)}, f32[5,3,32,128]{3,2,1,0:T(8,128)S(1)}, f32[8,128]{1,0:T(8,128)S(1)}) custom-call(f32[5,8,32,128]{3,2,1,0:T(8,128)S(1)} %get-tuple-element.21.refs_0_.state, f32[5,8,32,128]{3,2,1,0:T(8,128)S(1)} %planes.2.refs_1_, f32[5,3,32,128]{3,2,1,0:T(8,128)S(1)} %collective-permute-done.refs_2_, ...), custom_call_target="tpu_custom_call" | custom-call | flops 15000000 | bytes 2000000 | tf_op jit(solution)/shard_map/first_far/pallas_call | solution.py:585
  54.2 0.8 %collective-permute-start.3 = (f32[8,128]{1,0:T(8,128)S(1)}, f32[8,128]{1,0:T(8,128)S(1)}, u32[]{:S(2)}, u32[]{:S(2)}) collective-permute-start(f32[8,128]{1,0:T(8,128)S(1)} %get-tuple-element.28), channel_id=1, source_target_pairs={{0,8},{1,9},{2,10},{3,11},{4,12},{5,13},{6,14},{7,15},{8,0},{9,1},... | collective-permute-start | bytes 12296 | tf_op jit(solution)/shard_map/ppermute | solution.py:647
  54.9 3.6 %collective-permute-start.2 = (f32[8,128]{1,0:T(8,128)S(1)}, f32[8,128]{1,0:T(8,128)S(1)}, u32[]{:S(2)}, u32[]{:S(2)}) collective-permute-start(f32[8,128]{1,0:T(8,128)S(1)} %get-tuple-element.28), channel_id=1, source_target_pairs={{0,12},{1,13},{2,14},{3,15},{4,8},{5,9},{6,10},{7,11},{8,4},{9,5},... | collective-permute-start | bytes 12296 | tf_op jit(solution)/shard_map/ppermute | solution.py:647
  58.5 1.4 %collective-permute-start.8 = (f32[5,3,32,128]{3,2,1,0:T(8,128)S(1)}, f32[5,3,32,128]{3,2,1,0:T(8,128)S(1)}, u32[]{:S(2)}, u32[]{:S(2)}) collective-permute-start(f32[5,3,32,128]{3,2,1,0:T(8,128)S(1)} %get-tuple-element.29), channel_id=1, source_target_pairs={{0,15},{1,2},{2,1},{3,4},{4,3},{5,6},{6,5},{7,8},{8,7},{9,10},{10,... | collective-permute-start | bytes 737288 | tf_op jit(solution)/shard_map/ppermute | solution.py:148
  60.0 0.4 collective-permute-done.2
  60.4 1.1 %collective-permute-start.7 = (f32[8,128]{1,0:T(8,128)S(1)}, f32[8,128]{1,0:T(8,128)S(1)}, u32[]{:S(2)}, u32[]{:S(2)}) collective-permute-start(f32[8,128]{1,0:T(8,128)S(1)} %maximum_maximum_fusion.1), channel_id=1, source_target_pairs={{0,3},{1,2},{2,1},{3,0},{4,7},{5,6},{6,5},{7,4},{8,11},{9,10},{10,... | collective-permute-start | bytes 12296 | tf_op jit(solution)/shard_map/ppermute | solution.py:647
  61.5 0.8 %collective-permute-start.6 = (f32[8,128]{1,0:T(8,128)S(1)}, f32[8,128]{1,0:T(8,128)S(1)}, u32[]{:S(2)}, u32[]{:S(2)}) collective-permute-start(f32[8,128]{1,0:T(8,128)S(1)} %maximum_maximum_fusion.1), channel_id=1, source_target_pairs={{0,2},{1,3},{2,0},{3,1},{4,6},{5,7},{6,4},{7,5},{8,10},{9,11},{10,... | collective-permute-start | bytes 12296 | tf_op jit(solution)/shard_map/ppermute | solution.py:647
  62.2 1.2 %collective-permute-done.7 = f32[8,128]{1,0:T(8,128)S(1)} collective-permute-done((f32[8,128]{1,0:T(8,128)S(1)}, f32[8,128]{1,0:T(8,128)S(1)}, u32[]{:S(2)}, u32[]{:S(2)}) %collective-permute-start.7) | collective-permute-done | bytes 4128 | tf_op jit(solution)/shard_map/ppermute | solution.py:647
  63.4 2.0 %collective-permute-done.6 = f32[8,128]{1,0:T(8,128)S(1)} collective-permute-done((f32[8,128]{1,0:T(8,128)S(1)}, f32[8,128]{1,0:T(8,128)S(1)}, u32[]{:S(2)}, u32[]{:S(2)}) %collective-permute-start.6) | collective-permute-done | bytes 4128 | tf_op jit(solution)/shard_map/ppermute | solution.py:647
  65.4 4.0 %planes.3.sides = f32[5,8,32,128]{3,2,1,0:T(8,128)S(1)} custom-call(f32[5,4,32,128]{3,2,1,0:T(8,128)S(1)} %get-tuple-element.26.refs_0_.middle_far, f32[5,4,32,128]{3,2,1,0:T(8,128)S(1)} %get-tuple-element.27.refs_1_.middle_near, f32[8,128]{1,0:T(8,128)S(1)} %maximum_maximum_fusion.refs_2_.speed), custom_call_target="tpu_custom_call" | custom-call | flops 20000000 | bytes 1000000 | tf_op jit(solution)/shard_map/planes/pallas_call | solution.py:500
  69.4 3.3 %second_stage.1 = f32[5,8,32,128]{3,2,1,0:T(8,128)} custom-call(f32[5,8,32,128]{3,2,1,0:T(8,128)S(1)} %get-tuple-element.21.refs_0_.state, f32[5,4,32,128]{3,2,1,0:T(8,128)S(1)} %get-tuple-element.26.refs_0_.middle_far, f32[5,4,32,128]{3,2,1,0:T(8,128)S(1)} %get-tuple-element.27.refs_1_.middle_near, f32[5,8,32,128]{3,2,1,0:T(8,128)S(1)} %planes.3.sides, ...), custom_call_target="tpu_custom_call" | custom-call | flops 30000000 | bytes 3000000 | tf_op jit(solution)/shard_map/second_stage/pallas_call | solution.py:626
  (19 shorter events, 0.1 us)
Async XLA Ops:
  2.7 7.4 %copy-start = (s32[1024]{0:T(1024)S(1)}, s32[1024]{0:T(1024)}, u32[]{:S(2)}) copy-start(s32[1024]{0:T(1024)} %owner_hbm.1) | copy-start | bytes 12292
  2.7 7.4 %copy-start.1 = (s32[1024]{0:T(1024)S(1)}, s32[1024]{0:T(1024)}, u32[]{:S(2)}) copy-start(s32[1024]{0:T(1024)} %param.5) | copy-start | bytes 12292
  2.7 34.9 %all-to-all-start = ((f32[16,161,1,128]{3,2,1,0:T(1,128)}), f32[16,161,1,128]{3,2,1,0:T(1,128)S(1)}, u32[]{:S(2)}, u32[]{:S(2)}) async-start(f32[16,161,1,128]{3,2,1,0:T(1,128)} %pack.1), calls=%async_computation | async-start | bytes 2637824 | tf_op jit(solution)/shard_map/all_to_all | solution.py:661
  40.2 12.0 %collective-permute-start.1 = (f32[5,3,32,128]{3,2,1,0:T(8,128)S(1)}, f32[5,3,32,128]{3,2,1,0:T(8,128)S(1)}, u32[]{:S(2)}, u32[]{:S(2)}) collective-permute-start(f32[5,3,32,128]{3,2,1,0:T(8,128)S(1)} %get-tuple-element.24), channel_id=1, source_target_pairs={{0,1},{1,0},{2,3},{3,2},{4,5},{5,4},{6,7},{7,6},{8,9},{9,8},{10,11... | collective-permute-start | bytes 737288 | tf_op jit(solution)/shard_map/ppermute | solution.py:152
  41.0 12.0 %collective-permute-start = (f32[5,3,32,128]{3,2,1,0:T(8,128)S(1)}, f32[5,3,32,128]{3,2,1,0:T(8,128)S(1)}, u32[]{:S(2)}, u32[]{:S(2)}) collective-permute-start(f32[5,3,32,128]{3,2,1,0:T(8,128)S(1)} %get-tuple-element.23), channel_id=1, source_target_pairs={{0,15},{1,2},{2,1},{3,4},{4,3},{5,6},{6,5},{7,8},{8,7},{9,10},{10,... | collective-permute-start | bytes 737288 | tf_op jit(solution)/shard_map/ppermute | solution.py:148
  54.1 5.9 %collective-permute-start.4 = (f32[8,128]{1,0:T(8,128)S(1)}, f32[8,128]{1,0:T(8,128)S(1)}, u32[]{:S(2)}, u32[]{:S(2)}) collective-permute-start(f32[8,128]{1,0:T(8,128)S(1)} %get-tuple-element.28), channel_id=1, source_target_pairs={{0,4},{1,5},{2,6},{3,7},{4,0},{5,1},{6,2},{7,3},{8,12},{9,13},{10,... | collective-permute-start | bytes 12296 | tf_op jit(solution)/shard_map/ppermute | solution.py:647
  54.2 5.8 %collective-permute-start.3 = (f32[8,128]{1,0:T(8,128)S(1)}, f32[8,128]{1,0:T(8,128)S(1)}, u32[]{:S(2)}, u32[]{:S(2)}) collective-permute-start(f32[8,128]{1,0:T(8,128)S(1)} %get-tuple-element.28), channel_id=1, source_target_pairs={{0,8},{1,9},{2,10},{3,11},{4,12},{5,13},{6,14},{7,15},{8,0},{9,1},... | collective-permute-start | bytes 12296 | tf_op jit(solution)/shard_map/ppermute | solution.py:647
  54.9 5.4 %collective-permute-start.2 = (f32[8,128]{1,0:T(8,128)S(1)}, f32[8,128]{1,0:T(8,128)S(1)}, u32[]{:S(2)}, u32[]{:S(2)}) collective-permute-start(f32[8,128]{1,0:T(8,128)S(1)} %get-tuple-element.28), channel_id=1, source_target_pairs={{0,12},{1,13},{2,14},{3,15},{4,8},{5,9},{6,10},{7,11},{8,4},{9,5},... | collective-permute-start | bytes 12296 | tf_op jit(solution)/shard_map/ppermute | solution.py:647
  58.5 10.9 %collective-permute-start.8 = (f32[5,3,32,128]{3,2,1,0:T(8,128)S(1)}, f32[5,3,32,128]{3,2,1,0:T(8,128)S(1)}, u32[]{:S(2)}, u32[]{:S(2)}) collective-permute-start(f32[5,3,32,128]{3,2,1,0:T(8,128)S(1)} %get-tuple-element.29), channel_id=1, source_target_pairs={{0,15},{1,2},{2,1},{3,4},{4,3},{5,6},{6,5},{7,8},{8,7},{9,10},{10,... | collective-permute-start | bytes 737288 | tf_op jit(solution)/shard_map/ppermute | solution.py:148
  60.0 9.4 %collective-permute-start.9 = (f32[5,3,32,128]{3,2,1,0:T(8,128)S(1)}, f32[5,3,32,128]{3,2,1,0:T(8,128)S(1)}, u32[]{:S(2)}, u32[]{:S(2)}) collective-permute-start(f32[5,3,32,128]{3,2,1,0:T(8,128)S(1)} %get-tuple-element.30), channel_id=1, source_target_pairs={{0,1},{1,0},{2,3},{3,2},{4,5},{5,4},{6,7},{7,6},{8,9},{9,8},{10,11... | collective-permute-start | bytes 737288 | tf_op jit(solution)/shard_map/ppermute | solution.py:152
  60.4 3.0 %collective-permute-start.7 = (f32[8,128]{1,0:T(8,128)S(1)}, f32[8,128]{1,0:T(8,128)S(1)}, u32[]{:S(2)}, u32[]{:S(2)}) collective-permute-start(f32[8,128]{1,0:T(8,128)S(1)} %maximum_maximum_fusion.1), channel_id=1, source_target_pairs={{0,3},{1,2},{2,1},{3,0},{4,7},{5,6},{6,5},{7,4},{8,11},{9,10},{10,... | collective-permute-start | bytes 12296 | tf_op jit(solution)/shard_map/ppermute | solution.py:647
  61.5 4.0 %collective-permute-start.6 = (f32[8,128]{1,0:T(8,128)S(1)}, f32[8,128]{1,0:T(8,128)S(1)}, u32[]{:S(2)}, u32[]{:S(2)}) collective-permute-start(f32[8,128]{1,0:T(8,128)S(1)} %maximum_maximum_fusion.1), channel_id=1, source_target_pairs={{0,2},{1,3},{2,0},{3,1},{4,6},{5,7},{6,4},{7,5},{8,10},{9,11},{10,... | collective-permute-start | bytes 12296 | tf_op jit(solution)/shard_map/ppermute | solution.py:647
  62.2 3.2 %collective-permute-start.5 = (f32[8,128]{1,0:T(8,128)S(1)}, f32[8,128]{1,0:T(8,128)S(1)}, u32[]{:S(2)}, u32[]{:S(2)}) collective-permute-start(f32[8,128]{1,0:T(8,128)S(1)} %maximum_maximum_fusion.1), channel_id=1, source_target_pairs={{0,1},{1,0},{2,3},{3,2},{4,5},{5,4},{6,7},{7,6},{8,9},{9,8},{10,11... | collective-permute-start | bytes 12296 | tf_op jit(solution)/shard_map/ppermute | solution.py:647

commit v28 on v27

--- a/solution.py
+++ b/solution.py
@@ -640,7 +640,7 @@
         reach *= 4
     while reach:
         copies = [value]
-        for times in (3, 2, 1) if reach > 1 else (1, 2, 3):
+        for times in (1, 2, 3) if reach > 1 else (3, 2, 1):
             turn = reach * times
             if turn < size:
                 pairs = [(i, i ^ turn) for i in range(size)]

time: 72.9 us -> 72.5 us (level)
  no operation moved by 1% of the time
where the time goes in v28:
time: 72.5 us; the launch traced here: 72.3 us
  waiting for transfers between devices  29.9 us (41%)
  starting transfers between devices  22 us (30%)
  Pallas kernels  19.5 us (27%)
    all_to_all x1, waiting for transfers between devices, per_device(): come = lax.all_to_all(parts, 'gx', split_axis=0, concat_axis=0, tiled=True)  26.8 us
    pallas_call x2, Pallas kernels, along_planes(): pl.pallas_call(functools.partial(plane_kernel, with_inner), out_shape=jax...  9.11 us
    ppermute x2, starting transfers between devices, from_far(): return lax.ppermute(far_side, 'gx', pairs)  7.44 us
    all_to_all x1, starting transfers between devices, per_device(): come = lax.all_to_all(parts, 'gx', split_axis=0, concat_axis=0, tiled=True)  7.37 us
    ppermute x6, starting transfers between devices, everyone_max(): copies.append(lax.ppermute(value, axis, pairs))  6.33 us
    pallas_call x1, Pallas kernels, second_stage(): pl.pallas_call(second_kernel, out_shape=jax.ShapeDtypeStruct((FIELDS, BLO...  3.27 us
    ppermute x6, waiting for transfers between devices, everyone_max(): copies.append(lax.ppermute(value, axis, pairs))  3.13 us
    pallas_call x1, Pallas kernels, pack(): pl.pallas_call(functools.partial(pack_kernel, size, cap, per_dev), out_sh...  2.7 us
  transfers between devices with their start and end apart: 11, of which 4 were waited for; matrix products, arithmetic and copies ran while one was open for 1% of the time, Pallas kernels for 14%

profile of v28, /device:TPU:0, one launch (start us, length us, event | category | flops | bytes accessed | tf_op | source)
XLA Modules:
  0.0 72.3 jit_solution(5435164761705862560)
XLA Ops:
  0.0 2.7 %pack.1 = f32[16,161,1,128]{3,2,1,0:T(1,128)} custom-call(s32[1024]{0:T(1024)} %owner_hbm.1, f32[1280,1,128]{2,1,0:T(1,128)} %bitcast.7), custom_call_target="tpu_custom_call" | custom-call | flops 1000000 | bytes 3000000 | tf_op jit(solution)/shard_map/pack/pallas_call | solution.py:113
  2.7 7.4 %all-to-all-start = ((f32[16,161,1,128]{3,2,1,0:T(1,128)}), f32[16,161,1,128]{3,2,1,0:T(1,128)S(1)}, u32[]{:S(2)}, u32[]{:S(2)}) async-start(f32[16,161,1,128]{3,2,1,0:T(1,128)} %pack.1), calls=%async_computation | async-start | bytes 2637824 | tf_op jit(solution)/shard_map/all_to_all | solution.py:661
  10.1 0.1 eq.33
  10.2 0.3 convert_reduce_fusion
  10.7 0.1 select_reduce_fusion.table
  10.9 26.8 %all-to-all-done = f32[16,161,1,128]{3,2,1,0:T(1,128)S(1)} async-done(((f32[16,161,1,128]{3,2,1,0:T(1,128)}), f32[16,161,1,128]{3,2,1,0:T(1,128)S(1)}, u32[]{:S(2)}, u32[]{:S(2)}) %all-to-all-start) | async-done | bytes 1318944 | tf_op jit(solution)/shard_map/all_to_all | solution.py:661
  37.7 2.5 %unpack.1 = (f32[5,8,32,128]{3,2,1,0:T(8,128)S(1)}, f32[5,3,32,128]{3,2,1,0:T(8,128)S(1)}, f32[5,3,32,128]{3,2,1,0:T(8,128)S(1)}, f32[8,128]{1,0:T(8,128)S(1)}) custom-call(s32[64]{0:T(128)S(1)} %select_reduce_fusion.table, f32[2576,1,128]{2,1,0:T(1,128)S(1)} %bitcast.6), custom_call_target="tpu_custom_call" | custom-call | flops 5000000 | bytes 2000000 | tf_op jit(solution)/shard_map/unpack/pallas_call | solution.py:237
  40.2 0.8 %collective-permute-start.1 = (f32[5,3,32,128]{3,2,1,0:T(8,128)S(1)}, f32[5,3,32,128]{3,2,1,0:T(8,128)S(1)}, u32[]{:S(2)}, u32[]{:S(2)}) collective-permute-start(f32[5,3,32,128]{3,2,1,0:T(8,128)S(1)} %get-tuple-element.24), channel_id=1, source_target_pairs={{0,1},{1,0},{2,3},{3,2},{4,5},{5,4},{6,7},{7,6},{8,9},{9,8},{10,11... | collective-permute-start | bytes 737288 | tf_op jit(solution)/shard_map/ppermute | solution.py:152
  41.0 6.0 %collective-permute-start = (f32[5,3,32,128]{3,2,1,0:T(8,128)S(1)}, f32[5,3,32,128]{3,2,1,0:T(8,128)S(1)}, u32[]{:S(2)}, u32[]{:S(2)}) collective-permute-start(f32[5,3,32,128]{3,2,1,0:T(8,128)S(1)} %get-tuple-element.23), channel_id=1, source_target_pairs={{0,15},{1,2},{2,1},{3,4},{4,3},{5,6},{6,5},{7,8},{8,7},{9,10},{10,... | collective-permute-start | bytes 737288 | tf_op jit(solution)/shard_map/ppermute | solution.py:148
  47.0 5.1 %planes.2.refs_1_ = f32[5,8,32,128]{3,2,1,0:T(8,128)S(1)} custom-call(f32[5,8,32,128]{3,2,1,0:T(8,128)S(1)} %get-tuple-element.21.refs_0_.state, f32[8,128]{1,0:T(8,128)S(1)} %get-tuple-element.22.refs_1_.refs_3_.first_speed), custom_call_target="tpu_custom_call" | custom-call | flops 20000000 | bytes 1000000 | tf_op jit(solution)/shard_map/planes/pallas_call | solution.py:500
  52.2 0.9 %first_near.1 = (f32[5,4,32,128]{3,2,1,0:T(8,128)S(1)}, f32[5,3,32,128]{3,2,1,0:T(8,128)S(1)}, f32[8,128]{1,0:T(8,128)S(1)}) custom-call(f32[5,8,32,128]{3,2,1,0:T(8,128)S(1)} %get-tuple-element.21.refs_0_.state, f32[5,8,32,128]{3,2,1,0:T(8,128)S(1)} %planes.2.refs_1_, f32[5,3,32,128]{3,2,1,0:T(8,128)S(1)} %collective-permute-done.1.refs_2_, ...), custom_call_target="tpu_custom_call" | custom-call | flops 15000000 | bytes 2000000 | tf_op jit(solution)/shard_map/first_near/pallas_call | solution.py:585
  53.1 1.0 %first_far.1 = (f32[5,4,32,128]{3,2,1,0:T(8,128)S(1)}, f32[5,3,32,128]{3,2,1,0:T(8,128)S(1)}, f32[8,128]{1,0:T(8,128)S(1)}) custom-call(f32[5,8,32,128]{3,2,1,0:T(8,128)S(1)} %get-tuple-element.21.refs_0_.state, f32[5,8,32,128]{3,2,1,0:T(8,128)S(1)} %planes.2.refs_1_, f32[5,3,32,128]{3,2,1,0:T(8,128)S(1)} %collective-permute-done.refs_2_, ...), custom_call_target="tpu_custom_call" | custom-call | flops 15000000 | bytes 2000000 | tf_op jit(solution)/shard_map/first_far/pallas_call | solution.py:585
  54.1 0.3 collective-permute-start.4
  54.4 0.5 collective-permute-start.3
  54.9 3.6 %collective-permute-start.2 = (f32[8,128]{1,0:T(8,128)S(1)}, f32[8,128]{1,0:T(8,128)S(1)}, u32[]{:S(2)}, u32[]{:S(2)}) collective-permute-start(f32[8,128]{1,0:T(8,128)S(1)} %get-tuple-element.28), channel_id=1, source_target_pairs={{0,4},{1,5},{2,6},{3,7},{4,0},{5,1},{6,2},{7,3},{8,12},{9,13},{10,... | collective-permute-start | bytes 12296 | tf_op jit(solution)/shard_map/ppermute | solution.py:647
  58.5 1.4 %collective-permute-start.8 = (f32[5,3,32,128]{3,2,1,0:T(8,128)S(1)}, f32[5,3,32,128]{3,2,1,0:T(8,128)S(1)}, u32[]{:S(2)}, u32[]{:S(2)}) collective-permute-start(f32[5,3,32,128]{3,2,1,0:T(8,128)S(1)} %get-tuple-element.29), channel_id=1, source_target_pairs={{0,15},{1,2},{2,1},{3,4},{4,3},{5,6},{6,5},{7,8},{8,7},{9,10},{10,... | collective-permute-start | bytes 737288 | tf_op jit(solution)/shard_map/ppermute | solution.py:148
  60.0 0.1 collective-permute-done.2
  60.1 0.4 collective-permute-start.7
  60.6 0.9 %collective-permute-start.6 = (f32[8,128]{1,0:T(8,128)S(1)}, f32[8,128]{1,0:T(8,128)S(1)}, u32[]{:S(2)}, u32[]{:S(2)}) collective-permute-start(f32[8,128]{1,0:T(8,128)S(1)} %maximum_maximum_fusion.1), channel_id=1, source_target_pairs={{0,2},{1,3},{2,0},{3,1},{4,6},{5,7},{6,4},{7,5},{8,10},{9,11},{10,... | collective-permute-start | bytes 12296 | tf_op jit(solution)/shard_map/ppermute | solution.py:647
  61.5 0.6 collective-permute-start.5
  62.0 2.2 %collective-permute-done.6 = f32[8,128]{1,0:T(8,128)S(1)} collective-permute-done((f32[8,128]{1,0:T(8,128)S(1)}, f32[8,128]{1,0:T(8,128)S(1)}, u32[]{:S(2)}, u32[]{:S(2)}) %collective-permute-start.6) | collective-permute-done | bytes 4128 | tf_op jit(solution)/shard_map/ppermute | solution.py:647
  64.2 0.8 %collective-permute-done.5 = f32[8,128]{1,0:T(8,128)S(1)} collective-permute-done((f32[8,128]{1,0:T(8,128)S(1)}, f32[8,128]{1,0:T(8,128)S(1)}, u32[]{:S(2)}, u32[]{:S(2)}) %collective-permute-start.5) | collective-permute-done | bytes 4128 | tf_op jit(solution)/shard_map/ppermute | solution.py:647
  65.0 4.0 %planes.3.sides = f32[5,8,32,128]{3,2,1,0:T(8,128)S(1)} custom-call(f32[5,4,32,128]{3,2,1,0:T(8,128)S(1)} %get-tuple-element.26.refs_0_.middle_far, f32[5,4,32,128]{3,2,1,0:T(8,128)S(1)} %get-tuple-element.27.refs_1_.middle_near, f32[8,128]{1,0:T(8,128)S(1)} %maximum_maximum_fusion.refs_2_.speed), custom_call_target="tpu_custom_call" | custom-call | flops 20000000 | bytes 1000000 | tf_op jit(solution)/shard_map/planes/pallas_call | solution.py:500
  69.0 3.3 %second_stage.1 = f32[5,8,32,128]{3,2,1,0:T(8,128)} custom-call(f32[5,8,32,128]{3,2,1,0:T(8,128)S(1)} %get-tuple-element.21.refs_0_.state, f32[5,4,32,128]{3,2,1,0:T(8,128)S(1)} %get-tuple-element.26.refs_0_.middle_far, f32[5,4,32,128]{3,2,1,0:T(8,128)S(1)} %get-tuple-element.27.refs_1_.middle_near, f32[5,8,32,128]{3,2,1,0:T(8,128)S(1)} %planes.3.sides, ...), custom_call_target="tpu_custom_call" | custom-call | flops 30000000 | bytes 3000000 | tf_op jit(solution)/shard_map/second_stage/pallas_call | solution.py:626
  (19 shorter events, 0.2 us)
Async XLA Ops:
  2.7 7.4 %copy-start = (s32[1024]{0:T(1024)S(1)}, s32[1024]{0:T(1024)}, u32[]{:S(2)}) copy-start(s32[1024]{0:T(1024)} %owner_hbm.1) | copy-start | bytes 12292
  2.7 7.4 %copy-start.1 = (s32[1024]{0:T(1024)S(1)}, s32[1024]{0:T(1024)}, u32[]{:S(2)}) copy-start(s32[1024]{0:T(1024)} %param.5) | copy-start | bytes 12292
  2.7 34.9 %all-to-all-start = ((f32[16,161,1,128]{3,2,1,0:T(1,128)}), f32[16,161,1,128]{3,2,1,0:T(1,128)S(1)}, u32[]{:S(2)}, u32[]{:S(2)}) async-start(f32[16,161,1,128]{3,2,1,0:T(1,128)} %pack.1), calls=%async_computation | async-start | bytes 2637824 | tf_op jit(solution)/shard_map/all_to_all | solution.py:661
  40.2 12.0 %collective-permute-start.1 = (f32[5,3,32,128]{3,2,1,0:T(8,128)S(1)}, f32[5,3,32,128]{3,2,1,0:T(8,128)S(1)}, u32[]{:S(2)}, u32[]{:S(2)}) collective-permute-start(f32[5,3,32,128]{3,2,1,0:T(8,128)S(1)} %get-tuple-element.24), channel_id=1, source_target_pairs={{0,1},{1,0},{2,3},{3,2},{4,5},{5,4},{6,7},{7,6},{8,9},{9,8},{10,11... | collective-permute-start | bytes 737288 | tf_op jit(solution)/shard_map/ppermute | solution.py:152
  41.0 12.0 %collective-permute-start = (f32[5,3,32,128]{3,2,1,0:T(8,128)S(1)}, f32[5,3,32,128]{3,2,1,0:T(8,128)S(1)}, u32[]{:S(2)}, u32[]{:S(2)}) collective-permute-start(f32[5,3,32,128]{3,2,1,0:T(8,128)S(1)} %get-tuple-element.23), channel_id=1, source_target_pairs={{0,15},{1,2},{2,1},{3,4},{4,3},{5,6},{6,5},{7,8},{8,7},{9,10},{10,... | collective-permute-start | bytes 737288 | tf_op jit(solution)/shard_map/ppermute | solution.py:148
  54.1 5.9 %collective-permute-start.4 = (f32[8,128]{1,0:T(8,128)S(1)}, f32[8,128]{1,0:T(8,128)S(1)}, u32[]{:S(2)}, u32[]{:S(2)}) collective-permute-start(f32[8,128]{1,0:T(8,128)S(1)} %get-tuple-element.28), channel_id=1, source_target_pairs={{0,12},{1,13},{2,14},{3,15},{4,8},{5,9},{6,10},{7,11},{8,4},{9,5},... | collective-permute-start | bytes 12296 | tf_op jit(solution)/shard_map/ppermute | solution.py:647
  54.4 5.6 %collective-permute-start.3 = (f32[8,128]{1,0:T(8,128)S(1)}, f32[8,128]{1,0:T(8,128)S(1)}, u32[]{:S(2)}, u32[]{:S(2)}) collective-permute-start(f32[8,128]{1,0:T(8,128)S(1)} %get-tuple-element.28), channel_id=1, source_target_pairs={{0,8},{1,9},{2,10},{3,11},{4,12},{5,13},{6,14},{7,15},{8,0},{9,1},... | collective-permute-start | bytes 12296 | tf_op jit(solution)/shard_map/ppermute | solution.py:647
  54.9 5.2 %collective-permute-start.2 = (f32[8,128]{1,0:T(8,128)S(1)}, f32[8,128]{1,0:T(8,128)S(1)}, u32[]{:S(2)}, u32[]{:S(2)}) collective-permute-start(f32[8,128]{1,0:T(8,128)S(1)} %get-tuple-element.28), channel_id=1, source_target_pairs={{0,4},{1,5},{2,6},{3,7},{4,0},{5,1},{6,2},{7,3},{8,12},{9,13},{10,... | collective-permute-start | bytes 12296 | tf_op jit(solution)/shard_map/ppermute | solution.py:647
  58.5 10.5 %collective-permute-start.8 = (f32[5,3,32,128]{3,2,1,0:T(8,128)S(1)}, f32[5,3,32,128]{3,2,1,0:T(8,128)S(1)}, u32[]{:S(2)}, u32[]{:S(2)}) collective-permute-start(f32[5,3,32,128]{3,2,1,0:T(8,128)S(1)} %get-tuple-element.29), channel_id=1, source_target_pairs={{0,15},{1,2},{2,1},{3,4},{4,3},{5,6},{6,5},{7,8},{8,7},{9,10},{10,... | collective-permute-start | bytes 737288 | tf_op jit(solution)/shard_map/ppermute | solution.py:148
  60.0 9.0 %collective-permute-start.9 = (f32[5,3,32,128]{3,2,1,0:T(8,128)S(1)}, f32[5,3,32,128]{3,2,1,0:T(8,128)S(1)}, u32[]{:S(2)}, u32[]{:S(2)}) collective-permute-start(f32[5,3,32,128]{3,2,1,0:T(8,128)S(1)} %get-tuple-element.30), channel_id=1, source_target_pairs={{0,1},{1,0},{2,3},{3,2},{4,5},{5,4},{6,7},{7,6},{8,9},{9,8},{10,11... | collective-permute-start | bytes 737288 | tf_op jit(solution)/shard_map/ppermute | solution.py:152
  60.1 1.9 %collective-permute-start.7 = (f32[8,128]{1,0:T(8,128)S(1)}, f32[8,128]{1,0:T(8,128)S(1)}, u32[]{:S(2)}, u32[]{:S(2)}) collective-permute-start(f32[8,128]{1,0:T(8,128)S(1)} %maximum_maximum_fusion.1), channel_id=1, source_target_pairs={{0,1},{1,0},{2,3},{3,2},{4,5},{5,4},{6,7},{7,6},{8,9},{9,8},{10,11... | collective-permute-start | bytes 12296 | tf_op jit(solution)/shard_map/ppermute | solution.py:647
  60.6 3.6 %collective-permute-start.6 = (f32[8,128]{1,0:T(8,128)S(1)}, f32[8,128]{1,0:T(8,128)S(1)}, u32[]{:S(2)}, u32[]{:S(2)}) collective-permute-start(f32[8,128]{1,0:T(8,128)S(1)} %maximum_maximum_fusion.1), channel_id=1, source_target_pairs={{0,2},{1,3},{2,0},{3,1},{4,6},{5,7},{6,4},{7,5},{8,10},{9,11},{10,... | collective-permute-start | bytes 12296 | tf_op jit(solution)/shard_map/ppermute | solution.py:647
  61.5 3.5 %collective-permute-start.5 = (f32[8,128]{1,0:T(8,128)S(1)}, f32[8,128]{1,0:T(8,128)S(1)}, u32[]{:S(2)}, u32[]{:S(2)}) collective-permute-start(f32[8,128]{1,0:T(8,128)S(1)} %maximum_maximum_fusion.1), channel_id=1, source_target_pairs={{0,3},{1,2},{2,1},{3,0},{4,7},{5,6},{6,5},{7,4},{8,11},{9,10},{10,... | collective-permute-start | bytes 12296 | tf_op jit(solution)/shard_map/ppermute | solution.py:647
